TPU v7x, 32 devices: a whole 2x2x4 slice. The times are simulated.
32 devices in a mesh: grp: 2 (over y), exp: 4 (over z), dp: 4 (over x, core).
Axes of the slice: x: 2, y: 2, z: 4, core: 2. Of those that a mesh axis runs over, the one named last changes fastest.
Arguments:
- layer_inflows: bfloat16 [4096, 4096], P(('grp', 'exp', 'dp')), parts along dimension 0, may hold values from -6 to 6
- output_derivatives: bfloat16 [4096, 4096], P(('grp', 'exp', 'dp')), parts along dimension 0, may hold values from -6 to 6
- picked_specialists: int32 [4096, 8], P(('grp', 'exp', 'dp')), parts along dimension 0, may hold values from 0 to 127, as said below
- dispatch_shares: float32 [4096, 8], P(('grp', 'exp', 'dp')), parts along dimension 0, may hold values from 0.05 to 1
- item_sample: int32 [4096], P(('grp', 'exp', 'dp')), parts along dimension 0, may hold values from 0 to 7, as said below
- send_limits: int32 [256], P('grp'), parts along dimension 0, may hold values from 6 to 12, as said below
- gating_projection: bfloat16 [4, 4096, 768], P('exp', None, 'dp'), may hold values from -0.09375 to 0.09375
- raising_projection: bfloat16 [4, 4096, 768], P('exp', None, 'dp'), may hold values from -0.09375 to 0.09375
- inflow_compressor: bfloat16 [768, 64], replicated, may hold values from -0.21875 to 0.21875
- outgrad_compressor: bfloat16 [4096, 64], replicated, may hold values from -0.09375 to 0.09375
Outputs:
- sketches: float32 [16, 4, 4096], P(('grp', 'dp'), 'exp'), parts along dimension 0
There are 2 independent parts, one for each index of `grp`. A program takes and returns all parts, laid end to end along the dimension named above; an argument that names none is the same for every part. Nothing has to cross between parts.
Inputs may be any that keep to these rules, and one draw needn't show every extreme that they name: `picked_specialists`: each row names 8 different experts; for some expert below 4 whose capacity is 12, every aligned block of 128 rows names it in 12 rows or more. `item_sample`: tokens held by dp index j belong to examples j * 2 to (j + 1) * 2 - 1; along the tokens of that index in exp order the example never falls, and every example has a token. `send_limits`: some expert below 4 has capacity exactly 12.
All inputs are finite; a program needn't handle non-finite values.
Results may differ from a plain program's by a relative error of at most 0.0085.
Values may be sent and summed in bfloat16 or wider, within the bound.
No kernel may reach another device: no remote copies, remote signals or barrier semaphores. Data moves between devices by JAX's collectives and lax.ppermute only.
A program may use at most 64 MiB of HBM per device.

v0:
```python
import jax
import jax.numpy as jnp
from jax import lax
from jax.sharding import PartitionSpec as P

EX_DEV = 2
LOCAL_SEATS = 12


def placement_lookup(dispatch_group, send_limits, compressed_specialists, occupied_total):
    flat_ids = dispatch_group.reshape(-1)
    experts = lax.broadcasted_iota(jnp.int32, (1, compressed_specialists), 1)
    equality_flags = (flat_ids[:, None] == experts).astype(jnp.int32)
    earlier = jnp.cumsum(equality_flags, axis=0) - equality_flags
    position = jnp.sum(earlier * equality_flags, axis=1)
    allowance_flags = jnp.sum(
        equality_flags * send_limits[:compressed_specialists][None, :], axis=1
    )
    accepted = (flat_ids < compressed_specialists) & (position < allowance_flags)
    target = jnp.where(
        accepted, flat_ids * occupied_total + position, compressed_specialists * occupied_total
    )
    pair_ids = jnp.arange(flat_ids.shape[0], dtype=jnp.int32)
    blank_slots = jnp.full((compressed_specialists * occupied_total,), flat_ids.shape[0], jnp.int32)
    return blank_slots.at[target].set(pair_ids, mode="drop")


def body(
    layer_inflows,
    output_derivatives,
    picked_specialists,
    dispatch_shares,
    item_sample,
    send_limits,
    gating_projection,
    raising_projection,
    inflow_compressor,
    outgrad_compressor,
):
    compressed_specialists = lax.axis_size("exp")
    per_device, routes_per = picked_specialists.shape
    model_width = layer_inflows.shape[1]
    sketch_width = outgrad_compressor.shape[1]
    occupied_couples = placement_lookup(
        picked_specialists, send_limits, compressed_specialists, LOCAL_SEATS
    )
    occupied = occupied_couples < per_device * routes_per
    token_slot = occupied_couples // routes_per
    grad_proj = jnp.dot(output_derivatives, outgrad_compressor, preferred_element_type=jnp.float32)
    grad_pairs = (dispatch_shares[:, :, None] * grad_proj[:, None, :]).astype(jnp.bfloat16)
    grad_pairs = grad_pairs.reshape(per_device * routes_per, sketch_width)
    grad_pairs = jnp.concatenate([grad_pairs, jnp.zeros((1, sketch_width), jnp.bfloat16)], axis=0)
    grad_buffer = grad_pairs[occupied_couples].reshape(
        compressed_specialists, LOCAL_SEATS, sketch_width
    )
    padded_tokens = jnp.concatenate(
        [layer_inflows, jnp.zeros((1, model_width), jnp.bfloat16)], axis=0
    )
    token_buffer = padded_tokens[token_slot].reshape(
        compressed_specialists, LOCAL_SEATS, model_width
    )
    owners = item_sample - lax.axis_index("dp") * EX_DEV
    padded_owners = jnp.concatenate([owners, jnp.zeros((1,), jnp.int32)], axis=0)
    owner_slots = jnp.where(occupied, padded_owners[token_slot], 0).reshape(
        compressed_specialists, LOCAL_SEATS
    )
    gate_full, up_full = (
        lax.all_gather(gating_projection, "dp", axis=2, tiled=True),
        lax.all_gather(raising_projection, "dp", axis=2, tiled=True),
    )
    row_block = lax.all_to_all(token_buffer, "exp", split_axis=0, concat_axis=0, tiled=True)
    sources = row_block.shape[0]
    amount = row_block.shape[1]
    flat_rows = row_block.reshape(-1, model_width)
    gate_pre = jnp.dot(flat_rows, gate_full[0], preferred_element_type=jnp.float32)
    up_pre = jnp.dot(flat_rows, up_full[0], preferred_element_type=jnp.float32)
    hidden = (jax.nn.silu(gate_pre) * up_pre).astype(jnp.bfloat16)
    sketch_rows = jnp.dot(hidden, inflow_compressor, preferred_element_type=jnp.float32).astype(
        jnp.bfloat16
    )
    returned = lax.all_to_all(
        sketch_rows.reshape(sources, amount, sketch_width),
        "exp",
        split_axis=0,
        concat_axis=0,
        tiled=True,
    )
    selector = owner_slots[:, :, None] == jnp.arange(EX_DEV, dtype=jnp.int32)[None, None, :]
    weighted_all = jnp.where(
        selector[..., None], returned[:, :, None, :], jnp.zeros((), jnp.bfloat16)
    )
    weighted_all = weighted_all.reshape(compressed_specialists, LOCAL_SEATS, EX_DEV * sketch_width)
    partial_value = jnp.einsum(
        "ecm,ecb->emb", weighted_all, grad_buffer, preferred_element_type=jnp.float32
    )
    reduced = lax.psum_scatter(
        partial_value.reshape(1 * lax.axis_size("exp"), EX_DEV, sketch_width * sketch_width).astype(
            jnp.bfloat16
        ),
        "exp",
        scatter_dimension=0,
        tiled=True,
    ).astype(jnp.float32)
    sketches = jnp.transpose(reduced, (1, 0, 2))
    return sketches


def solution(mesh):
    in_specs = (
        P(("grp", "exp", "dp"), None),
        P(("grp", "exp", "dp"), None),
        P(("grp", "exp", "dp"), None),
        P(("grp", "exp", "dp"), None),
        P(("grp", "exp", "dp")),
        P("grp"),
        P("exp", None, "dp"),
        P("exp", None, "dp"),
        P(),
        P(),
    )
    out_specs = P(("grp", "dp"), "exp", None)
    return jax.shard_map(body, mesh=mesh, in_specs=in_specs, out_specs=out_specs, check_vma=False)
```

profile of v0, /device:TPU:0, one launch (start us, length us, event | category | flops | bytes accessed | tf_op | source)
XLA Modules:
  0.0 163.3 jit_solution(11225354423096714603)
XLA Ops:
  6.6 0.7 all-gather.3.cloned.1.call-update
  7.3 0.7 all-gather.5.cloned.1.call-update
  8.0 0.8 copy.24
  8.8 0.1 eq.48
  8.9 0.1 eq.44
  9.0 1.1 reduce-window.6
  10.2 0.2 slice_reduce_fusion
  10.4 0.2 reduce-window.9
  10.6 0.7 broadcast_multiply_fusion
  11.3 0.1 copy.26
  11.4 0.1 mul.60
  11.5 0.7 broadcast_compare_fusion
  12.1 0.1 copy.23
  12.3 0.1 lt.49
  12.4 1.3 concatenate.10
  13.8 0.7 select_reduce_fusion
  14.6 4.3 %scatter_custom_fusion = s32[48]{0:T(128)S(1)} fusion(s32[1024]{0:T(1024)S(1)} %bitcast.56, s32[1024]{0:T(1024)S(1)} %iota.17, s32[]{:T(128)} %constant.16.clone.1), kind=kCustom, calls=%fused_computation.50 | custom fusion | bytes 196 | tf_op jit(solution)/shard_map/scatter | solution.py:25
  18.9 0.8 gather_fusion.1
  19.7 0.9 reshape.102
  20.6 6.3 %all-to-all-start = ((bf16[4,12,4096]{2,1,0:T(8,128)(2,1)}), bf16[4,12,4096]{2,1,0:T(8,128)(2,1)S(1)}, u32[]{:S(2)}, u32[]{:S(2)}) async-start(bf16[4,12,4096]{2,1,0:T(8,128)(2,1)} %reshape.102), calls=%async_computation | async-start | bytes 1048576 | tf_op jit(solution)/shard_map/all_to_all | solution.py:71
  27.0 0.8 gather_fusion
  27.8 0.1 eq.52
  27.9 0.1 copy.27
  28.0 0.1 iota_compare_fusion
  28.1 0.1 copy.29
  28.2 0.1 mul.64
  28.3 0.4 fusion.31
  28.7 0.2 fusion.16
  28.9 12.5 %all-to-all-done = bf16[4,12,4096]{2,1,0:T(8,128)(2,1)S(1)} async-done(((bf16[4,12,4096]{2,1,0:T(8,128)(2,1)}), bf16[4,12,4096]{2,1,0:T(8,128)(2,1)S(1)}, u32[]{:S(2)}, u32[]{:S(2)}) %all-to-all-start) | async-done | bytes 393248 | tf_op jit(solution)/shard_map/all_to_all | solution.py:71
  41.4 0.1 reshape.103
  41.6 16.5 %all-gather.3.cloned.1.call-done = bf16[1,4096,768]{1,2,0:T(8,128)(2,1)} async-done(((bf16[1,4096,192]{1,2,0:T(8,128)(2,1)}), bf16[1,4096,768]{1,2,0:T(8,128)(2,1)}) %all-gather.3.cloned.1.call-update) | async-done | bytes 6291472 | tf_op jit(solution)/shard_map/all_gather | solution.py:68
  58.1 4.8 %fusion.2 = f32[48,768]{1,0:T(8,128)S(1)} fusion(bf16[48,4096]{1,0:T(8,128)(2,1)S(1)} %reshape.103, bf16[1,4096,768]{1,2,0:T(8,128)(2,1)} %all-gather.3.cloned.1.call-done), kind=kOutput, calls=%fused_computation.6 | convolution fusion | flops 301989888 | bytes 6832128 | tf_op jit(solution)/shard_map/dot_general | solution.py:75
  62.9 43.2 %all-gather.5.cloned.1.call-done = bf16[1,4096,768]{1,2,0:T(8,128)(2,1)} async-done(((bf16[1,4096,192]{1,2,0:T(8,128)(2,1)}), bf16[1,4096,768]{1,2,0:T(8,128)(2,1)}) %all-gather.5.cloned.1.call-update) | async-done | bytes 6291472 | tf_op jit(solution)/shard_map/all_gather | solution.py:69
  106.0 4.9 %fusion.13 = bf16[48,64]{1,0:T(8,128)(2,1)S(1)} fusion(bf16[768,64]{0,1:T(8,128)(2,1)S(1)} %copy-done.2, bf16[48,4096]{1,0:T(8,128)(2,1)S(1)} %reshape.103, bf16[1,4096,768]{1,2,0:T(8,128)(2,1)} %all-gather.5.cloned.1.call-done, f32[48,768]{1,0:T(8,128)S(1)} %fusion.2), kind=kOutput, calls=%fused_computation.12 | convolution fusion | flops 306932736 | bytes 6936576 | tf_op jit(solution)/shard_map/dot_general | solution.py:78
  111.0 0.7 reshape.146
  111.7 4.6 %all-to-all-start.1 = ((bf16[4,2,384]{2,1,0:T(2,128)(2,1)}), bf16[4,2,384]{2,1,0:T(2,128)(2,1)S(1)}, u32[]{:S(2)}, u32[]{:S(2)}) async-start(bf16[4,2,384]{2,1,0:T(2,128)(2,1)} %reshape.146), calls=%async_computation.1 | async-start | bytes 12288 | tf_op jit(solution)/shard_map/all_to_all | solution.py:81
  116.3 0.6 gather_fusion.2
  117.0 4.9 %all-to-all-done.1 = bf16[4,2,384]{2,1,0:T(2,128)(2,1)S(1)} async-done(((bf16[4,2,384]{2,1,0:T(2,128)(2,1)}), bf16[4,2,384]{2,1,0:T(2,128)(2,1)S(1)}, u32[]{:S(2)}, u32[]{:S(2)}) %all-to-all-start.1) | async-done | bytes 6176 | tf_op jit(solution)/shard_map/all_to_all | solution.py:81
  121.9 0.1 reshape.147
  121.9 0.1 broadcast_select_fusion
  122.1 0.1 select_n.51
  122.2 0.2 convolution_convert_fusion
  122.4 0.1 copy.32
  122.5 0.8 convert_element_type.30
  123.3 0.6 dynamic-slice
  123.9 30.8 %all-reduce.5.cloned.1.call-done = bf16[4,2,4096]{2,1,0:T(2,128)(2,1)} async-done(((bf16[4,2,4096]{2,1,0:T(2,128)(2,1)}), bf16[4,2,4096]{2,1,0:T(2,128)(2,1)}) %all-reduce.5.cloned.1.call-update) | async-done | bytes 65552
  154.8 1.4 bitcast_convert_fusion
  156.1 0.6 copy.33
  (30 shorter events, 0.4 us)
Async XLA Ops:
  6.5 21.7 %copy-start = (bf16[128,4096]{1,0:T(8,128)(2,1)S(1)}, bf16[128,4096]{1,0:T(8,128)(2,1)}, u32[]{:S(2)}) copy-start(bf16[128,4096]{1,0:T(8,128)(2,1)} %param.11) | copy-start | bytes 3145732
  6.5 20.4 %copy-start.4 = (s32[128]{0:T(128)S(1)}, s32[128]{0:T(128)}, u32[]{:S(2)}) copy-start(s32[128]{0:T(128)} %param.14) | copy-start | bytes 1540
  6.5 21.5 %copy-start.3 = (f32[128,8]{0,1:T(8,128)S(1)}, f32[128,8]{0,1:T(8,128)}, u32[]{:S(2)}) copy-start(f32[128,8]{0,1:T(8,128)} %param.13) | copy-start | bytes 12292
  6.5 21.7 %copy-start.1 = (bf16[4096,64]{0,1:T(8,128)(2,1)S(1)}, bf16[4096,64]{0,1:T(8,128)(2,1)}, u32[]{:S(2)}) copy-start(bf16[4096,64]{0,1:T(8,128)(2,1)} %param.19) | copy-start | bytes 1572868
  6.5 51.5 %all-gather.3.cloned.1.call-start = ((), (), s32[]{:S(2)}) async-start(), calls=%async_computation.2 | async-start | bytes 7864320 | tf_op jit(solution)/shard_map/all_gather | solution.py:68
  7.3 98.8 %all-gather.5.cloned.1.call-start = ((), (), s32[]{:S(2)}) async-start(), calls=%async_computation.3 | async-start | bytes 7864320 | tf_op jit(solution)/shard_map/all_gather | solution.py:69
  19.7 86.3 %copy-start.2 = (bf16[768,64]{0,1:T(8,128)(2,1)S(1)}, bf16[768,64]{0,1:T(8,128)(2,1)}, u32[]{:S(2)}) copy-start(bf16[768,64]{0,1:T(8,128)(2,1)} %param.18) | copy-start | bytes 294916
  20.6 20.8 %all-to-all-start = ((bf16[4,12,4096]{2,1,0:T(8,128)(2,1)}), bf16[4,12,4096]{2,1,0:T(8,128)(2,1)S(1)}, u32[]{:S(2)}, u32[]{:S(2)}) async-start(bf16[4,12,4096]{2,1,0:T(8,128)(2,1)} %reshape.102), calls=%async_computation | async-start | bytes 1048576 | tf_op jit(solution)/shard_map/all_to_all | solution.py:71
  41.5 81.8 %copy-start.5 = (u32[32]{0:T(128)S(1)}, u32[32]{0:T(128)}, u32[]{:S(2)}) copy-start(u32[32]{0:T(128)} %constant.60) | copy-start | bytes 388
  111.7 10.2 %all-to-all-start.1 = ((bf16[4,2,384]{2,1,0:T(2,128)(2,1)}), bf16[4,2,384]{2,1,0:T(2,128)(2,1)S(1)}, u32[]{:S(2)}, u32[]{:S(2)}) async-start(bf16[4,2,384]{2,1,0:T(2,128)(2,1)} %reshape.146), calls=%async_computation.1 | async-start | bytes 12288 | tf_op jit(solution)/shard_map/all_to_all | solution.py:81
  116.3 38.5 %all-reduce.5.cloned.1.call-start = ((), (), s32[]{:S(2)}) async-start(), calls=%async_computation.4 | async-start | bytes 131072
Sparse Core Ops, SparseCore 0:
  8.9 49.0 all-gather.2
  59.6 46.3 all-gather.4
  123.5 31.2 all-reduce.4
where the time goes:
time: 164 us; the launch traced here: 163 us
  waiting for transfers between devices  109 us (66%)
  local copies, waits for them, and re-layouts  14 us (9%)
  between operations  13.3 us (8%)
  starting transfers between devices  11 us (7%)
  matrix products  10.3 us (6%)
  other arithmetic  5.37 us (3%)
    all_gather x1, waiting for transfers between devices, body(): lax.all_gather(raising_projection, 'dp', axis=2, tiled=True)  43.2 us
    unnamed x4, waiting for transfers between devices  32.2 us
    all_gather x1, waiting for transfers between devices, body(): lax.all_gather(gating_projection, 'dp', axis=2, tiled=True)  16.5 us
    all_to_all x1, waiting for transfers between devices, body(): lax.all_to_all(token_buffer, 'exp', split_axis=0, concat_axis=0, tiled=True)  12.5 us
    all_to_all x1, starting transfers between devices, body(): lax.all_to_all(token_buffer, 'exp', split_axis=0, concat_axis=0, tiled=True)  6.32 us
    dot_general x1, matrix products, body(): jnp.dot(hidden, inflow_compressor, preferred_element_type=jnp.float32)  4.91 us
    all_to_all x1, waiting for transfers between devices, body(): lax.all_to_all(sketch_rows.reshape(sources, amount, sketch_width), 'exp',...  4.88 us
    dot_general x1, matrix products, body(): jnp.dot(flat_rows, gate_full[0], preferred_element_type=jnp.float32)  4.79 us
  transfers between devices with their start and end apart: 5, of which 5 were waited for; matrix products, arithmetic and copies ran while one was open for 13% of the time, Pallas kernels for 0%

commit v1 on v0

v1 whole, which is shorter than its diff:
```python
import functools

import jax
import jax.numpy as jnp
from jax import lax
from jax.experimental import pallas as pl
from jax.experimental.pallas import tpu as pltpu
from jax.sharding import PartitionSpec as P

EX_DEV = 2
LOCAL_SEATS = 12
ROWS = 16
SPARE = ROWS - LOCAL_SEATS
PARTS = LOCAL_SEATS // SPARE
VMEM_LIMIT = 48 * 1024 * 1024
BF16 = jnp.bfloat16
F32 = jnp.float32


def dot(a, b):
    return jnp.dot(a, b, preferred_element_type=F32)


def seats_of(limits_ref, picked_ref, experts):
    tokens = picked_ref.shape[0]
    picked = picked_ref[...].T
    flags = [jnp.max((picked == e).astype(F32), axis=0, keepdims=True) for e in experts]
    flags = jnp.concatenate(flags, axis=0)
    earlier = lax.broadcasted_iota(jnp.int32, (tokens, tokens), 0)
    later = lax.broadcasted_iota(jnp.int32, (tokens, tokens), 1)
    before = (earlier < later).astype(F32).astype(BF16)
    position = dot(flags.astype(BF16), before).astype(jnp.int32)
    rows = []
    for i, e in enumerate(experts):
        limit = jnp.minimum(limits_ref[e], LOCAL_SEATS)
        at = position[i : i + 1]
        rows.append(jnp.where((flags[i : i + 1] > 0.0) & (at < limit), at, -1))
    return rows


def one_hot(mask):
    return mask.astype(F32).astype(BF16)


def rows_kernel(count, limits_ref, picked_ref, tokens_ref, *out_refs):
    me = lax.axis_index("exp")
    tokens, width = tokens_ref.shape
    chunk = width // (PARTS + 1)
    seats = seats_of(limits_ref, picked_ref, [jnp.bitwise_xor(me, q) for q in range(count)])
    slot = lax.broadcasted_iota(jnp.int32, (ROWS, tokens), 0)
    near = jnp.concatenate([one_hot(slot == s) for s in seats], axis=0)
    for i in range(PARTS):
        shifted = jnp.where(slot >= LOCAL_SEATS, slot - LOCAL_SEATS + SPARE * i, -2)
        far = jnp.concatenate([one_hot(shifted == s) for s in seats], axis=0)
        columns = slice(i * chunk, (i + 1) * chunk)
        source = jnp.concatenate([tokens_ref[:, columns], tokens_ref[:, PARTS * chunk :]], axis=0)
        packed = dot(jnp.concatenate([near, far], axis=1), source).astype(BF16)
        for q in range(count):
            out_refs[q][:, columns] = packed[q * ROWS : (q + 1) * ROWS]


def grads_kernel(
    count, limits_ref, picked_ref, shares_ref, owner_ref, derivs_ref, compressor_ref, *out_refs
):
    me = lax.axis_index("exp")
    first = lax.axis_index("dp") * EX_DEV
    tokens = derivs_ref.shape[0]
    experts = [jnp.bitwise_xor(me, q) for q in range(count)]
    seats = seats_of(limits_ref, picked_ref, experts)
    slot = lax.broadcasted_iota(jnp.int32, (ROWS, tokens), 0)
    owner = owner_ref[...] - first
    proj = dot(derivs_ref[...], compressor_ref[...])
    for q in range(count):
        share = jnp.sum(
            jnp.where(picked_ref[...] == experts[q], shares_ref[...], 0.0), axis=1, keepdims=True
        )
        grad = (share * proj).astype(BF16)
        halves = [
            dot(one_hot((slot == seats[q]) & (owner == n)), grad).astype(BF16)
            for n in range(EX_DEV)
        ]
        out_refs[q][...] = jnp.concatenate(halves, axis=1)


def hidden_kernel(
    sizes, gate_ref, up_ref, compressor_ref, *refs
):
    block_refs, out_refs = refs[: -len(sizes)], refs[-len(sizes) :]
    units = gate_ref.shape[1]
    chunk = gate_ref.shape[0] // (PARTS + 1)
    total = sum(sizes)
    acc = [None, None]
    far = [[], []]
    for i in range(PARTS):
        columns = slice(i * chunk, (i + 1) * chunk)
        left = jnp.concatenate([r[:, columns] for r in block_refs], axis=0)
        for k, w in enumerate((gate_ref, up_ref)):
            near = dot(left, w[columns, :])
            acc[k] = near if acc[k] is None else acc[k] + near
            tail = dot(left, w[PARTS * chunk :, :])
            far[k].append(tail.reshape(total // ROWS, 2, ROWS // 2, units)[:, 1])
    sub = lax.broadcasted_iota(jnp.int32, (1, ROWS // 2, 1), 1)
    low = sub < SPARE
    full = []
    for k in range(2):
        halves = acc[k].reshape(total // ROWS, 2, ROWS // 2, units)

        def turned(a):
            return jnp.concatenate([a[:, SPARE:], a[:, :SPARE]], axis=1)

        top = halves[:, 0] + jnp.where(low, turned(far[k][0]), far[k][1])
        bottom = jnp.where(low, halves[:, 1] + turned(far[k][2]), 0.0)
        full.append(jnp.stack([top, bottom], axis=1).reshape(total, units))
    gate, up = full
    hidden = (gate / (1.0 + jnp.exp(-gate)) * up).astype(BF16)
    start = pl.multiple_of(lax.axis_index("dp") * units, 16)
    sketch = dot(hidden, compressor_ref[pl.ds(start, units), :])
    at = 0
    for size, out in zip(sizes, out_refs):
        half = size // 2
        pair = jnp.concatenate([sketch[at : at + half], sketch[at + half : at + size]], axis=1)
        out[...] = pair.astype(out.dtype)
        at += size


def outer_kernel(n_partial, *refs):
    partial_refs, grad_refs, out_ref = refs[:n_partial], refs[n_partial:-1], refs[-1]
    total = partial_refs[0][...].astype(F32)
    for r in partial_refs[1:]:
        total = total + r[...].astype(F32)
    rows, lanes = total.shape
    width = lanes // 2
    source = lax.broadcasted_iota(jnp.int32, (lanes, lanes), 0)
    target = lax.broadcasted_iota(jnp.int32, (lanes, lanes), 1)
    inner = target % width
    wanted = (target - inner) + jnp.where(
        inner < width // 2, 2 * inner, 2 * (inner - width // 2) + 1
    )
    order = one_hot(source == wanted)
    turned = dot(total.astype(BF16), order).T.astype(BF16)
    grads = jnp.concatenate([r[...] for r in grad_refs], axis=0)
    product = dot(turned[:width], grads[:rows]) + dot(turned[width:], grads[rows:])
    even, odd = product[: width // 2], product[width // 2 :]
    for n in range(EX_DEV):
        columns = slice(n * width, (n + 1) * width)
        out_ref[n] = jnp.concatenate([even[:, columns], odd[:, columns]], axis=1)


VMEM = pl.BlockSpec(memory_space=pltpu.VMEM)
SMEM = pl.BlockSpec(memory_space=pltpu.SMEM)


def call(kernel, out_shape, n_in, limits_first=False, flops=0, moved=0):
    return pl.pallas_call(
        kernel,
        out_shape=out_shape,
        in_specs=[SMEM if limits_first and i == 0 else VMEM for i in range(n_in)],
        out_specs=jax.tree.map(lambda _: VMEM, out_shape),
        compiler_params=pltpu.CompilerParams(vmem_limit_bytes=VMEM_LIMIT),
        cost_estimate=pl.CostEstimate(flops=flops, bytes_accessed=moved, transcendentals=0),
    )


def swap(a, axis, q):
    n = lax.axis_size(axis)
    return lax.ppermute(a, axis, [(i, i ^ q) for i in range(n)])


def body(
    layer_inflows,
    output_derivatives,
    picked_specialists,
    dispatch_shares,
    item_sample,
    send_limits,
    gating_projection,
    raising_projection,
    inflow_compressor,
    outgrad_compressor,
):
    n_exp, n_dp = lax.axis_size("exp"), lax.axis_size("dp")
    small = n_exp * n_dp <= 32
    tokens, width = layer_inflows.shape
    rank = outgrad_compressor.shape[1]
    packed = width * LOCAL_SEATS // ROWS
    units = gating_projection.shape[2]
    shape = jax.ShapeDtypeStruct

    rows = call(
        functools.partial(rows_kernel, n_exp),
        [shape((ROWS, packed), BF16)] * n_exp,
        3,
        True,
        flops=2 * n_exp * ROWS * 2 * tokens * packed,
        moved=2 * tokens * width,
    )(send_limits, picked_specialists, layer_inflows)
    rows = [rows[0]] + [swap(rows[q], "exp", q) for q in range(1, n_exp)]
    grads = call(
        functools.partial(grads_kernel, n_exp),
        [shape((ROWS, EX_DEV * rank), BF16)] * n_exp,
        6,
        True,
        flops=2 * tokens * width * rank,
        moved=2 * tokens * width + 2 * width * rank,
    )(
        send_limits,
        picked_specialists,
        dispatch_shares,
        item_sample.reshape(1, tokens),
        output_derivatives,
        outgrad_compressor,
    )
    grads = [grads[0]] + [swap(grads[q], "exp", q) for q in range(1, n_exp)]

    blocks = {0: rows} if small else {0: [jnp.concatenate(rows, axis=0)]}
    step = n_dp // 2
    while step:
        for d in list(blocks):
            blocks[d ^ step] = [swap(r, "dp", step) for r in blocks[d]]
        step //= 2
    size = n_exp * ROWS
    gate, up = gating_projection[0], raising_projection[0]

    def sketch(ds):
        parts = [r for d in ds for r in blocks[d]]
        return call(
            functools.partial(hidden_kernel, [size] * len(ds)),
            [shape((size // 2, 2 * rank), BF16 if d else F32) for d in ds],
            3 + len(parts),
            flops=4 * len(ds) * size * width * units,
            moved=4 * width * units + 2 * len(ds) * size * packed,
        )(gate, up, inflow_compressor, *parts)

    every = list(range(n_dp))
    groups = [every] if small else [[d] for d in every]
    partials = [p for g in groups for p in sketch(g)]
    partials = [partials[0]] + [swap(partials[d], "dp", d) for d in range(1, n_dp)]
    out = call(
        functools.partial(outer_kernel, n_dp),
        shape((EX_DEV, rank * rank // 128, 128), F32),
        n_dp + n_exp,
        flops=2 * size * rank * 2 * rank,
        moved=4 * EX_DEV * rank * rank,
    )(*partials, *grads)
    return out.reshape(EX_DEV, 1, rank * rank)


def solution(mesh):
    in_specs = (
        P(("grp", "exp", "dp"), None),
        P(("grp", "exp", "dp"), None),
        P(("grp", "exp", "dp"), None),
        P(("grp", "exp", "dp"), None),
        P(("grp", "exp", "dp")),
        P("grp"),
        P("exp", None, "dp"),
        P("exp", None, "dp"),
        P(),
        P(),
    )
    out_specs = P(("grp", "dp"), "exp", None)
    return jax.shard_map(body, mesh=mesh, in_specs=in_specs, out_specs=out_specs, check_vma=False)
```

time: 164 us -> 59.2 us (0.36)
  waiting for transfers between devices: 109 us -> 11.7 us
  between operations: 13.3 us -> 0.15 us
  matrix products: 10.3 us -> 0 us
  local copies, waits for them, and re-layouts: 14 us -> 22.7 us
  Pallas kernels: 0 us -> 6.71 us
  starting transfers between devices: 11 us -> 17.4 us
  other arithmetic: 5.37 us -> 0 us
    all_gather x2 -> x0, waiting for transfers between devices: 59.7 us -> none  [the longest x1 43.2 us: body(): lax.all_gather(raising_projection, 'dp', axis=2, tiled=True)]
    unnamed x4 -> x0, waiting for transfers between devices: 32.2 us -> none
    unnamed x17 -> x42, local copies, waits for them, and re-layouts: 2.28 us -> 22.7 us
    all_to_all x2 -> x0, waiting for transfers between devices: 17.4 us -> none  [the longest x1 12.5 us: body(): lax.all_to_all(token_buffer, 'exp', split_axis=0, concat_axis=0, tiled=True)]
    ppermute x0 -> x21, starting transfers between devices: none -> 17.4 us  [swap(): return lax.ppermute(a, axis, [(i, i ^ q) for i in range(n)])]
    ppermute x0 -> x21, waiting for transfers between devices: none -> 11.7 us  [swap(): return lax.ppermute(a, axis, [(i, i ^ q) for i in range(n)])]
    all_to_all x2 -> x0, starting transfers between devices: 10.9 us -> none  [the longest x1 6.32 us: body(): lax.all_to_all(token_buffer, 'exp', split_axis=0, concat_axis=0, tiled=True)]
    dot_general x4 -> x0, matrix products: 10.3 us -> none  [the longest x1 4.91 us: body(): jnp.dot(hidden, inflow_compressor, preferred_element_type=jnp.float32)]
  transfers between devices with their start and end apart: 5 -> 21, of which waited for: 5 -> 5; matrix products, arithmetic and copies ran while one was open for 13% -> 18% of each run, Pallas kernels for 0% -> 8%
where the time goes in v1:
time: 59.2 us; the launch traced here: 58.6 us
  local copies, waits for them, and re-layouts  22.7 us (38%)
  starting transfers between devices  17.4 us (29%)
  waiting for transfers between devices  11.7 us (20%)
  Pallas kernels  6.71 us (11%)
    unnamed x42, local copies, waits for them, and re-layouts  22.7 us
    ppermute x21, starting transfers between devices, swap(): return lax.ppermute(a, axis, [(i, i ^ q) for i in range(n)])  17.4 us
    ppermute x21, waiting for transfers between devices, swap(): return lax.ppermute(a, axis, [(i, i ^ q) for i in range(n)])  11.7 us
    pallas_call x1, Pallas kernels, sketch(): call(functools.partial(hidden_kernel, [size] * len(ds)), [shape((size //...  3.32 us
    pallas_call x1, Pallas kernels, body(): call(functools.partial(grads_kernel, n_exp), [shape((ROWS, EX_DEV * rank)...  1.25 us
  transfers between devices with their start and end apart: 21, of which 5 were waited for; matrix products, arithmetic and copies ran while one was open for 18% of the time, Pallas kernels for 8%

profile of v1, /device:TPU:0, one launch (start us, length us, event | category | flops | bytes accessed | tf_op | source)
XLA Modules:
  0.0 58.6 jit_solution(10639516750375345767)
XLA Ops:
  0.0 0.8 %copy.13.picked_ref = s32[128,8]{1,0:T(8,128)S(1)} copy(s32[128,8]{0,1:T(8,128)} %param.12) | data formatting | bytes 8192 | tf_op args[2]
  0.8 1.2 %copy-done.1 = bf16[128,4096]{1,0:T(8,128)(2,1)S(1)} copy-done((bf16[128,4096]{1,0:T(8,128)(2,1)S(1)}, bf16[128,4096]{1,0:T(8,128)(2,1)}, u32[]{:S(2)}) %copy-start.1) | copy-done | bytes 1048600
  2.0 0.7 %copy-done.15 = s32[128]{0:T(128)S(1)} copy-done((s32[128]{0:T(128)S(1)}, s32[128]{0:T(128)}, u32[]{:S(2)}) %copy-start.15) | copy-done | bytes 536
  2.7 1.1 %shard_map.100 = (bf16[16,3072]{1,0:T(8,128)(2,1)S(1)}, bf16[16,3072]{1,0:T(8,128)(2,1)S(1)}, bf16[16,3072]{1,0:T(8,128)(2,1)S(1)}, bf16[16,3072]{1,0:T(8,128)(2,1)S(1)}) custom-call(s32[128]{0:T(128)S(1)} %copy-done.15, s32[128,8]{1,0:T(8,128)S(1)} %copy.13.picked_ref, bf16[128,4096]{1,0:T(8,128)(2,1)S(1)} %copy-done.1), custom_call_target="tpu_custom_call" | custom-call | flops 100663296 | bytes 1048576 | tf_op jit(solution)/shard_map/pallas_call | solution.py:189
  3.8 3.1 %collective-permute-start = (bf16[16,3072]{1,0:T(8,128)(2,1)S(1)}, bf16[16,3072]{1,0:T(8,128)(2,1)S(1)}, u32[]{:S(2)}, u32[]{:S(2)}) collective-permute-start(bf16[16,3072]{1,0:T(8,128)(2,1)S(1)} %get-tuple-element.18), channel_id=1, source_target_pairs={{0,4},{4,0},{8,12},{12,8},{1,5},{5,1},{9,13},{13,9},{2,6},{6,2},{1... | collective-permute-start | bytes 294920 | tf_op jit(solution)/shard_map/ppermute | solution.py:166
  6.9 2.6 %collective-permute-start.1 = (bf16[16,3072]{1,0:T(8,128)(2,1)S(1)}, bf16[16,3072]{1,0:T(8,128)(2,1)S(1)}, u32[]{:S(2)}, u32[]{:S(2)}) collective-permute-start(bf16[16,3072]{1,0:T(8,128)(2,1)S(1)} %get-tuple-element.19), channel_id=1, source_target_pairs={{0,8},{4,12},{8,0},{12,4},{1,9},{5,13},{9,1},{13,5},{2,10},{6,14},... | collective-permute-start | bytes 294920 | tf_op jit(solution)/shard_map/ppermute | solution.py:166
  9.4 1.7 %collective-permute-start.7 = (bf16[16,3072]{1,0:T(8,128)(2,1)S(1)}, bf16[16,3072]{1,0:T(8,128)(2,1)}, u32[]{:S(2)}, u32[]{:S(2)}) collective-permute-start(bf16[16,3072]{1,0:T(8,128)(2,1)S(1)} %get-tuple-element.17.refs_0_), channel_id=1, source_target_pairs={{0,2},{1,3},{2,0},{3,1},{4,6},{5,7},{6,4},{7,5},{8,10},{9,11},{10,... | collective-permute-start | bytes 294920 | tf_op jit(solution)/shard_map/ppermute | solution.py:166
  11.2 0.6 %copy-done.3 = bf16[16,3072]{1,0:T(8,128)(2,1)} copy-done((bf16[16,3072]{1,0:T(8,128)(2,1)}, bf16[16,3072]{1,0:T(8,128)(2,1)S(1)}, u32[]{:S(2)}) %copy-start.3) | copy-done | bytes 98328
  11.8 0.3 collective-permute-start.8
  12.1 5.1 %collective-permute-done.1.refs_2_ = bf16[16,3072]{1,0:T(8,128)(2,1)S(1)} collective-permute-done((bf16[16,3072]{1,0:T(8,128)(2,1)S(1)}, bf16[16,3072]{1,0:T(8,128)(2,1)S(1)}, u32[]{:S(2)}, u32[]{:S(2)}) %collective-permute-start.1) | collective-permute-done | bytes 98336 | tf_op jit(solution)/shard_map/ppermute | solution.py:166
  17.3 0.6 %copy-done.5 = bf16[16,3072]{1,0:T(8,128)(2,1)} copy-done((bf16[16,3072]{1,0:T(8,128)(2,1)}, bf16[16,3072]{1,0:T(8,128)(2,1)S(1)}, u32[]{:S(2)}) %copy-start.5) | copy-done | bytes 98328
  17.9 1.5 %collective-permute-start.9 = (bf16[16,3072]{1,0:T(8,128)(2,1)S(1)}, bf16[16,3072]{1,0:T(8,128)(2,1)}, u32[]{:S(2)}, u32[]{:S(2)}) collective-permute-start(bf16[16,3072]{1,0:T(8,128)(2,1)S(1)} %collective-permute-done.1.refs_2_), channel_id=1, source_target_pairs={{0,2},{1,3},{2,0},{3,1},{4,6},{5,7},{6,4},{7,5},{8,10},{9,11},{10,... | collective-permute-start | bytes 294920 | tf_op jit(solution)/shard_map/ppermute | solution.py:166
  19.4 0.2 collective-permute-start.5
  19.6 0.6 %copy-done.7 = bf16[16,3072]{1,0:T(8,128)(2,1)} copy-done((bf16[16,3072]{1,0:T(8,128)(2,1)}, bf16[16,3072]{1,0:T(8,128)(2,1)S(1)}, u32[]{:S(2)}) %copy-start.7) | copy-done | bytes 98328
  20.3 0.6 %copy-done.9 = bf16[16,3072]{1,0:T(8,128)(2,1)} copy-done((bf16[16,3072]{1,0:T(8,128)(2,1)}, bf16[16,3072]{1,0:T(8,128)(2,1)S(1)}, u32[]{:S(2)}) %copy-start.9) | copy-done | bytes 98328
  20.9 0.5 collective-permute-start.10
  21.4 0.0 collective-permute-start.6
  21.5 0.6 %copy-done.11 = bf16[16,3072]{1,0:T(8,128)(2,1)} copy-done((bf16[16,3072]{1,0:T(8,128)(2,1)}, bf16[16,3072]{1,0:T(8,128)(2,1)S(1)}, u32[]{:S(2)}) %copy-start.11) | copy-done | bytes 98328
  22.1 0.5 collective-permute-start.11
  22.6 0.6 %collective-permute-done.9.refs_10_ = bf16[16,3072]{1,0:T(8,128)(2,1)} collective-permute-done((bf16[16,3072]{1,0:T(8,128)(2,1)S(1)}, bf16[16,3072]{1,0:T(8,128)(2,1)}, u32[]{:S(2)}, u32[]{:S(2)}) %collective-permute-start.9) | collective-permute-done | bytes 98336 | tf_op jit(solution)/shard_map/ppermute | solution.py:166
  23.2 0.6 %copy-done.13 = bf16[16,3072]{1,0:T(8,128)(2,1)} copy-done((bf16[16,3072]{1,0:T(8,128)(2,1)}, bf16[16,3072]{1,0:T(8,128)(2,1)S(1)}, u32[]{:S(2)}) %copy-start.13) | copy-done | bytes 98328
  23.9 0.5 collective-permute-start.13
  24.4 1.8 %collective-permute-done.10.refs_11_ = bf16[16,3072]{1,0:T(8,128)(2,1)} collective-permute-done((bf16[16,3072]{1,0:T(8,128)(2,1)}, bf16[16,3072]{1,0:T(8,128)(2,1)}, u32[]{:S(2)}, u32[]{:S(2)}) %collective-permute-start.10) | collective-permute-done | bytes 98336 | tf_op jit(solution)/shard_map/ppermute | solution.py:166
  26.2 0.8 %copy.16.shares_ref = f32[128,8]{1,0:T(8,128)S(1)} copy(f32[128,8]{0,1:T(8,128)} %param.13) | data formatting | bytes 8192 | tf_op args[3]
  27.0 1.1 %copy.14.compressor_ref = bf16[768,64]{1,0:T(8,128)(2,1)S(1)} copy(bf16[768,64]{0,1:T(8,128)(2,1)} %param.18) | data formatting | bytes 196608 | tf_op args[8]
  28.1 1.5 %copy.17.compressor_ref = bf16[4096,64]{1,0:T(8,128)(2,1)S(1)} copy(bf16[4096,64]{0,1:T(8,128)(2,1)} %param.19) | data formatting | bytes 1048576 | tf_op args[9]
  29.6 3.2 %copy.11 = bf16[1,4096,192]{2,1,0:T(8,128)(2,1)S(1)} copy(bf16[1,4096,192]{1,2,0:T(8,128)(2,1)} %param.16) | data formatting | bytes 3145728 | tf_op args[6]
  32.8 0.0 copy-start.16
  32.8 0.0 copy-start.17
  32.8 3.8 %copy.12 = bf16[1,4096,192]{2,1,0:T(8,128)(2,1)} copy(bf16[1,4096,192]{1,2,0:T(8,128)(2,1)} %param.17) | data formatting | bytes 3145728 | tf_op args[7]
  36.6 0.0 copy-start.2
  36.6 1.4 %copy-done.2 = bf16[128,4096]{1,0:T(8,128)(2,1)S(1)} copy-done((bf16[128,4096]{1,0:T(8,128)(2,1)S(1)}, bf16[128,4096]{1,0:T(8,128)(2,1)}, u32[]{:S(2)}) %copy-start.2) | copy-done | bytes 1048600
  38.0 1.3 %shard_map.102 = (bf16[16,128]{1,0:T(8,128)(2,1)S(1)}, bf16[16,128]{1,0:T(8,128)(2,1)S(1)}, bf16[16,128]{1,0:T(8,128)(2,1)S(1)}, bf16[16,128]{1,0:T(8,128)(2,1)S(1)}) custom-call(s32[128]{0:T(128)S(1)} %copy-done.16, s32[128,8]{1,0:T(8,128)S(1)} %copy.13.picked_ref, f32[128,8]{1,0:T(8,128)S(1)} %copy.16.shares_ref, s32[1,128]{1,0:T(1,128)S(1)} %bitcast.6, ...), custom_call_target="tpu_custom_call" | custom-call | flops 67108864 | bytes 1572864 | tf_op jit(solution)/shard_map/pallas_call | solution.py:198
  39.3 1.1 %collective-permute-start.18 = (bf16[16,128]{1,0:T(8,128)(2,1)S(1)}, bf16[16,128]{1,0:T(8,128)(2,1)S(1)}, u32[]{:S(2)}, u32[]{:S(2)}) collective-permute-start(bf16[16,128]{1,0:T(8,128)(2,1)S(1)} %get-tuple-element.26), channel_id=1, source_target_pairs={{0,4},{4,0},{8,12},{12,8},{1,5},{5,1},{9,13},{13,9},{2,6},{6,2},{1... | collective-permute-start | bytes 12296 | tf_op jit(solution)/shard_map/ppermute | solution.py:166
  40.5 0.9 %copy-done.6 = bf16[16,3072]{1,0:T(8,128)(2,1)S(1)} copy-done((bf16[16,3072]{1,0:T(8,128)(2,1)S(1)}, bf16[16,3072]{1,0:T(8,128)(2,1)}, u32[]{:S(2)}) %copy-start.6) | copy-done | bytes 98328
  41.3 0.9 %copy-done.8 = bf16[16,3072]{1,0:T(8,128)(2,1)S(1)} copy-done((bf16[16,3072]{1,0:T(8,128)(2,1)S(1)}, bf16[16,3072]{1,0:T(8,128)(2,1)}, u32[]{:S(2)}) %copy-start.8) | copy-done | bytes 98328
  42.2 0.9 %copy-done.10 = bf16[16,3072]{1,0:T(8,128)(2,1)S(1)} copy-done((bf16[16,3072]{1,0:T(8,128)(2,1)S(1)}, bf16[16,3072]{1,0:T(8,128)(2,1)}, u32[]{:S(2)}) %copy-start.10) | copy-done | bytes 98328
  43.1 0.9 %copy-done.12 = bf16[16,3072]{1,0:T(8,128)(2,1)S(1)} copy-done((bf16[16,3072]{1,0:T(8,128)(2,1)S(1)}, bf16[16,3072]{1,0:T(8,128)(2,1)}, u32[]{:S(2)}) %copy-start.12) | copy-done | bytes 98328
  44.0 0.9 %copy-done.14 = bf16[16,3072]{1,0:T(8,128)(2,1)S(1)} copy-done((bf16[16,3072]{1,0:T(8,128)(2,1)S(1)}, bf16[16,3072]{1,0:T(8,128)(2,1)}, u32[]{:S(2)}) %copy-start.14) | copy-done | bytes 98328
  44.9 3.3 %shard_map.101 = (f32[32,128]{1,0:T(8,128)S(1)}, bf16[32,128]{1,0:T(8,128)(2,1)S(1)}, bf16[32,128]{1,0:T(8,128)(2,1)S(1)}, bf16[32,128]{1,0:T(8,128)(2,1)S(1)}) custom-call(bf16[4096,192]{1,0:T(8,128)(2,1)S(1)} %bitcast.4, bf16[4096,192]{1,0:T(8,128)(2,1)S(1)} %bitcast.5, bf16[768,64]{1,0:T(8,128)(2,1)S(1)} %copy.14.compressor_ref, ...), custom_call_target="tpu_custom_call" | custom-call | flops 805306368 | bytes 4718592 | tf_op jit(solution)/shard_map/pallas_call | solution.py:226
  48.2 0.3 collective-permute-start.15
  48.5 0.5 collective-permute-start.16
  49.1 1.1 %collective-permute-start.17 = (bf16[32,128]{1,0:T(8,128)(2,1)S(1)}, bf16[32,128]{1,0:T(8,128)(2,1)S(1)}, u32[]{:S(2)}, u32[]{:S(2)}) collective-permute-start(bf16[32,128]{1,0:T(8,128)(2,1)S(1)} %get-tuple-element.24), channel_id=1, source_target_pairs={{0,3},{1,2},{2,1},{3,0},{4,7},{5,6},{6,5},{7,4},{8,11},{9,10},{10,... | collective-permute-start | bytes 24584 | tf_op jit(solution)/shard_map/ppermute | solution.py:166
  50.2 2.0 %collective-permute-start.19 = (bf16[16,128]{1,0:T(8,128)(2,1)S(1)}, bf16[16,128]{1,0:T(8,128)(2,1)S(1)}, u32[]{:S(2)}, u32[]{:S(2)}) collective-permute-start(bf16[16,128]{1,0:T(8,128)(2,1)S(1)} %get-tuple-element.27), channel_id=1, source_target_pairs={{0,8},{4,12},{8,0},{12,4},{1,9},{5,13},{9,1},{13,5},{2,10},{6,14},... | collective-permute-start | bytes 12296 | tf_op jit(solution)/shard_map/ppermute | solution.py:166
  52.1 1.4 %collective-permute-start.20 = (bf16[16,128]{1,0:T(8,128)(2,1)S(1)}, bf16[16,128]{1,0:T(8,128)(2,1)S(1)}, u32[]{:S(2)}, u32[]{:S(2)}) collective-permute-start(bf16[16,128]{1,0:T(8,128)(2,1)S(1)} %get-tuple-element.28), channel_id=1, source_target_pairs={{0,12},{4,8},{8,4},{12,0},{1,13},{5,9},{9,5},{13,1},{2,14},{6,10},... | collective-permute-start | bytes 12296 | tf_op jit(solution)/shard_map/ppermute | solution.py:166
  53.5 1.2 %collective-permute-done.19.refs_6_ = bf16[16,128]{1,0:T(8,128)(2,1)S(1)} collective-permute-done((bf16[16,128]{1,0:T(8,128)(2,1)S(1)}, bf16[16,128]{1,0:T(8,128)(2,1)S(1)}, u32[]{:S(2)}, u32[]{:S(2)}) %collective-permute-start.19) | collective-permute-done | bytes 4128 | tf_op jit(solution)/shard_map/ppermute | solution.py:166
  54.7 2.9 %collective-permute-done.20.refs_7_ = bf16[16,128]{1,0:T(8,128)(2,1)S(1)} collective-permute-done((bf16[16,128]{1,0:T(8,128)(2,1)S(1)}, bf16[16,128]{1,0:T(8,128)(2,1)S(1)}, u32[]{:S(2)}, u32[]{:S(2)}) %collective-permute-start.20) | collective-permute-done | bytes 4128 | tf_op jit(solution)/shard_map/ppermute | solution.py:166
  57.5 1.1 %shard_map.103 = f32[2,32,128]{2,1,0:T(8,128)} custom-call(f32[32,128]{1,0:T(8,128)S(1)} %get-tuple-element.21.refs_0_, bf16[32,128]{1,0:T(8,128)(2,1)S(1)} %collective-permute-done.15.refs_1_, bf16[32,128]{1,0:T(8,128)(2,1)S(1)} %collective-permute-done.16.refs_2_, bf16[32,128]{1,0:T(8,128)(2,1)S(1)} %collective-permute-done.17.refs_3_, ...), custom_call_target="tpu_custom_call" | custom-call | flops 1048576 | bytes 32768 | tf_op jit(solution)/shard_map/pallas_call | solution.py:238
  (40 shorter events, 0.1 us)
Async XLA Ops:
  0.8 1.2 %copy-start.1 = (bf16[128,4096]{1,0:T(8,128)(2,1)S(1)}, bf16[128,4096]{1,0:T(8,128)(2,1)}, u32[]{:S(2)}) copy-start(bf16[128,4096]{1,0:T(8,128)(2,1)} %tokens_ref.1) | copy-start | bytes 3145732
  2.0 0.7 %copy-start.15 = (s32[128]{0:T(128)S(1)}, s32[128]{0:T(128)}, u32[]{:S(2)}) copy-start(s32[128]{0:T(128)} %limits_ref.3) | copy-start | bytes 1540
  3.8 8.0 %collective-permute-start = (bf16[16,3072]{1,0:T(8,128)(2,1)S(1)}, bf16[16,3072]{1,0:T(8,128)(2,1)S(1)}, u32[]{:S(2)}, u32[]{:S(2)}) collective-permute-start(bf16[16,3072]{1,0:T(8,128)(2,1)S(1)} %get-tuple-element.18), channel_id=1, source_target_pairs={{0,4},{4,0},{8,12},{12,8},{1,5},{5,1},{9,13},{13,9},{2,6},{6,2},{1... | collective-permute-start | bytes 294920 | tf_op jit(solution)/shard_map/ppermute | solution.py:166
  6.9 10.4 %collective-permute-start.1 = (bf16[16,3072]{1,0:T(8,128)(2,1)S(1)}, bf16[16,3072]{1,0:T(8,128)(2,1)S(1)}, u32[]{:S(2)}, u32[]{:S(2)}) collective-permute-start(bf16[16,3072]{1,0:T(8,128)(2,1)S(1)} %get-tuple-element.19), channel_id=1, source_target_pairs={{0,8},{4,12},{8,0},{12,4},{1,9},{5,13},{9,1},{13,5},{2,10},{6,14},... | collective-permute-start | bytes 294920 | tf_op jit(solution)/shard_map/ppermute | solution.py:166
  9.4 8.5 %collective-permute-start.2 = (bf16[16,3072]{1,0:T(8,128)(2,1)S(1)}, bf16[16,3072]{1,0:T(8,128)(2,1)}, u32[]{:S(2)}, u32[]{:S(2)}) collective-permute-start(bf16[16,3072]{1,0:T(8,128)(2,1)S(1)} %get-tuple-element.20), channel_id=1, source_target_pairs={{0,12},{4,8},{8,4},{12,0},{1,13},{5,9},{9,5},{13,1},{2,14},{6,10},... | collective-permute-start | bytes 294920 | tf_op jit(solution)/shard_map/ppermute | solution.py:166
  9.4 10.0 %collective-permute-start.7 = (bf16[16,3072]{1,0:T(8,128)(2,1)S(1)}, bf16[16,3072]{1,0:T(8,128)(2,1)}, u32[]{:S(2)}, u32[]{:S(2)}) collective-permute-start(bf16[16,3072]{1,0:T(8,128)(2,1)S(1)} %get-tuple-element.17.refs_0_), channel_id=1, source_target_pairs={{0,2},{1,3},{2,0},{3,1},{4,6},{5,7},{6,4},{7,5},{8,10},{9,11},{10,... | collective-permute-start | bytes 294920 | tf_op jit(solution)/shard_map/ppermute | solution.py:166
  11.2 9.1 %collective-permute-start.3 = (bf16[16,3072]{1,0:T(8,128)(2,1)S(1)}, bf16[16,3072]{1,0:T(8,128)(2,1)S(1)}, u32[]{:S(2)}, u32[]{:S(2)}) collective-permute-start(bf16[16,3072]{1,0:T(8,128)(2,1)S(1)} %get-tuple-element.17.refs_0_), channel_id=1, source_target_pairs={{0,1},{1,0},{2,3},{3,2},{4,5},{5,4},{6,7},{7,6},{8,9},{9,8},{10,11... | collective-permute-start | bytes 294920 | tf_op jit(solution)/shard_map/ppermute | solution.py:166
  11.2 0.7 %copy-start.3 = (bf16[16,3072]{1,0:T(8,128)(2,1)}, bf16[16,3072]{1,0:T(8,128)(2,1)S(1)}, u32[]{:S(2)}) copy-start(bf16[16,3072]{1,0:T(8,128)(2,1)S(1)} %get-tuple-element.17.refs_0_) | copy-start | bytes 294916
  11.8 9.6 %collective-permute-start.8 = (bf16[16,3072]{1,0:T(8,128)(2,1)S(1)}, bf16[16,3072]{1,0:T(8,128)(2,1)}, u32[]{:S(2)}, u32[]{:S(2)}) collective-permute-start(bf16[16,3072]{1,0:T(8,128)(2,1)S(1)} %collective-permute-done.refs_1_), channel_id=1, source_target_pairs={{0,2},{1,3},{2,0},{3,1},{4,6},{5,7},{6,4},{7,5},{8,10},{9,11},{10,... | collective-permute-start | bytes 294920 | tf_op jit(solution)/shard_map/ppermute | solution.py:166
  17.3 4.2 %collective-permute-start.4 = (bf16[16,3072]{1,0:T(8,128)(2,1)S(1)}, bf16[16,3072]{1,0:T(8,128)(2,1)S(1)}, u32[]{:S(2)}, u32[]{:S(2)}) collective-permute-start(bf16[16,3072]{1,0:T(8,128)(2,1)S(1)} %collective-permute-done.refs_1_), channel_id=1, source_target_pairs={{0,1},{1,0},{2,3},{3,2},{4,5},{5,4},{6,7},{7,6},{8,9},{9,8},{10,11... | collective-permute-start | bytes 294920 | tf_op jit(solution)/shard_map/ppermute | solution.py:166
  17.3 0.6 %copy-start.5 = (bf16[16,3072]{1,0:T(8,128)(2,1)}, bf16[16,3072]{1,0:T(8,128)(2,1)S(1)}, u32[]{:S(2)}) copy-start(bf16[16,3072]{1,0:T(8,128)(2,1)S(1)} %collective-permute-done.refs_1_) | copy-start | bytes 294916
  17.9 5.3 %collective-permute-start.9 = (bf16[16,3072]{1,0:T(8,128)(2,1)S(1)}, bf16[16,3072]{1,0:T(8,128)(2,1)}, u32[]{:S(2)}, u32[]{:S(2)}) collective-permute-start(bf16[16,3072]{1,0:T(8,128)(2,1)S(1)} %collective-permute-done.1.refs_2_), channel_id=1, source_target_pairs={{0,2},{1,3},{2,0},{3,1},{4,6},{5,7},{6,4},{7,5},{8,10},{9,11},{10,... | collective-permute-start | bytes 294920 | tf_op jit(solution)/shard_map/ppermute | solution.py:166
  19.4 3.8 %collective-permute-start.5 = (bf16[16,3072]{1,0:T(8,128)(2,1)S(1)}, bf16[16,3072]{1,0:T(8,128)(2,1)S(1)}, u32[]{:S(2)}, u32[]{:S(2)}) collective-permute-start(bf16[16,3072]{1,0:T(8,128)(2,1)S(1)} %collective-permute-done.1.refs_2_), channel_id=1, source_target_pairs={{0,1},{1,0},{2,3},{3,2},{4,5},{5,4},{6,7},{7,6},{8,9},{9,8},{10,11... | collective-permute-start | bytes 294920 | tf_op jit(solution)/shard_map/ppermute | solution.py:166
  19.6 0.6 %copy-start.7 = (bf16[16,3072]{1,0:T(8,128)(2,1)}, bf16[16,3072]{1,0:T(8,128)(2,1)S(1)}, u32[]{:S(2)}) copy-start(bf16[16,3072]{1,0:T(8,128)(2,1)S(1)} %collective-permute-done.1.refs_2_) | copy-start | bytes 294916
  20.3 0.6 %copy-start.9 = (bf16[16,3072]{1,0:T(8,128)(2,1)}, bf16[16,3072]{1,0:T(8,128)(2,1)S(1)}, u32[]{:S(2)}) copy-start(bf16[16,3072]{1,0:T(8,128)(2,1)S(1)} %collective-permute-done.3.refs_4_) | copy-start | bytes 294916
  20.9 5.3 %collective-permute-start.10 = (bf16[16,3072]{1,0:T(8,128)(2,1)}, bf16[16,3072]{1,0:T(8,128)(2,1)}, u32[]{:S(2)}, u32[]{:S(2)}) collective-permute-start(bf16[16,3072]{1,0:T(8,128)(2,1)} %collective-permute-done.2.refs_3_), channel_id=1, source_target_pairs={{0,2},{1,3},{2,0},{3,1},{4,6},{5,7},{6,4},{7,5},{8,10},{9,11},{10,... | collective-permute-start | bytes 294920 | tf_op jit(solution)/shard_map/ppermute | solution.py:166
  21.4 17.8 %collective-permute-start.6 = (bf16[16,3072]{1,0:T(8,128)(2,1)}, bf16[16,3072]{1,0:T(8,128)(2,1)}, u32[]{:S(2)}, u32[]{:S(2)}) collective-permute-start(bf16[16,3072]{1,0:T(8,128)(2,1)} %collective-permute-done.2.refs_3_), channel_id=1, source_target_pairs={{0,1},{1,0},{2,3},{3,2},{4,5},{5,4},{6,7},{7,6},{8,9},{9,8},{10,11... | collective-permute-start | bytes 294920 | tf_op jit(solution)/shard_map/ppermute | solution.py:166
  21.5 0.6 %copy-start.11 = (bf16[16,3072]{1,0:T(8,128)(2,1)}, bf16[16,3072]{1,0:T(8,128)(2,1)S(1)}, u32[]{:S(2)}) copy-start(bf16[16,3072]{1,0:T(8,128)(2,1)S(1)} %collective-permute-done.4.refs_5_) | copy-start | bytes 294916
  22.1 18.3 %collective-permute-start.11 = (bf16[16,3072]{1,0:T(8,128)(2,1)}, bf16[16,3072]{1,0:T(8,128)(2,1)}, u32[]{:S(2)}, u32[]{:S(2)}) collective-permute-start(bf16[16,3072]{1,0:T(8,128)(2,1)} %collective-permute-done.7.refs_8_), channel_id=1, source_target_pairs={{0,1},{1,0},{2,3},{3,2},{4,5},{5,4},{6,7},{7,6},{8,9},{9,8},{10,11... | collective-permute-start | bytes 294920 | tf_op jit(solution)/shard_map/ppermute | solution.py:166
  23.2 17.2 %collective-permute-start.12 = (bf16[16,3072]{1,0:T(8,128)(2,1)}, bf16[16,3072]{1,0:T(8,128)(2,1)}, u32[]{:S(2)}, u32[]{:S(2)}) collective-permute-start(bf16[16,3072]{1,0:T(8,128)(2,1)} %collective-permute-done.8.refs_9_), channel_id=1, source_target_pairs={{0,1},{1,0},{2,3},{3,2},{4,5},{5,4},{6,7},{7,6},{8,9},{9,8},{10,11... | collective-permute-start | bytes 294920 | tf_op jit(solution)/shard_map/ppermute | solution.py:166
  23.2 0.6 %copy-start.13 = (bf16[16,3072]{1,0:T(8,128)(2,1)}, bf16[16,3072]{1,0:T(8,128)(2,1)S(1)}, u32[]{:S(2)}) copy-start(bf16[16,3072]{1,0:T(8,128)(2,1)S(1)} %collective-permute-done.5.refs_6_) | copy-start | bytes 294916
  23.9 16.5 %collective-permute-start.13 = (bf16[16,3072]{1,0:T(8,128)(2,1)}, bf16[16,3072]{1,0:T(8,128)(2,1)}, u32[]{:S(2)}, u32[]{:S(2)}) collective-permute-start(bf16[16,3072]{1,0:T(8,128)(2,1)} %collective-permute-done.9.refs_10_), channel_id=1, source_target_pairs={{0,1},{1,0},{2,3},{3,2},{4,5},{5,4},{6,7},{7,6},{8,9},{9,8},{10,11... | collective-permute-start | bytes 294920 | tf_op jit(solution)/shard_map/ppermute | solution.py:166
  26.2 14.2 %collective-permute-start.14 = (bf16[16,3072]{1,0:T(8,128)(2,1)}, bf16[16,3072]{1,0:T(8,128)(2,1)}, u32[]{:S(2)}, u32[]{:S(2)}) collective-permute-start(bf16[16,3072]{1,0:T(8,128)(2,1)} %collective-permute-done.10.refs_11_), channel_id=1, source_target_pairs={{0,1},{1,0},{2,3},{3,2},{4,5},{5,4},{6,7},{7,6},{8,9},{9,8},{10,11... | collective-permute-start | bytes 294920 | tf_op jit(solution)/shard_map/ppermute | solution.py:166
  32.8 3.9 %copy-start.16 = (s32[128]{0:T(128)S(1)}, s32[128]{0:T(128)}, u32[]{:S(2)}) copy-start(s32[128]{0:T(128)} %limits_ref.3) | copy-start | bytes 1540
  32.8 3.9 %copy-start.17 = (s32[128]{0:T(128)S(1)}, s32[128]{0:T(128)}, u32[]{:S(2)}) copy-start(s32[128]{0:T(128)} %param.14) | copy-start | bytes 1540
  36.6 3.8 %copy-start = (bf16[1,4096,192]{2,1,0:T(8,128)(2,1)S(1)}, bf16[1,4096,192]{2,1,0:T(8,128)(2,1)}, u32[]{:S(2)}) copy-start(bf16[1,4096,192]{2,1,0:T(8,128)(2,1)} %copy.12) | copy-start | bytes 4718596
  36.6 1.4 %copy-start.2 = (bf16[128,4096]{1,0:T(8,128)(2,1)S(1)}, bf16[128,4096]{1,0:T(8,128)(2,1)}, u32[]{:S(2)}) copy-start(bf16[128,4096]{1,0:T(8,128)(2,1)} %derivs_ref.1) | copy-start | bytes 3145732
  38.0 2.4 %copy-start.4 = (bf16[16,3072]{1,0:T(8,128)(2,1)S(1)}, bf16[16,3072]{1,0:T(8,128)(2,1)}, u32[]{:S(2)}) copy-start(bf16[16,3072]{1,0:T(8,128)(2,1)} %copy-done.3) | copy-start | bytes 294916
  39.3 12.9 %collective-permute-start.18 = (bf16[16,128]{1,0:T(8,128)(2,1)S(1)}, bf16[16,128]{1,0:T(8,128)(2,1)S(1)}, u32[]{:S(2)}, u32[]{:S(2)}) collective-permute-start(bf16[16,128]{1,0:T(8,128)(2,1)S(1)} %get-tuple-element.26), channel_id=1, source_target_pairs={{0,4},{4,0},{8,12},{12,8},{1,5},{5,1},{9,13},{13,9},{2,6},{6,2},{1... | collective-permute-start | bytes 12296 | tf_op jit(solution)/shard_map/ppermute | solution.py:166
  40.4 0.9 %copy-start.6 = (bf16[16,3072]{1,0:T(8,128)(2,1)S(1)}, bf16[16,3072]{1,0:T(8,128)(2,1)}, u32[]{:S(2)}) copy-start(bf16[16,3072]{1,0:T(8,128)(2,1)} %copy-done.5) | copy-start | bytes 294916
  41.3 0.9 %copy-start.8 = (bf16[16,3072]{1,0:T(8,128)(2,1)S(1)}, bf16[16,3072]{1,0:T(8,128)(2,1)}, u32[]{:S(2)}) copy-start(bf16[16,3072]{1,0:T(8,128)(2,1)} %copy-done.7) | copy-start | bytes 294916
  42.2 0.9 %copy-start.10 = (bf16[16,3072]{1,0:T(8,128)(2,1)S(1)}, bf16[16,3072]{1,0:T(8,128)(2,1)}, u32[]{:S(2)}) copy-start(bf16[16,3072]{1,0:T(8,128)(2,1)} %copy-done.9) | copy-start | bytes 294916
  43.1 0.9 %copy-start.12 = (bf16[16,3072]{1,0:T(8,128)(2,1)S(1)}, bf16[16,3072]{1,0:T(8,128)(2,1)}, u32[]{:S(2)}) copy-start(bf16[16,3072]{1,0:T(8,128)(2,1)} %copy-done.11) | copy-start | bytes 294916
  44.0 0.9 %copy-start.14 = (bf16[16,3072]{1,0:T(8,128)(2,1)S(1)}, bf16[16,3072]{1,0:T(8,128)(2,1)}, u32[]{:S(2)}) copy-start(bf16[16,3072]{1,0:T(8,128)(2,1)} %copy-done.13) | copy-start | bytes 294916
  48.2 9.3 %collective-permute-start.15 = (bf16[32,128]{1,0:T(8,128)(2,1)S(1)}, bf16[32,128]{1,0:T(8,128)(2,1)S(1)}, u32[]{:S(2)}, u32[]{:S(2)}) collective-permute-start(bf16[32,128]{1,0:T(8,128)(2,1)S(1)} %get-tuple-element.22), channel_id=1, source_target_pairs={{0,1},{1,0},{2,3},{3,2},{4,5},{5,4},{6,7},{7,6},{8,9},{9,8},{10,11... | collective-permute-start | bytes 24584 | tf_op jit(solution)/shard_map/ppermute | solution.py:166
  48.5 9.0 %collective-permute-start.16 = (bf16[32,128]{1,0:T(8,128)(2,1)S(1)}, bf16[32,128]{1,0:T(8,128)(2,1)S(1)}, u32[]{:S(2)}, u32[]{:S(2)}) collective-permute-start(bf16[32,128]{1,0:T(8,128)(2,1)S(1)} %get-tuple-element.23), channel_id=1, source_target_pairs={{0,2},{1,3},{2,0},{3,1},{4,6},{5,7},{6,4},{7,5},{8,10},{9,11},{10,... | collective-permute-start | bytes 24584 | tf_op jit(solution)/shard_map/ppermute | solution.py:166
  49.1 8.5 %collective-permute-start.17 = (bf16[32,128]{1,0:T(8,128)(2,1)S(1)}, bf16[32,128]{1,0:T(8,128)(2,1)S(1)}, u32[]{:S(2)}, u32[]{:S(2)}) collective-permute-start(bf16[32,128]{1,0:T(8,128)(2,1)S(1)} %get-tuple-element.24), channel_id=1, source_target_pairs={{0,3},{1,2},{2,1},{3,0},{4,7},{5,6},{6,5},{7,4},{8,11},{9,10},{10,... | collective-permute-start | bytes 24584 | tf_op jit(solution)/shard_map/ppermute | solution.py:166
  50.2 4.5 %collective-permute-start.19 = (bf16[16,128]{1,0:T(8,128)(2,1)S(1)}, bf16[16,128]{1,0:T(8,128)(2,1)S(1)}, u32[]{:S(2)}, u32[]{:S(2)}) collective-permute-start(bf16[16,128]{1,0:T(8,128)(2,1)S(1)} %get-tuple-element.27), channel_id=1, source_target_pairs={{0,8},{4,12},{8,0},{12,4},{1,9},{5,13},{9,1},{13,5},{2,10},{6,14},... | collective-permute-start | bytes 12296 | tf_op jit(solution)/shard_map/ppermute | solution.py:166
  52.1 5.4 %collective-permute-start.20 = (bf16[16,128]{1,0:T(8,128)(2,1)S(1)}, bf16[16,128]{1,0:T(8,128)(2,1)S(1)}, u32[]{:S(2)}, u32[]{:S(2)}) collective-permute-start(bf16[16,128]{1,0:T(8,128)(2,1)S(1)} %get-tuple-element.28), channel_id=1, source_target_pairs={{0,12},{4,8},{8,4},{12,0},{1,13},{5,9},{9,5},{13,1},{2,14},{6,10},... | collective-permute-start | bytes 12296 | tf_op jit(solution)/shard_map/ppermute | solution.py:166

commit v2 on v1

v2 whole, which is shorter than its diff:
```python
import functools

import jax
import jax.numpy as jnp
from jax import lax
from jax.experimental import pallas as pl
from jax.experimental.pallas import tpu as pltpu
from jax.sharding import PartitionSpec as P

EX_DEV = 2
LOCAL_SEATS = 12
ROWS = 16
SPARE = ROWS - LOCAL_SEATS
PARTS = LOCAL_SEATS // SPARE
HALF = ROWS // 2
MIB = 1024 * 1024
BF16 = jnp.bfloat16
F32 = jnp.float32


def dot(a, b):
    return jnp.dot(a, b, preferred_element_type=F32)


def dot_t(a, b):
    return lax.dot_general(a, b, (((1,), (1,)), ((), ())), preferred_element_type=F32)


def one_hot(mask):
    return mask.astype(F32).astype(BF16)


def seats_of(limits_ref, picked, experts):
    tokens = picked.shape[1]
    flags = [jnp.max((picked == e).astype(F32), axis=0, keepdims=True) for e in experts]
    flags = jnp.concatenate(flags, axis=0)
    earlier = lax.broadcasted_iota(jnp.int32, (tokens, tokens), 0)
    later = lax.broadcasted_iota(jnp.int32, (tokens, tokens), 1)
    position = dot(flags.astype(BF16), one_hot(earlier < later)).astype(jnp.int32)
    rows = []
    for i, e in enumerate(experts):
        limit = jnp.minimum(limits_ref[e], LOCAL_SEATS)
        at = position[i : i + 1]
        rows.append(jnp.where((flags[i : i + 1] > 0.0) & (at < limit), at, -1))
    return rows


def rows_kernel(count, limits_hbm, picked_hbm, tokens_hbm, *refs):
    out_refs = refs[:count]
    limits_ref, picked_ref, tokens_ref, sems = refs[count:]
    tokens, width = tokens_ref.shape
    chunk = width // (PARTS + 1)
    columns = [slice(i * chunk, (i + 1) * chunk) for i in range(PARTS + 1)]
    small = [
        pltpu.make_async_copy(limits_hbm, limits_ref, sems.at[0]),
        pltpu.make_async_copy(picked_hbm, picked_ref, sems.at[1]),
    ]
    large = [
        pltpu.make_async_copy(tokens_hbm.at[:, c], tokens_ref.at[:, c], sems.at[2 + i])
        for i, c in enumerate(columns)
    ]
    for copy in small + [large[-1]] + large[:-1]:
        copy.start()
    for copy in small:
        copy.wait()
    me = lax.axis_index("exp")
    experts = [jnp.bitwise_xor(me, q) for q in range(count)]
    seats = seats_of(limits_ref, picked_ref[...], experts)
    slot = lax.broadcasted_iota(jnp.int32, (ROWS, tokens), 0)
    near = jnp.concatenate([one_hot(slot == s) for s in seats], axis=0)
    large[-1].wait()
    for i in range(PARTS):
        shifted = jnp.where(slot >= LOCAL_SEATS, slot - LOCAL_SEATS + SPARE * i, -2)
        far = jnp.concatenate([one_hot(shifted == s) for s in seats], axis=0)
        large[i].wait()
        source = jnp.concatenate([tokens_ref[:, columns[i]], tokens_ref[:, columns[-1]]], axis=0)
        packed = dot(jnp.concatenate([near, far], axis=1), source).astype(BF16)
        for q in range(count):
            out_refs[q][:, columns[i]] = packed[q * ROWS : (q + 1) * ROWS]


def grads_kernel(
    count,
    limits_ref,
    picked_ref,
    shares_ref,
    owner_ref,
    derivs_ref,
    out_compressor_ref,
    in_compressor_ref,
    *out_refs,
):
    me = lax.axis_index("exp")
    place = lax.axis_index("dp")
    tokens = derivs_ref.shape[0]
    experts = [jnp.bitwise_xor(me, q) for q in range(count)]
    picked = picked_ref[...]
    seats = seats_of(limits_ref, picked, experts)
    slot = lax.broadcasted_iota(jnp.int32, (ROWS, tokens), 0)
    owner = owner_ref[...] - place * EX_DEV
    proj = dot_t(derivs_ref[...], out_compressor_ref[...])
    share_rows = [
        jnp.sum(jnp.where(picked == e, shares_ref[...], 0.0), axis=0, keepdims=True)
        for e in experts
    ]
    pad = [jnp.zeros((-count % 8, tokens), F32)] if count % 8 else []
    shares = jnp.concatenate(share_rows + pad, axis=0).T
    for q in range(count):
        grad = (shares[:, q : q + 1] * proj).astype(BF16)
        halves = [
            dot(one_hot((slot == seats[q]) & (owner == n)), grad).astype(BF16)
            for n in range(EX_DEV)
        ]
        out_refs[q][...] = jnp.concatenate(halves, axis=1)
    rank, total = in_compressor_ref.shape
    units = out_refs[count].shape[1]
    to = lax.broadcasted_iota(jnp.int32, (rank, rank), 0)
    at = lax.broadcasted_iota(jnp.int32, (rank, rank), 1)
    order = one_hot(at == jnp.where(to < rank // 2, 2 * to, 2 * to - rank + 1))
    turned = dot(order, in_compressor_ref[...]).astype(BF16)
    line = lax.broadcasted_iota(jnp.int32, (total, units), 0)
    unit = lax.broadcasted_iota(jnp.int32, (total, units), 1)
    for k in range(2):
        first = jnp.bitwise_xor(place, k) * units
        out_refs[count + k][...] = dot(turned, one_hot(line == unit + first)).astype(BF16)


def hidden_kernel(n_blocks, *refs):
    weights = (refs[0:2], refs[2:4])
    compressors = refs[4:6]
    block_refs, out_ref = refs[6 : 6 + n_blocks], refs[-1]
    units, width = weights[0][0].shape
    chunk = width // (PARTS + 1)
    messages = sum(r.shape[0] for r in block_refs) // ROWS
    low = lax.broadcasted_iota(jnp.int32, (1, HALF, 1), 1) < SPARE

    def turn(a):
        return jnp.concatenate([a[:, SPARE:], a[:, :SPARE]], axis=1)

    columns = [slice(i * chunk, (i + 1) * chunk) for i in range(PARTS + 1)]
    lefts = [jnp.concatenate([r[:, c] for r in block_refs], axis=0) for c in columns[:PARTS]]
    tails = []
    for left in lefts:
        tail = left.astype(F32).reshape(messages // 2, 2, 2, HALF, chunk)[:, :, 1]
        tails.append(jnp.where(low, turn(tail[:, 0]), tail[:, 1]))
    tail = jnp.stack(tails, axis=0).reshape(PARTS * messages * SPARE, chunk).astype(BF16)

    def product(w):
        near = dot_t(lefts[0], w[:, columns[0]])
        for i in range(1, PARTS):
            near = near + dot_t(lefts[i], w[:, columns[i]])
        near = near.reshape(messages // 2, 2, 2, HALF, units)
        far = dot_t(tail, w[:, columns[PARTS]]).reshape(PARTS, messages // 2, HALF, units)
        spun = [turn(far[i]) for i in range(PARTS)]
        first_top = near[:, 0, 0] + jnp.where(low, far[0], spun[1])
        first_low = jnp.where(low, near[:, 0, 1] + far[2], 0.0)
        second_top = near[:, 1, 0] + jnp.where(low, spun[0], far[1])
        second_low = jnp.where(low, near[:, 1, 1] + spun[2], 0.0)
        parts = jnp.stack([first_top, first_low, second_top, second_low], axis=1)
        return parts.reshape(messages * ROWS, units)

    sketch = None
    for (gate_ref, up_ref), compressor in zip(weights, compressors):
        gate, up = product(gate_ref), product(up_ref)
        hidden = (gate / (1.0 + jnp.exp(-gate)) * up).astype(BF16)
        term = dot_t(compressor[...], hidden)
        sketch = term if sketch is None else sketch + term
    out_ref[...] = sketch.astype(out_ref.dtype)


def outer_kernel(n_partial, *refs):
    partial_refs, grad_refs, out_ref = refs[:n_partial], refs[n_partial:-1], refs[-1]
    total = partial_refs[0][...].astype(F32)
    for r in partial_refs[1:]:
        total = total + r[...].astype(F32)
    rank = total.shape[0]
    grads = jnp.concatenate([r[...] for r in grad_refs], axis=0)
    product = dot(total.astype(BF16), grads)
    even, odd = product[: rank // 2], product[rank // 2 :]
    for n in range(EX_DEV):
        columns = slice(n * rank, (n + 1) * rank)
        out_ref[n] = jnp.concatenate([even[:, columns], odd[:, columns]], axis=1)


VMEM = pl.BlockSpec(memory_space=pltpu.VMEM)
SMEM = pl.BlockSpec(memory_space=pltpu.SMEM)
HBM = pl.BlockSpec(memory_space=pltpu.HBM)


def call(kernel, out_shape, in_specs, limit, flops=0, moved=0, scratch=()):
    return pl.pallas_call(
        kernel,
        out_shape=out_shape,
        in_specs=in_specs,
        out_specs=jax.tree.map(lambda _: VMEM, out_shape),
        scratch_shapes=list(scratch),
        compiler_params=pltpu.CompilerParams(vmem_limit_bytes=limit),
        cost_estimate=pl.CostEstimate(flops=flops, bytes_accessed=moved, transcendentals=0),
    )


def swap(a, axis, q):
    n = lax.axis_size(axis)
    return lax.ppermute(a, axis, [(i, i ^ q) for i in range(n)])


def body(
    layer_inflows,
    output_derivatives,
    picked_specialists,
    dispatch_shares,
    item_sample,
    send_limits,
    gating_projection,
    raising_projection,
    inflow_compressor,
    outgrad_compressor,
):
    n_exp, n_dp = lax.axis_size("exp"), lax.axis_size("dp")
    small = n_exp <= 8
    tokens, width = layer_inflows.shape
    rank = outgrad_compressor.shape[1]
    packed = width * LOCAL_SEATS // ROWS
    units = gating_projection.shape[2]
    size = n_exp * ROWS
    shape = jax.ShapeDtypeStruct
    picked = picked_specialists.T

    gate, up = gating_projection[0].T, raising_projection[0].T
    pair_gate, pair_up = swap(gate, "dp", 1), swap(up, "dp", 1)

    rows = call(
        functools.partial(rows_kernel, n_exp),
        [shape((ROWS, packed), BF16)] * n_exp,
        [HBM] * 3,
        24 * MIB,
        flops=2 * size * 2 * tokens * packed,
        moved=2 * tokens * width,
        scratch=[
            pltpu.SMEM(send_limits.shape, jnp.int32),
            pltpu.VMEM(picked.shape, jnp.int32),
            pltpu.VMEM((tokens, width), BF16),
            pltpu.SemaphoreType.DMA((PARTS + 3,)),
        ],
    )(send_limits, picked, layer_inflows)
    rows = [rows[0]] + [swap(rows[q], "exp", q) for q in range(1, n_exp)]

    made = call(
        functools.partial(grads_kernel, n_exp),
        [shape((ROWS, EX_DEV * rank), BF16)] * n_exp + [shape((rank, units), BF16)] * 2,
        [SMEM] + [VMEM] * 6,
        24 * MIB,
        flops=2 * tokens * width * rank,
        moved=2 * tokens * width + 2 * width * rank,
    )(
        send_limits,
        picked,
        dispatch_shares.T,
        item_sample.reshape(1, tokens),
        output_derivatives,
        outgrad_compressor.T,
        inflow_compressor.T,
    )
    compressors = made[n_exp:]
    grads = [made[0]] + [swap(made[q], "exp", q) for q in range(1, n_exp)]

    blocks = {0: rows if small else [jnp.concatenate(rows, axis=0)]}
    step = n_dp // 2
    while step > 1:
        for d in list(blocks):
            blocks[d ^ step] = [swap(r, "dp", step) for r in blocks[d]]
        step //= 2

    def sketch(d, dtype):
        parts = blocks[d]
        return call(
            functools.partial(hidden_kernel, len(parts)),
            shape((rank, size), dtype),
            [VMEM] * (6 + len(parts)),
            24 * MIB,
            flops=8 * size * width * units,
            moved=8 * width * units + 2 * size * packed,
        )(gate, up, pair_gate, pair_up, *compressors, *parts)

    blocks[0], grads = lax.optimization_barrier((blocks[0], grads))
    partials = [sketch(0, F32)]
    partials += [swap(sketch(d, BF16), "dp", d) for d in sorted(blocks) if d]
    out = call(
        functools.partial(outer_kernel, len(partials)),
        shape((EX_DEV, rank * rank // 128, 128), F32),
        [VMEM] * (len(partials) + n_exp),
        8 * MIB,
        flops=2 * size * rank * 2 * rank,
        moved=4 * EX_DEV * rank * rank,
    )(*partials, *grads)
    return out.reshape(EX_DEV, 1, rank * rank)


def solution(mesh):
    in_specs = (
        P(("grp", "exp", "dp"), None),
        P(("grp", "exp", "dp"), None),
        P(("grp", "exp", "dp"), None),
        P(("grp", "exp", "dp"), None),
        P(("grp", "exp", "dp")),
        P("grp"),
        P("exp", None, "dp"),
        P("exp", None, "dp"),
        P(),
        P(),
    )
    out_specs = P(("grp", "dp"), "exp", None)
    return jax.shard_map(body, mesh=mesh, in_specs=in_specs, out_specs=out_specs, check_vma=False)
```

time: 59.2 us -> 44.3 us (0.75)
  local copies, waits for them, and re-layouts: 22.7 us -> 8.47 us
  waiting for transfers between devices: 11.7 us -> 7.07 us
  starting transfers between devices: 17.4 us -> 19.9 us
  Pallas kernels: 6.71 us -> 8.37 us
    unnamed x42 -> x22, local copies, waits for them, and re-layouts: 22.7 us -> 8.47 us
    ppermute x21 -> x13, waiting for transfers between devices: 11.7 us -> 7.07 us  [swap(): return lax.ppermute(a, axis, [(i, i ^ q) for i in range(n)])]
    ppermute x21 -> x13, starting transfers between devices: 17.4 us -> 19.9 us  [swap(): return lax.ppermute(a, axis, [(i, i ^ q) for i in range(n)])]
    pallas_call x2 -> x3, Pallas kernels: 4.37 us -> 5.3 us  [the longest x2 4.49 us: sketch(): call(functools.partial(hidden_kernel, len(parts)), shape((rank, size), dt...]
  transfers between devices with their start and end apart: 21 -> 13, of which waited for: 5 -> 7; matrix products, arithmetic and copies ran while one was open for 18% -> 0% of each run, Pallas kernels for 8% -> 12%
where the time goes in v2:
time: 44.3 us; the launch traced here: 43.9 us
  starting transfers between devices  19.9 us (45%)
  local copies, waits for them, and re-layouts  8.47 us (19%)
  Pallas kernels  8.37 us (19%)
  waiting for transfers between devices  7.07 us (16%)
    ppermute x13, starting transfers between devices, swap(): return lax.ppermute(a, axis, [(i, i ^ q) for i in range(n)])  19.9 us
    unnamed x22, local copies, waits for them, and re-layouts  8.47 us
    ppermute x13, waiting for transfers between devices, swap(): return lax.ppermute(a, axis, [(i, i ^ q) for i in range(n)])  7.07 us
    pallas_call x2, Pallas kernels, sketch(): call(functools.partial(hidden_kernel, len(parts)), shape((rank, size), dt...  4.49 us
    pallas_call x1, Pallas kernels, body(): call(functools.partial(grads_kernel, n_exp), [shape((ROWS, EX_DEV * rank)...  1.7 us
    pallas_call x1, Pallas kernels, body(): call(functools.partial(rows_kernel, n_exp), [shape((ROWS, packed), BF16)]...  1.37 us
  transfers between devices with their start and end apart: 13, of which 7 were waited for; matrix products, arithmetic and copies ran while one was open for 0% of the time, Pallas kernels for 12%

profile of v2, /device:TPU:0, one launch (start us, length us, event | category | flops | bytes accessed | tf_op | source)
XLA Modules:
  0.0 43.9 jit_solution(14046776301708439747)
XLA Ops:
  0.0 0.0 copy-start
  0.0 0.5 %collective-permute-start = (bf16[192,4096]{1,0:T(8,128)(2,1)}, bf16[192,4096]{1,0:T(8,128)(2,1)S(1)}, u32[]{:S(2)}, u32[]{:S(2)}) collective-permute-start(bf16[192,4096]{1,0:T(8,128)(2,1)} %bitcast.12), channel_id=1, source_target_pairs={{0,1},{1,0},{2,3},{3,2},{4,5},{5,4},{6,7},{7,6},{8,9},{9,8},{10,11... | collective-permute-start | bytes 4718600 | tf_op jit(solution)/shard_map/ppermute | solution.py:204
  0.5 0.1 collective-permute-start.1
  0.5 0.0 copy-start.3
  0.5 1.2 %copy-done.3 = bf16[128,4096]{1,0:T(8,128)(2,1)S(1)} copy-done((bf16[128,4096]{1,0:T(8,128)(2,1)S(1)}, bf16[128,4096]{1,0:T(8,128)(2,1)}, u32[]{:S(2)}) %copy-start.3) | copy-done | bytes 1048600
  1.7 0.0 copy-start.7
  1.7 0.7 %copy-done.7 = s32[128,8]{0,1:T(8,128)S(1)} copy-done((s32[128,8]{0,1:T(8,128)S(1)}, s32[128,8]{0,1:T(8,128)}, u32[]{:S(2)}) %copy-start.7) | copy-done | bytes 4120
  2.4 0.0 copy-start.9
  2.4 0.7 %copy-done.9 = s32[128]{0:T(128)S(1)} copy-done((s32[128]{0:T(128)S(1)}, s32[128]{0:T(128)}, u32[]{:S(2)}) %copy-start.9) | copy-done | bytes 536
  3.1 1.4 %shard_map.101 = (bf16[16,3072]{1,0:T(8,128)(2,1)S(1)}, bf16[16,3072]{1,0:T(8,128)(2,1)S(1)}, bf16[16,3072]{1,0:T(8,128)(2,1)S(1)}, bf16[16,3072]{1,0:T(8,128)(2,1)S(1)}) custom-call(s32[128]{0:T(128)S(1)} %copy-done.9, s32[8,128]{1,0:T(8,128)S(1)} %bitcast.20, bf16[128,4096]{1,0:T(8,128)(2,1)S(1)} %copy-done.3), custom_call_target="tpu_custom_call" | custom-call | flops 100663296 | bytes 1048576 | tf_op jit(solution)/shard_map/pallas_call | solution.py:232
  4.5 3.1 %collective-permute-start.2 = (bf16[16,3072]{1,0:T(8,128)(2,1)S(1)}, bf16[16,3072]{1,0:T(8,128)(2,1)S(1)}, u32[]{:S(2)}, u32[]{:S(2)}) collective-permute-start(bf16[16,3072]{1,0:T(8,128)(2,1)S(1)} %get-tuple-element.26), channel_id=1, source_target_pairs={{0,4},{4,0},{8,12},{12,8},{1,5},{5,1},{9,13},{13,9},{2,6},{6,2},{1... | collective-permute-start | bytes 294920 | tf_op jit(solution)/shard_map/ppermute | solution.py:204
  7.5 0.0 copy-start.4
  7.6 1.2 %copy-done.4 = bf16[128,4096]{1,0:T(8,128)(2,1)S(1)} copy-done((bf16[128,4096]{1,0:T(8,128)(2,1)S(1)}, bf16[128,4096]{1,0:T(8,128)(2,1)}, u32[]{:S(2)}) %copy-start.4) | copy-done | bytes 1048600
  8.8 1.0 %copy-done.5 = bf16[4096,64]{0,1:T(8,128)(2,1)S(1)} copy-done((bf16[4096,64]{0,1:T(8,128)(2,1)S(1)}, bf16[4096,64]{0,1:T(8,128)(2,1)}, u32[]{:S(2)}) %copy-start.5) | copy-done | bytes 524312
  9.8 0.9 %copy-done.6 = bf16[768,64]{0,1:T(8,128)(2,1)S(1)} copy-done((bf16[768,64]{0,1:T(8,128)(2,1)S(1)}, bf16[768,64]{0,1:T(8,128)(2,1)}, u32[]{:S(2)}) %copy-start.6) | copy-done | bytes 98328
  10.7 0.7 %copy-done.8 = f32[128,8]{0,1:T(8,128)S(1)} copy-done((f32[128,8]{0,1:T(8,128)S(1)}, f32[128,8]{0,1:T(8,128)}, u32[]{:S(2)}) %copy-start.8) | copy-done | bytes 4120
  11.4 0.7 %copy-done.10 = s32[128]{0:T(128)S(1)} copy-done((s32[128]{0:T(128)S(1)}, s32[128]{0:T(128)}, u32[]{:S(2)}) %copy-start.10) | copy-done | bytes 536
  12.1 1.7 %shard_map.100 = (bf16[16,128]{1,0:T(8,128)(2,1)S(1)}, bf16[16,128]{1,0:T(8,128)(2,1)S(1)}, bf16[16,128]{1,0:T(8,128)(2,1)S(1)}, bf16[16,128]{1,0:T(8,128)(2,1)S...) custom-call(s32[128]{0:T(128)S(1)} %copy-done.9, s32[8,128]{1,0:T(8,128)S(1)} %bitcast.21, ...), custom_call_target="tpu_custom_call" | custom-call | flops 67108864 | bytes 1572864 | tf_op jit(solution)/shard_map/pallas_call | solution.py:248
  13.8 0.1 collective-permute-start.5
  13.8 3.0 %collective-permute-start.6 = (bf16[16,128]{1,0:T(8,128)(2,1)S(1)}, bf16[16,128]{1,0:T(8,128)(2,1)S(1)}, u32[]{:S(2)}, u32[]{:S(2)}) collective-permute-start(bf16[16,128]{1,0:T(8,128)(2,1)S(1)} %get-tuple-element.31), channel_id=1, source_target_pairs={{0,8},{4,12},{8,0},{12,4},{1,9},{5,13},{9,1},{13,5},{2,10},{6,14},... | collective-permute-start | bytes 12296 | tf_op jit(solution)/shard_map/ppermute | solution.py:204
  16.9 0.6 %collective-permute-done.5.refs_3_ = bf16[16,128]{1,0:T(8,128)(2,1)S(1)} collective-permute-done((bf16[16,128]{1,0:T(8,128)(2,1)S(1)}, bf16[16,128]{1,0:T(8,128)(2,1)S(1)}, u32[]{:S(2)}, u32[]{:S(2)}) %collective-permute-start.5) | collective-permute-done | bytes 4128 | tf_op jit(solution)/shard_map/ppermute | solution.py:204
  17.4 2.5 %collective-permute-start.7 = (bf16[16,128]{1,0:T(8,128)(2,1)S(1)}, bf16[16,128]{1,0:T(8,128)(2,1)S(1)}, u32[]{:S(2)}, u32[]{:S(2)}) collective-permute-start(bf16[16,128]{1,0:T(8,128)(2,1)S(1)} %get-tuple-element.32), channel_id=1, source_target_pairs={{0,12},{4,8},{8,4},{12,0},{1,13},{5,9},{9,5},{13,1},{2,14},{6,10},... | collective-permute-start | bytes 12296 | tf_op jit(solution)/shard_map/ppermute | solution.py:204
  19.9 0.0 collective-permute-done.6.refs_4_
  19.9 1.5 %collective-permute-start.3 = (bf16[16,3072]{1,0:T(8,128)(2,1)S(1)}, bf16[16,3072]{1,0:T(8,128)(2,1)S(1)}, u32[]{:S(2)}, u32[]{:S(2)}) collective-permute-start(bf16[16,3072]{1,0:T(8,128)(2,1)S(1)} %get-tuple-element.27), channel_id=1, source_target_pairs={{0,8},{4,12},{8,0},{12,4},{1,9},{5,13},{9,1},{13,5},{2,10},{6,14},... | collective-permute-start | bytes 294920 | tf_op jit(solution)/shard_map/ppermute | solution.py:204
  21.4 1.6 %collective-permute-done.7.refs_5_ = bf16[16,128]{1,0:T(8,128)(2,1)S(1)} collective-permute-done((bf16[16,128]{1,0:T(8,128)(2,1)S(1)}, bf16[16,128]{1,0:T(8,128)(2,1)S(1)}, u32[]{:S(2)}, u32[]{:S(2)}) %collective-permute-start.7) | collective-permute-done | bytes 4128 | tf_op jit(solution)/shard_map/ppermute | solution.py:204
  23.0 2.3 %collective-permute-start.4 = (bf16[16,3072]{1,0:T(8,128)(2,1)S(1)}, bf16[16,3072]{1,0:T(8,128)(2,1)S(1)}, u32[]{:S(2)}, u32[]{:S(2)}) collective-permute-start(bf16[16,3072]{1,0:T(8,128)(2,1)S(1)} %get-tuple-element.28), channel_id=1, source_target_pairs={{0,12},{4,8},{8,4},{12,0},{1,13},{5,9},{9,5},{13,1},{2,14},{6,10},... | collective-permute-start | bytes 294920 | tf_op jit(solution)/shard_map/ppermute | solution.py:204
  25.3 0.0 collective-permute-done.2.refs_7_
  25.3 1.5 %collective-permute-start.8 = (bf16[16,3072]{1,0:T(8,128)(2,1)S(1)}, bf16[16,3072]{1,0:T(8,128)(2,1)S(1)}, u32[]{:S(2)}, u32[]{:S(2)}) collective-permute-start(bf16[16,3072]{1,0:T(8,128)(2,1)S(1)} %get-tuple-element.33.refs_6_), channel_id=1, source_target_pairs={{0,2},{1,3},{2,0},{3,1},{4,6},{5,7},{6,4},{7,5},{8,10},{9,11},{10,... | collective-permute-start | bytes 294920 | tf_op jit(solution)/shard_map/ppermute | solution.py:204
  26.8 1.3 %collective-permute-done.3.refs_8_ = bf16[16,3072]{1,0:T(8,128)(2,1)S(1)} collective-permute-done((bf16[16,3072]{1,0:T(8,128)(2,1)S(1)}, bf16[16,3072]{1,0:T(8,128)(2,1)S(1)}, u32[]{:S(2)}, u32[]{:S(2)}) %collective-permute-start.3) | collective-permute-done | bytes 98336 | tf_op jit(solution)/shard_map/ppermute | solution.py:204
  28.1 1.5 %collective-permute-start.10 = (bf16[16,3072]{1,0:T(8,128)(2,1)S(1)}, bf16[16,3072]{1,0:T(8,128)(2,1)S(1)}, u32[]{:S(2)}, u32[]{:S(2)}) collective-permute-start(bf16[16,3072]{1,0:T(8,128)(2,1)S(1)} %collective-permute-done.3.refs_8_), channel_id=1, source_target_pairs={{0,2},{1,3},{2,0},{3,1},{4,6},{5,7},{6,4},{7,5},{8,10},{9,11},{10,... | collective-permute-start | bytes 294920 | tf_op jit(solution)/shard_map/ppermute | solution.py:204
  29.6 0.0 collective-permute-done.4.refs_9_
  29.6 1.4 %collective-permute-start.11 = (bf16[16,3072]{1,0:T(8,128)(2,1)S(1)}, bf16[16,3072]{1,0:T(8,128)(2,1)S(1)}, u32[]{:S(2)}, u32[]{:S(2)}) collective-permute-start(bf16[16,3072]{1,0:T(8,128)(2,1)S(1)} %collective-permute-done.4.refs_9_), channel_id=1, source_target_pairs={{0,2},{1,3},{2,0},{3,1},{4,6},{5,7},{6,4},{7,5},{8,10},{9,11},{10,... | collective-permute-start | bytes 294920 | tf_op jit(solution)/shard_map/ppermute | solution.py:204
  31.0 0.0 collective-permute-done.8.refs_6_
  31.0 1.3 %collective-permute-start.9 = (bf16[16,3072]{1,0:T(8,128)(2,1)S(1)}, bf16[16,3072]{1,0:T(8,128)(2,1)S(1)}, u32[]{:S(2)}, u32[]{:S(2)}) collective-permute-start(bf16[16,3072]{1,0:T(8,128)(2,1)S(1)} %collective-permute-done.2.refs_7_), channel_id=1, source_target_pairs={{0,2},{1,3},{2,0},{3,1},{4,6},{5,7},{6,4},{7,5},{8,10},{9,11},{10,... | collective-permute-start | bytes 294920 | tf_op jit(solution)/shard_map/ppermute | solution.py:204
  32.3 0.8 %collective-permute-done.10.refs_8_ = bf16[16,3072]{1,0:T(8,128)(2,1)S(1)} collective-permute-done((bf16[16,3072]{1,0:T(8,128)(2,1)S(1)}, bf16[16,3072]{1,0:T(8,128)(2,1)S(1)}, u32[]{:S(2)}, u32[]{:S(2)}) %collective-permute-start.10) | collective-permute-done | bytes 98336 | tf_op jit(solution)/shard_map/ppermute | solution.py:204
  33.1 1.1 %collective-permute-done.11.refs_9_ = bf16[16,3072]{1,0:T(8,128)(2,1)S(1)} collective-permute-done((bf16[16,3072]{1,0:T(8,128)(2,1)S(1)}, bf16[16,3072]{1,0:T(8,128)(2,1)S(1)}, u32[]{:S(2)}, u32[]{:S(2)}) %collective-permute-start.11) | collective-permute-done | bytes 98336 | tf_op jit(solution)/shard_map/ppermute | solution.py:204
  34.2 1.4 %collective-permute-done.9.refs_7_ = bf16[16,3072]{1,0:T(8,128)(2,1)S(1)} collective-permute-done((bf16[16,3072]{1,0:T(8,128)(2,1)S(1)}, bf16[16,3072]{1,0:T(8,128)(2,1)S(1)}, u32[]{:S(2)}, u32[]{:S(2)}) %collective-permute-start.9) | collective-permute-done | bytes 98336 | tf_op jit(solution)/shard_map/ppermute | solution.py:204
  35.6 0.0 collective-permute-done.refs_2_
  35.6 0.0 collective-permute-done.1.refs_3_
  35.6 0.0 copy-done
  35.6 0.0 copy-start.1
  35.6 1.4 %copy-done.1 = bf16[1,4096,192]{1,2,0:T(8,128)(2,1)S(1)} copy-done((bf16[1,4096,192]{1,2,0:T(8,128)(2,1)S(1)}, bf16[1,4096,192]{1,2,0:T(8,128)(2,1)}, u32[]{:S(2)}) %copy-start.1) | copy-done | bytes 1572888
  37.0 2.2 %shard_map.103 = bf16[64,64]{1,0:T(8,128)(2,1)S(1)} custom-call(bf16[192,4096]{1,0:T(8,128)(2,1)S(1)} %bitcast.13, bf16[192,4096]{1,0:T(8,128)(2,1)S(1)} %bitcast.16, bf16[192,4096]{1,0:T(8,128)(2,1)S(1)} %collective-permute-done.refs_2_, bf16[192,4096]{1,0:T(8,128)(2,1)S(1)} %collective-permute-done.1.refs_3_, ...), custom_call_target="tpu_custom_call" | custom-call | flops 402653184 | bytes 6684672 | tf_op jit(solution)/shard_map/pallas_call | solution.py:276
  39.3 1.3 %collective-permute-start.12 = (bf16[64,64]{1,0:T(8,128)(2,1)S(1)}, bf16[64,64]{1,0:T(8,128)(2,1)S(1)}, u32[]{:S(2)}, u32[]{:S(2)}) collective-permute-start(bf16[64,64]{1,0:T(8,128)(2,1)S(1)} %shard_map.103), channel_id=1, source_target_pairs={{0,2},{1,3},{2,0},{3,1},{4,6},{5,7},{6,4},{7,5},{8,10},{9,11},{10,... | collective-permute-start | bytes 24584 | tf_op jit(solution)/shard_map/ppermute | solution.py:204
  40.6 0.0 copy-done.2
  40.6 2.2 %shard_map.102.refs_0_ = f32[64,64]{1,0:T(8,128)S(1)} custom-call(bf16[192,4096]{1,0:T(8,128)(2,1)S(1)} %bitcast.14, bf16[192,4096]{1,0:T(8,128)(2,1)S(1)} %bitcast.17, bf16[192,4096]{1,0:T(8,128)(2,1)S(1)} %collective-permute-done.refs_2_, bf16[192,4096]{1,0:T(8,128)(2,1)S(1)} %collective-permute-done.1.refs_3_, ...), custom_call_target="tpu_custom_call" | custom-call | flops 402653184 | bytes 6684672 | tf_op jit(solution)/shard_map/pallas_call | solution.py:276
  42.9 0.2 collective-permute-done.12.refs_1_
  43.1 0.8 %shard_map.104 = f32[2,32,128]{2,1,0:T(8,128)} custom-call(f32[64,64]{1,0:T(8,128)S(1)} %shard_map.102.refs_0_, bf16[64,64]{1,0:T(8,128)(2,1)S(1)} %collective-permute-done.12.refs_1_, bf16[16,128]{1,0:T(8,128)(2,1)S(1)} %get-tuple-element.37.refs_2_, bf16[16,128]{1,0:T(8,128)(2,1)S(1)} %collective-permute-done.5.refs_3_, ...), custom_call_target="tpu_custom_call" | custom-call | flops 1048576 | bytes 32768 | tf_op jit(solution)/shard_map/pallas_call | solution.py:288
  (5 shorter events, 0.0 us)
Async XLA Ops:
  0.0 35.6 %copy-start = (bf16[1,4096,192]{1,2,0:T(8,128)(2,1)S(1)}, bf16[1,4096,192]{1,2,0:T(8,128)(2,1)}, u32[]{:S(2)}) copy-start(bf16[1,4096,192]{1,2,0:T(8,128)(2,1)} %param.16) | copy-start | bytes 4718596
  0.0 35.6 %collective-permute-start = (bf16[192,4096]{1,0:T(8,128)(2,1)}, bf16[192,4096]{1,0:T(8,128)(2,1)S(1)}, u32[]{:S(2)}, u32[]{:S(2)}) collective-permute-start(bf16[192,4096]{1,0:T(8,128)(2,1)} %bitcast.12), channel_id=1, source_target_pairs={{0,1},{1,0},{2,3},{3,2},{4,5},{5,4},{6,7},{7,6},{8,9},{9,8},{10,11... | collective-permute-start | bytes 4718600 | tf_op jit(solution)/shard_map/ppermute | solution.py:204
  0.5 35.2 %collective-permute-start.1 = (bf16[192,4096]{1,0:T(8,128)(2,1)}, bf16[192,4096]{1,0:T(8,128)(2,1)S(1)}, u32[]{:S(2)}, u32[]{:S(2)}) collective-permute-start(bf16[192,4096]{1,0:T(8,128)(2,1)} %bitcast.15), channel_id=1, source_target_pairs={{0,1},{1,0},{2,3},{3,2},{4,5},{5,4},{6,7},{7,6},{8,9},{9,8},{10,11... | collective-permute-start | bytes 4718600 | tf_op jit(solution)/shard_map/ppermute | solution.py:204
  0.5 1.2 %copy-start.3 = (bf16[128,4096]{1,0:T(8,128)(2,1)S(1)}, bf16[128,4096]{1,0:T(8,128)(2,1)}, u32[]{:S(2)}) copy-start(bf16[128,4096]{1,0:T(8,128)(2,1)} %tokens_hbm.1) | copy-start | bytes 3145732
  1.7 0.7 %copy-start.7 = (s32[128,8]{0,1:T(8,128)S(1)}, s32[128,8]{0,1:T(8,128)}, u32[]{:S(2)}) copy-start(s32[128,8]{0,1:T(8,128)} %param.12) | copy-start | bytes 12292
  2.4 0.7 %copy-start.9 = (s32[128]{0:T(128)S(1)}, s32[128]{0:T(128)}, u32[]{:S(2)}) copy-start(s32[128]{0:T(128)} %limits_hbm.1) | copy-start | bytes 1540
  4.5 20.9 %collective-permute-start.2 = (bf16[16,3072]{1,0:T(8,128)(2,1)S(1)}, bf16[16,3072]{1,0:T(8,128)(2,1)S(1)}, u32[]{:S(2)}, u32[]{:S(2)}) collective-permute-start(bf16[16,3072]{1,0:T(8,128)(2,1)S(1)} %get-tuple-element.26), channel_id=1, source_target_pairs={{0,4},{4,0},{8,12},{12,8},{1,5},{5,1},{9,13},{13,9},{2,6},{6,2},{1... | collective-permute-start | bytes 294920 | tf_op jit(solution)/shard_map/ppermute | solution.py:204
  7.5 1.2 %copy-start.4 = (bf16[128,4096]{1,0:T(8,128)(2,1)S(1)}, bf16[128,4096]{1,0:T(8,128)(2,1)}, u32[]{:S(2)}) copy-start(bf16[128,4096]{1,0:T(8,128)(2,1)} %derivs_ref.1) | copy-start | bytes 3145732
  8.8 1.0 %copy-start.5 = (bf16[4096,64]{0,1:T(8,128)(2,1)S(1)}, bf16[4096,64]{0,1:T(8,128)(2,1)}, u32[]{:S(2)}) copy-start(bf16[4096,64]{0,1:T(8,128)(2,1)} %param.19) | copy-start | bytes 1572868
  9.8 0.9 %copy-start.6 = (bf16[768,64]{0,1:T(8,128)(2,1)S(1)}, bf16[768,64]{0,1:T(8,128)(2,1)}, u32[]{:S(2)}) copy-start(bf16[768,64]{0,1:T(8,128)(2,1)} %param.18) | copy-start | bytes 294916
  10.7 0.7 %copy-start.8 = (f32[128,8]{0,1:T(8,128)S(1)}, f32[128,8]{0,1:T(8,128)}, u32[]{:S(2)}) copy-start(f32[128,8]{0,1:T(8,128)} %param.13) | copy-start | bytes 12292
  11.4 0.7 %copy-start.10 = (s32[128]{0:T(128)S(1)}, s32[128]{0:T(128)}, u32[]{:S(2)}) copy-start(s32[128]{0:T(128)} %param.14) | copy-start | bytes 1540
  13.8 3.7 %collective-permute-start.5 = (bf16[16,128]{1,0:T(8,128)(2,1)S(1)}, bf16[16,128]{1,0:T(8,128)(2,1)S(1)}, u32[]{:S(2)}, u32[]{:S(2)}) collective-permute-start(bf16[16,128]{1,0:T(8,128)(2,1)S(1)} %get-tuple-element.30), channel_id=1, source_target_pairs={{0,4},{4,0},{8,12},{12,8},{1,5},{5,1},{9,13},{13,9},{2,6},{6,2},{1... | collective-permute-start | bytes 12296 | tf_op jit(solution)/shard_map/ppermute | solution.py:204
  13.8 6.1 %collective-permute-start.6 = (bf16[16,128]{1,0:T(8,128)(2,1)S(1)}, bf16[16,128]{1,0:T(8,128)(2,1)S(1)}, u32[]{:S(2)}, u32[]{:S(2)}) collective-permute-start(bf16[16,128]{1,0:T(8,128)(2,1)S(1)} %get-tuple-element.31), channel_id=1, source_target_pairs={{0,8},{4,12},{8,0},{12,4},{1,9},{5,13},{9,1},{13,5},{2,10},{6,14},... | collective-permute-start | bytes 12296 | tf_op jit(solution)/shard_map/ppermute | solution.py:204
  17.4 5.5 %collective-permute-start.7 = (bf16[16,128]{1,0:T(8,128)(2,1)S(1)}, bf16[16,128]{1,0:T(8,128)(2,1)S(1)}, u32[]{:S(2)}, u32[]{:S(2)}) collective-permute-start(bf16[16,128]{1,0:T(8,128)(2,1)S(1)} %get-tuple-element.32), channel_id=1, source_target_pairs={{0,12},{4,8},{8,4},{12,0},{1,13},{5,9},{9,5},{13,1},{2,14},{6,10},... | collective-permute-start | bytes 12296 | tf_op jit(solution)/shard_map/ppermute | solution.py:204
  19.9 8.2 %collective-permute-start.3 = (bf16[16,3072]{1,0:T(8,128)(2,1)S(1)}, bf16[16,3072]{1,0:T(8,128)(2,1)S(1)}, u32[]{:S(2)}, u32[]{:S(2)}) collective-permute-start(bf16[16,3072]{1,0:T(8,128)(2,1)S(1)} %get-tuple-element.27), channel_id=1, source_target_pairs={{0,8},{4,12},{8,0},{12,4},{1,9},{5,13},{9,1},{13,5},{2,10},{6,14},... | collective-permute-start | bytes 294920 | tf_op jit(solution)/shard_map/ppermute | solution.py:204
  23.0 6.6 %collective-permute-start.4 = (bf16[16,3072]{1,0:T(8,128)(2,1)S(1)}, bf16[16,3072]{1,0:T(8,128)(2,1)S(1)}, u32[]{:S(2)}, u32[]{:S(2)}) collective-permute-start(bf16[16,3072]{1,0:T(8,128)(2,1)S(1)} %get-tuple-element.28), channel_id=1, source_target_pairs={{0,12},{4,8},{8,4},{12,0},{1,13},{5,9},{9,5},{13,1},{2,14},{6,10},... | collective-permute-start | bytes 294920 | tf_op jit(solution)/shard_map/ppermute | solution.py:204
  25.3 5.7 %collective-permute-start.8 = (bf16[16,3072]{1,0:T(8,128)(2,1)S(1)}, bf16[16,3072]{1,0:T(8,128)(2,1)S(1)}, u32[]{:S(2)}, u32[]{:S(2)}) collective-permute-start(bf16[16,3072]{1,0:T(8,128)(2,1)S(1)} %get-tuple-element.33.refs_6_), channel_id=1, source_target_pairs={{0,2},{1,3},{2,0},{3,1},{4,6},{5,7},{6,4},{7,5},{8,10},{9,11},{10,... | collective-permute-start | bytes 294920 | tf_op jit(solution)/shard_map/ppermute | solution.py:204
  28.1 5.0 %collective-permute-start.10 = (bf16[16,3072]{1,0:T(8,128)(2,1)S(1)}, bf16[16,3072]{1,0:T(8,128)(2,1)S(1)}, u32[]{:S(2)}, u32[]{:S(2)}) collective-permute-start(bf16[16,3072]{1,0:T(8,128)(2,1)S(1)} %collective-permute-done.3.refs_8_), channel_id=1, source_target_pairs={{0,2},{1,3},{2,0},{3,1},{4,6},{5,7},{6,4},{7,5},{8,10},{9,11},{10,... | collective-permute-start | bytes 294920 | tf_op jit(solution)/shard_map/ppermute | solution.py:204
  29.6 4.6 %collective-permute-start.11 = (bf16[16,3072]{1,0:T(8,128)(2,1)S(1)}, bf16[16,3072]{1,0:T(8,128)(2,1)S(1)}, u32[]{:S(2)}, u32[]{:S(2)}) collective-permute-start(bf16[16,3072]{1,0:T(8,128)(2,1)S(1)} %collective-permute-done.4.refs_9_), channel_id=1, source_target_pairs={{0,2},{1,3},{2,0},{3,1},{4,6},{5,7},{6,4},{7,5},{8,10},{9,11},{10,... | collective-permute-start | bytes 294920 | tf_op jit(solution)/shard_map/ppermute | solution.py:204
  31.0 4.6 %collective-permute-start.9 = (bf16[16,3072]{1,0:T(8,128)(2,1)S(1)}, bf16[16,3072]{1,0:T(8,128)(2,1)S(1)}, u32[]{:S(2)}, u32[]{:S(2)}) collective-permute-start(bf16[16,3072]{1,0:T(8,128)(2,1)S(1)} %collective-permute-done.2.refs_7_), channel_id=1, source_target_pairs={{0,2},{1,3},{2,0},{3,1},{4,6},{5,7},{6,4},{7,5},{8,10},{9,11},{10,... | collective-permute-start | bytes 294920 | tf_op jit(solution)/shard_map/ppermute | solution.py:204
  35.6 1.4 %copy-start.1 = (bf16[1,4096,192]{1,2,0:T(8,128)(2,1)S(1)}, bf16[1,4096,192]{1,2,0:T(8,128)(2,1)}, u32[]{:S(2)}) copy-start(bf16[1,4096,192]{1,2,0:T(8,128)(2,1)} %param.17) | copy-start | bytes 4718596
  37.0 3.6 %copy-start.2 = (bf16[1,4096,192]{1,2,0:T(8,128)(2,1)S(1)}, bf16[1,4096,192]{1,2,0:T(8,128)(2,1)}, u32[]{:S(2)}) copy-start(bf16[1,4096,192]{1,2,0:T(8,128)(2,1)} %param.17) | copy-start | bytes 4718596
  39.3 3.8 %collective-permute-start.12 = (bf16[64,64]{1,0:T(8,128)(2,1)S(1)}, bf16[64,64]{1,0:T(8,128)(2,1)S(1)}, u32[]{:S(2)}, u32[]{:S(2)}) collective-permute-start(bf16[64,64]{1,0:T(8,128)(2,1)S(1)} %shard_map.103), channel_id=1, source_target_pairs={{0,2},{1,3},{2,0},{3,1},{4,6},{5,7},{6,4},{7,5},{8,10},{9,11},{10,... | collective-permute-start | bytes 24584 | tf_op jit(solution)/shard_map/ppermute | solution.py:204

commit v3 on v2

v3 whole, which is shorter than its diff:
```python
import functools

import jax
import jax.numpy as jnp
from jax import lax
from jax.experimental import pallas as pl
from jax.experimental.pallas import tpu as pltpu
from jax.sharding import PartitionSpec as P

EX_DEV = 2
LOCAL_SEATS = 12
ROWS = 16
SPARE = ROWS - LOCAL_SEATS
PARTS = LOCAL_SEATS // SPARE
HALF = ROWS // 2
MIB = 1024 * 1024
BF16 = jnp.bfloat16
F32 = jnp.float32


def dot(a, b):
    return jnp.dot(a, b, preferred_element_type=F32)


def dot_t(a, b):
    return lax.dot_general(a, b, (((1,), (1,)), ((), ())), preferred_element_type=F32)


def one_hot(mask):
    return mask.astype(F32).astype(BF16)


def seats_of(limits_ref, picked, experts):
    tokens = picked.shape[1]
    flags = [jnp.max((picked == e).astype(F32), axis=0, keepdims=True) for e in experts]
    flags = jnp.concatenate(flags, axis=0)
    earlier = lax.broadcasted_iota(jnp.int32, (tokens, tokens), 0)
    later = lax.broadcasted_iota(jnp.int32, (tokens, tokens), 1)
    position = dot(flags.astype(BF16), one_hot(earlier < later)).astype(jnp.int32)
    rows = []
    for i, e in enumerate(experts):
        limit = jnp.minimum(limits_ref[e], LOCAL_SEATS)
        at = position[i : i + 1]
        rows.append(jnp.where((flags[i : i + 1] > 0.0) & (at < limit), at, -1))
    return rows


def send_kernel(count, limits_hbm, picked_hbm, shares_hbm, owner_hbm, tokens_hbm, derivs_hbm, compressor_hbm, *refs):
    out_refs = refs[:count]
    limits_ref, picked_ref, shares_ref, owner_ref, tokens_ref, derivs_ref, compressor_ref, sems = (
        refs[count:]
    )
    tokens, width = tokens_ref.shape
    chunk = width // (PARTS + 1)
    columns = [slice(i * chunk, (i + 1) * chunk) for i in range(PARTS + 1)]
    pairs = [
        (limits_hbm, limits_ref),
        (picked_hbm, picked_ref),
        (shares_hbm, shares_ref),
        (owner_hbm, owner_ref),
        (tokens_hbm, tokens_ref),
        (derivs_hbm, derivs_ref),
        (compressor_hbm, compressor_ref),
    ]
    copies = [pltpu.make_async_copy(a, b, sems.at[i]) for i, (a, b) in enumerate(pairs)]
    for copy in copies:
        copy.start()
    for copy in copies[:4]:
        copy.wait()
    me = lax.axis_index("exp")
    experts = [jnp.bitwise_xor(me, q) for q in range(count)]
    picked = picked_ref[...]
    seats = seats_of(limits_ref, picked, experts)
    slot = lax.broadcasted_iota(jnp.int32, (ROWS, tokens), 0)
    near = jnp.concatenate([one_hot(slot == s) for s in seats], axis=0)
    masks = []
    for i in range(PARTS):
        shifted = jnp.where(slot >= LOCAL_SEATS, slot - LOCAL_SEATS + SPARE * i, -2)
        far = jnp.concatenate([one_hot(shifted == s) for s in seats], axis=0)
        masks.append(jnp.concatenate([near, far], axis=1))
    owner = owner_ref[...] - lax.axis_index("dp") * EX_DEV
    owned = [
        jnp.concatenate([one_hot((slot == s) & (owner == n)) for n in range(EX_DEV)], axis=0)
        for s in seats
    ]
    share_rows = [
        jnp.sum(jnp.where(picked == e, shares_ref[...], 0.0), axis=0, keepdims=True)
        for e in experts
    ]
    pad = [jnp.zeros((-count % 8, tokens), F32)] if count % 8 else []
    shares = jnp.concatenate(share_rows + pad, axis=0).T
    for copy in copies[4:]:
        copy.wait()
    proj = dot_t(derivs_ref[...], compressor_ref[...])
    last = tokens_ref[:, columns[-1]]
    for i in range(PARTS):
        source = jnp.concatenate([tokens_ref[:, columns[i]], last], axis=0)
        packed = dot(masks[i], source).astype(BF16)
        for q in range(count):
            out_refs[q][:, columns[i]] = packed[q * ROWS : (q + 1) * ROWS]
    for q in range(count):
        grad = (shares[:, q : q + 1] * proj).astype(BF16)
        both = dot(owned[q], grad)
        halves = [both[n * ROWS : (n + 1) * ROWS] for n in range(EX_DEV)]
        out_refs[q][:, PARTS * chunk :] = jnp.concatenate(halves, axis=1).astype(BF16)


def pair_compressors(compressor_ref, units):
    place = lax.axis_index("dp")
    rank, total = compressor_ref.shape
    to = lax.broadcasted_iota(jnp.int32, (rank, rank), 0)
    at = lax.broadcasted_iota(jnp.int32, (rank, rank), 1)
    order = one_hot(at == jnp.where(to < rank // 2, 2 * to, 2 * to - rank + 1))
    turned = dot(order, compressor_ref[...]).astype(BF16)
    line = lax.broadcasted_iota(jnp.int32, (total, units), 0)
    unit = lax.broadcasted_iota(jnp.int32, (total, units), 1)
    return [
        dot(turned, one_hot(line == unit + jnp.bitwise_xor(place, k) * units)).astype(BF16)
        for k in range(2)
    ]


def sketch_of(weights, compressors, block_refs):
    width = weights[0][0].shape[1]
    chunk = width // (PARTS + 1)
    size = sum(r.shape[0] for r in block_refs)
    messages = size // ROWS
    low = lax.broadcasted_iota(jnp.int32, (1, HALF, 1), 1) < SPARE
    columns = [slice(i * chunk, (i + 1) * chunk) for i in range(PARTS + 1)]
    rows = [jnp.concatenate([r[:, c] for r in block_refs], axis=0) for c in columns[:PARTS]]
    tails = [r.astype(F32).reshape(messages, 2, HALF, chunk)[:, 1] for r in rows]

    def turn(a):
        return jnp.concatenate([a[:, SPARE:], a[:, :SPARE]], axis=1)

    top = jnp.where(low, turn(tails[0]), tails[1])
    bottom = jnp.where(low, turn(tails[2]), 0.0)
    rows.append(jnp.stack([top, bottom], axis=1).reshape(size, chunk).astype(BF16))
    seat = lax.broadcasted_iota(jnp.int32, (1, size), 1) % ROWS

    def product(w):
        total = dot_t(w[:, columns[0]], rows[0])
        for c, r in zip(columns[1:], rows[1:]):
            total = total + dot_t(w[:, c], r)
        return total

    sketch = None
    for (gate_ref, up_ref), compressor in zip(weights, compressors):
        gate, up = product(gate_ref), product(up_ref)
        hidden = gate / (1.0 + jnp.exp(-gate)) * up
        hidden = jnp.where(seat < LOCAL_SEATS, hidden, 0.0).astype(BF16)
        term = dot(compressor, hidden)
        sketch = term if sketch is None else sketch + term
    return sketch


def own_kernel(n_blocks, *refs):
    weights = (refs[0:2], refs[2:4])
    compressor_ref, block_refs = refs[4], refs[5 : 5 + n_blocks]
    sketch_ref, grads_ref, *chosen_refs = refs[5 + n_blocks :]
    units, width = weights[0][0].shape
    chosen = pair_compressors(compressor_ref, units)
    for ref, value in zip(chosen_refs, chosen):
        ref[...] = value
    grads_ref[...] = jnp.concatenate([r[:, width * LOCAL_SEATS // ROWS :] for r in block_refs], axis=0)
    sketch_ref[...] = sketch_of(weights, chosen, block_refs)


def far_kernel(n_blocks, *refs):
    weights = (refs[0:2], refs[2:4])
    chosen = [r[...] for r in refs[4:6]]
    refs[-1][...] = sketch_of(weights, chosen, refs[6 : 6 + n_blocks]).astype(refs[-1].dtype)


def outer_kernel(grads_ref, *refs):
    partial_refs, out_ref = refs[:-1], refs[-1]
    total = partial_refs[0][...]
    for r in partial_refs[1:]:
        total = total + r[...].astype(F32)
    rank = total.shape[0]
    product = dot(total.astype(BF16), grads_ref[...])
    even, odd = product[: rank // 2], product[rank // 2 :]
    for n in range(EX_DEV):
        columns = slice(n * rank, (n + 1) * rank)
        out_ref[n] = jnp.concatenate([even[:, columns], odd[:, columns]], axis=1)


VMEM = pl.BlockSpec(memory_space=pltpu.VMEM)
SMEM = pl.BlockSpec(memory_space=pltpu.SMEM)
HBM = pl.BlockSpec(memory_space=pltpu.HBM)


def call(kernel, out_shape, in_specs, limit, flops=0, moved=0, scratch=()):
    return pl.pallas_call(
        kernel,
        out_shape=out_shape,
        in_specs=in_specs,
        out_specs=jax.tree.map(lambda _: VMEM, out_shape),
        scratch_shapes=list(scratch),
        compiler_params=pltpu.CompilerParams(vmem_limit_bytes=limit),
        cost_estimate=pl.CostEstimate(flops=flops, bytes_accessed=moved, transcendentals=0),
    )


def swap(a, axis, q):
    n = lax.axis_size(axis)
    return lax.ppermute(a, axis, [(i, i ^ q) for i in range(n)])


def body(
    layer_inflows,
    output_derivatives,
    picked_specialists,
    dispatch_shares,
    item_sample,
    send_limits,
    gating_projection,
    raising_projection,
    inflow_compressor,
    outgrad_compressor,
):
    n_exp, n_dp = lax.axis_size("exp"), lax.axis_size("dp")
    small = n_exp <= 8
    tokens, width = layer_inflows.shape
    rank = outgrad_compressor.shape[1]
    packed = width * LOCAL_SEATS // ROWS
    units = gating_projection.shape[2]
    size = n_exp * ROWS
    shape = jax.ShapeDtypeStruct

    gate, up = gating_projection[0].T, raising_projection[0].T
    pair_gate, pair_up = swap(gate, "dp", 1), swap(up, "dp", 1)
    weights = (gate, up, pair_gate, pair_up)

    arguments = (
        send_limits,
        picked_specialists.T,
        dispatch_shares.T,
        item_sample.reshape(1, tokens),
        layer_inflows,
        output_derivatives,
        outgrad_compressor.T,
    )
    spaces = [pltpu.SMEM] + [pltpu.VMEM] * (len(arguments) - 1)
    rows = call(
        functools.partial(send_kernel, n_exp),
        [shape((ROWS, packed + EX_DEV * rank), BF16)] * n_exp,
        [HBM] * len(arguments),
        60 * MIB,
        flops=4 * size * tokens * packed + 2 * tokens * width * rank,
        moved=4 * tokens * width + 2 * rank * width,
        scratch=[space(a.shape, a.dtype) for space, a in zip(spaces, arguments)]
        + [pltpu.SemaphoreType.DMA((len(arguments),))],
    )(*arguments)
    rows = [rows[0]] + [swap(rows[q], "exp", q) for q in range(1, n_exp)]

    blocks = {0: rows if small else [jnp.concatenate(rows, axis=0)]}
    step = n_dp // 2
    while step > 1:
        for d in list(blocks):
            blocks[d ^ step] = [swap(r, "dp", step) for r in blocks[d]]
        step //= 2

    cost = dict(flops=8 * size * width * units, moved=8 * width * units + 2 * size * packed)
    chosen_shape = shape((rank, units), BF16)
    own, grads, *chosen = call(
        functools.partial(own_kernel, len(blocks[0])),
        [shape((rank, size), F32), shape((size, EX_DEV * rank), BF16), chosen_shape, chosen_shape],
        [VMEM] * (5 + len(blocks[0])),
        20 * MIB,
        **cost,
    )(*weights, inflow_compressor.T, *blocks[0])
    partials = [own]
    for d in sorted(blocks):
        if d:
            far = call(
                functools.partial(far_kernel, len(blocks[d])),
                shape((rank, size), BF16),
                [VMEM] * (6 + len(blocks[d])),
                20 * MIB,
                **cost,
            )(*weights, *chosen, *blocks[d])
            partials.append(swap(far, "dp", d))
    out = call(
        outer_kernel,
        shape((EX_DEV, rank * rank // 128, 128), F32),
        [VMEM] * (1 + len(partials)),
        8 * MIB,
        flops=2 * size * rank * 2 * rank,
        moved=4 * EX_DEV * rank * rank,
    )(grads, *partials)
    return out.reshape(EX_DEV, 1, rank * rank)


def solution(mesh):
    in_specs = (
        P(("grp", "exp", "dp"), None),
        P(("grp", "exp", "dp"), None),
        P(("grp", "exp", "dp"), None),
        P(("grp", "exp", "dp"), None),
        P(("grp", "exp", "dp")),
        P("grp"),
        P("exp", None, "dp"),
        P("exp", None, "dp"),
        P(),
        P(),
    )
    out_specs = P(("grp", "dp"), "exp", None)
    return jax.shard_map(body, mesh=mesh, in_specs=in_specs, out_specs=out_specs, check_vma=False)
```

time: 44.3 us -> 35.9 us (0.81)
  starting transfers between devices: 19.9 us -> 12 us
  local copies, waits for them, and re-layouts: 8.47 us -> 2.3 us
  waiting for transfers between devices: 7.07 us -> 10.1 us
  Pallas kernels: 8.37 us -> 11.1 us
    ppermute x13 -> x10, starting transfers between devices: 19.9 us -> 12 us  [swap(): return lax.ppermute(a, axis, [(i, i ^ q) for i in range(n)])]
    unnamed x22 -> x8, local copies, waits for them, and re-layouts: 8.47 us -> 2.3 us
    ppermute x13 -> x10, waiting for transfers between devices: 7.07 us -> 10.1 us  [swap(): return lax.ppermute(a, axis, [(i, i ^ q) for i in range(n)])]
    pallas_call x5 -> x4, Pallas kernels: 8.37 us -> 11.1 us  [the longest x1 3.56 us: body(): call(functools.partial(own_kernel, len(blocks[0])), [shape((rank, size),...]
  transfers between devices with their start and end apart: 13 -> 10, of which waited for: 7 -> 3; matrix products, arithmetic and copies ran while one was open for 0% -> 0% of each run, Pallas kernels for 12% -> 20%
where the time goes in v3:
time: 35.9 us; the launch traced here: 35.6 us
  starting transfers between devices  12 us (33%)
  Pallas kernels  11.1 us (31%)
  waiting for transfers between devices  10.1 us (28%)
  local copies, waits for them, and re-layouts  2.3 us (6%)
    ppermute x10, starting transfers between devices, swap(): return lax.ppermute(a, axis, [(i, i ^ q) for i in range(n)])  12 us
    ppermute x10, waiting for transfers between devices, swap(): return lax.ppermute(a, axis, [(i, i ^ q) for i in range(n)])  10.1 us
    pallas_call x1, Pallas kernels, body(): call(functools.partial(own_kernel, len(blocks[0])), [shape((rank, size),...  3.56 us
    pallas_call x1, Pallas kernels, body(): call(functools.partial(send_kernel, n_exp), [shape((ROWS, packed + EX_DEV...  3.43 us
    pallas_call x1, Pallas kernels, body(): call(functools.partial(far_kernel, len(blocks[d])), shape((rank, size), B...  3.33 us
    unnamed x8, local copies, waits for them, and re-layouts  2.3 us
    pallas_call x1, Pallas kernels, body(): call(outer_kernel, shape((EX_DEV, rank * rank // 128, 128), F32), [VMEM]...  0.81 us
  transfers between devices with their start and end apart: 10, of which 3 were waited for; matrix products, arithmetic and copies ran while one was open for 0% of the time, Pallas kernels for 20%

profile of v3, /device:TPU:0, one launch (start us, length us, event | category | flops | bytes accessed | tf_op | source)
XLA Modules:
  0.0 35.6 jit_solution(13181795465468800008)
XLA Ops:
  0.0 0.0 copy-start
  0.0 0.0 copy-start.3
  0.0 0.5 %collective-permute-start = (bf16[192,4096]{1,0:T(8,128)(2,1)}, bf16[192,4096]{1,0:T(8,128)(2,1)S(1)}, u32[]{:S(2)}, u32[]{:S(2)}) collective-permute-start(bf16[192,4096]{1,0:T(8,128)(2,1)} %bitcast.12), channel_id=1, source_target_pairs={{0,1},{1,0},{2,3},{3,2},{4,5},{5,4},{6,7},{7,6},{8,9},{9,8},{10,11... | collective-permute-start | bytes 4718600 | tf_op jit(solution)/shard_map/ppermute | solution.py:207
  0.5 0.1 collective-permute-start.1
  0.5 3.4 %shard_map.100 = (bf16[16,3200]{1,0:T(8,128)(2,1)}, bf16[16,3200]{1,0:T(8,128)(2,1)}, bf16[16,3200]{1,0:T(8,128)(2,1)}, bf16[16,3200]{1,0:T(8,128)(2,1)}) custom-call(s32[128]{0:T(128)} %limits_hbm.1, s32[8,128]{1,0:T(8,128)} %bitcast.20, f32[8,128]{1,0:T(8,128)} %bitcast.21, s32[1,128]{1,0:T(1,128)} %bitcast.22, bf16[128,4096]{1,0:T(8,128)(2,1)} %tokens_hbm.1, ...), custom_call_target="tpu_custom_call" | custom-call | flops 167772160 | bytes 2621440 | tf_op jit(solution)/shard_map/pallas_call | solution.py:245
  4.0 3.1 %collective-permute-start.2 = (bf16[16,3200]{1,0:T(8,128)(2,1)}, bf16[16,3200]{1,0:T(8,128)(2,1)S(1)}, u32[]{:S(2)}, u32[]{:S(2)}) collective-permute-start(bf16[16,3200]{1,0:T(8,128)(2,1)} %get-tuple-element.14), channel_id=1, source_target_pairs={{0,4},{4,0},{8,12},{12,8},{1,5},{5,1},{9,13},{13,9},{2,6},{6,2},{1... | collective-permute-start | bytes 307208 | tf_op jit(solution)/shard_map/ppermute | solution.py:207
  7.0 2.6 %collective-permute-start.3 = (bf16[16,3200]{1,0:T(8,128)(2,1)}, bf16[16,3200]{1,0:T(8,128)(2,1)S(1)}, u32[]{:S(2)}, u32[]{:S(2)}) collective-permute-start(bf16[16,3200]{1,0:T(8,128)(2,1)} %get-tuple-element.15), channel_id=1, source_target_pairs={{0,8},{4,12},{8,0},{12,4},{1,9},{5,13},{9,1},{13,5},{2,10},{6,14},... | collective-permute-start | bytes 307208 | tf_op jit(solution)/shard_map/ppermute | solution.py:207
  9.6 0.0 collective-permute-start.4
  9.6 0.7 %collective-permute-done.2.refs_6_ = bf16[16,3200]{1,0:T(8,128)(2,1)S(1)} collective-permute-done((bf16[16,3200]{1,0:T(8,128)(2,1)}, bf16[16,3200]{1,0:T(8,128)(2,1)S(1)}, u32[]{:S(2)}, u32[]{:S(2)}) %collective-permute-start.2) | collective-permute-done | bytes 102432 | tf_op jit(solution)/shard_map/ppermute | solution.py:207
  10.4 1.7 %collective-permute-start.5 = (bf16[16,3200]{1,0:T(8,128)(2,1)}, bf16[16,3200]{1,0:T(8,128)(2,1)S(1)}, u32[]{:S(2)}, u32[]{:S(2)}) collective-permute-start(bf16[16,3200]{1,0:T(8,128)(2,1)} %get-tuple-element.13.refs_5_), channel_id=1, source_target_pairs={{0,2},{1,3},{2,0},{3,1},{4,6},{5,7},{6,4},{7,5},{8,10},{9,11},{10,... | collective-permute-start | bytes 307208 | tf_op jit(solution)/shard_map/ppermute | solution.py:207
  12.0 6.2 %collective-permute-done.3.refs_7_ = bf16[16,3200]{1,0:T(8,128)(2,1)S(1)} collective-permute-done((bf16[16,3200]{1,0:T(8,128)(2,1)}, bf16[16,3200]{1,0:T(8,128)(2,1)S(1)}, u32[]{:S(2)}, u32[]{:S(2)}) %collective-permute-start.3) | collective-permute-done | bytes 102432 | tf_op jit(solution)/shard_map/ppermute | solution.py:207
  18.2 1.5 %collective-permute-start.6 = (bf16[16,3200]{1,0:T(8,128)(2,1)S(1)}, bf16[16,3200]{1,0:T(8,128)(2,1)S(1)}, u32[]{:S(2)}, u32[]{:S(2)}) collective-permute-start(bf16[16,3200]{1,0:T(8,128)(2,1)S(1)} %collective-permute-done.2.refs_6_), channel_id=1, source_target_pairs={{0,2},{1,3},{2,0},{3,1},{4,6},{5,7},{6,4},{7,5},{8,10},{9,11},{10,... | collective-permute-start | bytes 307208 | tf_op jit(solution)/shard_map/ppermute | solution.py:207
  19.7 0.0 collective-permute-done.4.refs_8_
  19.7 0.5 %collective-permute-start.7 = (bf16[16,3200]{1,0:T(8,128)(2,1)S(1)}, bf16[16,3200]{1,0:T(8,128)(2,1)S(1)}, u32[]{:S(2)}, u32[]{:S(2)}) collective-permute-start(bf16[16,3200]{1,0:T(8,128)(2,1)S(1)} %collective-permute-done.3.refs_7_), channel_id=1, source_target_pairs={{0,2},{1,3},{2,0},{3,1},{4,6},{5,7},{6,4},{7,5},{8,10},{9,11},{10,... | collective-permute-start | bytes 307208 | tf_op jit(solution)/shard_map/ppermute | solution.py:207
  20.3 0.0 collective-permute-done.refs_2_
  20.3 1.5 %collective-permute-start.8 = (bf16[16,3200]{1,0:T(8,128)(2,1)S(1)}, bf16[16,3200]{1,0:T(8,128)(2,1)S(1)}, u32[]{:S(2)}, u32[]{:S(2)}) collective-permute-start(bf16[16,3200]{1,0:T(8,128)(2,1)S(1)} %collective-permute-done.4.refs_8_), channel_id=1, source_target_pairs={{0,2},{1,3},{2,0},{3,1},{4,6},{5,7},{6,4},{7,5},{8,10},{9,11},{10,... | collective-permute-start | bytes 307208 | tf_op jit(solution)/shard_map/ppermute | solution.py:207
  21.8 0.0 collective-permute-done.1.refs_3_
  21.8 0.0 copy-done
  21.8 0.0 copy-done.3
  21.8 0.0 copy-start.1
  21.8 1.4 %copy-done.1 = bf16[1,4096,192]{1,2,0:T(8,128)(2,1)S(1)} copy-done((bf16[1,4096,192]{1,2,0:T(8,128)(2,1)S(1)}, bf16[1,4096,192]{1,2,0:T(8,128)(2,1)}, u32[]{:S(2)}) %copy-start.1) | copy-done | bytes 1572888
  23.2 0.0 copy-start.2
  23.2 0.9 %copy-done.2 = bf16[16,3200]{1,0:T(8,128)(2,1)S(1)} copy-done((bf16[16,3200]{1,0:T(8,128)(2,1)S(1)}, bf16[16,3200]{1,0:T(8,128)(2,1)}, u32[]{:S(2)}) %copy-start.2) | copy-done | bytes 102424
  24.1 3.6 %shard_map.101 = (f32[64,64]{1,0:T(8,128)S(1)}, bf16[64,128]{1,0:T(8,128)(2,1)S(1)}, bf16[64,192]{1,0:T(8,128)(2,1)S(1)}, bf16[64,192]{1,0:T(8,128)(2,1)S(1)}) custom-call(bf16[192,4096]{1,0:T(8,128)(2,1)S(1)} %bitcast.13, bf16[192,4096]{1,0:T(8,128)(2,1)S(1)} %bitcast.16, bf16[192,4096]{1,0:T(8,128)(2,1)S(1)} %collective-permute-done.refs_2_, ...), custom_call_target="tpu_custom_call" | custom-call | flops 402653184 | bytes 6684672 | tf_op jit(solution)/shard_map/pallas_call | solution.py:266
  27.6 0.0 collective-permute-done.5.refs_6_
  27.6 0.0 collective-permute-done.6.refs_7_
  27.6 0.0 collective-permute-done.7.refs_8_
  27.7 0.0 collective-permute-done.8.refs_9_
  27.7 3.3 %shard_map.102 = bf16[64,64]{1,0:T(8,128)(2,1)S(1)} custom-call(bf16[192,4096]{1,0:T(8,128)(2,1)S(1)} %bitcast.14, bf16[192,4096]{1,0:T(8,128)(2,1)S(1)} %bitcast.17, bf16[192,4096]{1,0:T(8,128)(2,1)S(1)} %collective-permute-done.refs_2_, bf16[192,4096]{1,0:T(8,128)(2,1)} %collective-permute-done.1.refs_3_, bf16[64,192]{1,0:T(8,128)(2,1)S(1)} %get-tuple-element.19.refs_4_, ...), custom_call_target="tpu_custom_call" | custom-call | flops 402653184 | bytes 6684672 | tf_op jit(solution)/shard_map/pallas_call | solution.py:276
  31.0 0.6 %collective-permute-start.9 = (bf16[64,64]{1,0:T(8,128)(2,1)S(1)}, bf16[64,64]{1,0:T(8,128)(2,1)S(1)}, u32[]{:S(2)}, u32[]{:S(2)}) collective-permute-start(bf16[64,64]{1,0:T(8,128)(2,1)S(1)} %shard_map.102), channel_id=1, source_target_pairs={{0,2},{1,3},{2,0},{3,1},{4,6},{5,7},{6,4},{7,5},{8,10},{9,11},{10,... | collective-permute-start | bytes 24584 | tf_op jit(solution)/shard_map/ppermute | solution.py:207
  31.6 3.2 %collective-permute-done.9.refs_1_ = bf16[64,64]{1,0:T(8,128)(2,1)S(1)} collective-permute-done((bf16[64,64]{1,0:T(8,128)(2,1)S(1)}, bf16[64,64]{1,0:T(8,128)(2,1)S(1)}, u32[]{:S(2)}, u32[]{:S(2)}) %collective-permute-start.9) | collective-permute-done | bytes 8224 | tf_op jit(solution)/shard_map/ppermute | solution.py:207
  34.8 0.8 %shard_map.103 = f32[2,32,128]{2,1,0:T(8,128)} custom-call(bf16[64,128]{1,0:T(8,128)(2,1)S(1)} %get-tuple-element.17.grads_ref, f32[64,64]{1,0:T(8,128)S(1)} %get-tuple-element.18.refs_0_, bf16[64,64]{1,0:T(8,128)(2,1)S(1)} %collective-permute-done.9.refs_1_), custom_call_target="tpu_custom_call" | custom-call | flops 1048576 | bytes 32768 | tf_op jit(solution)/shard_map/pallas_call | solution.py:284
Async XLA Ops:
  0.0 21.8 %copy-start = (bf16[1,4096,192]{1,2,0:T(8,128)(2,1)S(1)}, bf16[1,4096,192]{1,2,0:T(8,128)(2,1)}, u32[]{:S(2)}) copy-start(bf16[1,4096,192]{1,2,0:T(8,128)(2,1)} %param.16) | copy-start | bytes 4718596
  0.0 21.8 %copy-start.3 = (bf16[768,64]{0,1:T(8,128)(2,1)S(1)}, bf16[768,64]{0,1:T(8,128)(2,1)}, u32[]{:S(2)}) copy-start(bf16[768,64]{0,1:T(8,128)(2,1)} %param.18) | copy-start | bytes 294916
  0.0 20.2 %collective-permute-start = (bf16[192,4096]{1,0:T(8,128)(2,1)}, bf16[192,4096]{1,0:T(8,128)(2,1)S(1)}, u32[]{:S(2)}, u32[]{:S(2)}) collective-permute-start(bf16[192,4096]{1,0:T(8,128)(2,1)} %bitcast.12), channel_id=1, source_target_pairs={{0,1},{1,0},{2,3},{3,2},{4,5},{5,4},{6,7},{7,6},{8,9},{9,8},{10,11... | collective-permute-start | bytes 4718600 | tf_op jit(solution)/shard_map/ppermute | solution.py:207
  0.5 21.3 %collective-permute-start.1 = (bf16[192,4096]{1,0:T(8,128)(2,1)}, bf16[192,4096]{1,0:T(8,128)(2,1)}, u32[]{:S(2)}, u32[]{:S(2)}) collective-permute-start(bf16[192,4096]{1,0:T(8,128)(2,1)} %bitcast.15), channel_id=1, source_target_pairs={{0,1},{1,0},{2,3},{3,2},{4,5},{5,4},{6,7},{7,6},{8,9},{9,8},{10,11... | collective-permute-start | bytes 4718600 | tf_op jit(solution)/shard_map/ppermute | solution.py:207
  4.0 6.4 %collective-permute-start.2 = (bf16[16,3200]{1,0:T(8,128)(2,1)}, bf16[16,3200]{1,0:T(8,128)(2,1)S(1)}, u32[]{:S(2)}, u32[]{:S(2)}) collective-permute-start(bf16[16,3200]{1,0:T(8,128)(2,1)} %get-tuple-element.14), channel_id=1, source_target_pairs={{0,4},{4,0},{8,12},{12,8},{1,5},{5,1},{9,13},{13,9},{2,6},{6,2},{1... | collective-permute-start | bytes 307208 | tf_op jit(solution)/shard_map/ppermute | solution.py:207
  7.0 11.2 %collective-permute-start.3 = (bf16[16,3200]{1,0:T(8,128)(2,1)}, bf16[16,3200]{1,0:T(8,128)(2,1)S(1)}, u32[]{:S(2)}, u32[]{:S(2)}) collective-permute-start(bf16[16,3200]{1,0:T(8,128)(2,1)} %get-tuple-element.15), channel_id=1, source_target_pairs={{0,8},{4,12},{8,0},{12,4},{1,9},{5,13},{9,1},{13,5},{2,10},{6,14},... | collective-permute-start | bytes 307208 | tf_op jit(solution)/shard_map/ppermute | solution.py:207
  9.6 10.1 %collective-permute-start.4 = (bf16[16,3200]{1,0:T(8,128)(2,1)}, bf16[16,3200]{1,0:T(8,128)(2,1)S(1)}, u32[]{:S(2)}, u32[]{:S(2)}) collective-permute-start(bf16[16,3200]{1,0:T(8,128)(2,1)} %get-tuple-element.16), channel_id=1, source_target_pairs={{0,12},{4,8},{8,4},{12,0},{1,13},{5,9},{9,5},{13,1},{2,14},{6,10},... | collective-permute-start | bytes 307208 | tf_op jit(solution)/shard_map/ppermute | solution.py:207
  10.4 17.3 %collective-permute-start.5 = (bf16[16,3200]{1,0:T(8,128)(2,1)}, bf16[16,3200]{1,0:T(8,128)(2,1)S(1)}, u32[]{:S(2)}, u32[]{:S(2)}) collective-permute-start(bf16[16,3200]{1,0:T(8,128)(2,1)} %get-tuple-element.13.refs_5_), channel_id=1, source_target_pairs={{0,2},{1,3},{2,0},{3,1},{4,6},{5,7},{6,4},{7,5},{8,10},{9,11},{10,... | collective-permute-start | bytes 307208 | tf_op jit(solution)/shard_map/ppermute | solution.py:207
  18.2 9.4 %collective-permute-start.6 = (bf16[16,3200]{1,0:T(8,128)(2,1)S(1)}, bf16[16,3200]{1,0:T(8,128)(2,1)S(1)}, u32[]{:S(2)}, u32[]{:S(2)}) collective-permute-start(bf16[16,3200]{1,0:T(8,128)(2,1)S(1)} %collective-permute-done.2.refs_6_), channel_id=1, source_target_pairs={{0,2},{1,3},{2,0},{3,1},{4,6},{5,7},{6,4},{7,5},{8,10},{9,11},{10,... | collective-permute-start | bytes 307208 | tf_op jit(solution)/shard_map/ppermute | solution.py:207
  19.7 7.9 %collective-permute-start.7 = (bf16[16,3200]{1,0:T(8,128)(2,1)S(1)}, bf16[16,3200]{1,0:T(8,128)(2,1)S(1)}, u32[]{:S(2)}, u32[]{:S(2)}) collective-permute-start(bf16[16,3200]{1,0:T(8,128)(2,1)S(1)} %collective-permute-done.3.refs_7_), channel_id=1, source_target_pairs={{0,2},{1,3},{2,0},{3,1},{4,6},{5,7},{6,4},{7,5},{8,10},{9,11},{10,... | collective-permute-start | bytes 307208 | tf_op jit(solution)/shard_map/ppermute | solution.py:207
  20.3 7.4 %collective-permute-start.8 = (bf16[16,3200]{1,0:T(8,128)(2,1)S(1)}, bf16[16,3200]{1,0:T(8,128)(2,1)S(1)}, u32[]{:S(2)}, u32[]{:S(2)}) collective-permute-start(bf16[16,3200]{1,0:T(8,128)(2,1)S(1)} %collective-permute-done.4.refs_8_), channel_id=1, source_target_pairs={{0,2},{1,3},{2,0},{3,1},{4,6},{5,7},{6,4},{7,5},{8,10},{9,11},{10,... | collective-permute-start | bytes 307208 | tf_op jit(solution)/shard_map/ppermute | solution.py:207
  21.8 1.4 %copy-start.1 = (bf16[1,4096,192]{1,2,0:T(8,128)(2,1)S(1)}, bf16[1,4096,192]{1,2,0:T(8,128)(2,1)}, u32[]{:S(2)}) copy-start(bf16[1,4096,192]{1,2,0:T(8,128)(2,1)} %param.17) | copy-start | bytes 4718596
  23.2 0.9 %copy-start.2 = (bf16[16,3200]{1,0:T(8,128)(2,1)S(1)}, bf16[16,3200]{1,0:T(8,128)(2,1)}, u32[]{:S(2)}) copy-start(bf16[16,3200]{1,0:T(8,128)(2,1)} %get-tuple-element.13.refs_5_) | copy-start | bytes 307204
  31.0 3.8 %collective-permute-start.9 = (bf16[64,64]{1,0:T(8,128)(2,1)S(1)}, bf16[64,64]{1,0:T(8,128)(2,1)S(1)}, u32[]{:S(2)}, u32[]{:S(2)}) collective-permute-start(bf16[64,64]{1,0:T(8,128)(2,1)S(1)} %shard_map.102), channel_id=1, source_target_pairs={{0,2},{1,3},{2,0},{3,1},{4,6},{5,7},{6,4},{7,5},{8,10},{9,11},{10,... | collective-permute-start | bytes 24584 | tf_op jit(solution)/shard_map/ppermute | solution.py:207

commit v4 on v3

--- a/solution.py
+++ b/solution.py
@@ -14,6 +14,8 @@
 PARTS = LOCAL_SEATS // SPARE
 HALF = ROWS // 2
 MIB = 1024 * 1024
+SEND_LIMIT = 56
+OWN_LIMIT = 20
 BF16 = jnp.bfloat16
 F32 = jnp.float32
 
@@ -105,24 +107,22 @@
         out_refs[q][:, PARTS * chunk :] = jnp.concatenate(halves, axis=1).astype(BF16)
 
 
-def pair_compressors(compressor_ref, units):
+def pair_compressor(compressor_ref, units):
     place = lax.axis_index("dp")
     rank, total = compressor_ref.shape
     to = lax.broadcasted_iota(jnp.int32, (rank, rank), 0)
     at = lax.broadcasted_iota(jnp.int32, (rank, rank), 1)
     order = one_hot(at == jnp.where(to < rank // 2, 2 * to, 2 * to - rank + 1))
     turned = dot(order, compressor_ref[...]).astype(BF16)
-    line = lax.broadcasted_iota(jnp.int32, (total, units), 0)
-    unit = lax.broadcasted_iota(jnp.int32, (total, units), 1)
-    return [
-        dot(turned, one_hot(line == unit + jnp.bitwise_xor(place, k) * units)).astype(BF16)
-        for k in range(2)
-    ]
-
-
-def sketch_of(weights, compressors, block_refs):
-    width = weights[0][0].shape[1]
-    chunk = width // (PARTS + 1)
+    line = lax.broadcasted_iota(jnp.int32, (total, 2 * units), 0)
+    unit = lax.broadcasted_iota(jnp.int32, (total, 2 * units), 1)
+    pair = jnp.bitwise_xor(place, 1)
+    wanted = jnp.where(unit < units, place * units + unit, (pair - 1) * units + unit)
+    return dot(turned, one_hot(line == wanted)).astype(BF16)
+
+
+def sketch_of(weights_ref, compressor, block_refs, ready=lambda i: None):
+    chunk = weights_ref.shape[1] // (PARTS + 1)
     size = sum(r.shape[0] for r in block_refs)
     messages = size // ROWS
     low = lax.broadcasted_iota(jnp.int32, (1, HALF, 1), 1) < SPARE
@@ -136,40 +136,46 @@
     top = jnp.where(low, turn(tails[0]), tails[1])
     bottom = jnp.where(low, turn(tails[2]), 0.0)
     rows.append(jnp.stack([top, bottom], axis=1).reshape(size, chunk).astype(BF16))
-    seat = lax.broadcasted_iota(jnp.int32, (1, size), 1) % ROWS
-
-    def product(w):
-        total = dot_t(w[:, columns[0]], rows[0])
-        for c, r in zip(columns[1:], rows[1:]):
-            total = total + dot_t(w[:, c], r)
-        return total
-
-    sketch = None
-    for (gate_ref, up_ref), compressor in zip(weights, compressors):
-        gate, up = product(gate_ref), product(up_ref)
-        hidden = gate / (1.0 + jnp.exp(-gate)) * up
-        hidden = jnp.where(seat < LOCAL_SEATS, hidden, 0.0).astype(BF16)
-        term = dot(compressor, hidden)
-        sketch = term if sketch is None else sketch + term
-    return sketch
-
-
-def own_kernel(n_blocks, *refs):
-    weights = (refs[0:2], refs[2:4])
-    compressor_ref, block_refs = refs[4], refs[5 : 5 + n_blocks]
-    sketch_ref, grads_ref, *chosen_refs = refs[5 + n_blocks :]
-    units, width = weights[0][0].shape
-    chosen = pair_compressors(compressor_ref, units)
-    for ref, value in zip(chosen_refs, chosen):
-        ref[...] = value
-    grads_ref[...] = jnp.concatenate([r[:, width * LOCAL_SEATS // ROWS :] for r in block_refs], axis=0)
-    sketch_ref[...] = sketch_of(weights, chosen, block_refs)
-
-
-def far_kernel(n_blocks, *refs):
-    weights = (refs[0:2], refs[2:4])
-    chosen = [r[...] for r in refs[4:6]]
-    refs[-1][...] = sketch_of(weights, chosen, refs[6 : 6 + n_blocks]).astype(refs[-1].dtype)
+    total = None
+    for i, r in enumerate(rows):
+        ready(i)
+        term = dot_t(r, weights_ref[:, columns[i]])
+        total = term if total is None else total + term
+    half = total.shape[1] // 2
+    gate, up = total[:, :half], total[:, half:]
+    hidden = gate / (1.0 + jnp.exp(-gate)) * up
+    seat = lax.broadcasted_iota(jnp.int32, (size, 1), 0) % ROWS
+    hidden = jnp.where(seat < LOCAL_SEATS, hidden, 0.0).astype(BF16)
+    return dot_t(compressor, hidden)
+
+
+def own_kernel(gate_hbm, pair_gate_hbm, up_hbm, pair_up_hbm, compressor_ref, *refs):
+    block_refs, (sketch_ref, grads_ref, chosen_ref, weights_ref, sems) = refs[:-5], refs[-5:]
+    units, width = gate_hbm.shape
+    chunk = width // (PARTS + 1)
+    copies = []
+    for i in range(PARTS + 1):
+        columns = pl.ds(i * chunk, chunk)
+        for k, source in enumerate((gate_hbm, pair_gate_hbm, up_hbm, pair_up_hbm)):
+            target = weights_ref.at[pl.ds(k * units, units), columns]
+            copies.append(
+                pltpu.make_async_copy(source.at[:, columns], target, sems.at[len(copies)])
+            )
+    for copy in copies:
+        copy.start()
+    chosen = pair_compressor(compressor_ref, units)
+    chosen_ref[...] = chosen
+    grads_ref[...] = jnp.concatenate([r[:, PARTS * chunk :] for r in block_refs], axis=0)
+
+    def ready(i):
+        for copy in copies[4 * i : 4 * i + 4]:
+            copy.wait()
+
+    sketch_ref[...] = sketch_of(weights_ref, chosen, block_refs, ready)
+
+
+def far_kernel(weights_ref, chosen_ref, *refs):
+    refs[-1][...] = sketch_of(weights_ref, chosen_ref[...], refs[:-1]).astype(refs[-1].dtype)
 
 
 def outer_kernel(grads_ref, *refs):
@@ -230,8 +236,6 @@
 
     gate, up = gating_projection[0].T, raising_projection[0].T
     pair_gate, pair_up = swap(gate, "dp", 1), swap(up, "dp", 1)
-    weights = (gate, up, pair_gate, pair_up)
-
     arguments = (
         send_limits,
         picked_specialists.T,
@@ -246,40 +250,61 @@
         functools.partial(send_kernel, n_exp),
         [shape((ROWS, packed + EX_DEV * rank), BF16)] * n_exp,
         [HBM] * len(arguments),
-        60 * MIB,
+        SEND_LIMIT * MIB,
         flops=4 * size * tokens * packed + 2 * tokens * width * rank,
         moved=4 * tokens * width + 2 * rank * width,
         scratch=[space(a.shape, a.dtype) for space, a in zip(spaces, arguments)]
         + [pltpu.SemaphoreType.DMA((len(arguments),))],
     )(*arguments)
-    rows = [rows[0]] + [swap(rows[q], "exp", q) for q in range(1, n_exp)]
-
-    blocks = {0: rows if small else [jnp.concatenate(rows, axis=0)]}
-    step = n_dp // 2
+    hold = lax.optimization_barrier
+    order = [n_exp - 1] + list(range(1, n_exp - 1))
+    half = n_dp // 2
+    rows = list(rows)
+    pair_gate, pair_up, rows[0] = hold((pair_gate, pair_up, rows[0]))
+    moved = {q: swap(rows[q], "exp", q) for q in order}
+    rows[order[0]] = moved[order[0]]
+    for q, r in zip(order, order[1:]):
+        rows[q], rows[r] = hold((rows[q], moved[r]))
+    if small:
+        crossed = {q: swap(rows[q], "dp", half) for q in [0] + order[:-1]}
+        last = order[-1]
+        crossed[0], crossed[order[0]], rows[last] = hold((crossed[0], crossed[order[0]], rows[last]))
+        crossed[last] = swap(rows[last], "dp", half)
+        crossed = [crossed[q] for q in range(n_exp)]
+    else:
+        rows = [jnp.concatenate(rows, axis=0)]
+        crossed = [swap(rows[0], "dp", half)]
+    blocks = {0: rows, half: crossed}
+    step = half // 2
     while step > 1:
         for d in list(blocks):
             blocks[d ^ step] = [swap(r, "dp", step) for r in blocks[d]]
         step //= 2
 
     cost = dict(flops=8 * size * width * units, moved=8 * width * units + 2 * size * packed)
-    chosen_shape = shape((rank, units), BF16)
-    own, grads, *chosen = call(
-        functools.partial(own_kernel, len(blocks[0])),
-        [shape((rank, size), F32), shape((size, EX_DEV * rank), BF16), chosen_shape, chosen_shape],
-        [VMEM] * (5 + len(blocks[0])),
-        20 * MIB,
+    own, grads, chosen, weights = call(
+        own_kernel,
+        [
+            shape((rank, size), F32),
+            shape((size, EX_DEV * rank), BF16),
+            shape((rank, 2 * units), BF16),
+            shape((4 * units, width), BF16),
+        ],
+        [HBM] * 4 + [VMEM] * (1 + len(rows)),
+        OWN_LIMIT * MIB,
         **cost,
-    )(*weights, inflow_compressor.T, *blocks[0])
+        scratch=[pltpu.SemaphoreType.DMA((4 * (PARTS + 1),))],
+    )(gate, pair_gate, up, pair_up, inflow_compressor.T, *rows)
     partials = [own]
     for d in sorted(blocks):
         if d:
             far = call(
-                functools.partial(far_kernel, len(blocks[d])),
+                far_kernel,
                 shape((rank, size), BF16),
-                [VMEM] * (6 + len(blocks[d])),
+                [VMEM] * (2 + len(blocks[d])),
                 20 * MIB,
                 **cost,
-            )(*weights, *chosen, *blocks[d])
+            )(weights, chosen, *blocks[d])
             partials.append(swap(far, "dp", d))
     out = call(
         outer_kernel,

time: 35.9 us -> 37.7 us (1.050)
  waiting for transfers between devices: 10.1 us -> 13.1 us
  Pallas kernels: 11.1 us -> 10.2 us
    ppermute x10, waiting for transfers between devices: 10.1 us -> 13.1 us  [swap(): return lax.ppermute(a, axis, [(i, i ^ q) for i in range(n)])]
    pallas_call x2, Pallas kernels: 6.88 us -> 5.93 us  [the longest x1 3.76 us: body(): call(own_kernel, [shape((rank, size), F32), shape((size, EX_DEV * rank),...]
  transfers between devices with their start and end apart: 10 -> 10, of which waited for: 3 -> 6; matrix products, arithmetic and copies ran while one was open for 0% -> 0% of each run, Pallas kernels for 20% -> 19%
where the time goes in v4:
time: 37.7 us; the launch traced here: 37.5 us
  waiting for transfers between devices  13.1 us (35%)
  starting transfers between devices  11.9 us (32%)
  Pallas kernels  10.2 us (27%)
  local copies, waits for them, and re-layouts  2.31 us (6%)
    ppermute x10, waiting for transfers between devices, swap(): return lax.ppermute(a, axis, [(i, i ^ q) for i in range(n)])  13.1 us
    ppermute x10, starting transfers between devices, swap(): return lax.ppermute(a, axis, [(i, i ^ q) for i in range(n)])  11.9 us
    pallas_call x1, Pallas kernels, body(): call(own_kernel, [shape((rank, size), F32), shape((size, EX_DEV * rank),...  3.76 us
    pallas_call x1, Pallas kernels, body(): call(functools.partial(send_kernel, n_exp), [shape((ROWS, packed + EX_DEV...  3.41 us
    unnamed x8, local copies, waits for them, and re-layouts  2.31 us
    pallas_call x1, Pallas kernels, body(): call(far_kernel, shape((rank, size), BF16), [VMEM] * (2 + len(blocks[d]))...  2.17 us
    pallas_call x1, Pallas kernels, body(): call(outer_kernel, shape((EX_DEV, rank * rank // 128, 128), F32), [VMEM]...  0.81 us
  transfers between devices with their start and end apart: 10, of which 6 were waited for; matrix products, arithmetic and copies ran while one was open for 0% of the time, Pallas kernels for 19%

profile of v4, /device:TPU:0, one launch (start us, length us, event | category | flops | bytes accessed | tf_op | source)
XLA Modules:
  0.0 37.5 jit_solution(17844074060324179041)
XLA Ops:
  0.0 0.0 copy-start
  0.0 0.0 copy-start.3
  0.0 0.5 %collective-permute-start = (bf16[192,4096]{1,0:T(8,128)(2,1)}, bf16[192,4096]{1,0:T(8,128)(2,1)S(1)}, u32[]{:S(2)}, u32[]{:S(2)}) collective-permute-start(bf16[192,4096]{1,0:T(8,128)(2,1)} %bitcast.12), channel_id=1, source_target_pairs={{0,1},{1,0},{2,3},{3,2},{4,5},{5,4},{6,7},{7,6},{8,9},{9,8},{10,11... | collective-permute-start | bytes 4718600 | tf_op jit(solution)/shard_map/ppermute | solution.py:213
  0.5 0.1 collective-permute-start.1
  0.5 3.4 %shard_map.100 = (bf16[16,3200]{1,0:T(8,128)(2,1)}, bf16[16,3200]{1,0:T(8,128)(2,1)}, bf16[16,3200]{1,0:T(8,128)(2,1)}, bf16[16,3200]{1,0:T(8,128)(2,1)}) custom-call(s32[128]{0:T(128)} %limits_hbm.1, s32[8,128]{1,0:T(8,128)} %bitcast.18, f32[8,128]{1,0:T(8,128)} %bitcast.19, s32[1,128]{1,0:T(1,128)} %bitcast.20, bf16[128,4096]{1,0:T(8,128)(2,1)} %tokens_hbm.1, ...), custom_call_target="tpu_custom_call" | custom-call | flops 167772160 | bytes 2621440 | tf_op jit(solution)/shard_map/pallas_call | solution.py:249
  4.0 5.1 %collective-permute-start.2 = (bf16[16,3200]{1,0:T(8,128)(2,1)}, bf16[16,3200]{1,0:T(8,128)(2,1)S(1)}, u32[]{:S(2)}, u32[]{:S(2)}) collective-permute-start(bf16[16,3200]{1,0:T(8,128)(2,1)} %get-tuple-element.27), channel_id=1, source_target_pairs={{0,12},{4,8},{8,4},{12,0},{1,13},{5,9},{9,5},{13,1},{2,14},{6,10},... | collective-permute-start | bytes 307208 | tf_op jit(solution)/shard_map/ppermute | solution.py:213
  9.1 0.0 collective-permute-start.3
  9.1 0.6 %collective-permute-start.4 = (bf16[16,3200]{1,0:T(8,128)(2,1)}, bf16[16,3200]{1,0:T(8,128)(2,1)S(1)}, u32[]{:S(2)}, u32[]{:S(2)}) collective-permute-start(bf16[16,3200]{1,0:T(8,128)(2,1)} %get-tuple-element.30), channel_id=1, source_target_pairs={{0,8},{4,12},{8,0},{12,4},{1,9},{5,13},{9,1},{13,5},{2,10},{6,14},... | collective-permute-start | bytes 307208 | tf_op jit(solution)/shard_map/ppermute | solution.py:213
  9.7 3.3 %collective-permute-done.2.refs_3_ = bf16[16,3200]{1,0:T(8,128)(2,1)S(1)} collective-permute-done((bf16[16,3200]{1,0:T(8,128)(2,1)}, bf16[16,3200]{1,0:T(8,128)(2,1)S(1)}, u32[]{:S(2)}, u32[]{:S(2)}) %collective-permute-start.2) | collective-permute-done | bytes 102432 | tf_op jit(solution)/shard_map/ppermute | solution.py:213
  13.0 2.7 %collective-permute-done.3.refs_1_ = bf16[16,3200]{1,0:T(8,128)(2,1)S(1)} collective-permute-done((bf16[16,3200]{1,0:T(8,128)(2,1)}, bf16[16,3200]{1,0:T(8,128)(2,1)S(1)}, u32[]{:S(2)}, u32[]{:S(2)}) %collective-permute-start.3) | collective-permute-done | bytes 102432 | tf_op jit(solution)/shard_map/ppermute | solution.py:213
  15.7 1.5 %collective-permute-start.6 = (bf16[16,3200]{1,0:T(8,128)(2,1)S(1)}, bf16[16,3200]{1,0:T(8,128)(2,1)S(1)}, u32[]{:S(2)}, u32[]{:S(2)}) collective-permute-start(bf16[16,3200]{1,0:T(8,128)(2,1)S(1)} %collective-permute-done.2.refs_3_), channel_id=1, source_target_pairs={{0,2},{1,3},{2,0},{3,1},{4,6},{5,7},{6,4},{7,5},{8,10},{9,11},{10,... | collective-permute-start | bytes 307208 | tf_op jit(solution)/shard_map/ppermute | solution.py:213
  17.2 0.0 collective-permute-done.pair_gate_hbm
  17.2 0.0 collective-permute-done.1.pair_up_hbm
  17.2 0.6 %collective-permute-start.5 = (bf16[16,3200]{1,0:T(8,128)(2,1)}, bf16[16,3200]{1,0:T(8,128)(2,1)S(1)}, u32[]{:S(2)}, u32[]{:S(2)}) collective-permute-start(bf16[16,3200]{1,0:T(8,128)(2,1)} %get-tuple-element.26.refs_0_), channel_id=1, source_target_pairs={{0,2},{1,3},{2,0},{3,1},{4,6},{5,7},{6,4},{7,5},{8,10},{9,11},{10,... | collective-permute-start | bytes 307208 | tf_op jit(solution)/shard_map/ppermute | solution.py:213
  17.7 0.4 %collective-permute-done.4.refs_2_ = bf16[16,3200]{1,0:T(8,128)(2,1)S(1)} collective-permute-done((bf16[16,3200]{1,0:T(8,128)(2,1)}, bf16[16,3200]{1,0:T(8,128)(2,1)S(1)}, u32[]{:S(2)}, u32[]{:S(2)}) %collective-permute-start.4) | collective-permute-done | bytes 102432 | tf_op jit(solution)/shard_map/ppermute | solution.py:213
  18.1 1.5 %collective-permute-start.7 = (bf16[16,3200]{1,0:T(8,128)(2,1)S(1)}, bf16[16,3200]{1,0:T(8,128)(2,1)S(1)}, u32[]{:S(2)}, u32[]{:S(2)}) collective-permute-start(bf16[16,3200]{1,0:T(8,128)(2,1)S(1)} %collective-permute-done.3.refs_1_), channel_id=1, source_target_pairs={{0,2},{1,3},{2,0},{3,1},{4,6},{5,7},{6,4},{7,5},{8,10},{9,11},{10,... | collective-permute-start | bytes 307208 | tf_op jit(solution)/shard_map/ppermute | solution.py:213
  19.6 1.8 %collective-permute-done.6.refs_3_ = bf16[16,3200]{1,0:T(8,128)(2,1)S(1)} collective-permute-done((bf16[16,3200]{1,0:T(8,128)(2,1)S(1)}, bf16[16,3200]{1,0:T(8,128)(2,1)S(1)}, u32[]{:S(2)}, u32[]{:S(2)}) %collective-permute-start.6) | collective-permute-done | bytes 102432 | tf_op jit(solution)/shard_map/ppermute | solution.py:213
  21.4 2.0 %collective-permute-done.5.refs_0_ = bf16[16,3200]{1,0:T(8,128)(2,1)S(1)} collective-permute-done((bf16[16,3200]{1,0:T(8,128)(2,1)}, bf16[16,3200]{1,0:T(8,128)(2,1)S(1)}, u32[]{:S(2)}, u32[]{:S(2)}) %collective-permute-start.5) | collective-permute-done | bytes 102432 | tf_op jit(solution)/shard_map/ppermute | solution.py:213
  23.4 1.2 %collective-permute-start.8 = (bf16[16,3200]{1,0:T(8,128)(2,1)S(1)}, bf16[16,3200]{1,0:T(8,128)(2,1)S(1)}, u32[]{:S(2)}, u32[]{:S(2)}) collective-permute-start(bf16[16,3200]{1,0:T(8,128)(2,1)S(1)} %collective-permute-done.4.refs_2_), channel_id=1, source_target_pairs={{0,2},{1,3},{2,0},{3,1},{4,6},{5,7},{6,4},{7,5},{8,10},{9,11},{10,... | collective-permute-start | bytes 307208 | tf_op jit(solution)/shard_map/ppermute | solution.py:213
  24.6 0.0 copy-done
  24.6 0.0 copy-done.3
  24.6 0.0 copy-start.1
  24.6 1.4 %copy-done.1 = bf16[1,4096,192]{1,2,0:T(8,128)(2,1)S(1)} copy-done((bf16[1,4096,192]{1,2,0:T(8,128)(2,1)S(1)}, bf16[1,4096,192]{1,2,0:T(8,128)(2,1)}, u32[]{:S(2)}) %copy-start.1) | copy-done | bytes 1572888
  26.0 0.0 copy-start.2
  26.0 0.9 %copy-done.2 = bf16[16,3200]{1,0:T(8,128)(2,1)S(1)} copy-done((bf16[16,3200]{1,0:T(8,128)(2,1)S(1)}, bf16[16,3200]{1,0:T(8,128)(2,1)}, u32[]{:S(2)}) %copy-start.2) | copy-done | bytes 102424
  26.9 3.8 %shard_map.101 = (f32[64,64]{1,0:T(8,128)S(1)}, bf16[64,128]{1,0:T(8,128)(2,1)S(1)}, bf16[64,384]{1,0:T(8,128)(2,1)S(1)}, bf16[768,4096]{1,0:T(8,128)(2,1)S(1)}) custom-call(bf16[192,4096]{1,0:T(8,128)(2,1)S(1)} %bitcast.13, bf16[192,4096]{1,0:T(8,128)(2,1)S(1)} %collective-permute-done.pair_gate_hbm, bf16[192,4096]{1,0:T(8,128)(2,1)S(1)} %bitcast.15, ...), custom_call_target="tpu_custom_call" | custom-call | flops 402653184 | bytes 6684672 | tf_op jit(solution)/shard_map/pallas_call | solution.py:285
  30.7 0.0 collective-permute-done.7.refs_1_
  30.7 0.0 collective-permute-done.8.refs_2_
  30.7 2.2 %shard_map.102 = bf16[64,64]{1,0:T(8,128)(2,1)S(1)} custom-call(bf16[768,4096]{1,0:T(8,128)(2,1)S(1)} %get-tuple-element.37.weights_ref, bf16[64,384]{1,0:T(8,128)(2,1)S(1)} %get-tuple-element.38.chosen_ref, bf16[16,3200]{1,0:T(8,128)(2,1)S(1)} %collective-permute-done.5.refs_0_, bf16[16,3200]{1,0:T(8,128)(2,1)S(1)} %collective-permute-done.7.refs_1_, ...), custom_call_target="tpu_custom_call" | custom-call | flops 402653184 | bytes 6684672 | tf_op jit(solution)/shard_map/pallas_call | solution.py:301
  32.9 0.9 %collective-permute-start.9 = (bf16[64,64]{1,0:T(8,128)(2,1)S(1)}, bf16[64,64]{1,0:T(8,128)(2,1)S(1)}, u32[]{:S(2)}, u32[]{:S(2)}) collective-permute-start(bf16[64,64]{1,0:T(8,128)(2,1)S(1)} %shard_map.102), channel_id=1, source_target_pairs={{0,2},{1,3},{2,0},{3,1},{4,6},{5,7},{6,4},{7,5},{8,10},{9,11},{10,... | collective-permute-start | bytes 24584 | tf_op jit(solution)/shard_map/ppermute | solution.py:213
  33.8 2.9 %collective-permute-done.9.refs_1_ = bf16[64,64]{1,0:T(8,128)(2,1)S(1)} collective-permute-done((bf16[64,64]{1,0:T(8,128)(2,1)S(1)}, bf16[64,64]{1,0:T(8,128)(2,1)S(1)}, u32[]{:S(2)}, u32[]{:S(2)}) %collective-permute-start.9) | collective-permute-done | bytes 8224 | tf_op jit(solution)/shard_map/ppermute | solution.py:213
  36.7 0.8 %shard_map.103 = f32[2,32,128]{2,1,0:T(8,128)} custom-call(bf16[64,128]{1,0:T(8,128)(2,1)S(1)} %get-tuple-element.35.grads_ref, f32[64,64]{1,0:T(8,128)S(1)} %get-tuple-element.36.refs_0_, bf16[64,64]{1,0:T(8,128)(2,1)S(1)} %collective-permute-done.9.refs_1_), custom_call_target="tpu_custom_call" | custom-call | flops 1048576 | bytes 32768 | tf_op jit(solution)/shard_map/pallas_call | solution.py:309
Async XLA Ops:
  0.0 24.6 %copy-start = (bf16[1,4096,192]{1,2,0:T(8,128)(2,1)S(1)}, bf16[1,4096,192]{1,2,0:T(8,128)(2,1)}, u32[]{:S(2)}) copy-start(bf16[1,4096,192]{1,2,0:T(8,128)(2,1)} %param.16) | copy-start | bytes 4718596
  0.0 24.6 %copy-start.3 = (bf16[768,64]{0,1:T(8,128)(2,1)S(1)}, bf16[768,64]{0,1:T(8,128)(2,1)}, u32[]{:S(2)}) copy-start(bf16[768,64]{0,1:T(8,128)(2,1)} %param.18) | copy-start | bytes 294916
  0.0 17.2 %collective-permute-start = (bf16[192,4096]{1,0:T(8,128)(2,1)}, bf16[192,4096]{1,0:T(8,128)(2,1)S(1)}, u32[]{:S(2)}, u32[]{:S(2)}) collective-permute-start(bf16[192,4096]{1,0:T(8,128)(2,1)} %bitcast.12), channel_id=1, source_target_pairs={{0,1},{1,0},{2,3},{3,2},{4,5},{5,4},{6,7},{7,6},{8,9},{9,8},{10,11... | collective-permute-start | bytes 4718600 | tf_op jit(solution)/shard_map/ppermute | solution.py:213
  0.5 16.7 %collective-permute-start.1 = (bf16[192,4096]{1,0:T(8,128)(2,1)}, bf16[192,4096]{1,0:T(8,128)(2,1)S(1)}, u32[]{:S(2)}, u32[]{:S(2)}) collective-permute-start(bf16[192,4096]{1,0:T(8,128)(2,1)} %bitcast.14), channel_id=1, source_target_pairs={{0,1},{1,0},{2,3},{3,2},{4,5},{5,4},{6,7},{7,6},{8,9},{9,8},{10,11... | collective-permute-start | bytes 4718600 | tf_op jit(solution)/shard_map/ppermute | solution.py:213
  4.0 9.0 %collective-permute-start.2 = (bf16[16,3200]{1,0:T(8,128)(2,1)}, bf16[16,3200]{1,0:T(8,128)(2,1)S(1)}, u32[]{:S(2)}, u32[]{:S(2)}) collective-permute-start(bf16[16,3200]{1,0:T(8,128)(2,1)} %get-tuple-element.27), channel_id=1, source_target_pairs={{0,12},{4,8},{8,4},{12,0},{1,13},{5,9},{9,5},{13,1},{2,14},{6,10},... | collective-permute-start | bytes 307208 | tf_op jit(solution)/shard_map/ppermute | solution.py:213
  9.1 6.6 %collective-permute-start.3 = (bf16[16,3200]{1,0:T(8,128)(2,1)}, bf16[16,3200]{1,0:T(8,128)(2,1)S(1)}, u32[]{:S(2)}, u32[]{:S(2)}) collective-permute-start(bf16[16,3200]{1,0:T(8,128)(2,1)} %get-tuple-element.28), channel_id=1, source_target_pairs={{0,4},{4,0},{8,12},{12,8},{1,5},{5,1},{9,13},{13,9},{2,6},{6,2},{1... | collective-permute-start | bytes 307208 | tf_op jit(solution)/shard_map/ppermute | solution.py:213
  9.1 9.1 %collective-permute-start.4 = (bf16[16,3200]{1,0:T(8,128)(2,1)}, bf16[16,3200]{1,0:T(8,128)(2,1)S(1)}, u32[]{:S(2)}, u32[]{:S(2)}) collective-permute-start(bf16[16,3200]{1,0:T(8,128)(2,1)} %get-tuple-element.30), channel_id=1, source_target_pairs={{0,8},{4,12},{8,0},{12,4},{1,9},{5,13},{9,1},{13,5},{2,10},{6,14},... | collective-permute-start | bytes 307208 | tf_op jit(solution)/shard_map/ppermute | solution.py:213
  15.7 5.8 %collective-permute-start.6 = (bf16[16,3200]{1,0:T(8,128)(2,1)S(1)}, bf16[16,3200]{1,0:T(8,128)(2,1)S(1)}, u32[]{:S(2)}, u32[]{:S(2)}) collective-permute-start(bf16[16,3200]{1,0:T(8,128)(2,1)S(1)} %collective-permute-done.2.refs_3_), channel_id=1, source_target_pairs={{0,2},{1,3},{2,0},{3,1},{4,6},{5,7},{6,4},{7,5},{8,10},{9,11},{10,... | collective-permute-start | bytes 307208 | tf_op jit(solution)/shard_map/ppermute | solution.py:213
  17.2 6.3 %collective-permute-start.5 = (bf16[16,3200]{1,0:T(8,128)(2,1)}, bf16[16,3200]{1,0:T(8,128)(2,1)S(1)}, u32[]{:S(2)}, u32[]{:S(2)}) collective-permute-start(bf16[16,3200]{1,0:T(8,128)(2,1)} %get-tuple-element.26.refs_0_), channel_id=1, source_target_pairs={{0,2},{1,3},{2,0},{3,1},{4,6},{5,7},{6,4},{7,5},{8,10},{9,11},{10,... | collective-permute-start | bytes 307208 | tf_op jit(solution)/shard_map/ppermute | solution.py:213
  18.1 12.6 %collective-permute-start.7 = (bf16[16,3200]{1,0:T(8,128)(2,1)S(1)}, bf16[16,3200]{1,0:T(8,128)(2,1)S(1)}, u32[]{:S(2)}, u32[]{:S(2)}) collective-permute-start(bf16[16,3200]{1,0:T(8,128)(2,1)S(1)} %collective-permute-done.3.refs_1_), channel_id=1, source_target_pairs={{0,2},{1,3},{2,0},{3,1},{4,6},{5,7},{6,4},{7,5},{8,10},{9,11},{10,... | collective-permute-start | bytes 307208 | tf_op jit(solution)/shard_map/ppermute | solution.py:213
  23.4 7.2 %collective-permute-start.8 = (bf16[16,3200]{1,0:T(8,128)(2,1)S(1)}, bf16[16,3200]{1,0:T(8,128)(2,1)S(1)}, u32[]{:S(2)}, u32[]{:S(2)}) collective-permute-start(bf16[16,3200]{1,0:T(8,128)(2,1)S(1)} %collective-permute-done.4.refs_2_), channel_id=1, source_target_pairs={{0,2},{1,3},{2,0},{3,1},{4,6},{5,7},{6,4},{7,5},{8,10},{9,11},{10,... | collective-permute-start | bytes 307208 | tf_op jit(solution)/shard_map/ppermute | solution.py:213
  24.6 1.4 %copy-start.1 = (bf16[1,4096,192]{1,2,0:T(8,128)(2,1)S(1)}, bf16[1,4096,192]{1,2,0:T(8,128)(2,1)}, u32[]{:S(2)}) copy-start(bf16[1,4096,192]{1,2,0:T(8,128)(2,1)} %param.17) | copy-start | bytes 4718596
  26.0 0.9 %copy-start.2 = (bf16[16,3200]{1,0:T(8,128)(2,1)S(1)}, bf16[16,3200]{1,0:T(8,128)(2,1)}, u32[]{:S(2)}) copy-start(bf16[16,3200]{1,0:T(8,128)(2,1)} %get-tuple-element.26.refs_0_) | copy-start | bytes 307204
  32.9 3.8 %collective-permute-start.9 = (bf16[64,64]{1,0:T(8,128)(2,1)S(1)}, bf16[64,64]{1,0:T(8,128)(2,1)S(1)}, u32[]{:S(2)}, u32[]{:S(2)}) collective-permute-start(bf16[64,64]{1,0:T(8,128)(2,1)S(1)} %shard_map.102), channel_id=1, source_target_pairs={{0,2},{1,3},{2,0},{3,1},{4,6},{5,7},{6,4},{7,5},{8,10},{9,11},{10,... | collective-permute-start | bytes 24584 | tf_op jit(solution)/shard_map/ppermute | solution.py:213

commit v5 on v3

--- a/solution.py
+++ b/solution.py
@@ -14,6 +14,8 @@
 PARTS = LOCAL_SEATS // SPARE
 HALF = ROWS // 2
 MIB = 1024 * 1024
+KEEP_LIMIT = 48
+SEND_LIMIT = 56
 BF16 = jnp.bfloat16
 F32 = jnp.float32
 
@@ -45,22 +47,18 @@
     return rows
 
 
-def send_kernel(count, limits_hbm, picked_hbm, shares_hbm, owner_hbm, tokens_hbm, derivs_hbm, compressor_hbm, *refs):
-    out_refs = refs[:count]
-    limits_ref, picked_ref, shares_ref, owner_ref, tokens_ref, derivs_ref, compressor_ref, sems = (
-        refs[count:]
-    )
+def send_kernel(hops, *refs):
+    count = len(hops)
+    in_refs, (gate_hbm, up_hbm), refs = refs[:7], refs[7:9], refs[9:]
+    out_refs, weights_ref, scratch, sems = refs[:count], refs[count], refs[count + 1 : -1], refs[-1]
+    limits_ref, picked_ref, shares_ref, owner_ref, tokens_ref, derivs_ref, compressor_ref = scratch
+    units = gate_hbm.shape[0]
     tokens, width = tokens_ref.shape
     chunk = width // (PARTS + 1)
     columns = [slice(i * chunk, (i + 1) * chunk) for i in range(PARTS + 1)]
-    pairs = [
-        (limits_hbm, limits_ref),
-        (picked_hbm, picked_ref),
-        (shares_hbm, shares_ref),
-        (owner_hbm, owner_ref),
-        (tokens_hbm, tokens_ref),
-        (derivs_hbm, derivs_ref),
-        (compressor_hbm, compressor_ref),
+    pairs = list(zip(in_refs, scratch)) + [
+        (gate_hbm, weights_ref.at[:units]),
+        (up_hbm, weights_ref.at[units:]),
     ]
     copies = [pltpu.make_async_copy(a, b, sems.at[i]) for i, (a, b) in enumerate(pairs)]
     for copy in copies:
@@ -68,7 +66,7 @@
     for copy in copies[:4]:
         copy.wait()
     me = lax.axis_index("exp")
-    experts = [jnp.bitwise_xor(me, q) for q in range(count)]
+    experts = [jnp.bitwise_xor(me, q) for q in hops]
     picked = picked_ref[...]
     seats = seats_of(limits_ref, picked, experts)
     slot = lax.broadcasted_iota(jnp.int32, (ROWS, tokens), 0)
@@ -89,7 +87,7 @@
     ]
     pad = [jnp.zeros((-count % 8, tokens), F32)] if count % 8 else []
     shares = jnp.concatenate(share_rows + pad, axis=0).T
-    for copy in copies[4:]:
+    for copy in copies[4:7]:
         copy.wait()
     proj = dot_t(derivs_ref[...], compressor_ref[...])
     last = tokens_ref[:, columns[-1]]
@@ -103,9 +101,25 @@
         both = dot(owned[q], grad)
         halves = [both[n * ROWS : (n + 1) * ROWS] for n in range(EX_DEV)]
         out_refs[q][:, PARTS * chunk :] = jnp.concatenate(halves, axis=1).astype(BF16)
-
-
-def pair_compressors(compressor_ref, units):
+    for copy in copies[7:]:
+        copy.wait()
+
+
+def keep_kernel(compressor_ref, weights_hbm, rows_hbm, *refs):
+    weights_ref, rows_ref, first_ref, second_ref, sems = refs
+    copies = [
+        pltpu.make_async_copy(weights_hbm, weights_ref, sems.at[0]),
+        pltpu.make_async_copy(rows_hbm, rows_ref, sems.at[1]),
+    ]
+    for copy in copies:
+        copy.start()
+    chosen = chosen_compressors(compressor_ref, first_ref.shape[1])
+    first_ref[...], second_ref[...] = chosen
+    for copy in copies:
+        copy.wait()
+
+
+def chosen_compressors(compressor_ref, units):
     place = lax.axis_index("dp")
     rank, total = compressor_ref.shape
     to = lax.broadcasted_iota(jnp.int32, (rank, rank), 0)
@@ -120,10 +134,12 @@
     ]
 
 
-def sketch_of(weights, compressors, block_refs):
-    width = weights[0][0].shape[1]
+def sketch_kernel(sizes, own_ref, pair_ref, first_ref, second_ref, *refs):
+    out_refs, grads_ref = refs[-1 - len(sizes) : -1], refs[-1]
+    block_refs = refs[: -1 - len(sizes)]
+    units, width = own_ref.shape[0] // 2, own_ref.shape[1]
     chunk = width // (PARTS + 1)
-    size = sum(r.shape[0] for r in block_refs)
+    size = sum(sizes)
     messages = size // ROWS
     low = lax.broadcasted_iota(jnp.int32, (1, HALF, 1), 1) < SPARE
     columns = [slice(i * chunk, (i + 1) * chunk) for i in range(PARTS + 1)]
@@ -136,40 +152,30 @@
     top = jnp.where(low, turn(tails[0]), tails[1])
     bottom = jnp.where(low, turn(tails[2]), 0.0)
     rows.append(jnp.stack([top, bottom], axis=1).reshape(size, chunk).astype(BF16))
-    seat = lax.broadcasted_iota(jnp.int32, (1, size), 1) % ROWS
-
-    def product(w):
-        total = dot_t(w[:, columns[0]], rows[0])
+    seat = lax.broadcasted_iota(jnp.int32, (size, 1), 0) % ROWS
+
+    def product(w, lines):
+        total = dot_t(rows[0], w[lines, columns[0]])
         for c, r in zip(columns[1:], rows[1:]):
-            total = total + dot_t(w[:, c], r)
+            total = total + dot_t(r, w[lines, c])
         return total
 
     sketch = None
-    for (gate_ref, up_ref), compressor in zip(weights, compressors):
-        gate, up = product(gate_ref), product(up_ref)
+    for ref, compressor in ((own_ref, first_ref), (pair_ref, second_ref)):
+        gate, up = product(ref, slice(0, units)), product(ref, slice(units, 2 * units))
         hidden = gate / (1.0 + jnp.exp(-gate)) * up
         hidden = jnp.where(seat < LOCAL_SEATS, hidden, 0.0).astype(BF16)
-        term = dot(compressor, hidden)
+        term = dot_t(compressor[...], hidden)
         sketch = term if sketch is None else sketch + term
-    return sketch
-
-
-def own_kernel(n_blocks, *refs):
-    weights = (refs[0:2], refs[2:4])
-    compressor_ref, block_refs = refs[4], refs[5 : 5 + n_blocks]
-    sketch_ref, grads_ref, *chosen_refs = refs[5 + n_blocks :]
-    units, width = weights[0][0].shape
-    chosen = pair_compressors(compressor_ref, units)
-    for ref, value in zip(chosen_refs, chosen):
-        ref[...] = value
-    grads_ref[...] = jnp.concatenate([r[:, width * LOCAL_SEATS // ROWS :] for r in block_refs], axis=0)
-    sketch_ref[...] = sketch_of(weights, chosen, block_refs)
-
-
-def far_kernel(n_blocks, *refs):
-    weights = (refs[0:2], refs[2:4])
-    chosen = [r[...] for r in refs[4:6]]
-    refs[-1][...] = sketch_of(weights, chosen, refs[6 : 6 + n_blocks]).astype(refs[-1].dtype)
+    at = 0
+    for n, ref in zip(sizes, out_refs):
+        ref[...] = sketch[:, at : at + n].astype(ref.dtype)
+        at += n
+    first = 0
+    for r in block_refs:
+        if first < sizes[0]:
+            grads_ref[first : first + r.shape[0]] = r[:, PARTS * chunk :]
+        first += r.shape[0]
 
 
 def outer_kernel(grads_ref, *refs):
@@ -188,14 +194,15 @@
 VMEM = pl.BlockSpec(memory_space=pltpu.VMEM)
 SMEM = pl.BlockSpec(memory_space=pltpu.SMEM)
 HBM = pl.BlockSpec(memory_space=pltpu.HBM)
-
-
-def call(kernel, out_shape, in_specs, limit, flops=0, moved=0, scratch=()):
+ANY = pl.BlockSpec(memory_space=pl.ANY)
+
+
+def call(kernel, out_shape, in_specs, limit, flops=0, moved=0, scratch=(), out_specs=None):
     return pl.pallas_call(
         kernel,
         out_shape=out_shape,
         in_specs=in_specs,
-        out_specs=jax.tree.map(lambda _: VMEM, out_shape),
+        out_specs=out_specs or jax.tree.map(lambda _: VMEM, out_shape),
         scratch_shapes=list(scratch),
         compiler_params=pltpu.CompilerParams(vmem_limit_bytes=limit),
         cost_estimate=pl.CostEstimate(flops=flops, bytes_accessed=moved, transcendentals=0),
@@ -229,9 +236,6 @@
     shape = jax.ShapeDtypeStruct
 
     gate, up = gating_projection[0].T, raising_projection[0].T
-    pair_gate, pair_up = swap(gate, "dp", 1), swap(up, "dp", 1)
-    weights = (gate, up, pair_gate, pair_up)
-
     arguments = (
         send_limits,
         picked_specialists.T,
@@ -241,46 +245,61 @@
         output_derivatives,
         outgrad_compressor.T,
     )
+    hops = [0, n_exp - 1] + list(range(1, n_exp - 1))
     spaces = [pltpu.SMEM] + [pltpu.VMEM] * (len(arguments) - 1)
-    rows = call(
-        functools.partial(send_kernel, n_exp),
-        [shape((ROWS, packed + EX_DEV * rank), BF16)] * n_exp,
-        [HBM] * len(arguments),
-        60 * MIB,
+    *rows, weights = call(
+        functools.partial(send_kernel, hops),
+        [shape((ROWS, packed + EX_DEV * rank), BF16)] * n_exp + [shape((2 * units, width), BF16)],
+        [HBM] * (len(arguments) + 2),
+        SEND_LIMIT * MIB,
+        out_specs=[VMEM] * n_exp + [ANY],
         flops=4 * size * tokens * packed + 2 * tokens * width * rank,
-        moved=4 * tokens * width + 2 * rank * width,
+        moved=4 * tokens * width + 2 * rank * width + 8 * units * width,
         scratch=[space(a.shape, a.dtype) for space, a in zip(spaces, arguments)]
-        + [pltpu.SemaphoreType.DMA((len(arguments),))],
-    )(*arguments)
-    rows = [rows[0]] + [swap(rows[q], "exp", q) for q in range(1, n_exp)]
-
-    blocks = {0: rows if small else [jnp.concatenate(rows, axis=0)]}
-    step = n_dp // 2
+        + [pltpu.SemaphoreType.DMA((len(arguments) + 2,))],
+    )(*arguments, gate, up)
+    pair_weights = swap(weights, "dp", 1)
+
+    half = n_dp // 2
+    crossed = [swap(rows[0], "dp", half)]
+    chosen_shape = shape((rank, units), BF16)
+    weights, rows[0], *chosen = call(
+        keep_kernel,
+        [shape(weights.shape, BF16), shape(rows[0].shape, BF16), chosen_shape, chosen_shape],
+        [VMEM, ANY, ANY],
+        KEEP_LIMIT * MIB,
+        out_specs=[ANY, ANY, VMEM, VMEM],
+        moved=8 * units * width,
+        scratch=[pltpu.SemaphoreType.DMA((2,))],
+    )(inflow_compressor.T, weights, rows[0])
+    for i, q in enumerate(hops):
+        if i:
+            rows[i] = swap(rows[i], "exp", q)
+            if i == 1:
+                rows[i], weights = lax.optimization_barrier((rows[i], weights))
+            crossed.append(swap(rows[i], "dp", half))
+    blocks = {0: rows, half: crossed}
+    step = half // 2
     while step > 1:
         for d in list(blocks):
             blocks[d ^ step] = [swap(r, "dp", step) for r in blocks[d]]
         step //= 2
 
-    cost = dict(flops=8 * size * width * units, moved=8 * width * units + 2 * size * packed)
-    chosen_shape = shape((rank, units), BF16)
-    own, grads, *chosen = call(
-        functools.partial(own_kernel, len(blocks[0])),
-        [shape((rank, size), F32), shape((size, EX_DEV * rank), BF16), chosen_shape, chosen_shape],
-        [VMEM] * (5 + len(blocks[0])),
-        20 * MIB,
-        **cost,
-    )(*weights, inflow_compressor.T, *blocks[0])
-    partials = [own]
-    for d in sorted(blocks):
-        if d:
-            far = call(
-                functools.partial(far_kernel, len(blocks[d])),
-                shape((rank, size), BF16),
-                [VMEM] * (6 + len(blocks[d])),
-                20 * MIB,
-                **cost,
-            )(*weights, *chosen, *blocks[d])
-            partials.append(swap(far, "dp", d))
+    partials, grads = [], None
+    ends = sorted(blocks)
+    for ds in [ends] if small else [[d] for d in ends]:
+        parts = [r for d in ds for r in blocks[d]]
+        *made, first = call(
+            functools.partial(sketch_kernel, [size] * len(ds)),
+            [shape((rank, size), BF16 if d else F32) for d in ds]
+            + [shape((size, EX_DEV * rank), BF16)],
+            [VMEM] * (4 + len(parts)),
+            20 * MIB,
+            flops=8 * len(ds) * size * width * units,
+            moved=8 * width * units + 2 * len(ds) * size * packed,
+        )(weights, pair_weights, *chosen, *parts)
+        grads = first if grads is None else grads
+        partials += [swap(p, "dp", d) if d else p for d, p in zip(ds, made)]
     out = call(
         outer_kernel,
         shape((EX_DEV, rank * rank // 128, 128), F32),

time: 35.9 us -> 124 us (3.45)
  Pallas kernels: 11.1 us -> 102 us
  waiting for transfers between devices: 10.1 us -> 8.04 us
  local copies, waits for them, and re-layouts: 2.3 us -> 0.93 us
    pallas_call x3, Pallas kernels: 10.3 us -> 102 us  [the longest x1 97.2 us: body(): call(functools.partial(send_kernel, hops), [shape((ROWS, packed + EX_DEV...]
    ppermute x10 -> x9, waiting for transfers between devices: 10.1 us -> 8.04 us  [swap(): return lax.ppermute(a, axis, [(i, i ^ q) for i in range(n)])]
    unnamed x8 -> x4, local copies, waits for them, and re-layouts: 2.3 us -> 0.93 us
    ppermute x10 -> x9, starting transfers between devices: 12 us -> 12.3 us  [swap(): return lax.ppermute(a, axis, [(i, i ^ q) for i in range(n)])]
  transfers between devices with their start and end apart: 10 -> 9, of which waited for: 3 -> 5; matrix products, arithmetic and copies ran while one was open for 0% -> 0% of each run, Pallas kernels for 20% -> 2%
where the time goes in v5:
time: 124 us
  Pallas kernels  102 us (82%)
  starting transfers between devices  12.3 us (10%)
  waiting for transfers between devices  8.04 us (6%)
    pallas_call x1, Pallas kernels, body(): call(functools.partial(send_kernel, hops), [shape((ROWS, packed + EX_DEV...  97.2 us
    ppermute x9, starting transfers between devices, swap(): return lax.ppermute(a, axis, [(i, i ^ q) for i in range(n)])  12.3 us
    ppermute x9, waiting for transfers between devices, swap(): return lax.ppermute(a, axis, [(i, i ^ q) for i in range(n)])  8.04 us
  transfers between devices with their start and end apart: 9, of which 5 were waited for; matrix products, arithmetic and copies ran while one was open for 0% of the time, Pallas kernels for 2%

profile of v5, /device:TPU:0, one launch (start us, length us, event | category | flops | bytes accessed | tf_op | source)
XLA Modules:
  0.0 123.7 jit_solution(11184446753595396535)
XLA Ops:
  0.0 0.0 copy-start.1
  0.0 97.2 %shard_map.100 = (bf16[16,3200]{1,0:T(8,128)(2,1)}, bf16[16,3200]{1,0:T(8,128)(2,1)}, bf16[16,3200]{1,0:T(8,128)(2,1)}, bf16[16,3200]{1,0:T(8,128)(2,1)}, bf16[384,4096]{1,0:T(8,128)(2,1)}) custom-call(s32[128]{0:T(128)} %refs_0_.1, s32[8,128]{1,0:T(8,128)} %bitcast.16, f32[8,128]{1,0:T(8,128)} %bitcast.17, s32[1,128]{1,0:T(1,128)} %bitcast.18, ...), custom_call_target="tpu_custom_call" | custom-call | flops 167772160 | bytes 8912896 | tf_op jit(solution)/shard_map/pallas_call | solution.py:250
  97.2 0.5 collective-permute-start.1
  97.8 4.7 %collective-permute-start = (bf16[16,3200]{1,0:T(8,128)(2,1)}, bf16[16,3200]{1,0:T(8,128)(2,1)S(1)}, u32[]{:S(2)}, u32[]{:S(2)}) collective-permute-start(bf16[16,3200]{1,0:T(8,128)(2,1)} %get-tuple-element.19), channel_id=1, source_target_pairs={{0,12},{4,8},{8,4},{12,0},{1,13},{5,9},{9,5},{13,1},{2,14},{6,10},... | collective-permute-start | bytes 307208 | tf_op jit(solution)/shard_map/ppermute | solution.py:214
  102.4 0.0 collective-permute-start.2
  102.4 0.7 collective-permute-start.3
  103.1 1.6 %collective-permute-start.4 = (bf16[16,3200]{1,0:T(8,128)(2,1)}, bf16[16,3200]{1,0:T(8,128)(2,1)S(1)}, u32[]{:S(2)}, u32[]{:S(2)}) collective-permute-start(bf16[16,3200]{1,0:T(8,128)(2,1)} %get-tuple-element.21.rows_hbm), channel_id=1, source_target_pairs={{0,2},{1,3},{2,0},{3,1},{4,6},{5,7},{6,4},{7,5},{8,10},{9,11},{10,... | collective-permute-start | bytes 307208 | tf_op jit(solution)/shard_map/ppermute | solution.py:214
  104.7 0.0 copy-done.1
  104.7 0.0 copy-start
  104.7 0.9 copy-done
  105.6 1.9 %shard_map.101 = (bf16[384,4096]{1,0:T(8,128)(2,1)S(1)}, bf16[16,3200]{1,0:T(8,128)(2,1)S(1)}, bf16[64,192]{1,0:T(8,128)(2,1)S(1)}, bf16[64,192]{1,0:T(8,128)(2,1)S(1)}) custom-call(bf16[64,768]{1,0:T(8,128)(2,1)S(1)} %bitcast.12, bf16[384,4096]{1,0:T(8,128)(2,1)} %get-tuple-element.20.weights_hbm, bf16[16,3200]{1,0:T(8,128)(2,1)S(1)} %copy-done), custom_call_target="tpu_custom_call" | custom-call | bytes 6291456 | tf_op jit(solution)/shard_map/pallas_call | solution.py:266
  107.6 0.0 collective-permute-done.refs_1_
  107.6 0.5 collective-permute-start.5
  108.1 1.3 %collective-permute-done.2.refs_2_ = bf16[16,3200]{1,0:T(8,128)(2,1)S(1)} collective-permute-done((bf16[16,3200]{1,0:T(8,128)(2,1)}, bf16[16,3200]{1,0:T(8,128)(2,1)S(1)}, u32[]{:S(2)}, u32[]{:S(2)}) %collective-permute-start.2) | collective-permute-done | bytes 102432 | tf_op jit(solution)/shard_map/ppermute | solution.py:214
  109.4 1.5 %collective-permute-start.6 = (bf16[16,3200]{1,0:T(8,128)(2,1)S(1)}, bf16[16,3200]{1,0:T(8,128)(2,1)S(1)}, u32[]{:S(2)}, u32[]{:S(2)}) collective-permute-start(bf16[16,3200]{1,0:T(8,128)(2,1)S(1)} %collective-permute-done.2.refs_2_), channel_id=1, source_target_pairs={{0,2},{1,3},{2,0},{3,1},{4,6},{5,7},{6,4},{7,5},{8,10},{9,11},{10,... | collective-permute-start | bytes 307208 | tf_op jit(solution)/shard_map/ppermute | solution.py:214
  110.9 1.0 collective-permute-done.3.refs_3_
  111.9 1.5 %collective-permute-start.7 = (bf16[16,3200]{1,0:T(8,128)(2,1)S(1)}, bf16[16,3200]{1,0:T(8,128)(2,1)S(1)}, u32[]{:S(2)}, u32[]{:S(2)}) collective-permute-start(bf16[16,3200]{1,0:T(8,128)(2,1)S(1)} %collective-permute-done.3.refs_3_), channel_id=1, source_target_pairs={{0,2},{1,3},{2,0},{3,1},{4,6},{5,7},{6,4},{7,5},{8,10},{9,11},{10,... | collective-permute-start | bytes 307208 | tf_op jit(solution)/shard_map/ppermute | solution.py:214
  113.4 0.0 collective-permute-done.4.refs_4_
  113.4 0.0 collective-permute-done.5.refs_5_
  113.4 1.5 %collective-permute-done.6.refs_6_ = bf16[16,3200]{1,0:T(8,128)(2,1)S(1)} collective-permute-done((bf16[16,3200]{1,0:T(8,128)(2,1)S(1)}, bf16[16,3200]{1,0:T(8,128)(2,1)S(1)}, u32[]{:S(2)}, u32[]{:S(2)}) %collective-permute-start.6) | collective-permute-done | bytes 102432 | tf_op jit(solution)/shard_map/ppermute | solution.py:214
  114.8 1.9 %collective-permute-done.7.refs_7_ = bf16[16,3200]{1,0:T(8,128)(2,1)S(1)} collective-permute-done((bf16[16,3200]{1,0:T(8,128)(2,1)S(1)}, bf16[16,3200]{1,0:T(8,128)(2,1)S(1)}, u32[]{:S(2)}, u32[]{:S(2)}) %collective-permute-start.7) | collective-permute-done | bytes 102432 | tf_op jit(solution)/shard_map/ppermute | solution.py:214
  116.7 0.0 collective-permute-done.1.pair_ref
  116.7 2.4 %shard_map.102 = (f32[64,64]{1,0:T(8,128)S(1)}, bf16[64,64]{1,0:T(8,128)(2,1)S(1)}, bf16[64,128]{1,0:T(8,128)(2,1)S(1)}) custom-call(bf16[384,4096]{1,0:T(8,128)(2,1)S(1)} %get-tuple-element.23.own_ref, bf16[384,4096]{1,0:T(8,128)(2,1)S(1)} %collective-permute-done.1.pair_ref, bf16[64,192]{1,0:T(8,128)(2,1)S(1)} %get-tuple-element.24.first_ref, ...), custom_call_target="tpu_custom_call" | custom-call | flops 805306368 | bytes 7077888 | tf_op jit(solution)/shard_map/pallas_call | solution.py:292
  119.1 1.4 %collective-permute-start.8 = (bf16[64,64]{1,0:T(8,128)(2,1)S(1)}, bf16[64,64]{1,0:T(8,128)(2,1)S(1)}, u32[]{:S(2)}, u32[]{:S(2)}) collective-permute-start(bf16[64,64]{1,0:T(8,128)(2,1)S(1)} %get-tuple-element.32), channel_id=1, source_target_pairs={{0,2},{1,3},{2,0},{3,1},{4,6},{5,7},{6,4},{7,5},{8,10},{9,11},{10,... | collective-permute-start | bytes 24584 | tf_op jit(solution)/shard_map/ppermute | solution.py:214
  120.5 2.4 %collective-permute-done.8.refs_1_ = bf16[64,64]{1,0:T(8,128)(2,1)S(1)} collective-permute-done((bf16[64,64]{1,0:T(8,128)(2,1)S(1)}, bf16[64,64]{1,0:T(8,128)(2,1)S(1)}, u32[]{:S(2)}, u32[]{:S(2)}) %collective-permute-start.8) | collective-permute-done | bytes 8224 | tf_op jit(solution)/shard_map/ppermute | solution.py:214
  122.9 0.8 shard_map.103
Async XLA Ops:
  0.0 104.7 %copy-start.1 = (bf16[768,64]{0,1:T(8,128)(2,1)S(1)}, bf16[768,64]{0,1:T(8,128)(2,1)}, u32[]{:S(2)}) copy-start(bf16[768,64]{0,1:T(8,128)(2,1)} %param.18) | copy-start | bytes 294916
  97.2 19.4 %collective-permute-start.1 = (bf16[384,4096]{1,0:T(8,128)(2,1)}, bf16[384,4096]{1,0:T(8,128)(2,1)S(1)}, u32[]{:S(2)}, u32[]{:S(2)}) collective-permute-start(bf16[384,4096]{1,0:T(8,128)(2,1)} %get-tuple-element.20.weights_hbm), channel_id=1, source_target_pairs={{0,1},{1,0},{2,3},{3,2},{4,5},{5,4},{6,7},{7,6},{8,9},{9,8},{10,11... | collective-permute-start | bytes 9437192 | tf_op jit(solution)/shard_map/ppermute | solution.py:214
  97.8 9.8 %collective-permute-start = (bf16[16,3200]{1,0:T(8,128)(2,1)}, bf16[16,3200]{1,0:T(8,128)(2,1)S(1)}, u32[]{:S(2)}, u32[]{:S(2)}) collective-permute-start(bf16[16,3200]{1,0:T(8,128)(2,1)} %get-tuple-element.19), channel_id=1, source_target_pairs={{0,12},{4,8},{8,4},{12,0},{1,13},{5,9},{9,5},{13,1},{2,14},{6,10},... | collective-permute-start | bytes 307208 | tf_op jit(solution)/shard_map/ppermute | solution.py:214
  102.4 7.0 %collective-permute-start.2 = (bf16[16,3200]{1,0:T(8,128)(2,1)}, bf16[16,3200]{1,0:T(8,128)(2,1)S(1)}, u32[]{:S(2)}, u32[]{:S(2)}) collective-permute-start(bf16[16,3200]{1,0:T(8,128)(2,1)} %get-tuple-element.28), channel_id=1, source_target_pairs={{0,4},{4,0},{8,12},{12,8},{1,5},{5,1},{9,13},{13,9},{2,6},{6,2},{1... | collective-permute-start | bytes 307208 | tf_op jit(solution)/shard_map/ppermute | solution.py:214
  102.4 9.4 %collective-permute-start.3 = (bf16[16,3200]{1,0:T(8,128)(2,1)}, bf16[16,3200]{1,0:T(8,128)(2,1)S(1)}, u32[]{:S(2)}, u32[]{:S(2)}) collective-permute-start(bf16[16,3200]{1,0:T(8,128)(2,1)} %get-tuple-element.29), channel_id=1, source_target_pairs={{0,8},{4,12},{8,0},{12,4},{1,9},{5,13},{9,1},{13,5},{2,10},{6,14},... | collective-permute-start | bytes 307208 | tf_op jit(solution)/shard_map/ppermute | solution.py:214
  103.1 10.3 %collective-permute-start.4 = (bf16[16,3200]{1,0:T(8,128)(2,1)}, bf16[16,3200]{1,0:T(8,128)(2,1)S(1)}, u32[]{:S(2)}, u32[]{:S(2)}) collective-permute-start(bf16[16,3200]{1,0:T(8,128)(2,1)} %get-tuple-element.21.rows_hbm), channel_id=1, source_target_pairs={{0,2},{1,3},{2,0},{3,1},{4,6},{5,7},{6,4},{7,5},{8,10},{9,11},{10,... | collective-permute-start | bytes 307208 | tf_op jit(solution)/shard_map/ppermute | solution.py:214
  104.7 0.9 copy-start
  107.6 5.8 %collective-permute-start.5 = (bf16[16,3200]{1,0:T(8,128)(2,1)S(1)}, bf16[16,3200]{1,0:T(8,128)(2,1)S(1)}, u32[]{:S(2)}, u32[]{:S(2)}) collective-permute-start(bf16[16,3200]{1,0:T(8,128)(2,1)S(1)} %collective-permute-done.refs_1_), channel_id=1, source_target_pairs={{0,2},{1,3},{2,0},{3,1},{4,6},{5,7},{6,4},{7,5},{8,10},{9,11},{10,... | collective-permute-start | bytes 307208 | tf_op jit(solution)/shard_map/ppermute | solution.py:214
  109.4 5.4 %collective-permute-start.6 = (bf16[16,3200]{1,0:T(8,128)(2,1)S(1)}, bf16[16,3200]{1,0:T(8,128)(2,1)S(1)}, u32[]{:S(2)}, u32[]{:S(2)}) collective-permute-start(bf16[16,3200]{1,0:T(8,128)(2,1)S(1)} %collective-permute-done.2.refs_2_), channel_id=1, source_target_pairs={{0,2},{1,3},{2,0},{3,1},{4,6},{5,7},{6,4},{7,5},{8,10},{9,11},{10,... | collective-permute-start | bytes 307208 | tf_op jit(solution)/shard_map/ppermute | solution.py:214
  111.9 4.8 %collective-permute-start.7 = (bf16[16,3200]{1,0:T(8,128)(2,1)S(1)}, bf16[16,3200]{1,0:T(8,128)(2,1)S(1)}, u32[]{:S(2)}, u32[]{:S(2)}) collective-permute-start(bf16[16,3200]{1,0:T(8,128)(2,1)S(1)} %collective-permute-done.3.refs_3_), channel_id=1, source_target_pairs={{0,2},{1,3},{2,0},{3,1},{4,6},{5,7},{6,4},{7,5},{8,10},{9,11},{10,... | collective-permute-start | bytes 307208 | tf_op jit(solution)/shard_map/ppermute | solution.py:214
  119.1 3.8 %collective-permute-start.8 = (bf16[64,64]{1,0:T(8,128)(2,1)S(1)}, bf16[64,64]{1,0:T(8,128)(2,1)S(1)}, u32[]{:S(2)}, u32[]{:S(2)}) collective-permute-start(bf16[64,64]{1,0:T(8,128)(2,1)S(1)} %get-tuple-element.32), channel_id=1, source_target_pairs={{0,2},{1,3},{2,0},{3,1},{4,6},{5,7},{6,4},{7,5},{8,10},{9,11},{10,... | collective-permute-start | bytes 24584 | tf_op jit(solution)/shard_map/ppermute | solution.py:214

commit v6 on v5

--- a/solution.py
+++ b/solution.py
@@ -51,14 +51,15 @@
     count = len(hops)
     in_refs, (gate_hbm, up_hbm), refs = refs[:7], refs[7:9], refs[9:]
     out_refs, weights_ref, scratch, sems = refs[:count], refs[count], refs[count + 1 : -1], refs[-1]
+    *scratch, held_ref = scratch
     limits_ref, picked_ref, shares_ref, owner_ref, tokens_ref, derivs_ref, compressor_ref = scratch
     units = gate_hbm.shape[0]
     tokens, width = tokens_ref.shape
     chunk = width // (PARTS + 1)
     columns = [slice(i * chunk, (i + 1) * chunk) for i in range(PARTS + 1)]
     pairs = list(zip(in_refs, scratch)) + [
-        (gate_hbm, weights_ref.at[:units]),
-        (up_hbm, weights_ref.at[units:]),
+        (gate_hbm, held_ref.at[pl.ds(0, units)]),
+        (up_hbm, held_ref.at[pl.ds(units, units)]),
     ]
     copies = [pltpu.make_async_copy(a, b, sems.at[i]) for i, (a, b) in enumerate(pairs)]
     for copy in copies:
@@ -87,8 +88,10 @@
     ]
     pad = [jnp.zeros((-count % 8, tokens), F32)] if count % 8 else []
     shares = jnp.concatenate(share_rows + pad, axis=0).T
-    for copy in copies[4:7]:
+    for copy in copies[4:]:
         copy.wait()
+    store = pltpu.make_async_copy(held_ref, weights_ref, sems.at[len(pairs)])
+    store.start()
     proj = dot_t(derivs_ref[...], compressor_ref[...])
     last = tokens_ref[:, columns[-1]]
     for i in range(PARTS):
@@ -101,8 +104,7 @@
         both = dot(owned[q], grad)
         halves = [both[n * ROWS : (n + 1) * ROWS] for n in range(EX_DEV)]
         out_refs[q][:, PARTS * chunk :] = jnp.concatenate(halves, axis=1).astype(BF16)
-    for copy in copies[7:]:
-        copy.wait()
+    store.wait()
 
 
 def keep_kernel(compressor_ref, weights_hbm, rows_hbm, *refs):
@@ -256,7 +258,7 @@
         flops=4 * size * tokens * packed + 2 * tokens * width * rank,
         moved=4 * tokens * width + 2 * rank * width + 8 * units * width,
         scratch=[space(a.shape, a.dtype) for space, a in zip(spaces, arguments)]
-        + [pltpu.SemaphoreType.DMA((len(arguments) + 2,))],
+        + [pltpu.VMEM((2 * units, width), BF16), pltpu.SemaphoreType.DMA((len(arguments) + 3,))],
     )(*arguments, gate, up)
     pair_weights = swap(weights, "dp", 1)
 

time: 124 us -> 31.9 us (0.26)
  Pallas kernels: 102 us -> 10.4 us
    pallas_call x1, Pallas kernels: 97.2 us -> 5.23 us  [body(): call(functools.partial(send_kernel, hops), [shape((ROWS, packed + EX_DEV...]
  transfers between devices with their start and end apart: 9 -> 9, of which waited for: 5 -> 5; matrix products, arithmetic and copies ran while one was open for 0% -> 0% of each run, Pallas kernels for 2% -> 6%
where the time goes in v6:
time: 31.9 us; the launch traced here: 31.7 us
  starting transfers between devices  12.3 us (39%)
  Pallas kernels  10.4 us (33%)
  waiting for transfers between devices  8.03 us (25%)
  local copies, waits for them, and re-layouts  0.93 us (3%)
    ppermute x9, starting transfers between devices, swap(): return lax.ppermute(a, axis, [(i, i ^ q) for i in range(n)])  12.3 us
    ppermute x9, waiting for transfers between devices, swap(): return lax.ppermute(a, axis, [(i, i ^ q) for i in range(n)])  8.03 us
    pallas_call x1, Pallas kernels, body(): call(functools.partial(send_kernel, hops), [shape((ROWS, packed + EX_DEV...  5.23 us
    pallas_call x1, Pallas kernels, body(): call(functools.partial(sketch_kernel, [size] * len(ds)), [shape((rank, si...  2.41 us
    pallas_call x1, Pallas kernels, body(): call(keep_kernel, [shape(weights.shape, BF16), shape(rows[0].shape, BF16)...  1.91 us
    unnamed x4, local copies, waits for them, and re-layouts  0.93 us
    pallas_call x1, Pallas kernels, body(): call(outer_kernel, shape((EX_DEV, rank * rank // 128, 128), F32), [VMEM]...  0.81 us
  transfers between devices with their start and end apart: 9, of which 5 were waited for; matrix products, arithmetic and copies ran while one was open for 0% of the time, Pallas kernels for 6%

profile of v6, /device:TPU:0, one launch (start us, length us, event | category | flops | bytes accessed | tf_op | source)
XLA Modules:
  0.0 31.7 jit_solution(71753732218994419)
XLA Ops:
  0.0 0.0 copy-start.1
  0.0 5.2 %shard_map.100 = (bf16[16,3200]{1,0:T(8,128)(2,1)}, bf16[16,3200]{1,0:T(8,128)(2,1)}, bf16[16,3200]{1,0:T(8,128)(2,1)}, bf16[16,3200]{1,0:T(8,128)(2,1)}, bf16[384,4096]{1,0:T(8,128)(2,1)}) custom-call(s32[128]{0:T(128)} %refs_0_.1, s32[8,128]{1,0:T(8,128)} %bitcast.16, f32[8,128]{1,0:T(8,128)} %bitcast.17, s32[1,128]{1,0:T(1,128)} %bitcast.18, ...), custom_call_target="tpu_custom_call" | custom-call | flops 167772160 | bytes 8912896 | tf_op jit(solution)/shard_map/pallas_call | solution.py:252
  5.2 0.5 %collective-permute-start.1 = (bf16[384,4096]{1,0:T(8,128)(2,1)}, bf16[384,4096]{1,0:T(8,128)(2,1)S(1)}, u32[]{:S(2)}, u32[]{:S(2)}) collective-permute-start(bf16[384,4096]{1,0:T(8,128)(2,1)} %get-tuple-element.20.weights_hbm), channel_id=1, source_target_pairs={{0,1},{1,0},{2,3},{3,2},{4,5},{5,4},{6,7},{7,6},{8,9},{9,8},{10,11... | collective-permute-start | bytes 9437192 | tf_op jit(solution)/shard_map/ppermute | solution.py:216
  5.8 4.7 %collective-permute-start = (bf16[16,3200]{1,0:T(8,128)(2,1)}, bf16[16,3200]{1,0:T(8,128)(2,1)S(1)}, u32[]{:S(2)}, u32[]{:S(2)}) collective-permute-start(bf16[16,3200]{1,0:T(8,128)(2,1)} %get-tuple-element.19), channel_id=1, source_target_pairs={{0,12},{4,8},{8,4},{12,0},{1,13},{5,9},{9,5},{13,1},{2,14},{6,10},... | collective-permute-start | bytes 307208 | tf_op jit(solution)/shard_map/ppermute | solution.py:216
  10.4 0.0 collective-permute-start.2
  10.4 0.7 %collective-permute-start.3 = (bf16[16,3200]{1,0:T(8,128)(2,1)}, bf16[16,3200]{1,0:T(8,128)(2,1)S(1)}, u32[]{:S(2)}, u32[]{:S(2)}) collective-permute-start(bf16[16,3200]{1,0:T(8,128)(2,1)} %get-tuple-element.29), channel_id=1, source_target_pairs={{0,8},{4,12},{8,0},{12,4},{1,9},{5,13},{9,1},{13,5},{2,10},{6,14},... | collective-permute-start | bytes 307208 | tf_op jit(solution)/shard_map/ppermute | solution.py:216
  11.1 1.6 %collective-permute-start.4 = (bf16[16,3200]{1,0:T(8,128)(2,1)}, bf16[16,3200]{1,0:T(8,128)(2,1)S(1)}, u32[]{:S(2)}, u32[]{:S(2)}) collective-permute-start(bf16[16,3200]{1,0:T(8,128)(2,1)} %get-tuple-element.21.rows_hbm), channel_id=1, source_target_pairs={{0,2},{1,3},{2,0},{3,1},{4,6},{5,7},{6,4},{7,5},{8,10},{9,11},{10,... | collective-permute-start | bytes 307208 | tf_op jit(solution)/shard_map/ppermute | solution.py:216
  12.7 0.0 copy-done.1
  12.7 0.0 copy-start
  12.7 0.9 %copy-done = bf16[16,3200]{1,0:T(8,128)(2,1)S(1)} copy-done((bf16[16,3200]{1,0:T(8,128)(2,1)S(1)}, bf16[16,3200]{1,0:T(8,128)(2,1)}, u32[]{:S(2)}) %copy-start) | copy-done | bytes 102424
  13.6 1.9 %shard_map.101 = (bf16[384,4096]{1,0:T(8,128)(2,1)S(1)}, bf16[16,3200]{1,0:T(8,128)(2,1)S(1)}, bf16[64,192]{1,0:T(8,128)(2,1)S(1)}, bf16[64,192]{1,0:T(8,128)(2,1)S(1)}) custom-call(bf16[64,768]{1,0:T(8,128)(2,1)S(1)} %bitcast.12, bf16[384,4096]{1,0:T(8,128)(2,1)} %get-tuple-element.20.weights_hbm, bf16[16,3200]{1,0:T(8,128)(2,1)S(1)} %copy-done), custom_call_target="tpu_custom_call" | custom-call | bytes 6291456 | tf_op jit(solution)/shard_map/pallas_call | solution.py:268
  15.6 0.0 collective-permute-done.refs_1_
  15.6 0.5 %collective-permute-start.5 = (bf16[16,3200]{1,0:T(8,128)(2,1)S(1)}, bf16[16,3200]{1,0:T(8,128)(2,1)S(1)}, u32[]{:S(2)}, u32[]{:S(2)}) collective-permute-start(bf16[16,3200]{1,0:T(8,128)(2,1)S(1)} %collective-permute-done.refs_1_), channel_id=1, source_target_pairs={{0,2},{1,3},{2,0},{3,1},{4,6},{5,7},{6,4},{7,5},{8,10},{9,11},{10,... | collective-permute-start | bytes 307208 | tf_op jit(solution)/shard_map/ppermute | solution.py:216
  16.1 1.3 %collective-permute-done.2.refs_2_ = bf16[16,3200]{1,0:T(8,128)(2,1)S(1)} collective-permute-done((bf16[16,3200]{1,0:T(8,128)(2,1)}, bf16[16,3200]{1,0:T(8,128)(2,1)S(1)}, u32[]{:S(2)}, u32[]{:S(2)}) %collective-permute-start.2) | collective-permute-done | bytes 102432 | tf_op jit(solution)/shard_map/ppermute | solution.py:216
  17.4 1.5 %collective-permute-start.6 = (bf16[16,3200]{1,0:T(8,128)(2,1)S(1)}, bf16[16,3200]{1,0:T(8,128)(2,1)S(1)}, u32[]{:S(2)}, u32[]{:S(2)}) collective-permute-start(bf16[16,3200]{1,0:T(8,128)(2,1)S(1)} %collective-permute-done.2.refs_2_), channel_id=1, source_target_pairs={{0,2},{1,3},{2,0},{3,1},{4,6},{5,7},{6,4},{7,5},{8,10},{9,11},{10,... | collective-permute-start | bytes 307208 | tf_op jit(solution)/shard_map/ppermute | solution.py:216
  18.9 1.0 %collective-permute-done.3.refs_3_ = bf16[16,3200]{1,0:T(8,128)(2,1)S(1)} collective-permute-done((bf16[16,3200]{1,0:T(8,128)(2,1)}, bf16[16,3200]{1,0:T(8,128)(2,1)S(1)}, u32[]{:S(2)}, u32[]{:S(2)}) %collective-permute-start.3) | collective-permute-done | bytes 102432 | tf_op jit(solution)/shard_map/ppermute | solution.py:216
  19.9 1.5 %collective-permute-start.7 = (bf16[16,3200]{1,0:T(8,128)(2,1)S(1)}, bf16[16,3200]{1,0:T(8,128)(2,1)S(1)}, u32[]{:S(2)}, u32[]{:S(2)}) collective-permute-start(bf16[16,3200]{1,0:T(8,128)(2,1)S(1)} %collective-permute-done.3.refs_3_), channel_id=1, source_target_pairs={{0,2},{1,3},{2,0},{3,1},{4,6},{5,7},{6,4},{7,5},{8,10},{9,11},{10,... | collective-permute-start | bytes 307208 | tf_op jit(solution)/shard_map/ppermute | solution.py:216
  21.4 0.0 collective-permute-done.4.refs_4_
  21.4 0.0 collective-permute-done.5.refs_5_
  21.4 1.5 %collective-permute-done.6.refs_6_ = bf16[16,3200]{1,0:T(8,128)(2,1)S(1)} collective-permute-done((bf16[16,3200]{1,0:T(8,128)(2,1)S(1)}, bf16[16,3200]{1,0:T(8,128)(2,1)S(1)}, u32[]{:S(2)}, u32[]{:S(2)}) %collective-permute-start.6) | collective-permute-done | bytes 102432 | tf_op jit(solution)/shard_map/ppermute | solution.py:216
  22.8 1.9 %collective-permute-done.7.refs_7_ = bf16[16,3200]{1,0:T(8,128)(2,1)S(1)} collective-permute-done((bf16[16,3200]{1,0:T(8,128)(2,1)S(1)}, bf16[16,3200]{1,0:T(8,128)(2,1)S(1)}, u32[]{:S(2)}, u32[]{:S(2)}) %collective-permute-start.7) | collective-permute-done | bytes 102432 | tf_op jit(solution)/shard_map/ppermute | solution.py:216
  24.7 0.0 collective-permute-done.1.pair_ref
  24.7 2.4 %shard_map.102 = (f32[64,64]{1,0:T(8,128)S(1)}, bf16[64,64]{1,0:T(8,128)(2,1)S(1)}, bf16[64,128]{1,0:T(8,128)(2,1)S(1)}) custom-call(bf16[384,4096]{1,0:T(8,128)(2,1)S(1)} %get-tuple-element.23.own_ref, bf16[384,4096]{1,0:T(8,128)(2,1)S(1)} %collective-permute-done.1.pair_ref, bf16[64,192]{1,0:T(8,128)(2,1)S(1)} %get-tuple-element.24.first_ref, ...), custom_call_target="tpu_custom_call" | custom-call | flops 805306368 | bytes 7077888 | tf_op jit(solution)/shard_map/pallas_call | solution.py:294
  27.1 1.4 %collective-permute-start.8 = (bf16[64,64]{1,0:T(8,128)(2,1)S(1)}, bf16[64,64]{1,0:T(8,128)(2,1)S(1)}, u32[]{:S(2)}, u32[]{:S(2)}) collective-permute-start(bf16[64,64]{1,0:T(8,128)(2,1)S(1)} %get-tuple-element.32), channel_id=1, source_target_pairs={{0,2},{1,3},{2,0},{3,1},{4,6},{5,7},{6,4},{7,5},{8,10},{9,11},{10,... | collective-permute-start | bytes 24584 | tf_op jit(solution)/shard_map/ppermute | solution.py:216
  28.5 2.4 %collective-permute-done.8.refs_1_ = bf16[64,64]{1,0:T(8,128)(2,1)S(1)} collective-permute-done((bf16[64,64]{1,0:T(8,128)(2,1)S(1)}, bf16[64,64]{1,0:T(8,128)(2,1)S(1)}, u32[]{:S(2)}, u32[]{:S(2)}) %collective-permute-start.8) | collective-permute-done | bytes 8224 | tf_op jit(solution)/shard_map/ppermute | solution.py:216
  30.9 0.8 %shard_map.103 = f32[2,32,128]{2,1,0:T(8,128)} custom-call(bf16[64,128]{1,0:T(8,128)(2,1)S(1)} %get-tuple-element.30.grads_ref, f32[64,64]{1,0:T(8,128)S(1)} %get-tuple-element.31.refs_0_, bf16[64,64]{1,0:T(8,128)(2,1)S(1)} %collective-permute-done.8.refs_1_), custom_call_target="tpu_custom_call" | custom-call | flops 1048576 | bytes 32768 | tf_op jit(solution)/shard_map/pallas_call | solution.py:305
Async XLA Ops:
  0.0 12.7 %copy-start.1 = (bf16[768,64]{0,1:T(8,128)(2,1)S(1)}, bf16[768,64]{0,1:T(8,128)(2,1)}, u32[]{:S(2)}) copy-start(bf16[768,64]{0,1:T(8,128)(2,1)} %param.18) | copy-start | bytes 294916
  5.2 19.4 %collective-permute-start.1 = (bf16[384,4096]{1,0:T(8,128)(2,1)}, bf16[384,4096]{1,0:T(8,128)(2,1)S(1)}, u32[]{:S(2)}, u32[]{:S(2)}) collective-permute-start(bf16[384,4096]{1,0:T(8,128)(2,1)} %get-tuple-element.20.weights_hbm), channel_id=1, source_target_pairs={{0,1},{1,0},{2,3},{3,2},{4,5},{5,4},{6,7},{7,6},{8,9},{9,8},{10,11... | collective-permute-start | bytes 9437192 | tf_op jit(solution)/shard_map/ppermute | solution.py:216
  5.8 9.8 %collective-permute-start = (bf16[16,3200]{1,0:T(8,128)(2,1)}, bf16[16,3200]{1,0:T(8,128)(2,1)S(1)}, u32[]{:S(2)}, u32[]{:S(2)}) collective-permute-start(bf16[16,3200]{1,0:T(8,128)(2,1)} %get-tuple-element.19), channel_id=1, source_target_pairs={{0,12},{4,8},{8,4},{12,0},{1,13},{5,9},{9,5},{13,1},{2,14},{6,10},... | collective-permute-start | bytes 307208 | tf_op jit(solution)/shard_map/ppermute | solution.py:216
  10.4 7.0 %collective-permute-start.2 = (bf16[16,3200]{1,0:T(8,128)(2,1)}, bf16[16,3200]{1,0:T(8,128)(2,1)S(1)}, u32[]{:S(2)}, u32[]{:S(2)}) collective-permute-start(bf16[16,3200]{1,0:T(8,128)(2,1)} %get-tuple-element.28), channel_id=1, source_target_pairs={{0,4},{4,0},{8,12},{12,8},{1,5},{5,1},{9,13},{13,9},{2,6},{6,2},{1... | collective-permute-start | bytes 307208 | tf_op jit(solution)/shard_map/ppermute | solution.py:216
  10.4 9.4 %collective-permute-start.3 = (bf16[16,3200]{1,0:T(8,128)(2,1)}, bf16[16,3200]{1,0:T(8,128)(2,1)S(1)}, u32[]{:S(2)}, u32[]{:S(2)}) collective-permute-start(bf16[16,3200]{1,0:T(8,128)(2,1)} %get-tuple-element.29), channel_id=1, source_target_pairs={{0,8},{4,12},{8,0},{12,4},{1,9},{5,13},{9,1},{13,5},{2,10},{6,14},... | collective-permute-start | bytes 307208 | tf_op jit(solution)/shard_map/ppermute | solution.py:216
  11.1 10.3 %collective-permute-start.4 = (bf16[16,3200]{1,0:T(8,128)(2,1)}, bf16[16,3200]{1,0:T(8,128)(2,1)S(1)}, u32[]{:S(2)}, u32[]{:S(2)}) collective-permute-start(bf16[16,3200]{1,0:T(8,128)(2,1)} %get-tuple-element.21.rows_hbm), channel_id=1, source_target_pairs={{0,2},{1,3},{2,0},{3,1},{4,6},{5,7},{6,4},{7,5},{8,10},{9,11},{10,... | collective-permute-start | bytes 307208 | tf_op jit(solution)/shard_map/ppermute | solution.py:216
  12.7 0.9 %copy-start = (bf16[16,3200]{1,0:T(8,128)(2,1)S(1)}, bf16[16,3200]{1,0:T(8,128)(2,1)}, u32[]{:S(2)}) copy-start(bf16[16,3200]{1,0:T(8,128)(2,1)} %get-tuple-element.21.rows_hbm) | copy-start | bytes 307204
  15.6 5.8 %collective-permute-start.5 = (bf16[16,3200]{1,0:T(8,128)(2,1)S(1)}, bf16[16,3200]{1,0:T(8,128)(2,1)S(1)}, u32[]{:S(2)}, u32[]{:S(2)}) collective-permute-start(bf16[16,3200]{1,0:T(8,128)(2,1)S(1)} %collective-permute-done.refs_1_), channel_id=1, source_target_pairs={{0,2},{1,3},{2,0},{3,1},{4,6},{5,7},{6,4},{7,5},{8,10},{9,11},{10,... | collective-permute-start | bytes 307208 | tf_op jit(solution)/shard_map/ppermute | solution.py:216
  17.4 5.4 %collective-permute-start.6 = (bf16[16,3200]{1,0:T(8,128)(2,1)S(1)}, bf16[16,3200]{1,0:T(8,128)(2,1)S(1)}, u32[]{:S(2)}, u32[]{:S(2)}) collective-permute-start(bf16[16,3200]{1,0:T(8,128)(2,1)S(1)} %collective-permute-done.2.refs_2_), channel_id=1, source_target_pairs={{0,2},{1,3},{2,0},{3,1},{4,6},{5,7},{6,4},{7,5},{8,10},{9,11},{10,... | collective-permute-start | bytes 307208 | tf_op jit(solution)/shard_map/ppermute | solution.py:216
  19.9 4.8 %collective-permute-start.7 = (bf16[16,3200]{1,0:T(8,128)(2,1)S(1)}, bf16[16,3200]{1,0:T(8,128)(2,1)S(1)}, u32[]{:S(2)}, u32[]{:S(2)}) collective-permute-start(bf16[16,3200]{1,0:T(8,128)(2,1)S(1)} %collective-permute-done.3.refs_3_), channel_id=1, source_target_pairs={{0,2},{1,3},{2,0},{3,1},{4,6},{5,7},{6,4},{7,5},{8,10},{9,11},{10,... | collective-permute-start | bytes 307208 | tf_op jit(solution)/shard_map/ppermute | solution.py:216
  27.1 3.8 %collective-permute-start.8 = (bf16[64,64]{1,0:T(8,128)(2,1)S(1)}, bf16[64,64]{1,0:T(8,128)(2,1)S(1)}, u32[]{:S(2)}, u32[]{:S(2)}) collective-permute-start(bf16[64,64]{1,0:T(8,128)(2,1)S(1)} %get-tuple-element.32), channel_id=1, source_target_pairs={{0,2},{1,3},{2,0},{3,1},{4,6},{5,7},{6,4},{7,5},{8,10},{9,11},{10,... | collective-permute-start | bytes 24584 | tf_op jit(solution)/shard_map/ppermute | solution.py:216

commit v7 on v6

--- a/solution.py
+++ b/solution.py
@@ -49,19 +49,14 @@
 
 def send_kernel(hops, *refs):
     count = len(hops)
-    in_refs, (gate_hbm, up_hbm), refs = refs[:7], refs[7:9], refs[9:]
-    out_refs, weights_ref, scratch, sems = refs[:count], refs[count], refs[count + 1 : -1], refs[-1]
-    *scratch, held_ref = scratch
+    in_refs, out_refs, scratch, sems = refs[:7], refs[7 : 7 + count], refs[7 + count : -1], refs[-1]
     limits_ref, picked_ref, shares_ref, owner_ref, tokens_ref, derivs_ref, compressor_ref = scratch
-    units = gate_hbm.shape[0]
     tokens, width = tokens_ref.shape
     chunk = width // (PARTS + 1)
     columns = [slice(i * chunk, (i + 1) * chunk) for i in range(PARTS + 1)]
-    pairs = list(zip(in_refs, scratch)) + [
-        (gate_hbm, held_ref.at[pl.ds(0, units)]),
-        (up_hbm, held_ref.at[pl.ds(units, units)]),
+    copies = [
+        pltpu.make_async_copy(a, b, sems.at[i]) for i, (a, b) in enumerate(zip(in_refs, scratch))
     ]
-    copies = [pltpu.make_async_copy(a, b, sems.at[i]) for i, (a, b) in enumerate(pairs)]
     for copy in copies:
         copy.start()
     for copy in copies[:4]:
@@ -90,8 +85,6 @@
     shares = jnp.concatenate(share_rows + pad, axis=0).T
     for copy in copies[4:]:
         copy.wait()
-    store = pltpu.make_async_copy(held_ref, weights_ref, sems.at[len(pairs)])
-    store.start()
     proj = dot_t(derivs_ref[...], compressor_ref[...])
     last = tokens_ref[:, columns[-1]]
     for i in range(PARTS):
@@ -104,15 +97,12 @@
         both = dot(owned[q], grad)
         halves = [both[n * ROWS : (n + 1) * ROWS] for n in range(EX_DEV)]
         out_refs[q][:, PARTS * chunk :] = jnp.concatenate(halves, axis=1).astype(BF16)
-    store.wait()
-
-
-def keep_kernel(compressor_ref, weights_hbm, rows_hbm, *refs):
-    weights_ref, rows_ref, first_ref, second_ref, sems = refs
-    copies = [
-        pltpu.make_async_copy(weights_hbm, weights_ref, sems.at[0]),
-        pltpu.make_async_copy(rows_hbm, rows_ref, sems.at[1]),
-    ]
+
+
+def keep_kernel(compressor_ref, gate_hbm, up_hbm, rows_hbm, *refs):
+    gate_ref, up_ref, rows_ref, first_ref, second_ref, sems = refs
+    pairs = ((gate_hbm, gate_ref), (up_hbm, up_ref), (rows_hbm, rows_ref))
+    copies = [pltpu.make_async_copy(a, b, sems.at[i]) for i, (a, b) in enumerate(pairs)]
     for copy in copies:
         copy.start()
     chosen = chosen_compressors(compressor_ref, first_ref.shape[1])
@@ -136,10 +126,10 @@
     ]
 
 
-def sketch_kernel(sizes, own_ref, pair_ref, first_ref, second_ref, *refs):
+def sketch_kernel(sizes, gate_ref, up_ref, pair_gate_ref, pair_up_ref, first_ref, second_ref, *refs):
     out_refs, grads_ref = refs[-1 - len(sizes) : -1], refs[-1]
     block_refs = refs[: -1 - len(sizes)]
-    units, width = own_ref.shape[0] // 2, own_ref.shape[1]
+    units, width = gate_ref.shape
     chunk = width // (PARTS + 1)
     size = sum(sizes)
     messages = size // ROWS
@@ -156,15 +146,18 @@
     rows.append(jnp.stack([top, bottom], axis=1).reshape(size, chunk).astype(BF16))
     seat = lax.broadcasted_iota(jnp.int32, (size, 1), 0) % ROWS
 
-    def product(w, lines):
-        total = dot_t(rows[0], w[lines, columns[0]])
+    def product(w):
+        total = dot_t(rows[0], w[:, columns[0]])
         for c, r in zip(columns[1:], rows[1:]):
-            total = total + dot_t(r, w[lines, c])
+            total = total + dot_t(r, w[:, c])
         return total
 
     sketch = None
-    for ref, compressor in ((own_ref, first_ref), (pair_ref, second_ref)):
-        gate, up = product(ref, slice(0, units)), product(ref, slice(units, 2 * units))
+    for gate_w, up_w, compressor in (
+        (gate_ref, up_ref, first_ref),
+        (pair_gate_ref, pair_up_ref, second_ref),
+    ):
+        gate, up = product(gate_w), product(up_w)
         hidden = gate / (1.0 + jnp.exp(-gate)) * up
         hidden = jnp.where(seat < LOCAL_SEATS, hidden, 0.0).astype(BF16)
         term = dot_t(compressor[...], hidden)
@@ -238,6 +231,7 @@
     shape = jax.ShapeDtypeStruct
 
     gate, up = gating_projection[0].T, raising_projection[0].T
+    pair_gate, pair_up = swap(gate, "dp", 1), swap(up, "dp", 1)
     arguments = (
         send_limits,
         picked_specialists.T,
@@ -247,38 +241,39 @@
         output_derivatives,
         outgrad_compressor.T,
     )
-    hops = [0, n_exp - 1] + list(range(1, n_exp - 1))
+    hops = [0, 1] + list(range(n_exp - 1, 1, -1))
     spaces = [pltpu.SMEM] + [pltpu.VMEM] * (len(arguments) - 1)
-    *rows, weights = call(
+    rows = call(
         functools.partial(send_kernel, hops),
-        [shape((ROWS, packed + EX_DEV * rank), BF16)] * n_exp + [shape((2 * units, width), BF16)],
-        [HBM] * (len(arguments) + 2),
+        [shape((ROWS, packed + EX_DEV * rank), BF16)] * n_exp,
+        [HBM] * len(arguments),
         SEND_LIMIT * MIB,
-        out_specs=[VMEM] * n_exp + [ANY],
         flops=4 * size * tokens * packed + 2 * tokens * width * rank,
-        moved=4 * tokens * width + 2 * rank * width + 8 * units * width,
+        moved=4 * tokens * width + 2 * rank * width,
         scratch=[space(a.shape, a.dtype) for space, a in zip(spaces, arguments)]
-        + [pltpu.VMEM((2 * units, width), BF16), pltpu.SemaphoreType.DMA((len(arguments) + 3,))],
-    )(*arguments, gate, up)
-    pair_weights = swap(weights, "dp", 1)
+        + [pltpu.SemaphoreType.DMA((len(arguments),))],
+    )(*arguments)
 
     half = n_dp // 2
+    hold = lax.optimization_barrier
+    rows = list(rows)
     crossed = [swap(rows[0], "dp", half)]
+    pair_gate, pair_up, rows[0] = hold((pair_gate, pair_up, rows[0]))
     chosen_shape = shape((rank, units), BF16)
-    weights, rows[0], *chosen = call(
+    gate, up, rows[0], *chosen = call(
         keep_kernel,
-        [shape(weights.shape, BF16), shape(rows[0].shape, BF16), chosen_shape, chosen_shape],
-        [VMEM, ANY, ANY],
+        [shape(a.shape, BF16) for a in (gate, up, rows[0])] + [chosen_shape] * 2,
+        [VMEM, ANY, ANY, ANY],
         KEEP_LIMIT * MIB,
-        out_specs=[ANY, ANY, VMEM, VMEM],
+        out_specs=[ANY, ANY, ANY, VMEM, VMEM],
         moved=8 * units * width,
-        scratch=[pltpu.SemaphoreType.DMA((2,))],
-    )(inflow_compressor.T, weights, rows[0])
+        scratch=[pltpu.SemaphoreType.DMA((3,))],
+    )(inflow_compressor.T, gate, up, rows[0])
     for i, q in enumerate(hops):
         if i:
             rows[i] = swap(rows[i], "exp", q)
-            if i == 1:
-                rows[i], weights = lax.optimization_barrier((rows[i], weights))
+            if i == n_exp - 1:
+                rows[i], gate, up = hold((rows[i], gate, up))
             crossed.append(swap(rows[i], "dp", half))
     blocks = {0: rows, half: crossed}
     step = half // 2
@@ -295,11 +290,11 @@
             functools.partial(sketch_kernel, [size] * len(ds)),
             [shape((rank, size), BF16 if d else F32) for d in ds]
             + [shape((size, EX_DEV * rank), BF16)],
-            [VMEM] * (4 + len(parts)),
+            [VMEM] * (6 + len(parts)),
             20 * MIB,
             flops=8 * len(ds) * size * width * units,
             moved=8 * width * units + 2 * len(ds) * size * packed,
-        )(weights, pair_weights, *chosen, *parts)
+        )(gate, up, pair_gate, pair_up, *chosen, *parts)
         grads = first if grads is None else grads
         partials += [swap(p, "dp", d) if d else p for d, p in zip(ds, made)]
     out = call(

time: 31.9 us -> 32.1 us (level)
  Pallas kernels: 10.4 us -> 8.13 us
  waiting for transfers between devices: 8.03 us -> 9.86 us
  starting transfers between devices: 12.3 us -> 13 us
    ppermute x9 -> x10, waiting for transfers between devices: 8.03 us -> 9.86 us  [swap(): return lax.ppermute(a, axis, [(i, i ^ q) for i in range(n)])]
    pallas_call x1, Pallas kernels: 5.23 us -> 3.41 us  [body(): call(functools.partial(send_kernel, hops), [shape((ROWS, packed + EX_DEV...]
    ppermute x9 -> x10, starting transfers between devices: 12.3 us -> 13 us  [swap(): return lax.ppermute(a, axis, [(i, i ^ q) for i in range(n)])]
    pallas_call x1, Pallas kernels: 1.91 us -> 1.54 us  [body(): call(keep_kernel, [shape(a.shape, BF16) for a in (gate, up, rows[0])] + [...]
    unnamed x4 -> x6, local copies, waits for them, and re-layouts: 0.93 us -> 0.89 us
  transfers between devices with their start and end apart: 9 -> 10, of which waited for: 5 -> 5; matrix products, arithmetic and copies ran while one was open for 0% -> 0% of each run, Pallas kernels for 6% -> 16%
where the time goes in v7:
time: 32.1 us; the launch traced here: 31.9 us
  starting transfers between devices  13 us (40%)
  waiting for transfers between devices  9.86 us (31%)
  Pallas kernels  8.13 us (25%)
  local copies, waits for them, and re-layouts  0.89 us (3%)
    ppermute x10, starting transfers between devices, swap(): return lax.ppermute(a, axis, [(i, i ^ q) for i in range(n)])  13 us
    ppermute x10, waiting for transfers between devices, swap(): return lax.ppermute(a, axis, [(i, i ^ q) for i in range(n)])  9.86 us
    pallas_call x1, Pallas kernels, body(): call(functools.partial(send_kernel, hops), [shape((ROWS, packed + EX_DEV...  3.41 us
    pallas_call x1, Pallas kernels, body(): call(functools.partial(sketch_kernel, [size] * len(ds)), [shape((rank, si...  2.36 us
    pallas_call x1, Pallas kernels, body(): call(keep_kernel, [shape(a.shape, BF16) for a in (gate, up, rows[0])] + [...  1.54 us
    unnamed x6, local copies, waits for them, and re-layouts  0.89 us
    pallas_call x1, Pallas kernels, body(): call(outer_kernel, shape((EX_DEV, rank * rank // 128, 128), F32), [VMEM]...  0.81 us
  transfers between devices with their start and end apart: 10, of which 5 were waited for; matrix products, arithmetic and copies ran while one was open for 0% of the time, Pallas kernels for 16%

profile of v7, /device:TPU:0, one launch (start us, length us, event | category | flops | bytes accessed | tf_op | source)
XLA Modules:
  0.0 31.9 jit_solution(436779371374604182)
XLA Ops:
  0.0 0.0 copy-start
  0.0 0.0 copy-start.2
  0.0 0.5 %collective-permute-start.1 = (bf16[192,4096]{1,0:T(8,128)(2,1)}, bf16[192,4096]{1,0:T(8,128)(2,1)S(1)}, u32[]{:S(2)}, u32[]{:S(2)}) collective-permute-start(bf16[192,4096]{1,0:T(8,128)(2,1)} %bitcast.12), channel_id=1, source_target_pairs={{0,1},{1,0},{2,3},{3,2},{4,5},{5,4},{6,7},{7,6},{8,9},{9,8},{10,11... | collective-permute-start | bytes 4718600 | tf_op jit(solution)/shard_map/ppermute | solution.py:209
  0.5 0.1 collective-permute-start.2
  0.5 3.4 %shard_map.100 = (bf16[16,3200]{1,0:T(8,128)(2,1)}, bf16[16,3200]{1,0:T(8,128)(2,1)}, bf16[16,3200]{1,0:T(8,128)(2,1)}, bf16[16,3200]{1,0:T(8,128)(2,1)}) custom-call(s32[128]{0:T(128)} %refs_0_.1, s32[8,128]{1,0:T(8,128)} %bitcast.18, f32[8,128]{1,0:T(8,128)} %bitcast.19, s32[1,128]{1,0:T(1,128)} %bitcast.20, bf16[128,4096]{1,0:T(8,128)(2,1)} %refs_4_.1, ...), custom_call_target="tpu_custom_call" | custom-call | flops 167772160 | bytes 2621440 | tf_op jit(solution)/shard_map/pallas_call | solution.py:246
  4.0 3.1 %collective-permute-start.3 = (bf16[16,3200]{1,0:T(8,128)(2,1)}, bf16[16,3200]{1,0:T(8,128)(2,1)S(1)}, u32[]{:S(2)}, u32[]{:S(2)}) collective-permute-start(bf16[16,3200]{1,0:T(8,128)(2,1)} %get-tuple-element.35), channel_id=1, source_target_pairs={{0,4},{4,0},{8,12},{12,8},{1,5},{5,1},{9,13},{13,9},{2,6},{6,2},{1... | collective-permute-start | bytes 307208 | tf_op jit(solution)/shard_map/ppermute | solution.py:209
  7.0 2.5 %collective-permute-start.4 = (bf16[16,3200]{1,0:T(8,128)(2,1)}, bf16[16,3200]{1,0:T(8,128)(2,1)S(1)}, u32[]{:S(2)}, u32[]{:S(2)}) collective-permute-start(bf16[16,3200]{1,0:T(8,128)(2,1)} %get-tuple-element.36), channel_id=1, source_target_pairs={{0,12},{4,8},{8,4},{12,0},{1,13},{5,9},{9,5},{13,1},{2,14},{6,10},... | collective-permute-start | bytes 307208 | tf_op jit(solution)/shard_map/ppermute | solution.py:209
  9.5 0.1 collective-permute-start
  9.6 0.7 %collective-permute-done.3.refs_1_ = bf16[16,3200]{1,0:T(8,128)(2,1)S(1)} collective-permute-done((bf16[16,3200]{1,0:T(8,128)(2,1)}, bf16[16,3200]{1,0:T(8,128)(2,1)S(1)}, u32[]{:S(2)}, u32[]{:S(2)}) %collective-permute-start.3) | collective-permute-done | bytes 102432 | tf_op jit(solution)/shard_map/ppermute | solution.py:209
  10.4 1.7 %collective-permute-start.5 = (bf16[16,3200]{1,0:T(8,128)(2,1)}, bf16[16,3200]{1,0:T(8,128)(2,1)S(1)}, u32[]{:S(2)}, u32[]{:S(2)}) collective-permute-start(bf16[16,3200]{1,0:T(8,128)(2,1)} %get-tuple-element.25.rows_hbm), channel_id=1, source_target_pairs={{0,2},{1,3},{2,0},{3,1},{4,6},{5,7},{6,4},{7,5},{8,10},{9,11},{10,... | collective-permute-start | bytes 307208 | tf_op jit(solution)/shard_map/ppermute | solution.py:209
  12.0 3.7 %collective-permute-done.4.refs_2_ = bf16[16,3200]{1,0:T(8,128)(2,1)S(1)} collective-permute-done((bf16[16,3200]{1,0:T(8,128)(2,1)}, bf16[16,3200]{1,0:T(8,128)(2,1)S(1)}, u32[]{:S(2)}, u32[]{:S(2)}) %collective-permute-start.4) | collective-permute-done | bytes 102432 | tf_op jit(solution)/shard_map/ppermute | solution.py:209
  15.7 1.5 %collective-permute-start.6 = (bf16[16,3200]{1,0:T(8,128)(2,1)S(1)}, bf16[16,3200]{1,0:T(8,128)(2,1)S(1)}, u32[]{:S(2)}, u32[]{:S(2)}) collective-permute-start(bf16[16,3200]{1,0:T(8,128)(2,1)S(1)} %collective-permute-done.3.refs_1_), channel_id=1, source_target_pairs={{0,2},{1,3},{2,0},{3,1},{4,6},{5,7},{6,4},{7,5},{8,10},{9,11},{10,... | collective-permute-start | bytes 307208 | tf_op jit(solution)/shard_map/ppermute | solution.py:209
  17.2 0.0 collective-permute-done.1.pair_gate_ref
  17.2 0.5 %collective-permute-start.7 = (bf16[16,3200]{1,0:T(8,128)(2,1)S(1)}, bf16[16,3200]{1,0:T(8,128)(2,1)S(1)}, u32[]{:S(2)}, u32[]{:S(2)}) collective-permute-start(bf16[16,3200]{1,0:T(8,128)(2,1)S(1)} %collective-permute-done.4.refs_2_), channel_id=1, source_target_pairs={{0,2},{1,3},{2,0},{3,1},{4,6},{5,7},{6,4},{7,5},{8,10},{9,11},{10,... | collective-permute-start | bytes 307208 | tf_op jit(solution)/shard_map/ppermute | solution.py:209
  17.8 0.0 collective-permute-done.2.pair_up_ref
  17.8 0.0 copy-done
  17.8 0.0 copy-done.2
  17.8 0.0 copy-start.1
  17.8 0.9 %copy-done.1 = bf16[16,3200]{1,0:T(8,128)(2,1)S(1)} copy-done((bf16[16,3200]{1,0:T(8,128)(2,1)S(1)}, bf16[16,3200]{1,0:T(8,128)(2,1)}, u32[]{:S(2)}) %copy-start.1) | copy-done | bytes 102424
  18.7 1.5 %shard_map.101 = (bf16[192,4096]{1,0:T(8,128)(2,1)S(1)}, bf16[192,4096]{1,0:T(8,128)(2,1)S(1)}, bf16[16,3200]{1,0:T(8,128)(2,1)S(1)}, bf16[64,192]{1,0:T(8,128)(2,1)S(1)}, bf16[64,192]{1,0:T(8,128)(2,1)S(1)}) custom-call(bf16[64,768]{1,0:T(8,128)(2,1)S(1)} %bitcast.14, bf16[192,4096]{1,0:T(8,128)(2,1)S(1)} %bitcast.13, bf16[192,4096]{1,0:T(8,128)(2,1)} %bitcast.16, ...), custom_call_target="tpu_custom_call" | custom-call | bytes 6291456 | tf_op jit(solution)/shard_map/pallas_call | solution.py:263
  20.2 0.0 collective-permute-done.refs_3_
  20.2 1.6 %collective-permute-start.8 = (bf16[16,3200]{1,0:T(8,128)(2,1)S(1)}, bf16[16,3200]{1,0:T(8,128)(2,1)S(1)}, u32[]{:S(2)}, u32[]{:S(2)}) collective-permute-start(bf16[16,3200]{1,0:T(8,128)(2,1)S(1)} %collective-permute-done.refs_3_), channel_id=1, source_target_pairs={{0,2},{1,3},{2,0},{3,1},{4,6},{5,7},{6,4},{7,5},{8,10},{9,11},{10,... | collective-permute-start | bytes 307208 | tf_op jit(solution)/shard_map/ppermute | solution.py:209
  21.8 0.0 collective-permute-done.5.refs_4_
  21.8 0.0 collective-permute-done.6.refs_5_
  21.8 0.5 %collective-permute-done.7.refs_6_ = bf16[16,3200]{1,0:T(8,128)(2,1)S(1)} collective-permute-done((bf16[16,3200]{1,0:T(8,128)(2,1)S(1)}, bf16[16,3200]{1,0:T(8,128)(2,1)S(1)}, u32[]{:S(2)}, u32[]{:S(2)}) %collective-permute-start.7) | collective-permute-done | bytes 102432 | tf_op jit(solution)/shard_map/ppermute | solution.py:209
  22.3 2.7 %collective-permute-done.8.refs_7_ = bf16[16,3200]{1,0:T(8,128)(2,1)S(1)} collective-permute-done((bf16[16,3200]{1,0:T(8,128)(2,1)S(1)}, bf16[16,3200]{1,0:T(8,128)(2,1)S(1)}, u32[]{:S(2)}, u32[]{:S(2)}) %collective-permute-start.8) | collective-permute-done | bytes 102432 | tf_op jit(solution)/shard_map/ppermute | solution.py:209
  24.9 2.4 %shard_map.102 = (f32[64,64]{1,0:T(8,128)S(1)}, bf16[64,64]{1,0:T(8,128)(2,1)S(1)}, bf16[64,128]{1,0:T(8,128)(2,1)S(1)}) custom-call(bf16[192,4096]{1,0:T(8,128)(2,1)S(1)} %get-tuple-element.28.gate_ref, bf16[192,4096]{1,0:T(8,128)(2,1)S(1)} %get-tuple-element.29.up_ref, bf16[192,4096]{1,0:T(8,128)(2,1)S(1)} %collective-permute-done.1.pair_gate_ref, ...), custom_call_target="tpu_custom_call" | custom-call | flops 805306368 | bytes 7077888 | tf_op jit(solution)/shard_map/pallas_call | solution.py:289
  27.3 1.5 %collective-permute-start.9 = (bf16[64,64]{1,0:T(8,128)(2,1)S(1)}, bf16[64,64]{1,0:T(8,128)(2,1)S(1)}, u32[]{:S(2)}, u32[]{:S(2)}) collective-permute-start(bf16[64,64]{1,0:T(8,128)(2,1)S(1)} %get-tuple-element.40), channel_id=1, source_target_pairs={{0,2},{1,3},{2,0},{3,1},{4,6},{5,7},{6,4},{7,5},{8,10},{9,11},{10,... | collective-permute-start | bytes 24584 | tf_op jit(solution)/shard_map/ppermute | solution.py:209
  28.8 2.2 %collective-permute-done.9.refs_1_ = bf16[64,64]{1,0:T(8,128)(2,1)S(1)} collective-permute-done((bf16[64,64]{1,0:T(8,128)(2,1)S(1)}, bf16[64,64]{1,0:T(8,128)(2,1)S(1)}, u32[]{:S(2)}, u32[]{:S(2)}) %collective-permute-start.9) | collective-permute-done | bytes 8224 | tf_op jit(solution)/shard_map/ppermute | solution.py:209
  31.1 0.8 %shard_map.103 = f32[2,32,128]{2,1,0:T(8,128)} custom-call(bf16[64,128]{1,0:T(8,128)(2,1)S(1)} %get-tuple-element.38.grads_ref, f32[64,64]{1,0:T(8,128)S(1)} %get-tuple-element.39.refs_0_, bf16[64,64]{1,0:T(8,128)(2,1)S(1)} %collective-permute-done.9.refs_1_), custom_call_target="tpu_custom_call" | custom-call | flops 1048576 | bytes 32768 | tf_op jit(solution)/shard_map/pallas_call | solution.py:300
Async XLA Ops:
  0.0 17.8 %copy-start = (bf16[1,4096,192]{1,2,0:T(8,128)(2,1)S(1)}, bf16[1,4096,192]{1,2,0:T(8,128)(2,1)}, u32[]{:S(2)}) copy-start(bf16[1,4096,192]{1,2,0:T(8,128)(2,1)} %param.16) | copy-start | bytes 4718596
  0.0 17.8 %copy-start.2 = (bf16[768,64]{0,1:T(8,128)(2,1)S(1)}, bf16[768,64]{0,1:T(8,128)(2,1)}, u32[]{:S(2)}) copy-start(bf16[768,64]{0,1:T(8,128)(2,1)} %param.18) | copy-start | bytes 294916
  0.0 17.2 %collective-permute-start.1 = (bf16[192,4096]{1,0:T(8,128)(2,1)}, bf16[192,4096]{1,0:T(8,128)(2,1)S(1)}, u32[]{:S(2)}, u32[]{:S(2)}) collective-permute-start(bf16[192,4096]{1,0:T(8,128)(2,1)} %bitcast.12), channel_id=1, source_target_pairs={{0,1},{1,0},{2,3},{3,2},{4,5},{5,4},{6,7},{7,6},{8,9},{9,8},{10,11... | collective-permute-start | bytes 4718600 | tf_op jit(solution)/shard_map/ppermute | solution.py:209
  0.5 17.3 %collective-permute-start.2 = (bf16[192,4096]{1,0:T(8,128)(2,1)}, bf16[192,4096]{1,0:T(8,128)(2,1)S(1)}, u32[]{:S(2)}, u32[]{:S(2)}) collective-permute-start(bf16[192,4096]{1,0:T(8,128)(2,1)} %bitcast.15), channel_id=1, source_target_pairs={{0,1},{1,0},{2,3},{3,2},{4,5},{5,4},{6,7},{7,6},{8,9},{9,8},{10,11... | collective-permute-start | bytes 4718600 | tf_op jit(solution)/shard_map/ppermute | solution.py:209
  4.0 6.4 %collective-permute-start.3 = (bf16[16,3200]{1,0:T(8,128)(2,1)}, bf16[16,3200]{1,0:T(8,128)(2,1)S(1)}, u32[]{:S(2)}, u32[]{:S(2)}) collective-permute-start(bf16[16,3200]{1,0:T(8,128)(2,1)} %get-tuple-element.35), channel_id=1, source_target_pairs={{0,4},{4,0},{8,12},{12,8},{1,5},{5,1},{9,13},{13,9},{2,6},{6,2},{1... | collective-permute-start | bytes 307208 | tf_op jit(solution)/shard_map/ppermute | solution.py:209
  7.0 8.7 %collective-permute-start.4 = (bf16[16,3200]{1,0:T(8,128)(2,1)}, bf16[16,3200]{1,0:T(8,128)(2,1)S(1)}, u32[]{:S(2)}, u32[]{:S(2)}) collective-permute-start(bf16[16,3200]{1,0:T(8,128)(2,1)} %get-tuple-element.36), channel_id=1, source_target_pairs={{0,12},{4,8},{8,4},{12,0},{1,13},{5,9},{9,5},{13,1},{2,14},{6,10},... | collective-permute-start | bytes 307208 | tf_op jit(solution)/shard_map/ppermute | solution.py:209
  9.5 10.7 %collective-permute-start = (bf16[16,3200]{1,0:T(8,128)(2,1)}, bf16[16,3200]{1,0:T(8,128)(2,1)S(1)}, u32[]{:S(2)}, u32[]{:S(2)}) collective-permute-start(bf16[16,3200]{1,0:T(8,128)(2,1)} %get-tuple-element.23), channel_id=1, source_target_pairs={{0,8},{4,12},{8,0},{12,4},{1,9},{5,13},{9,1},{13,5},{2,10},{6,14},... | collective-permute-start | bytes 307208 | tf_op jit(solution)/shard_map/ppermute | solution.py:209
  10.4 11.4 %collective-permute-start.5 = (bf16[16,3200]{1,0:T(8,128)(2,1)}, bf16[16,3200]{1,0:T(8,128)(2,1)S(1)}, u32[]{:S(2)}, u32[]{:S(2)}) collective-permute-start(bf16[16,3200]{1,0:T(8,128)(2,1)} %get-tuple-element.25.rows_hbm), channel_id=1, source_target_pairs={{0,2},{1,3},{2,0},{3,1},{4,6},{5,7},{6,4},{7,5},{8,10},{9,11},{10,... | collective-permute-start | bytes 307208 | tf_op jit(solution)/shard_map/ppermute | solution.py:209
  15.7 6.1 %collective-permute-start.6 = (bf16[16,3200]{1,0:T(8,128)(2,1)S(1)}, bf16[16,3200]{1,0:T(8,128)(2,1)S(1)}, u32[]{:S(2)}, u32[]{:S(2)}) collective-permute-start(bf16[16,3200]{1,0:T(8,128)(2,1)S(1)} %collective-permute-done.3.refs_1_), channel_id=1, source_target_pairs={{0,2},{1,3},{2,0},{3,1},{4,6},{5,7},{6,4},{7,5},{8,10},{9,11},{10,... | collective-permute-start | bytes 307208 | tf_op jit(solution)/shard_map/ppermute | solution.py:209
  17.2 5.0 %collective-permute-start.7 = (bf16[16,3200]{1,0:T(8,128)(2,1)S(1)}, bf16[16,3200]{1,0:T(8,128)(2,1)S(1)}, u32[]{:S(2)}, u32[]{:S(2)}) collective-permute-start(bf16[16,3200]{1,0:T(8,128)(2,1)S(1)} %collective-permute-done.4.refs_2_), channel_id=1, source_target_pairs={{0,2},{1,3},{2,0},{3,1},{4,6},{5,7},{6,4},{7,5},{8,10},{9,11},{10,... | collective-permute-start | bytes 307208 | tf_op jit(solution)/shard_map/ppermute | solution.py:209
  17.8 0.9 %copy-start.1 = (bf16[16,3200]{1,0:T(8,128)(2,1)S(1)}, bf16[16,3200]{1,0:T(8,128)(2,1)}, u32[]{:S(2)}) copy-start(bf16[16,3200]{1,0:T(8,128)(2,1)} %get-tuple-element.25.rows_hbm) | copy-start | bytes 307204
  20.2 4.7 %collective-permute-start.8 = (bf16[16,3200]{1,0:T(8,128)(2,1)S(1)}, bf16[16,3200]{1,0:T(8,128)(2,1)S(1)}, u32[]{:S(2)}, u32[]{:S(2)}) collective-permute-start(bf16[16,3200]{1,0:T(8,128)(2,1)S(1)} %collective-permute-done.refs_3_), channel_id=1, source_target_pairs={{0,2},{1,3},{2,0},{3,1},{4,6},{5,7},{6,4},{7,5},{8,10},{9,11},{10,... | collective-permute-start | bytes 307208 | tf_op jit(solution)/shard_map/ppermute | solution.py:209
  27.3 3.8 %collective-permute-start.9 = (bf16[64,64]{1,0:T(8,128)(2,1)S(1)}, bf16[64,64]{1,0:T(8,128)(2,1)S(1)}, u32[]{:S(2)}, u32[]{:S(2)}) collective-permute-start(bf16[64,64]{1,0:T(8,128)(2,1)S(1)} %get-tuple-element.40), channel_id=1, source_target_pairs={{0,2},{1,3},{2,0},{3,1},{4,6},{5,7},{6,4},{7,5},{8,10},{9,11},{10,... | collective-permute-start | bytes 24584 | tf_op jit(solution)/shard_map/ppermute | solution.py:209

commit v8 on v6

--- a/solution.py
+++ b/solution.py
@@ -15,6 +15,7 @@
 HALF = ROWS // 2
 MIB = 1024 * 1024
 KEEP_LIMIT = 48
+PIECES = 6
 SEND_LIMIT = 56
 BF16 = jnp.bfloat16
 F32 = jnp.float32
@@ -57,12 +58,24 @@
     tokens, width = tokens_ref.shape
     chunk = width // (PARTS + 1)
     columns = [slice(i * chunk, (i + 1) * chunk) for i in range(PARTS + 1)]
-    pairs = list(zip(in_refs, scratch)) + [
-        (gate_hbm, held_ref.at[pl.ds(0, units)]),
-        (up_hbm, held_ref.at[pl.ds(units, units)]),
-    ]
-    copies = [pltpu.make_async_copy(a, b, sems.at[i]) for i, (a, b) in enumerate(pairs)]
-    for copy in copies:
+    copies = [
+        pltpu.make_async_copy(a, b, sems.at[i]) for i, (a, b) in enumerate(zip(in_refs, scratch))
+    ]
+    loads, stores = [], []
+    piece = units // PIECES
+    for k, source in enumerate((gate_hbm, up_hbm)):
+        for j in range(PIECES):
+            lines = pl.ds(k * units + j * piece, piece)
+            load_sem, store_sem = [sems.at[len(copies) + len(loads) + n] for n in (0, 2 * PIECES)]
+            loads.append(
+                pltpu.make_async_copy(
+                    source.at[pl.ds(j * piece, piece)], held_ref.at[lines], load_sem
+                )
+            )
+            stores.append(
+                pltpu.make_async_copy(held_ref.at[lines], weights_ref.at[lines], store_sem)
+            )
+    for copy in copies[:4] + copies[5:] + copies[4:5] + loads:
         copy.start()
     for copy in copies[:4]:
         copy.wait()
@@ -88,10 +101,11 @@
     ]
     pad = [jnp.zeros((-count % 8, tokens), F32)] if count % 8 else []
     shares = jnp.concatenate(share_rows + pad, axis=0).T
+    for load, store in zip(loads, stores):
+        load.wait()
+        store.start()
     for copy in copies[4:]:
         copy.wait()
-    store = pltpu.make_async_copy(held_ref, weights_ref, sems.at[len(pairs)])
-    store.start()
     proj = dot_t(derivs_ref[...], compressor_ref[...])
     last = tokens_ref[:, columns[-1]]
     for i in range(PARTS):
@@ -104,7 +118,8 @@
         both = dot(owned[q], grad)
         halves = [both[n * ROWS : (n + 1) * ROWS] for n in range(EX_DEV)]
         out_refs[q][:, PARTS * chunk :] = jnp.concatenate(halves, axis=1).astype(BF16)
-    store.wait()
+    for store in stores:
+        store.wait()
 
 
 def keep_kernel(compressor_ref, weights_hbm, rows_hbm, *refs):
@@ -258,7 +273,7 @@
         flops=4 * size * tokens * packed + 2 * tokens * width * rank,
         moved=4 * tokens * width + 2 * rank * width + 8 * units * width,
         scratch=[space(a.shape, a.dtype) for space, a in zip(spaces, arguments)]
-        + [pltpu.VMEM((2 * units, width), BF16), pltpu.SemaphoreType.DMA((len(arguments) + 3,))],
+        + [pltpu.VMEM((2 * units, width), BF16), pltpu.SemaphoreType.DMA((len(arguments) + 4 * PIECES,))],
     )(*arguments, gate, up)
     pair_weights = swap(weights, "dp", 1)
 

time: 31.9 us -> 31.3 us (0.981)
  Pallas kernels: 10.4 us -> 9.8 us
    pallas_call x1, Pallas kernels: 5.23 us -> 4.67 us  [body(): call(functools.partial(send_kernel, hops), [shape((ROWS, packed + EX_DEV...]
where the time goes in v8:
time: 31.3 us; the launch traced here: 31.1 us
  starting transfers between devices  12.3 us (39%)
  Pallas kernels  9.8 us (31%)
  waiting for transfers between devices  8.04 us (26%)
  local copies, waits for them, and re-layouts  0.93 us (3%)
    ppermute x9, starting transfers between devices, swap(): return lax.ppermute(a, axis, [(i, i ^ q) for i in range(n)])  12.3 us
    ppermute x9, waiting for transfers between devices, swap(): return lax.ppermute(a, axis, [(i, i ^ q) for i in range(n)])  8.04 us
    pallas_call x1, Pallas kernels, body(): call(functools.partial(send_kernel, hops), [shape((ROWS, packed + EX_DEV...  4.67 us
    pallas_call x1, Pallas kernels, body(): call(functools.partial(sketch_kernel, [size] * len(ds)), [shape((rank, si...  2.41 us
    pallas_call x1, Pallas kernels, body(): call(keep_kernel, [shape(weights.shape, BF16), shape(rows[0].shape, BF16)...  1.91 us
    unnamed x4, local copies, waits for them, and re-layouts  0.93 us
    pallas_call x1, Pallas kernels, body(): call(outer_kernel, shape((EX_DEV, rank * rank // 128, 128), F32), [VMEM]...  0.81 us
  transfers between devices with their start and end apart: 9, of which 5 were waited for; matrix products, arithmetic and copies ran while one was open for 0% of the time, Pallas kernels for 6%

profile of v8, /device:TPU:0, one launch (start us, length us, event | category | flops | bytes accessed | tf_op | source)
XLA Modules:
  0.0 31.1 jit_solution(17307925432465391648)
XLA Ops:
  0.0 0.0 copy-start.1
  0.0 4.7 %shard_map.100 = (bf16[16,3200]{1,0:T(8,128)(2,1)}, bf16[16,3200]{1,0:T(8,128)(2,1)}, bf16[16,3200]{1,0:T(8,128)(2,1)}, bf16[16,3200]{1,0:T(8,128)(2,1)}, bf16[384,4096]{1,0:T(8,128)(2,1)}) custom-call(s32[128]{0:T(128)} %refs_0_.1, s32[8,128]{1,0:T(8,128)} %bitcast.16, f32[8,128]{1,0:T(8,128)} %bitcast.17, s32[1,128]{1,0:T(1,128)} %bitcast.18, ...), custom_call_target="tpu_custom_call" | custom-call | flops 167772160 | bytes 8912896 | tf_op jit(solution)/shard_map/pallas_call | solution.py:267
  4.7 0.5 %collective-permute-start.1 = (bf16[384,4096]{1,0:T(8,128)(2,1)}, bf16[384,4096]{1,0:T(8,128)(2,1)S(1)}, u32[]{:S(2)}, u32[]{:S(2)}) collective-permute-start(bf16[384,4096]{1,0:T(8,128)(2,1)} %get-tuple-element.20.weights_hbm), channel_id=1, source_target_pairs={{0,1},{1,0},{2,3},{3,2},{4,5},{5,4},{6,7},{7,6},{8,9},{9,8},{10,11... | collective-permute-start | bytes 9437192 | tf_op jit(solution)/shard_map/ppermute | solution.py:231
  5.2 4.7 %collective-permute-start = (bf16[16,3200]{1,0:T(8,128)(2,1)}, bf16[16,3200]{1,0:T(8,128)(2,1)S(1)}, u32[]{:S(2)}, u32[]{:S(2)}) collective-permute-start(bf16[16,3200]{1,0:T(8,128)(2,1)} %get-tuple-element.19), channel_id=1, source_target_pairs={{0,12},{4,8},{8,4},{12,0},{1,13},{5,9},{9,5},{13,1},{2,14},{6,10},... | collective-permute-start | bytes 307208 | tf_op jit(solution)/shard_map/ppermute | solution.py:231
  9.9 0.0 collective-permute-start.2
  9.9 0.7 %collective-permute-start.3 = (bf16[16,3200]{1,0:T(8,128)(2,1)}, bf16[16,3200]{1,0:T(8,128)(2,1)S(1)}, u32[]{:S(2)}, u32[]{:S(2)}) collective-permute-start(bf16[16,3200]{1,0:T(8,128)(2,1)} %get-tuple-element.29), channel_id=1, source_target_pairs={{0,8},{4,12},{8,0},{12,4},{1,9},{5,13},{9,1},{13,5},{2,10},{6,14},... | collective-permute-start | bytes 307208 | tf_op jit(solution)/shard_map/ppermute | solution.py:231
  10.5 1.6 %collective-permute-start.4 = (bf16[16,3200]{1,0:T(8,128)(2,1)}, bf16[16,3200]{1,0:T(8,128)(2,1)S(1)}, u32[]{:S(2)}, u32[]{:S(2)}) collective-permute-start(bf16[16,3200]{1,0:T(8,128)(2,1)} %get-tuple-element.21.rows_hbm), channel_id=1, source_target_pairs={{0,2},{1,3},{2,0},{3,1},{4,6},{5,7},{6,4},{7,5},{8,10},{9,11},{10,... | collective-permute-start | bytes 307208 | tf_op jit(solution)/shard_map/ppermute | solution.py:231
  12.2 0.0 copy-done.1
  12.2 0.0 copy-start
  12.2 0.9 %copy-done = bf16[16,3200]{1,0:T(8,128)(2,1)S(1)} copy-done((bf16[16,3200]{1,0:T(8,128)(2,1)S(1)}, bf16[16,3200]{1,0:T(8,128)(2,1)}, u32[]{:S(2)}) %copy-start) | copy-done | bytes 102424
  13.1 1.9 %shard_map.101 = (bf16[384,4096]{1,0:T(8,128)(2,1)S(1)}, bf16[16,3200]{1,0:T(8,128)(2,1)S(1)}, bf16[64,192]{1,0:T(8,128)(2,1)S(1)}, bf16[64,192]{1,0:T(8,128)(2,1)S(1)}) custom-call(bf16[64,768]{1,0:T(8,128)(2,1)S(1)} %bitcast.12, bf16[384,4096]{1,0:T(8,128)(2,1)} %get-tuple-element.20.weights_hbm, bf16[16,3200]{1,0:T(8,128)(2,1)S(1)} %copy-done), custom_call_target="tpu_custom_call" | custom-call | bytes 6291456 | tf_op jit(solution)/shard_map/pallas_call | solution.py:283
  15.0 0.0 collective-permute-done.refs_1_
  15.0 0.5 %collective-permute-start.5 = (bf16[16,3200]{1,0:T(8,128)(2,1)S(1)}, bf16[16,3200]{1,0:T(8,128)(2,1)S(1)}, u32[]{:S(2)}, u32[]{:S(2)}) collective-permute-start(bf16[16,3200]{1,0:T(8,128)(2,1)S(1)} %collective-permute-done.refs_1_), channel_id=1, source_target_pairs={{0,2},{1,3},{2,0},{3,1},{4,6},{5,7},{6,4},{7,5},{8,10},{9,11},{10,... | collective-permute-start | bytes 307208 | tf_op jit(solution)/shard_map/ppermute | solution.py:231
  15.5 1.3 %collective-permute-done.2.refs_2_ = bf16[16,3200]{1,0:T(8,128)(2,1)S(1)} collective-permute-done((bf16[16,3200]{1,0:T(8,128)(2,1)}, bf16[16,3200]{1,0:T(8,128)(2,1)S(1)}, u32[]{:S(2)}, u32[]{:S(2)}) %collective-permute-start.2) | collective-permute-done | bytes 102432 | tf_op jit(solution)/shard_map/ppermute | solution.py:231
  16.8 1.5 %collective-permute-start.6 = (bf16[16,3200]{1,0:T(8,128)(2,1)S(1)}, bf16[16,3200]{1,0:T(8,128)(2,1)S(1)}, u32[]{:S(2)}, u32[]{:S(2)}) collective-permute-start(bf16[16,3200]{1,0:T(8,128)(2,1)S(1)} %collective-permute-done.2.refs_2_), channel_id=1, source_target_pairs={{0,2},{1,3},{2,0},{3,1},{4,6},{5,7},{6,4},{7,5},{8,10},{9,11},{10,... | collective-permute-start | bytes 307208 | tf_op jit(solution)/shard_map/ppermute | solution.py:231
  18.3 1.0 %collective-permute-done.3.refs_3_ = bf16[16,3200]{1,0:T(8,128)(2,1)S(1)} collective-permute-done((bf16[16,3200]{1,0:T(8,128)(2,1)}, bf16[16,3200]{1,0:T(8,128)(2,1)S(1)}, u32[]{:S(2)}, u32[]{:S(2)}) %collective-permute-start.3) | collective-permute-done | bytes 102432 | tf_op jit(solution)/shard_map/ppermute | solution.py:231
  19.3 1.5 %collective-permute-start.7 = (bf16[16,3200]{1,0:T(8,128)(2,1)S(1)}, bf16[16,3200]{1,0:T(8,128)(2,1)S(1)}, u32[]{:S(2)}, u32[]{:S(2)}) collective-permute-start(bf16[16,3200]{1,0:T(8,128)(2,1)S(1)} %collective-permute-done.3.refs_3_), channel_id=1, source_target_pairs={{0,2},{1,3},{2,0},{3,1},{4,6},{5,7},{6,4},{7,5},{8,10},{9,11},{10,... | collective-permute-start | bytes 307208 | tf_op jit(solution)/shard_map/ppermute | solution.py:231
  20.8 0.0 collective-permute-done.4.refs_4_
  20.8 0.0 collective-permute-done.5.refs_5_
  20.8 1.5 %collective-permute-done.6.refs_6_ = bf16[16,3200]{1,0:T(8,128)(2,1)S(1)} collective-permute-done((bf16[16,3200]{1,0:T(8,128)(2,1)S(1)}, bf16[16,3200]{1,0:T(8,128)(2,1)S(1)}, u32[]{:S(2)}, u32[]{:S(2)}) %collective-permute-start.6) | collective-permute-done | bytes 102432 | tf_op jit(solution)/shard_map/ppermute | solution.py:231
  22.3 1.9 %collective-permute-done.7.refs_7_ = bf16[16,3200]{1,0:T(8,128)(2,1)S(1)} collective-permute-done((bf16[16,3200]{1,0:T(8,128)(2,1)S(1)}, bf16[16,3200]{1,0:T(8,128)(2,1)S(1)}, u32[]{:S(2)}, u32[]{:S(2)}) %collective-permute-start.7) | collective-permute-done | bytes 102432 | tf_op jit(solution)/shard_map/ppermute | solution.py:231
  24.1 0.0 collective-permute-done.1.pair_ref
  24.1 2.4 %shard_map.102 = (f32[64,64]{1,0:T(8,128)S(1)}, bf16[64,64]{1,0:T(8,128)(2,1)S(1)}, bf16[64,128]{1,0:T(8,128)(2,1)S(1)}) custom-call(bf16[384,4096]{1,0:T(8,128)(2,1)S(1)} %get-tuple-element.23.own_ref, bf16[384,4096]{1,0:T(8,128)(2,1)S(1)} %collective-permute-done.1.pair_ref, bf16[64,192]{1,0:T(8,128)(2,1)S(1)} %get-tuple-element.24.first_ref, ...), custom_call_target="tpu_custom_call" | custom-call | flops 805306368 | bytes 7077888 | tf_op jit(solution)/shard_map/pallas_call | solution.py:309
  26.5 1.4 %collective-permute-start.8 = (bf16[64,64]{1,0:T(8,128)(2,1)S(1)}, bf16[64,64]{1,0:T(8,128)(2,1)S(1)}, u32[]{:S(2)}, u32[]{:S(2)}) collective-permute-start(bf16[64,64]{1,0:T(8,128)(2,1)S(1)} %get-tuple-element.32), channel_id=1, source_target_pairs={{0,2},{1,3},{2,0},{3,1},{4,6},{5,7},{6,4},{7,5},{8,10},{9,11},{10,... | collective-permute-start | bytes 24584 | tf_op jit(solution)/shard_map/ppermute | solution.py:231
  27.9 2.4 %collective-permute-done.8.refs_1_ = bf16[64,64]{1,0:T(8,128)(2,1)S(1)} collective-permute-done((bf16[64,64]{1,0:T(8,128)(2,1)S(1)}, bf16[64,64]{1,0:T(8,128)(2,1)S(1)}, u32[]{:S(2)}, u32[]{:S(2)}) %collective-permute-start.8) | collective-permute-done | bytes 8224 | tf_op jit(solution)/shard_map/ppermute | solution.py:231
  30.3 0.8 %shard_map.103 = f32[2,32,128]{2,1,0:T(8,128)} custom-call(bf16[64,128]{1,0:T(8,128)(2,1)S(1)} %get-tuple-element.30.grads_ref, f32[64,64]{1,0:T(8,128)S(1)} %get-tuple-element.31.refs_0_, bf16[64,64]{1,0:T(8,128)(2,1)S(1)} %collective-permute-done.8.refs_1_), custom_call_target="tpu_custom_call" | custom-call | flops 1048576 | bytes 32768 | tf_op jit(solution)/shard_map/pallas_call | solution.py:320
Async XLA Ops:
  0.0 12.2 %copy-start.1 = (bf16[768,64]{0,1:T(8,128)(2,1)S(1)}, bf16[768,64]{0,1:T(8,128)(2,1)}, u32[]{:S(2)}) copy-start(bf16[768,64]{0,1:T(8,128)(2,1)} %param.18) | copy-start | bytes 294916
  4.7 19.4 %collective-permute-start.1 = (bf16[384,4096]{1,0:T(8,128)(2,1)}, bf16[384,4096]{1,0:T(8,128)(2,1)S(1)}, u32[]{:S(2)}, u32[]{:S(2)}) collective-permute-start(bf16[384,4096]{1,0:T(8,128)(2,1)} %get-tuple-element.20.weights_hbm), channel_id=1, source_target_pairs={{0,1},{1,0},{2,3},{3,2},{4,5},{5,4},{6,7},{7,6},{8,9},{9,8},{10,11... | collective-permute-start | bytes 9437192 | tf_op jit(solution)/shard_map/ppermute | solution.py:231
  5.2 9.8 %collective-permute-start = (bf16[16,3200]{1,0:T(8,128)(2,1)}, bf16[16,3200]{1,0:T(8,128)(2,1)S(1)}, u32[]{:S(2)}, u32[]{:S(2)}) collective-permute-start(bf16[16,3200]{1,0:T(8,128)(2,1)} %get-tuple-element.19), channel_id=1, source_target_pairs={{0,12},{4,8},{8,4},{12,0},{1,13},{5,9},{9,5},{13,1},{2,14},{6,10},... | collective-permute-start | bytes 307208 | tf_op jit(solution)/shard_map/ppermute | solution.py:231
  9.9 7.0 %collective-permute-start.2 = (bf16[16,3200]{1,0:T(8,128)(2,1)}, bf16[16,3200]{1,0:T(8,128)(2,1)S(1)}, u32[]{:S(2)}, u32[]{:S(2)}) collective-permute-start(bf16[16,3200]{1,0:T(8,128)(2,1)} %get-tuple-element.28), channel_id=1, source_target_pairs={{0,4},{4,0},{8,12},{12,8},{1,5},{5,1},{9,13},{13,9},{2,6},{6,2},{1... | collective-permute-start | bytes 307208 | tf_op jit(solution)/shard_map/ppermute | solution.py:231
  9.9 9.4 %collective-permute-start.3 = (bf16[16,3200]{1,0:T(8,128)(2,1)}, bf16[16,3200]{1,0:T(8,128)(2,1)S(1)}, u32[]{:S(2)}, u32[]{:S(2)}) collective-permute-start(bf16[16,3200]{1,0:T(8,128)(2,1)} %get-tuple-element.29), channel_id=1, source_target_pairs={{0,8},{4,12},{8,0},{12,4},{1,9},{5,13},{9,1},{13,5},{2,10},{6,14},... | collective-permute-start | bytes 307208 | tf_op jit(solution)/shard_map/ppermute | solution.py:231
  10.5 10.3 %collective-permute-start.4 = (bf16[16,3200]{1,0:T(8,128)(2,1)}, bf16[16,3200]{1,0:T(8,128)(2,1)S(1)}, u32[]{:S(2)}, u32[]{:S(2)}) collective-permute-start(bf16[16,3200]{1,0:T(8,128)(2,1)} %get-tuple-element.21.rows_hbm), channel_id=1, source_target_pairs={{0,2},{1,3},{2,0},{3,1},{4,6},{5,7},{6,4},{7,5},{8,10},{9,11},{10,... | collective-permute-start | bytes 307208 | tf_op jit(solution)/shard_map/ppermute | solution.py:231
  12.2 0.9 %copy-start = (bf16[16,3200]{1,0:T(8,128)(2,1)S(1)}, bf16[16,3200]{1,0:T(8,128)(2,1)}, u32[]{:S(2)}) copy-start(bf16[16,3200]{1,0:T(8,128)(2,1)} %get-tuple-element.21.rows_hbm) | copy-start | bytes 307204
  15.0 5.8 %collective-permute-start.5 = (bf16[16,3200]{1,0:T(8,128)(2,1)S(1)}, bf16[16,3200]{1,0:T(8,128)(2,1)S(1)}, u32[]{:S(2)}, u32[]{:S(2)}) collective-permute-start(bf16[16,3200]{1,0:T(8,128)(2,1)S(1)} %collective-permute-done.refs_1_), channel_id=1, source_target_pairs={{0,2},{1,3},{2,0},{3,1},{4,6},{5,7},{6,4},{7,5},{8,10},{9,11},{10,... | collective-permute-start | bytes 307208 | tf_op jit(solution)/shard_map/ppermute | solution.py:231
  16.8 5.4 %collective-permute-start.6 = (bf16[16,3200]{1,0:T(8,128)(2,1)S(1)}, bf16[16,3200]{1,0:T(8,128)(2,1)S(1)}, u32[]{:S(2)}, u32[]{:S(2)}) collective-permute-start(bf16[16,3200]{1,0:T(8,128)(2,1)S(1)} %collective-permute-done.2.refs_2_), channel_id=1, source_target_pairs={{0,2},{1,3},{2,0},{3,1},{4,6},{5,7},{6,4},{7,5},{8,10},{9,11},{10,... | collective-permute-start | bytes 307208 | tf_op jit(solution)/shard_map/ppermute | solution.py:231
  19.3 4.8 %collective-permute-start.7 = (bf16[16,3200]{1,0:T(8,128)(2,1)S(1)}, bf16[16,3200]{1,0:T(8,128)(2,1)S(1)}, u32[]{:S(2)}, u32[]{:S(2)}) collective-permute-start(bf16[16,3200]{1,0:T(8,128)(2,1)S(1)} %collective-permute-done.3.refs_3_), channel_id=1, source_target_pairs={{0,2},{1,3},{2,0},{3,1},{4,6},{5,7},{6,4},{7,5},{8,10},{9,11},{10,... | collective-permute-start | bytes 307208 | tf_op jit(solution)/shard_map/ppermute | solution.py:231
  26.5 3.8 %collective-permute-start.8 = (bf16[64,64]{1,0:T(8,128)(2,1)S(1)}, bf16[64,64]{1,0:T(8,128)(2,1)S(1)}, u32[]{:S(2)}, u32[]{:S(2)}) collective-permute-start(bf16[64,64]{1,0:T(8,128)(2,1)S(1)} %get-tuple-element.32), channel_id=1, source_target_pairs={{0,2},{1,3},{2,0},{3,1},{4,6},{5,7},{6,4},{7,5},{8,10},{9,11},{10,... | collective-permute-start | bytes 24584 | tf_op jit(solution)/shard_map/ppermute | solution.py:231

commit v9 on v8

--- a/solution.py
+++ b/solution.py
@@ -14,7 +14,7 @@
 PARTS = LOCAL_SEATS // SPARE
 HALF = ROWS // 2
 MIB = 1024 * 1024
-KEEP_LIMIT = 48
+KEEP_LIMIT = 49
 PIECES = 6
 SEND_LIMIT = 56
 BF16 = jnp.bfloat16
@@ -124,10 +124,16 @@
 
 def keep_kernel(compressor_ref, weights_hbm, rows_hbm, *refs):
     weights_ref, rows_ref, first_ref, second_ref, sems = refs
+    piece = weights_ref.shape[0] // PIECES
     copies = [
-        pltpu.make_async_copy(weights_hbm, weights_ref, sems.at[0]),
-        pltpu.make_async_copy(rows_hbm, rows_ref, sems.at[1]),
-    ]
+        pltpu.make_async_copy(
+            weights_hbm.at[pl.ds(i * piece, piece)],
+            weights_ref.at[pl.ds(i * piece, piece)],
+            sems.at[i],
+        )
+        for i in range(PIECES)
+    ]
+    copies.append(pltpu.make_async_copy(rows_hbm, rows_ref, sems.at[PIECES]))
     for copy in copies:
         copy.start()
     chosen = chosen_compressors(compressor_ref, first_ref.shape[1])
@@ -229,6 +235,14 @@
 def swap(a, axis, q):
     n = lax.axis_size(axis)
     return lax.ppermute(a, axis, [(i, i ^ q) for i in range(n)])
+
+
+def swap_both(a, q, d):
+    n_exp, n_dp = lax.axis_size("exp"), lax.axis_size("dp")
+    pairs = [
+        (e * n_dp + i, (e ^ q) * n_dp + (i ^ d)) for e in range(n_exp) for i in range(n_dp)
+    ]
+    return lax.ppermute(a, ("exp", "dp"), pairs)
 
 
 def body(
@@ -287,14 +301,17 @@
         KEEP_LIMIT * MIB,
         out_specs=[ANY, ANY, VMEM, VMEM],
         moved=8 * units * width,
-        scratch=[pltpu.SemaphoreType.DMA((2,))],
+        scratch=[pltpu.SemaphoreType.DMA((PIECES + 1,))],
     )(inflow_compressor.T, weights, rows[0])
     for i, q in enumerate(hops):
         if i:
+            if q == 1:
+                crossed.append(swap_both(rows[i], q, half))
             rows[i] = swap(rows[i], "exp", q)
-            if i == 1:
+            if q == 1:
                 rows[i], weights = lax.optimization_barrier((rows[i], weights))
-            crossed.append(swap(rows[i], "dp", half))
+            if q != 1:
+                crossed.append(swap(rows[i], "dp", half))
     blocks = {0: rows, half: crossed}
     step = half // 2
     while step > 1:

time: 31.3 us -> 32.4 us (1.035)
  starting transfers between devices: 12.3 us -> 13.5 us
    ppermute x0 -> x1, starting transfers between devices: none -> 2.72 us  [swap_both(): return lax.ppermute(a, ('exp', 'dp'), pairs)]
    ppermute x9 -> x8, starting transfers between devices: 12.3 us -> 10.8 us  [swap(): return lax.ppermute(a, axis, [(i, i ^ q) for i in range(n)])]
    ppermute x9 -> x8, waiting for transfers between devices: 8.04 us -> 7.94 us  [swap(): return lax.ppermute(a, axis, [(i, i ^ q) for i in range(n)])]
  transfers between devices with their start and end apart: 9 -> 9, of which waited for: 5 -> 4; matrix products, arithmetic and copies ran while one was open for 0% -> 0% of each run, Pallas kernels for 6% -> 6%
where the time goes in v9:
time: 32.4 us; the launch traced here: 32.2 us
  starting transfers between devices  13.5 us (42%)
  Pallas kernels  9.83 us (30%)
  waiting for transfers between devices  7.94 us (25%)
  local copies, waits for them, and re-layouts  0.9 us (3%)
    ppermute x8, starting transfers between devices, swap(): return lax.ppermute(a, axis, [(i, i ^ q) for i in range(n)])  10.8 us
    ppermute x8, waiting for transfers between devices, swap(): return lax.ppermute(a, axis, [(i, i ^ q) for i in range(n)])  7.94 us
    pallas_call x1, Pallas kernels, body(): call(functools.partial(send_kernel, hops), [shape((ROWS, packed + EX_DEV...  4.67 us
    ppermute x1, starting transfers between devices, swap_both(): return lax.ppermute(a, ('exp', 'dp'), pairs)  2.72 us
    pallas_call x1, Pallas kernels, body(): call(functools.partial(sketch_kernel, [size] * len(ds)), [shape((rank, si...  2.45 us
    pallas_call x1, Pallas kernels, body(): call(keep_kernel, [shape(weights.shape, BF16), shape(rows[0].shape, BF16)...  1.89 us
    unnamed x4, local copies, waits for them, and re-layouts  0.9 us
    pallas_call x1, Pallas kernels, body(): call(outer_kernel, shape((EX_DEV, rank * rank // 128, 128), F32), [VMEM]...  0.81 us
  transfers between devices with their start and end apart: 9, of which 4 were waited for; matrix products, arithmetic and copies ran while one was open for 0% of the time, Pallas kernels for 6%

profile of v9, /device:TPU:0, one launch (start us, length us, event | category | flops | bytes accessed | tf_op | source)
XLA Modules:
  0.0 32.2 jit_solution(9251733467319477004)
XLA Ops:
  0.0 0.0 copy-start.1
  0.0 4.7 %shard_map.100 = (bf16[16,3200]{1,0:T(8,128)(2,1)}, bf16[16,3200]{1,0:T(8,128)(2,1)}, bf16[16,3200]{1,0:T(8,128)(2,1)}, bf16[16,3200]{1,0:T(8,128)(2,1)}, bf16[384,4096]{1,0:T(8,128)(2,1)}) custom-call(s32[128]{0:T(128)} %refs_0_.1, s32[8,128]{1,0:T(8,128)} %bitcast.16, f32[8,128]{1,0:T(8,128)} %bitcast.17, s32[1,128]{1,0:T(1,128)} %bitcast.18, ...), custom_call_target="tpu_custom_call" | custom-call | flops 167772160 | bytes 8912896 | tf_op jit(solution)/shard_map/pallas_call | solution.py:281
  4.7 0.5 %collective-permute-start.1 = (bf16[384,4096]{1,0:T(8,128)(2,1)}, bf16[384,4096]{1,0:T(8,128)(2,1)S(1)}, u32[]{:S(2)}, u32[]{:S(2)}) collective-permute-start(bf16[384,4096]{1,0:T(8,128)(2,1)} %get-tuple-element.20.weights_hbm), channel_id=1, source_target_pairs={{0,1},{1,0},{2,3},{3,2},{4,5},{5,4},{6,7},{7,6},{8,9},{9,8},{10,11... | collective-permute-start | bytes 9437192 | tf_op jit(solution)/shard_map/ppermute | solution.py:237
  5.2 2.6 %collective-permute-start = (bf16[16,3200]{1,0:T(8,128)(2,1)}, bf16[16,3200]{1,0:T(8,128)(2,1)S(1)}, u32[]{:S(2)}, u32[]{:S(2)}) collective-permute-start(bf16[16,3200]{1,0:T(8,128)(2,1)} %get-tuple-element.19), channel_id=1, source_target_pairs={{0,4},{4,0},{8,12},{12,8},{1,5},{5,1},{9,13},{13,9},{2,6},{6,2},{1... | collective-permute-start | bytes 307208 | tf_op jit(solution)/shard_map/ppermute | solution.py:237
  7.8 2.5 %collective-permute-start.2 = (bf16[16,3200]{1,0:T(8,128)(2,1)}, bf16[16,3200]{1,0:T(8,128)(2,1)S(1)}, u32[]{:S(2)}, u32[]{:S(2)}) collective-permute-start(bf16[16,3200]{1,0:T(8,128)(2,1)} %get-tuple-element.27), channel_id=1, source_target_pairs={{0,12},{4,8},{8,4},{12,0},{1,13},{5,9},{9,5},{13,1},{2,14},{6,10},... | collective-permute-start | bytes 307208 | tf_op jit(solution)/shard_map/ppermute | solution.py:237
  10.3 0.1 collective-permute-start.3
  10.4 2.7 %collective-permute-start.6 = (bf16[16,3200]{1,0:T(8,128)(2,1)}, bf16[16,3200]{1,0:T(8,128)(2,1)S(1)}, u32[]{:S(2)}, u32[]{:S(2)}) collective-permute-start(bf16[16,3200]{1,0:T(8,128)(2,1)} %get-tuple-element.19), channel_id=1, source_target_pairs={{0,6},{1,7},{2,4},{3,5},{4,2},{5,3},{6,0},{7,1},{8,14},{9,15},{10,... | collective-permute-start | bytes 307208 | tf_op jit(solution)/shard_map/ppermute | solution.py:245
  13.2 0.0 collective-permute-done.refs_2_
  13.2 0.5 %collective-permute-start.4 = (bf16[16,3200]{1,0:T(8,128)(2,1)}, bf16[16,3200]{1,0:T(8,128)(2,1)S(1)}, u32[]{:S(2)}, u32[]{:S(2)}) collective-permute-start(bf16[16,3200]{1,0:T(8,128)(2,1)} %get-tuple-element.21.rows_hbm), channel_id=1, source_target_pairs={{0,2},{1,3},{2,0},{3,1},{4,6},{5,7},{6,4},{7,5},{8,10},{9,11},{10,... | collective-permute-start | bytes 307208 | tf_op jit(solution)/shard_map/ppermute | solution.py:237
  13.7 2.8 %collective-permute-done.2.refs_1_ = bf16[16,3200]{1,0:T(8,128)(2,1)S(1)} collective-permute-done((bf16[16,3200]{1,0:T(8,128)(2,1)}, bf16[16,3200]{1,0:T(8,128)(2,1)S(1)}, u32[]{:S(2)}, u32[]{:S(2)}) %collective-permute-start.2) | collective-permute-done | bytes 102432 | tf_op jit(solution)/shard_map/ppermute | solution.py:237
  16.5 1.5 %collective-permute-start.5 = (bf16[16,3200]{1,0:T(8,128)(2,1)S(1)}, bf16[16,3200]{1,0:T(8,128)(2,1)S(1)}, u32[]{:S(2)}, u32[]{:S(2)}) collective-permute-start(bf16[16,3200]{1,0:T(8,128)(2,1)S(1)} %collective-permute-done.2.refs_1_), channel_id=1, source_target_pairs={{0,2},{1,3},{2,0},{3,1},{4,6},{5,7},{6,4},{7,5},{8,10},{9,11},{10,... | collective-permute-start | bytes 307208 | tf_op jit(solution)/shard_map/ppermute | solution.py:237
  18.0 2.5 %collective-permute-done.3.refs_3_ = bf16[16,3200]{1,0:T(8,128)(2,1)S(1)} collective-permute-done((bf16[16,3200]{1,0:T(8,128)(2,1)}, bf16[16,3200]{1,0:T(8,128)(2,1)S(1)}, u32[]{:S(2)}, u32[]{:S(2)}) %collective-permute-start.3) | collective-permute-done | bytes 102432 | tf_op jit(solution)/shard_map/ppermute | solution.py:237
  20.4 1.5 %collective-permute-start.7 = (bf16[16,3200]{1,0:T(8,128)(2,1)S(1)}, bf16[16,3200]{1,0:T(8,128)(2,1)S(1)}, u32[]{:S(2)}, u32[]{:S(2)}) collective-permute-start(bf16[16,3200]{1,0:T(8,128)(2,1)S(1)} %collective-permute-done.3.refs_3_), channel_id=1, source_target_pairs={{0,2},{1,3},{2,0},{3,1},{4,6},{5,7},{6,4},{7,5},{8,10},{9,11},{10,... | collective-permute-start | bytes 307208 | tf_op jit(solution)/shard_map/ppermute | solution.py:237
  21.9 0.0 copy-done.1
  21.9 0.0 copy-start
  21.9 0.9 %copy-done = bf16[16,3200]{1,0:T(8,128)(2,1)S(1)} copy-done((bf16[16,3200]{1,0:T(8,128)(2,1)S(1)}, bf16[16,3200]{1,0:T(8,128)(2,1)}, u32[]{:S(2)}) %copy-start) | copy-done | bytes 102424
  22.8 1.9 %shard_map.101 = (bf16[384,4096]{1,0:T(8,128)(2,1)S(1)}, bf16[16,3200]{1,0:T(8,128)(2,1)S(1)}, bf16[64,192]{1,0:T(8,128)(2,1)S(1)}, bf16[64,192]{1,0:T(8,128)(2,1)S(1)}) custom-call(bf16[64,768]{1,0:T(8,128)(2,1)S(1)} %bitcast.12, bf16[384,4096]{1,0:T(8,128)(2,1)} %get-tuple-element.20.weights_hbm, bf16[16,3200]{1,0:T(8,128)(2,1)S(1)} %copy-done), custom_call_target="tpu_custom_call" | custom-call | bytes 6291456 | tf_op jit(solution)/shard_map/pallas_call | solution.py:297
  24.7 0.0 collective-permute-done.4.refs_4_
  24.7 0.0 collective-permute-done.6.refs_6_
  24.7 0.0 collective-permute-done.5.refs_5_
  24.8 0.4 %collective-permute-done.7.refs_7_ = bf16[16,3200]{1,0:T(8,128)(2,1)S(1)} collective-permute-done((bf16[16,3200]{1,0:T(8,128)(2,1)S(1)}, bf16[16,3200]{1,0:T(8,128)(2,1)S(1)}, u32[]{:S(2)}, u32[]{:S(2)}) %collective-permute-start.7) | collective-permute-done | bytes 102432 | tf_op jit(solution)/shard_map/ppermute | solution.py:237
  25.2 0.0 collective-permute-done.1.pair_ref
  25.2 2.5 %shard_map.102 = (f32[64,64]{1,0:T(8,128)S(1)}, bf16[64,64]{1,0:T(8,128)(2,1)S(1)}, bf16[64,128]{1,0:T(8,128)(2,1)S(1)}) custom-call(bf16[384,4096]{1,0:T(8,128)(2,1)S(1)} %get-tuple-element.23.own_ref, bf16[384,4096]{1,0:T(8,128)(2,1)S(1)} %collective-permute-done.1.pair_ref, bf16[64,192]{1,0:T(8,128)(2,1)S(1)} %get-tuple-element.24.first_ref, ...), custom_call_target="tpu_custom_call" | custom-call | flops 805306368 | bytes 7077888 | tf_op jit(solution)/shard_map/pallas_call | solution.py:326
  27.6 1.5 %collective-permute-start.8 = (bf16[64,64]{1,0:T(8,128)(2,1)S(1)}, bf16[64,64]{1,0:T(8,128)(2,1)S(1)}, u32[]{:S(2)}, u32[]{:S(2)}) collective-permute-start(bf16[64,64]{1,0:T(8,128)(2,1)S(1)} %get-tuple-element.32), channel_id=1, source_target_pairs={{0,2},{1,3},{2,0},{3,1},{4,6},{5,7},{6,4},{7,5},{8,10},{9,11},{10,... | collective-permute-start | bytes 24584 | tf_op jit(solution)/shard_map/ppermute | solution.py:237
  29.1 2.3 %collective-permute-done.8.refs_1_ = bf16[64,64]{1,0:T(8,128)(2,1)S(1)} collective-permute-done((bf16[64,64]{1,0:T(8,128)(2,1)S(1)}, bf16[64,64]{1,0:T(8,128)(2,1)S(1)}, u32[]{:S(2)}, u32[]{:S(2)}) %collective-permute-start.8) | collective-permute-done | bytes 8224 | tf_op jit(solution)/shard_map/ppermute | solution.py:237
  31.4 0.8 %shard_map.103 = f32[2,32,128]{2,1,0:T(8,128)} custom-call(bf16[64,128]{1,0:T(8,128)(2,1)S(1)} %get-tuple-element.30.grads_ref, f32[64,64]{1,0:T(8,128)S(1)} %get-tuple-element.31.refs_0_, bf16[64,64]{1,0:T(8,128)(2,1)S(1)} %collective-permute-done.8.refs_1_), custom_call_target="tpu_custom_call" | custom-call | flops 1048576 | bytes 32768 | tf_op jit(solution)/shard_map/pallas_call | solution.py:337
Async XLA Ops:
  0.0 21.9 %copy-start.1 = (bf16[768,64]{0,1:T(8,128)(2,1)S(1)}, bf16[768,64]{0,1:T(8,128)(2,1)}, u32[]{:S(2)}) copy-start(bf16[768,64]{0,1:T(8,128)(2,1)} %param.18) | copy-start | bytes 294916
  4.7 20.5 %collective-permute-start.1 = (bf16[384,4096]{1,0:T(8,128)(2,1)}, bf16[384,4096]{1,0:T(8,128)(2,1)S(1)}, u32[]{:S(2)}, u32[]{:S(2)}) collective-permute-start(bf16[384,4096]{1,0:T(8,128)(2,1)} %get-tuple-element.20.weights_hbm), channel_id=1, source_target_pairs={{0,1},{1,0},{2,3},{3,2},{4,5},{5,4},{6,7},{7,6},{8,9},{9,8},{10,11... | collective-permute-start | bytes 9437192 | tf_op jit(solution)/shard_map/ppermute | solution.py:237
  5.2 8.0 %collective-permute-start = (bf16[16,3200]{1,0:T(8,128)(2,1)}, bf16[16,3200]{1,0:T(8,128)(2,1)S(1)}, u32[]{:S(2)}, u32[]{:S(2)}) collective-permute-start(bf16[16,3200]{1,0:T(8,128)(2,1)} %get-tuple-element.19), channel_id=1, source_target_pairs={{0,4},{4,0},{8,12},{12,8},{1,5},{5,1},{9,13},{13,9},{2,6},{6,2},{1... | collective-permute-start | bytes 307208 | tf_op jit(solution)/shard_map/ppermute | solution.py:237
  7.8 8.6 %collective-permute-start.2 = (bf16[16,3200]{1,0:T(8,128)(2,1)}, bf16[16,3200]{1,0:T(8,128)(2,1)S(1)}, u32[]{:S(2)}, u32[]{:S(2)}) collective-permute-start(bf16[16,3200]{1,0:T(8,128)(2,1)} %get-tuple-element.27), channel_id=1, source_target_pairs={{0,12},{4,8},{8,4},{12,0},{1,13},{5,9},{9,5},{13,1},{2,14},{6,10},... | collective-permute-start | bytes 307208 | tf_op jit(solution)/shard_map/ppermute | solution.py:237
  10.3 10.1 %collective-permute-start.3 = (bf16[16,3200]{1,0:T(8,128)(2,1)}, bf16[16,3200]{1,0:T(8,128)(2,1)S(1)}, u32[]{:S(2)}, u32[]{:S(2)}) collective-permute-start(bf16[16,3200]{1,0:T(8,128)(2,1)} %get-tuple-element.29), channel_id=1, source_target_pairs={{0,8},{4,12},{8,0},{12,4},{1,9},{5,13},{9,1},{13,5},{2,10},{6,14},... | collective-permute-start | bytes 307208 | tf_op jit(solution)/shard_map/ppermute | solution.py:237
  10.4 14.3 %collective-permute-start.6 = (bf16[16,3200]{1,0:T(8,128)(2,1)}, bf16[16,3200]{1,0:T(8,128)(2,1)S(1)}, u32[]{:S(2)}, u32[]{:S(2)}) collective-permute-start(bf16[16,3200]{1,0:T(8,128)(2,1)} %get-tuple-element.19), channel_id=1, source_target_pairs={{0,6},{1,7},{2,4},{3,5},{4,2},{5,3},{6,0},{7,1},{8,14},{9,15},{10,... | collective-permute-start | bytes 307208 | tf_op jit(solution)/shard_map/ppermute | solution.py:245
  13.2 11.6 %collective-permute-start.4 = (bf16[16,3200]{1,0:T(8,128)(2,1)}, bf16[16,3200]{1,0:T(8,128)(2,1)S(1)}, u32[]{:S(2)}, u32[]{:S(2)}) collective-permute-start(bf16[16,3200]{1,0:T(8,128)(2,1)} %get-tuple-element.21.rows_hbm), channel_id=1, source_target_pairs={{0,2},{1,3},{2,0},{3,1},{4,6},{5,7},{6,4},{7,5},{8,10},{9,11},{10,... | collective-permute-start | bytes 307208 | tf_op jit(solution)/shard_map/ppermute | solution.py:237
  16.5 8.3 %collective-permute-start.5 = (bf16[16,3200]{1,0:T(8,128)(2,1)S(1)}, bf16[16,3200]{1,0:T(8,128)(2,1)S(1)}, u32[]{:S(2)}, u32[]{:S(2)}) collective-permute-start(bf16[16,3200]{1,0:T(8,128)(2,1)S(1)} %collective-permute-done.2.refs_1_), channel_id=1, source_target_pairs={{0,2},{1,3},{2,0},{3,1},{4,6},{5,7},{6,4},{7,5},{8,10},{9,11},{10,... | collective-permute-start | bytes 307208 | tf_op jit(solution)/shard_map/ppermute | solution.py:237
  20.4 4.7 %collective-permute-start.7 = (bf16[16,3200]{1,0:T(8,128)(2,1)S(1)}, bf16[16,3200]{1,0:T(8,128)(2,1)S(1)}, u32[]{:S(2)}, u32[]{:S(2)}) collective-permute-start(bf16[16,3200]{1,0:T(8,128)(2,1)S(1)} %collective-permute-done.3.refs_3_), channel_id=1, source_target_pairs={{0,2},{1,3},{2,0},{3,1},{4,6},{5,7},{6,4},{7,5},{8,10},{9,11},{10,... | collective-permute-start | bytes 307208 | tf_op jit(solution)/shard_map/ppermute | solution.py:237
  21.9 0.9 %copy-start = (bf16[16,3200]{1,0:T(8,128)(2,1)S(1)}, bf16[16,3200]{1,0:T(8,128)(2,1)}, u32[]{:S(2)}) copy-start(bf16[16,3200]{1,0:T(8,128)(2,1)} %get-tuple-element.21.rows_hbm) | copy-start | bytes 307204
  27.6 3.8 %collective-permute-start.8 = (bf16[64,64]{1,0:T(8,128)(2,1)S(1)}, bf16[64,64]{1,0:T(8,128)(2,1)S(1)}, u32[]{:S(2)}, u32[]{:S(2)}) collective-permute-start(bf16[64,64]{1,0:T(8,128)(2,1)S(1)} %get-tuple-element.32), channel_id=1, source_target_pairs={{0,2},{1,3},{2,0},{3,1},{4,6},{5,7},{6,4},{7,5},{8,10},{9,11},{10,... | collective-permute-start | bytes 24584 | tf_op jit(solution)/shard_map/ppermute | solution.py:237

commit v10 on v9

--- a/solution.py
+++ b/solution.py
@@ -237,14 +237,6 @@
     return lax.ppermute(a, axis, [(i, i ^ q) for i in range(n)])
 
 
-def swap_both(a, q, d):
-    n_exp, n_dp = lax.axis_size("exp"), lax.axis_size("dp")
-    pairs = [
-        (e * n_dp + i, (e ^ q) * n_dp + (i ^ d)) for e in range(n_exp) for i in range(n_dp)
-    ]
-    return lax.ppermute(a, ("exp", "dp"), pairs)
-
-
 def body(
     layer_inflows,
     output_derivatives,
@@ -305,13 +297,8 @@
     )(inflow_compressor.T, weights, rows[0])
     for i, q in enumerate(hops):
         if i:
-            if q == 1:
-                crossed.append(swap_both(rows[i], q, half))
             rows[i] = swap(rows[i], "exp", q)
-            if q == 1:
-                rows[i], weights = lax.optimization_barrier((rows[i], weights))
-            if q != 1:
-                crossed.append(swap(rows[i], "dp", half))
+            crossed.append(swap(rows[i], "dp", half))
     blocks = {0: rows, half: crossed}
     step = half // 2
     while step > 1:

time: 32.4 us -> 31.2 us (0.963)
  waiting for transfers between devices: 7.94 us -> 6.62 us
    ppermute x8 -> x9, starting transfers between devices: 10.8 us -> 13.6 us  [swap(): return lax.ppermute(a, axis, [(i, i ^ q) for i in range(n)])]
    ppermute x1 -> x0, starting transfers between devices: 2.72 us -> none  [swap_both(): return lax.ppermute(a, ('exp', 'dp'), pairs)]
    ppermute x8 -> x9, waiting for transfers between devices: 7.94 us -> 6.62 us  [swap(): return lax.ppermute(a, axis, [(i, i ^ q) for i in range(n)])]
  transfers between devices with their start and end apart: 9 -> 9, of which waited for: 4 -> 5; matrix products, arithmetic and copies ran while one was open for 0% -> 0% of each run, Pallas kernels for 6% -> 6%
where the time goes in v10:
time: 31.2 us; the launch traced here: 31 us
  starting transfers between devices  13.6 us (44%)
  Pallas kernels  9.84 us (32%)
  waiting for transfers between devices  6.62 us (21%)
  local copies, waits for them, and re-layouts  0.9 us (3%)
    ppermute x9, starting transfers between devices, swap(): return lax.ppermute(a, axis, [(i, i ^ q) for i in range(n)])  13.6 us
    ppermute x9, waiting for transfers between devices, swap(): return lax.ppermute(a, axis, [(i, i ^ q) for i in range(n)])  6.62 us
    pallas_call x1, Pallas kernels, body(): call(functools.partial(send_kernel, hops), [shape((ROWS, packed + EX_DEV...  4.67 us
    pallas_call x1, Pallas kernels, body(): call(functools.partial(sketch_kernel, [size] * len(ds)), [shape((rank, si...  2.47 us
    pallas_call x1, Pallas kernels, body(): call(keep_kernel, [shape(weights.shape, BF16), shape(rows[0].shape, BF16)...  1.89 us
    unnamed x4, local copies, waits for them, and re-layouts  0.9 us
    pallas_call x1, Pallas kernels, body(): call(outer_kernel, shape((EX_DEV, rank * rank // 128, 128), F32), [VMEM]...  0.81 us
  transfers between devices with their start and end apart: 9, of which 5 were waited for; matrix products, arithmetic and copies ran while one was open for 0% of the time, Pallas kernels for 6%

profile of v10, /device:TPU:0, one launch (start us, length us, event | category | flops | bytes accessed | tf_op | source)
XLA Modules:
  0.0 31.0 jit_solution(6709317099300887674)
XLA Ops:
  0.0 0.0 copy-start.1
  0.0 4.7 %shard_map.100 = (bf16[16,3200]{1,0:T(8,128)(2,1)}, bf16[16,3200]{1,0:T(8,128)(2,1)}, bf16[16,3200]{1,0:T(8,128)(2,1)}, bf16[16,3200]{1,0:T(8,128)(2,1)}, bf16[384,4096]{1,0:T(8,128)(2,1)}) custom-call(s32[128]{0:T(128)} %refs_0_.1, s32[8,128]{1,0:T(8,128)} %bitcast.16, f32[8,128]{1,0:T(8,128)} %bitcast.17, s32[1,128]{1,0:T(1,128)} %bitcast.18, ...), custom_call_target="tpu_custom_call" | custom-call | flops 167772160 | bytes 8912896 | tf_op jit(solution)/shard_map/pallas_call | solution.py:273
  4.7 0.5 %collective-permute-start = (bf16[384,4096]{1,0:T(8,128)(2,1)}, bf16[384,4096]{1,0:T(8,128)(2,1)S(1)}, u32[]{:S(2)}, u32[]{:S(2)}) collective-permute-start(bf16[384,4096]{1,0:T(8,128)(2,1)} %get-tuple-element.17.weights_hbm), channel_id=1, source_target_pairs={{0,1},{1,0},{2,3},{3,2},{4,5},{5,4},{6,7},{7,6},{8,9},{9,8},{10,11... | collective-permute-start | bytes 9437192 | tf_op jit(solution)/shard_map/ppermute | solution.py:237
  5.2 4.7 %collective-permute-start.1 = (bf16[16,3200]{1,0:T(8,128)(2,1)}, bf16[16,3200]{1,0:T(8,128)(2,1)S(1)}, u32[]{:S(2)}, u32[]{:S(2)}) collective-permute-start(bf16[16,3200]{1,0:T(8,128)(2,1)} %get-tuple-element.23), channel_id=1, source_target_pairs={{0,12},{4,8},{8,4},{12,0},{1,13},{5,9},{9,5},{13,1},{2,14},{6,10},... | collective-permute-start | bytes 307208 | tf_op jit(solution)/shard_map/ppermute | solution.py:237
  9.9 0.0 collective-permute-start.2
  9.9 0.7 %collective-permute-start.3 = (bf16[16,3200]{1,0:T(8,128)(2,1)}, bf16[16,3200]{1,0:T(8,128)(2,1)S(1)}, u32[]{:S(2)}, u32[]{:S(2)}) collective-permute-start(bf16[16,3200]{1,0:T(8,128)(2,1)} %get-tuple-element.25), channel_id=1, source_target_pairs={{0,8},{4,12},{8,0},{12,4},{1,9},{5,13},{9,1},{13,5},{2,10},{6,14},... | collective-permute-start | bytes 307208 | tf_op jit(solution)/shard_map/ppermute | solution.py:237
  10.5 1.6 %collective-permute-start.4 = (bf16[16,3200]{1,0:T(8,128)(2,1)}, bf16[16,3200]{1,0:T(8,128)(2,1)S(1)}, u32[]{:S(2)}, u32[]{:S(2)}) collective-permute-start(bf16[16,3200]{1,0:T(8,128)(2,1)} %get-tuple-element.18.rows_hbm), channel_id=1, source_target_pairs={{0,2},{1,3},{2,0},{3,1},{4,6},{5,7},{6,4},{7,5},{8,10},{9,11},{10,... | collective-permute-start | bytes 307208 | tf_op jit(solution)/shard_map/ppermute | solution.py:237
  12.2 1.7 %collective-permute-done.1.refs_1_ = bf16[16,3200]{1,0:T(8,128)(2,1)S(1)} collective-permute-done((bf16[16,3200]{1,0:T(8,128)(2,1)}, bf16[16,3200]{1,0:T(8,128)(2,1)S(1)}, u32[]{:S(2)}, u32[]{:S(2)}) %collective-permute-start.1) | collective-permute-done | bytes 102432 | tf_op jit(solution)/shard_map/ppermute | solution.py:237
  13.9 1.6 %collective-permute-start.5 = (bf16[16,3200]{1,0:T(8,128)(2,1)S(1)}, bf16[16,3200]{1,0:T(8,128)(2,1)S(1)}, u32[]{:S(2)}, u32[]{:S(2)}) collective-permute-start(bf16[16,3200]{1,0:T(8,128)(2,1)S(1)} %collective-permute-done.1.refs_1_), channel_id=1, source_target_pairs={{0,2},{1,3},{2,0},{3,1},{4,6},{5,7},{6,4},{7,5},{8,10},{9,11},{10,... | collective-permute-start | bytes 307208 | tf_op jit(solution)/shard_map/ppermute | solution.py:237
  15.5 1.3 %collective-permute-done.2.refs_2_ = bf16[16,3200]{1,0:T(8,128)(2,1)S(1)} collective-permute-done((bf16[16,3200]{1,0:T(8,128)(2,1)}, bf16[16,3200]{1,0:T(8,128)(2,1)S(1)}, u32[]{:S(2)}, u32[]{:S(2)}) %collective-permute-start.2) | collective-permute-done | bytes 102432 | tf_op jit(solution)/shard_map/ppermute | solution.py:237
  16.8 1.5 %collective-permute-start.6 = (bf16[16,3200]{1,0:T(8,128)(2,1)S(1)}, bf16[16,3200]{1,0:T(8,128)(2,1)S(1)}, u32[]{:S(2)}, u32[]{:S(2)}) collective-permute-start(bf16[16,3200]{1,0:T(8,128)(2,1)S(1)} %collective-permute-done.2.refs_2_), channel_id=1, source_target_pairs={{0,2},{1,3},{2,0},{3,1},{4,6},{5,7},{6,4},{7,5},{8,10},{9,11},{10,... | collective-permute-start | bytes 307208 | tf_op jit(solution)/shard_map/ppermute | solution.py:237
  18.3 1.0 %collective-permute-done.3.refs_3_ = bf16[16,3200]{1,0:T(8,128)(2,1)S(1)} collective-permute-done((bf16[16,3200]{1,0:T(8,128)(2,1)}, bf16[16,3200]{1,0:T(8,128)(2,1)S(1)}, u32[]{:S(2)}, u32[]{:S(2)}) %collective-permute-start.3) | collective-permute-done | bytes 102432 | tf_op jit(solution)/shard_map/ppermute | solution.py:237
  19.3 1.5 %collective-permute-start.7 = (bf16[16,3200]{1,0:T(8,128)(2,1)S(1)}, bf16[16,3200]{1,0:T(8,128)(2,1)S(1)}, u32[]{:S(2)}, u32[]{:S(2)}) collective-permute-start(bf16[16,3200]{1,0:T(8,128)(2,1)S(1)} %collective-permute-done.3.refs_3_), channel_id=1, source_target_pairs={{0,2},{1,3},{2,0},{3,1},{4,6},{5,7},{6,4},{7,5},{8,10},{9,11},{10,... | collective-permute-start | bytes 307208 | tf_op jit(solution)/shard_map/ppermute | solution.py:237
  20.8 0.0 copy-done.1
  20.8 0.0 copy-start
  20.8 0.9 %copy-done = bf16[16,3200]{1,0:T(8,128)(2,1)S(1)} copy-done((bf16[16,3200]{1,0:T(8,128)(2,1)S(1)}, bf16[16,3200]{1,0:T(8,128)(2,1)}, u32[]{:S(2)}) %copy-start) | copy-done | bytes 102424
  21.7 1.9 %shard_map.101 = (bf16[384,4096]{1,0:T(8,128)(2,1)S(1)}, bf16[16,3200]{1,0:T(8,128)(2,1)S(1)}, bf16[64,192]{1,0:T(8,128)(2,1)S(1)}, bf16[64,192]{1,0:T(8,128)(2,1)S(1)}) custom-call(bf16[64,768]{1,0:T(8,128)(2,1)S(1)} %bitcast.12, bf16[384,4096]{1,0:T(8,128)(2,1)} %get-tuple-element.17.weights_hbm, bf16[16,3200]{1,0:T(8,128)(2,1)S(1)} %copy-done), custom_call_target="tpu_custom_call" | custom-call | bytes 6291456 | tf_op jit(solution)/shard_map/pallas_call | solution.py:289
  23.6 0.0 collective-permute-done.4.refs_4_
  23.6 0.0 collective-permute-done.5.refs_5_
  23.6 0.0 collective-permute-done.6.refs_6_
  23.6 0.3 %collective-permute-done.7.refs_7_ = bf16[16,3200]{1,0:T(8,128)(2,1)S(1)} collective-permute-done((bf16[16,3200]{1,0:T(8,128)(2,1)S(1)}, bf16[16,3200]{1,0:T(8,128)(2,1)S(1)}, u32[]{:S(2)}, u32[]{:S(2)}) %collective-permute-start.7) | collective-permute-done | bytes 102432 | tf_op jit(solution)/shard_map/ppermute | solution.py:237
  24.0 0.0 collective-permute-done.pair_ref
  24.0 2.5 %shard_map.102 = (f32[64,64]{1,0:T(8,128)S(1)}, bf16[64,64]{1,0:T(8,128)(2,1)S(1)}, bf16[64,128]{1,0:T(8,128)(2,1)S(1)}) custom-call(bf16[384,4096]{1,0:T(8,128)(2,1)S(1)} %get-tuple-element.19.own_ref, bf16[384,4096]{1,0:T(8,128)(2,1)S(1)} %collective-permute-done.pair_ref, bf16[64,192]{1,0:T(8,128)(2,1)S(1)} %get-tuple-element.20.first_ref, ...), custom_call_target="tpu_custom_call" | custom-call | flops 805306368 | bytes 7077888 | tf_op jit(solution)/shard_map/pallas_call | solution.py:313
  26.4 1.5 %collective-permute-start.8 = (bf16[64,64]{1,0:T(8,128)(2,1)S(1)}, bf16[64,64]{1,0:T(8,128)(2,1)S(1)}, u32[]{:S(2)}, u32[]{:S(2)}) collective-permute-start(bf16[64,64]{1,0:T(8,128)(2,1)S(1)} %get-tuple-element.28), channel_id=1, source_target_pairs={{0,2},{1,3},{2,0},{3,1},{4,6},{5,7},{6,4},{7,5},{8,10},{9,11},{10,... | collective-permute-start | bytes 24584 | tf_op jit(solution)/shard_map/ppermute | solution.py:237
  28.0 2.2 %collective-permute-done.8.refs_1_ = bf16[64,64]{1,0:T(8,128)(2,1)S(1)} collective-permute-done((bf16[64,64]{1,0:T(8,128)(2,1)S(1)}, bf16[64,64]{1,0:T(8,128)(2,1)S(1)}, u32[]{:S(2)}, u32[]{:S(2)}) %collective-permute-start.8) | collective-permute-done | bytes 8224 | tf_op jit(solution)/shard_map/ppermute | solution.py:237
  30.2 0.8 %shard_map.103 = f32[2,32,128]{2,1,0:T(8,128)} custom-call(bf16[64,128]{1,0:T(8,128)(2,1)S(1)} %get-tuple-element.26.grads_ref, f32[64,64]{1,0:T(8,128)S(1)} %get-tuple-element.27.refs_0_, bf16[64,64]{1,0:T(8,128)(2,1)S(1)} %collective-permute-done.8.refs_1_), custom_call_target="tpu_custom_call" | custom-call | flops 1048576 | bytes 32768 | tf_op jit(solution)/shard_map/pallas_call | solution.py:324
Async XLA Ops:
  0.0 20.8 %copy-start.1 = (bf16[768,64]{0,1:T(8,128)(2,1)S(1)}, bf16[768,64]{0,1:T(8,128)(2,1)}, u32[]{:S(2)}) copy-start(bf16[768,64]{0,1:T(8,128)(2,1)} %param.18) | copy-start | bytes 294916
  4.7 19.3 %collective-permute-start = (bf16[384,4096]{1,0:T(8,128)(2,1)}, bf16[384,4096]{1,0:T(8,128)(2,1)S(1)}, u32[]{:S(2)}, u32[]{:S(2)}) collective-permute-start(bf16[384,4096]{1,0:T(8,128)(2,1)} %get-tuple-element.17.weights_hbm), channel_id=1, source_target_pairs={{0,1},{1,0},{2,3},{3,2},{4,5},{5,4},{6,7},{7,6},{8,9},{9,8},{10,11... | collective-permute-start | bytes 9437192 | tf_op jit(solution)/shard_map/ppermute | solution.py:237
  5.2 8.7 %collective-permute-start.1 = (bf16[16,3200]{1,0:T(8,128)(2,1)}, bf16[16,3200]{1,0:T(8,128)(2,1)S(1)}, u32[]{:S(2)}, u32[]{:S(2)}) collective-permute-start(bf16[16,3200]{1,0:T(8,128)(2,1)} %get-tuple-element.23), channel_id=1, source_target_pairs={{0,12},{4,8},{8,4},{12,0},{1,13},{5,9},{9,5},{13,1},{2,14},{6,10},... | collective-permute-start | bytes 307208 | tf_op jit(solution)/shard_map/ppermute | solution.py:237
  9.9 7.0 %collective-permute-start.2 = (bf16[16,3200]{1,0:T(8,128)(2,1)}, bf16[16,3200]{1,0:T(8,128)(2,1)S(1)}, u32[]{:S(2)}, u32[]{:S(2)}) collective-permute-start(bf16[16,3200]{1,0:T(8,128)(2,1)} %get-tuple-element.24), channel_id=1, source_target_pairs={{0,4},{4,0},{8,12},{12,8},{1,5},{5,1},{9,13},{13,9},{2,6},{6,2},{1... | collective-permute-start | bytes 307208 | tf_op jit(solution)/shard_map/ppermute | solution.py:237
  9.9 9.4 %collective-permute-start.3 = (bf16[16,3200]{1,0:T(8,128)(2,1)}, bf16[16,3200]{1,0:T(8,128)(2,1)S(1)}, u32[]{:S(2)}, u32[]{:S(2)}) collective-permute-start(bf16[16,3200]{1,0:T(8,128)(2,1)} %get-tuple-element.25), channel_id=1, source_target_pairs={{0,8},{4,12},{8,0},{12,4},{1,9},{5,13},{9,1},{13,5},{2,10},{6,14},... | collective-permute-start | bytes 307208 | tf_op jit(solution)/shard_map/ppermute | solution.py:237
  10.5 13.1 %collective-permute-start.4 = (bf16[16,3200]{1,0:T(8,128)(2,1)}, bf16[16,3200]{1,0:T(8,128)(2,1)S(1)}, u32[]{:S(2)}, u32[]{:S(2)}) collective-permute-start(bf16[16,3200]{1,0:T(8,128)(2,1)} %get-tuple-element.18.rows_hbm), channel_id=1, source_target_pairs={{0,2},{1,3},{2,0},{3,1},{4,6},{5,7},{6,4},{7,5},{8,10},{9,11},{10,... | collective-permute-start | bytes 307208 | tf_op jit(solution)/shard_map/ppermute | solution.py:237
  13.9 9.7 %collective-permute-start.5 = (bf16[16,3200]{1,0:T(8,128)(2,1)S(1)}, bf16[16,3200]{1,0:T(8,128)(2,1)S(1)}, u32[]{:S(2)}, u32[]{:S(2)}) collective-permute-start(bf16[16,3200]{1,0:T(8,128)(2,1)S(1)} %collective-permute-done.1.refs_1_), channel_id=1, source_target_pairs={{0,2},{1,3},{2,0},{3,1},{4,6},{5,7},{6,4},{7,5},{8,10},{9,11},{10,... | collective-permute-start | bytes 307208 | tf_op jit(solution)/shard_map/ppermute | solution.py:237
  16.8 6.8 %collective-permute-start.6 = (bf16[16,3200]{1,0:T(8,128)(2,1)S(1)}, bf16[16,3200]{1,0:T(8,128)(2,1)S(1)}, u32[]{:S(2)}, u32[]{:S(2)}) collective-permute-start(bf16[16,3200]{1,0:T(8,128)(2,1)S(1)} %collective-permute-done.2.refs_2_), channel_id=1, source_target_pairs={{0,2},{1,3},{2,0},{3,1},{4,6},{5,7},{6,4},{7,5},{8,10},{9,11},{10,... | collective-permute-start | bytes 307208 | tf_op jit(solution)/shard_map/ppermute | solution.py:237
  19.3 4.7 %collective-permute-start.7 = (bf16[16,3200]{1,0:T(8,128)(2,1)S(1)}, bf16[16,3200]{1,0:T(8,128)(2,1)S(1)}, u32[]{:S(2)}, u32[]{:S(2)}) collective-permute-start(bf16[16,3200]{1,0:T(8,128)(2,1)S(1)} %collective-permute-done.3.refs_3_), channel_id=1, source_target_pairs={{0,2},{1,3},{2,0},{3,1},{4,6},{5,7},{6,4},{7,5},{8,10},{9,11},{10,... | collective-permute-start | bytes 307208 | tf_op jit(solution)/shard_map/ppermute | solution.py:237
  20.8 0.9 %copy-start = (bf16[16,3200]{1,0:T(8,128)(2,1)S(1)}, bf16[16,3200]{1,0:T(8,128)(2,1)}, u32[]{:S(2)}) copy-start(bf16[16,3200]{1,0:T(8,128)(2,1)} %get-tuple-element.18.rows_hbm) | copy-start | bytes 307204
  26.4 3.8 %collective-permute-start.8 = (bf16[64,64]{1,0:T(8,128)(2,1)S(1)}, bf16[64,64]{1,0:T(8,128)(2,1)S(1)}, u32[]{:S(2)}, u32[]{:S(2)}) collective-permute-start(bf16[64,64]{1,0:T(8,128)(2,1)S(1)} %get-tuple-element.28), channel_id=1, source_target_pairs={{0,2},{1,3},{2,0},{3,1},{4,6},{5,7},{6,4},{7,5},{8,10},{9,11},{10,... | collective-permute-start | bytes 24584 | tf_op jit(solution)/shard_map/ppermute | solution.py:237

commit v11 on v7

--- a/solution.py
+++ b/solution.py
@@ -241,7 +241,7 @@
         output_derivatives,
         outgrad_compressor.T,
     )
-    hops = [0, 1] + list(range(n_exp - 1, 1, -1))
+    hops = [0, n_exp - 1] + list(range(1, n_exp - 1))
     spaces = [pltpu.SMEM] + [pltpu.VMEM] * (len(arguments) - 1)
     rows = call(
         functools.partial(send_kernel, hops),
@@ -272,8 +272,6 @@
     for i, q in enumerate(hops):
         if i:
             rows[i] = swap(rows[i], "exp", q)
-            if i == n_exp - 1:
-                rows[i], gate, up = hold((rows[i], gate, up))
             crossed.append(swap(rows[i], "dp", half))
     blocks = {0: rows, half: crossed}
     step = half // 2

time: 32.1 us -> 31.9 us (level)
  transfers between devices with their start and end apart: 10 -> 10, of which waited for: 5 -> 6; matrix products, arithmetic and copies ran while one was open for 0% -> 0% of each run, Pallas kernels for 16% -> 16%
where the time goes in v11:
time: 31.9 us; the launch traced here: 31.7 us
  starting transfers between devices  13 us (41%)
  waiting for transfers between devices  9.64 us (30%)
  Pallas kernels  8.13 us (25%)
  local copies, waits for them, and re-layouts  0.89 us (3%)
    ppermute x10, starting transfers between devices, swap(): return lax.ppermute(a, axis, [(i, i ^ q) for i in range(n)])  13 us
    ppermute x10, waiting for transfers between devices, swap(): return lax.ppermute(a, axis, [(i, i ^ q) for i in range(n)])  9.64 us
    pallas_call x1, Pallas kernels, body(): call(functools.partial(send_kernel, hops), [shape((ROWS, packed + EX_DEV...  3.41 us
    pallas_call x1, Pallas kernels, body(): call(functools.partial(sketch_kernel, [size] * len(ds)), [shape((rank, si...  2.36 us
    pallas_call x1, Pallas kernels, body(): call(keep_kernel, [shape(a.shape, BF16) for a in (gate, up, rows[0])] + [...  1.54 us
    unnamed x6, local copies, waits for them, and re-layouts  0.89 us
    pallas_call x1, Pallas kernels, body(): call(outer_kernel, shape((EX_DEV, rank * rank // 128, 128), F32), [VMEM]...  0.81 us
  transfers between devices with their start and end apart: 10, of which 6 were waited for; matrix products, arithmetic and copies ran while one was open for 0% of the time, Pallas kernels for 16%

profile of v11, /device:TPU:0, one launch (start us, length us, event | category | flops | bytes accessed | tf_op | source)
XLA Modules:
  0.0 31.7 jit_solution(18372178263027504997)
XLA Ops:
  0.0 0.0 copy-start
  0.0 0.0 copy-start.2
  0.0 0.5 %collective-permute-start = (bf16[192,4096]{1,0:T(8,128)(2,1)}, bf16[192,4096]{1,0:T(8,128)(2,1)S(1)}, u32[]{:S(2)}, u32[]{:S(2)}) collective-permute-start(bf16[192,4096]{1,0:T(8,128)(2,1)} %bitcast.12), channel_id=1, source_target_pairs={{0,1},{1,0},{2,3},{3,2},{4,5},{5,4},{6,7},{7,6},{8,9},{9,8},{10,11... | collective-permute-start | bytes 4718600 | tf_op jit(solution)/shard_map/ppermute | solution.py:209
  0.5 0.1 collective-permute-start.1
  0.5 3.4 %shard_map.100 = (bf16[16,3200]{1,0:T(8,128)(2,1)}, bf16[16,3200]{1,0:T(8,128)(2,1)}, bf16[16,3200]{1,0:T(8,128)(2,1)}, bf16[16,3200]{1,0:T(8,128)(2,1)}) custom-call(s32[128]{0:T(128)} %refs_0_.1, s32[8,128]{1,0:T(8,128)} %bitcast.18, f32[8,128]{1,0:T(8,128)} %bitcast.19, s32[1,128]{1,0:T(1,128)} %bitcast.20, bf16[128,4096]{1,0:T(8,128)(2,1)} %refs_4_.1, ...), custom_call_target="tpu_custom_call" | custom-call | flops 167772160 | bytes 2621440 | tf_op jit(solution)/shard_map/pallas_call | solution.py:246
  4.0 5.1 %collective-permute-start.2 = (bf16[16,3200]{1,0:T(8,128)(2,1)}, bf16[16,3200]{1,0:T(8,128)(2,1)S(1)}, u32[]{:S(2)}, u32[]{:S(2)}) collective-permute-start(bf16[16,3200]{1,0:T(8,128)(2,1)} %get-tuple-element.29), channel_id=1, source_target_pairs={{0,12},{4,8},{8,4},{12,0},{1,13},{5,9},{9,5},{13,1},{2,14},{6,10},... | collective-permute-start | bytes 307208 | tf_op jit(solution)/shard_map/ppermute | solution.py:209
  9.1 0.0 collective-permute-start.3
  9.1 0.6 %collective-permute-start.4 = (bf16[16,3200]{1,0:T(8,128)(2,1)}, bf16[16,3200]{1,0:T(8,128)(2,1)S(1)}, u32[]{:S(2)}, u32[]{:S(2)}) collective-permute-start(bf16[16,3200]{1,0:T(8,128)(2,1)} %get-tuple-element.31), channel_id=1, source_target_pairs={{0,8},{4,12},{8,0},{12,4},{1,9},{5,13},{9,1},{13,5},{2,10},{6,14},... | collective-permute-start | bytes 307208 | tf_op jit(solution)/shard_map/ppermute | solution.py:209
  9.7 3.3 %collective-permute-done.2.refs_1_ = bf16[16,3200]{1,0:T(8,128)(2,1)S(1)} collective-permute-done((bf16[16,3200]{1,0:T(8,128)(2,1)}, bf16[16,3200]{1,0:T(8,128)(2,1)S(1)}, u32[]{:S(2)}, u32[]{:S(2)}) %collective-permute-start.2) | collective-permute-done | bytes 102432 | tf_op jit(solution)/shard_map/ppermute | solution.py:209
  13.0 1.7 %collective-permute-start.5 = (bf16[16,3200]{1,0:T(8,128)(2,1)}, bf16[16,3200]{1,0:T(8,128)(2,1)S(1)}, u32[]{:S(2)}, u32[]{:S(2)}) collective-permute-start(bf16[16,3200]{1,0:T(8,128)(2,1)} %get-tuple-element.21.rows_hbm), channel_id=1, source_target_pairs={{0,2},{1,3},{2,0},{3,1},{4,6},{5,7},{6,4},{7,5},{8,10},{9,11},{10,... | collective-permute-start | bytes 307208 | tf_op jit(solution)/shard_map/ppermute | solution.py:209
  14.7 1.0 %collective-permute-done.3.refs_2_ = bf16[16,3200]{1,0:T(8,128)(2,1)S(1)} collective-permute-done((bf16[16,3200]{1,0:T(8,128)(2,1)}, bf16[16,3200]{1,0:T(8,128)(2,1)S(1)}, u32[]{:S(2)}, u32[]{:S(2)}) %collective-permute-start.3) | collective-permute-done | bytes 102432 | tf_op jit(solution)/shard_map/ppermute | solution.py:209
  15.7 1.5 %collective-permute-start.6 = (bf16[16,3200]{1,0:T(8,128)(2,1)S(1)}, bf16[16,3200]{1,0:T(8,128)(2,1)S(1)}, u32[]{:S(2)}, u32[]{:S(2)}) collective-permute-start(bf16[16,3200]{1,0:T(8,128)(2,1)S(1)} %collective-permute-done.2.refs_1_), channel_id=1, source_target_pairs={{0,2},{1,3},{2,0},{3,1},{4,6},{5,7},{6,4},{7,5},{8,10},{9,11},{10,... | collective-permute-start | bytes 307208 | tf_op jit(solution)/shard_map/ppermute | solution.py:209
  17.2 1.0 %collective-permute-done.4.refs_3_ = bf16[16,3200]{1,0:T(8,128)(2,1)S(1)} collective-permute-done((bf16[16,3200]{1,0:T(8,128)(2,1)}, bf16[16,3200]{1,0:T(8,128)(2,1)S(1)}, u32[]{:S(2)}, u32[]{:S(2)}) %collective-permute-start.4) | collective-permute-done | bytes 102432 | tf_op jit(solution)/shard_map/ppermute | solution.py:209
  18.1 1.5 %collective-permute-start.7 = (bf16[16,3200]{1,0:T(8,128)(2,1)S(1)}, bf16[16,3200]{1,0:T(8,128)(2,1)S(1)}, u32[]{:S(2)}, u32[]{:S(2)}) collective-permute-start(bf16[16,3200]{1,0:T(8,128)(2,1)S(1)} %collective-permute-done.3.refs_2_), channel_id=1, source_target_pairs={{0,2},{1,3},{2,0},{3,1},{4,6},{5,7},{6,4},{7,5},{8,10},{9,11},{10,... | collective-permute-start | bytes 307208 | tf_op jit(solution)/shard_map/ppermute | solution.py:209
  19.6 0.0 collective-permute-done.pair_gate_ref
  19.6 0.5 %collective-permute-start.8 = (bf16[16,3200]{1,0:T(8,128)(2,1)S(1)}, bf16[16,3200]{1,0:T(8,128)(2,1)S(1)}, u32[]{:S(2)}, u32[]{:S(2)}) collective-permute-start(bf16[16,3200]{1,0:T(8,128)(2,1)S(1)} %collective-permute-done.4.refs_3_), channel_id=1, source_target_pairs={{0,2},{1,3},{2,0},{3,1},{4,6},{5,7},{6,4},{7,5},{8,10},{9,11},{10,... | collective-permute-start | bytes 307208 | tf_op jit(solution)/shard_map/ppermute | solution.py:209
  20.1 0.0 collective-permute-done.1.pair_up_ref
  20.1 0.0 copy-done
  20.2 0.0 copy-done.2
  20.2 0.0 copy-start.1
  20.2 0.9 %copy-done.1 = bf16[16,3200]{1,0:T(8,128)(2,1)S(1)} copy-done((bf16[16,3200]{1,0:T(8,128)(2,1)S(1)}, bf16[16,3200]{1,0:T(8,128)(2,1)}, u32[]{:S(2)}) %copy-start.1) | copy-done | bytes 102424
  21.1 1.5 %shard_map.101 = (bf16[192,4096]{1,0:T(8,128)(2,1)S(1)}, bf16[192,4096]{1,0:T(8,128)(2,1)S(1)}, bf16[16,3200]{1,0:T(8,128)(2,1)S(1)}, bf16[64,192]{1,0:T(8,128)(2,1)S(1)}, bf16[64,192]{1,0:T(8,128)(2,1)S(1)}) custom-call(bf16[64,768]{1,0:T(8,128)(2,1)S(1)} %bitcast.14, bf16[192,4096]{1,0:T(8,128)(2,1)S(1)} %bitcast.13, bf16[192,4096]{1,0:T(8,128)(2,1)} %bitcast.16, ...), custom_call_target="tpu_custom_call" | custom-call | bytes 6291456 | tf_op jit(solution)/shard_map/pallas_call | solution.py:263
  22.6 0.0 collective-permute-done.5.refs_4_
  22.6 0.0 collective-permute-done.6.refs_5_
  22.6 1.0 %collective-permute-done.7.refs_6_ = bf16[16,3200]{1,0:T(8,128)(2,1)S(1)} collective-permute-done((bf16[16,3200]{1,0:T(8,128)(2,1)S(1)}, bf16[16,3200]{1,0:T(8,128)(2,1)S(1)}, u32[]{:S(2)}, u32[]{:S(2)}) %collective-permute-start.7) | collective-permute-done | bytes 102432 | tf_op jit(solution)/shard_map/ppermute | solution.py:209
  23.6 1.1 %collective-permute-done.8.refs_7_ = bf16[16,3200]{1,0:T(8,128)(2,1)S(1)} collective-permute-done((bf16[16,3200]{1,0:T(8,128)(2,1)S(1)}, bf16[16,3200]{1,0:T(8,128)(2,1)S(1)}, u32[]{:S(2)}, u32[]{:S(2)}) %collective-permute-start.8) | collective-permute-done | bytes 102432 | tf_op jit(solution)/shard_map/ppermute | solution.py:209
  24.7 2.4 %shard_map.102 = (f32[64,64]{1,0:T(8,128)S(1)}, bf16[64,64]{1,0:T(8,128)(2,1)S(1)}, bf16[64,128]{1,0:T(8,128)(2,1)S(1)}) custom-call(bf16[192,4096]{1,0:T(8,128)(2,1)S(1)} %get-tuple-element.22.gate_ref, bf16[192,4096]{1,0:T(8,128)(2,1)S(1)} %get-tuple-element.23.up_ref, bf16[192,4096]{1,0:T(8,128)(2,1)S(1)} %collective-permute-done.pair_gate_ref, ...), custom_call_target="tpu_custom_call" | custom-call | flops 805306368 | bytes 7077888 | tf_op jit(solution)/shard_map/pallas_call | solution.py:287
  27.1 1.5 %collective-permute-start.9 = (bf16[64,64]{1,0:T(8,128)(2,1)S(1)}, bf16[64,64]{1,0:T(8,128)(2,1)S(1)}, u32[]{:S(2)}, u32[]{:S(2)}) collective-permute-start(bf16[64,64]{1,0:T(8,128)(2,1)S(1)} %get-tuple-element.34), channel_id=1, source_target_pairs={{0,2},{1,3},{2,0},{3,1},{4,6},{5,7},{6,4},{7,5},{8,10},{9,11},{10,... | collective-permute-start | bytes 24584 | tf_op jit(solution)/shard_map/ppermute | solution.py:209
  28.6 2.3 %collective-permute-done.9.refs_1_ = bf16[64,64]{1,0:T(8,128)(2,1)S(1)} collective-permute-done((bf16[64,64]{1,0:T(8,128)(2,1)S(1)}, bf16[64,64]{1,0:T(8,128)(2,1)S(1)}, u32[]{:S(2)}, u32[]{:S(2)}) %collective-permute-start.9) | collective-permute-done | bytes 8224 | tf_op jit(solution)/shard_map/ppermute | solution.py:209
  30.9 0.8 %shard_map.103 = f32[2,32,128]{2,1,0:T(8,128)} custom-call(bf16[64,128]{1,0:T(8,128)(2,1)S(1)} %get-tuple-element.32.grads_ref, f32[64,64]{1,0:T(8,128)S(1)} %get-tuple-element.33.refs_0_, bf16[64,64]{1,0:T(8,128)(2,1)S(1)} %collective-permute-done.9.refs_1_), custom_call_target="tpu_custom_call" | custom-call | flops 1048576 | bytes 32768 | tf_op jit(solution)/shard_map/pallas_call | solution.py:298
Async XLA Ops:
  0.0 20.2 %copy-start = (bf16[1,4096,192]{1,2,0:T(8,128)(2,1)S(1)}, bf16[1,4096,192]{1,2,0:T(8,128)(2,1)}, u32[]{:S(2)}) copy-start(bf16[1,4096,192]{1,2,0:T(8,128)(2,1)} %param.16) | copy-start | bytes 4718596
  0.0 20.2 %copy-start.2 = (bf16[768,64]{0,1:T(8,128)(2,1)S(1)}, bf16[768,64]{0,1:T(8,128)(2,1)}, u32[]{:S(2)}) copy-start(bf16[768,64]{0,1:T(8,128)(2,1)} %param.18) | copy-start | bytes 294916
  0.0 19.6 %collective-permute-start = (bf16[192,4096]{1,0:T(8,128)(2,1)}, bf16[192,4096]{1,0:T(8,128)(2,1)S(1)}, u32[]{:S(2)}, u32[]{:S(2)}) collective-permute-start(bf16[192,4096]{1,0:T(8,128)(2,1)} %bitcast.12), channel_id=1, source_target_pairs={{0,1},{1,0},{2,3},{3,2},{4,5},{5,4},{6,7},{7,6},{8,9},{9,8},{10,11... | collective-permute-start | bytes 4718600 | tf_op jit(solution)/shard_map/ppermute | solution.py:209
  0.5 19.7 %collective-permute-start.1 = (bf16[192,4096]{1,0:T(8,128)(2,1)}, bf16[192,4096]{1,0:T(8,128)(2,1)S(1)}, u32[]{:S(2)}, u32[]{:S(2)}) collective-permute-start(bf16[192,4096]{1,0:T(8,128)(2,1)} %bitcast.15), channel_id=1, source_target_pairs={{0,1},{1,0},{2,3},{3,2},{4,5},{5,4},{6,7},{7,6},{8,9},{9,8},{10,11... | collective-permute-start | bytes 4718600 | tf_op jit(solution)/shard_map/ppermute | solution.py:209
  4.0 9.0 %collective-permute-start.2 = (bf16[16,3200]{1,0:T(8,128)(2,1)}, bf16[16,3200]{1,0:T(8,128)(2,1)S(1)}, u32[]{:S(2)}, u32[]{:S(2)}) collective-permute-start(bf16[16,3200]{1,0:T(8,128)(2,1)} %get-tuple-element.29), channel_id=1, source_target_pairs={{0,12},{4,8},{8,4},{12,0},{1,13},{5,9},{9,5},{13,1},{2,14},{6,10},... | collective-permute-start | bytes 307208 | tf_op jit(solution)/shard_map/ppermute | solution.py:209
  9.1 6.6 %collective-permute-start.3 = (bf16[16,3200]{1,0:T(8,128)(2,1)}, bf16[16,3200]{1,0:T(8,128)(2,1)S(1)}, u32[]{:S(2)}, u32[]{:S(2)}) collective-permute-start(bf16[16,3200]{1,0:T(8,128)(2,1)} %get-tuple-element.30), channel_id=1, source_target_pairs={{0,4},{4,0},{8,12},{12,8},{1,5},{5,1},{9,13},{13,9},{2,6},{6,2},{1... | collective-permute-start | bytes 307208 | tf_op jit(solution)/shard_map/ppermute | solution.py:209
  9.1 9.1 %collective-permute-start.4 = (bf16[16,3200]{1,0:T(8,128)(2,1)}, bf16[16,3200]{1,0:T(8,128)(2,1)S(1)}, u32[]{:S(2)}, u32[]{:S(2)}) collective-permute-start(bf16[16,3200]{1,0:T(8,128)(2,1)} %get-tuple-element.31), channel_id=1, source_target_pairs={{0,8},{4,12},{8,0},{12,4},{1,9},{5,13},{9,1},{13,5},{2,10},{6,14},... | collective-permute-start | bytes 307208 | tf_op jit(solution)/shard_map/ppermute | solution.py:209
  13.0 9.6 %collective-permute-start.5 = (bf16[16,3200]{1,0:T(8,128)(2,1)}, bf16[16,3200]{1,0:T(8,128)(2,1)S(1)}, u32[]{:S(2)}, u32[]{:S(2)}) collective-permute-start(bf16[16,3200]{1,0:T(8,128)(2,1)} %get-tuple-element.21.rows_hbm), channel_id=1, source_target_pairs={{0,2},{1,3},{2,0},{3,1},{4,6},{5,7},{6,4},{7,5},{8,10},{9,11},{10,... | collective-permute-start | bytes 307208 | tf_op jit(solution)/shard_map/ppermute | solution.py:209
  15.7 6.9 %collective-permute-start.6 = (bf16[16,3200]{1,0:T(8,128)(2,1)S(1)}, bf16[16,3200]{1,0:T(8,128)(2,1)S(1)}, u32[]{:S(2)}, u32[]{:S(2)}) collective-permute-start(bf16[16,3200]{1,0:T(8,128)(2,1)S(1)} %collective-permute-done.2.refs_1_), channel_id=1, source_target_pairs={{0,2},{1,3},{2,0},{3,1},{4,6},{5,7},{6,4},{7,5},{8,10},{9,11},{10,... | collective-permute-start | bytes 307208 | tf_op jit(solution)/shard_map/ppermute | solution.py:209
  18.1 5.5 %collective-permute-start.7 = (bf16[16,3200]{1,0:T(8,128)(2,1)S(1)}, bf16[16,3200]{1,0:T(8,128)(2,1)S(1)}, u32[]{:S(2)}, u32[]{:S(2)}) collective-permute-start(bf16[16,3200]{1,0:T(8,128)(2,1)S(1)} %collective-permute-done.3.refs_2_), channel_id=1, source_target_pairs={{0,2},{1,3},{2,0},{3,1},{4,6},{5,7},{6,4},{7,5},{8,10},{9,11},{10,... | collective-permute-start | bytes 307208 | tf_op jit(solution)/shard_map/ppermute | solution.py:209
  19.6 5.1 %collective-permute-start.8 = (bf16[16,3200]{1,0:T(8,128)(2,1)S(1)}, bf16[16,3200]{1,0:T(8,128)(2,1)S(1)}, u32[]{:S(2)}, u32[]{:S(2)}) collective-permute-start(bf16[16,3200]{1,0:T(8,128)(2,1)S(1)} %collective-permute-done.4.refs_3_), channel_id=1, source_target_pairs={{0,2},{1,3},{2,0},{3,1},{4,6},{5,7},{6,4},{7,5},{8,10},{9,11},{10,... | collective-permute-start | bytes 307208 | tf_op jit(solution)/shard_map/ppermute | solution.py:209
  20.2 0.9 %copy-start.1 = (bf16[16,3200]{1,0:T(8,128)(2,1)S(1)}, bf16[16,3200]{1,0:T(8,128)(2,1)}, u32[]{:S(2)}) copy-start(bf16[16,3200]{1,0:T(8,128)(2,1)} %get-tuple-element.21.rows_hbm) | copy-start | bytes 307204
  27.1 3.8 %collective-permute-start.9 = (bf16[64,64]{1,0:T(8,128)(2,1)S(1)}, bf16[64,64]{1,0:T(8,128)(2,1)S(1)}, u32[]{:S(2)}, u32[]{:S(2)}) collective-permute-start(bf16[64,64]{1,0:T(8,128)(2,1)S(1)} %get-tuple-element.34), channel_id=1, source_target_pairs={{0,2},{1,3},{2,0},{3,1},{4,6},{5,7},{6,4},{7,5},{8,10},{9,11},{10,... | collective-permute-start | bytes 24584 | tf_op jit(solution)/shard_map/ppermute | solution.py:209

commit v12 on v10

--- a/solution.py
+++ b/solution.py
@@ -268,7 +268,7 @@
         output_derivatives,
         outgrad_compressor.T,
     )
-    hops = [0, n_exp - 1] + list(range(1, n_exp - 1))
+    hops = [0, 1] + list(range(n_exp - 1, 1, -1))
     spaces = [pltpu.SMEM] + [pltpu.VMEM] * (len(arguments) - 1)
     *rows, weights = call(
         functools.partial(send_kernel, hops),

time: 31.2 us -> 32.4 us (1.038)
  waiting for transfers between devices: 6.62 us -> 8.41 us
  starting transfers between devices: 13.6 us -> 13 us
    ppermute x9, waiting for transfers between devices: 6.62 us -> 8.41 us  [swap(): return lax.ppermute(a, axis, [(i, i ^ q) for i in range(n)])]
    ppermute x9, starting transfers between devices: 13.6 us -> 13 us  [swap(): return lax.ppermute(a, axis, [(i, i ^ q) for i in range(n)])]
  transfers between devices with their start and end apart: 9 -> 9, of which waited for: 5 -> 4; matrix products, arithmetic and copies ran while one was open for 0% -> 0% of each run, Pallas kernels for 6% -> 6%
where the time goes in v12:
time: 32.4 us; the launch traced here: 32.2 us
  starting transfers between devices  13 us (40%)
  Pallas kernels  9.85 us (30%)
  waiting for transfers between devices  8.41 us (26%)
  local copies, waits for them, and re-layouts  0.9 us (3%)
    ppermute x9, starting transfers between devices, swap(): return lax.ppermute(a, axis, [(i, i ^ q) for i in range(n)])  13 us
    ppermute x9, waiting for transfers between devices, swap(): return lax.ppermute(a, axis, [(i, i ^ q) for i in range(n)])  8.41 us
    pallas_call x1, Pallas kernels, body(): call(functools.partial(send_kernel, hops), [shape((ROWS, packed + EX_DEV...  4.67 us
    pallas_call x1, Pallas kernels, body(): call(functools.partial(sketch_kernel, [size] * len(ds)), [shape((rank, si...  2.47 us
    pallas_call x1, Pallas kernels, body(): call(keep_kernel, [shape(weights.shape, BF16), shape(rows[0].shape, BF16)...  1.89 us
    unnamed x4, local copies, waits for them, and re-layouts  0.9 us
    pallas_call x1, Pallas kernels, body(): call(outer_kernel, shape((EX_DEV, rank * rank // 128, 128), F32), [VMEM]...  0.81 us
  transfers between devices with their start and end apart: 9, of which 4 were waited for; matrix products, arithmetic and copies ran while one was open for 0% of the time, Pallas kernels for 6%

profile of v12, /device:TPU:0, one launch (start us, length us, event | category | flops | bytes accessed | tf_op | source)
XLA Modules:
  0.0 32.2 jit_solution(15716738622448208943)
XLA Ops:
  0.0 0.0 copy-start.1
  0.0 4.7 %shard_map.100 = (bf16[16,3200]{1,0:T(8,128)(2,1)}, bf16[16,3200]{1,0:T(8,128)(2,1)}, bf16[16,3200]{1,0:T(8,128)(2,1)}, bf16[16,3200]{1,0:T(8,128)(2,1)}, bf16[384,4096]{1,0:T(8,128)(2,1)}) custom-call(s32[128]{0:T(128)} %refs_0_.1, s32[8,128]{1,0:T(8,128)} %bitcast.16, f32[8,128]{1,0:T(8,128)} %bitcast.17, s32[1,128]{1,0:T(1,128)} %bitcast.18, ...), custom_call_target="tpu_custom_call" | custom-call | flops 167772160 | bytes 8912896 | tf_op jit(solution)/shard_map/pallas_call | solution.py:273
  4.7 0.5 %collective-permute-start = (bf16[384,4096]{1,0:T(8,128)(2,1)}, bf16[384,4096]{1,0:T(8,128)(2,1)S(1)}, u32[]{:S(2)}, u32[]{:S(2)}) collective-permute-start(bf16[384,4096]{1,0:T(8,128)(2,1)} %get-tuple-element.17.weights_hbm), channel_id=1, source_target_pairs={{0,1},{1,0},{2,3},{3,2},{4,5},{5,4},{6,7},{7,6},{8,9},{9,8},{10,11... | collective-permute-start | bytes 9437192 | tf_op jit(solution)/shard_map/ppermute | solution.py:237
  5.2 2.6 %collective-permute-start.1 = (bf16[16,3200]{1,0:T(8,128)(2,1)}, bf16[16,3200]{1,0:T(8,128)(2,1)S(1)}, u32[]{:S(2)}, u32[]{:S(2)}) collective-permute-start(bf16[16,3200]{1,0:T(8,128)(2,1)} %get-tuple-element.23), channel_id=1, source_target_pairs={{0,4},{4,0},{8,12},{12,8},{1,5},{5,1},{9,13},{13,9},{2,6},{6,2},{1... | collective-permute-start | bytes 307208 | tf_op jit(solution)/shard_map/ppermute | solution.py:237
  7.8 2.5 %collective-permute-start.2 = (bf16[16,3200]{1,0:T(8,128)(2,1)}, bf16[16,3200]{1,0:T(8,128)(2,1)S(1)}, u32[]{:S(2)}, u32[]{:S(2)}) collective-permute-start(bf16[16,3200]{1,0:T(8,128)(2,1)} %get-tuple-element.24), channel_id=1, source_target_pairs={{0,12},{4,8},{8,4},{12,0},{1,13},{5,9},{9,5},{13,1},{2,14},{6,10},... | collective-permute-start | bytes 307208 | tf_op jit(solution)/shard_map/ppermute | solution.py:237
  10.3 0.1 collective-permute-start.3
  10.4 1.5 %collective-permute-start.4 = (bf16[16,3200]{1,0:T(8,128)(2,1)}, bf16[16,3200]{1,0:T(8,128)(2,1)S(1)}, u32[]{:S(2)}, u32[]{:S(2)}) collective-permute-start(bf16[16,3200]{1,0:T(8,128)(2,1)} %get-tuple-element.18.rows_hbm), channel_id=1, source_target_pairs={{0,2},{1,3},{2,0},{3,1},{4,6},{5,7},{6,4},{7,5},{8,10},{9,11},{10,... | collective-permute-start | bytes 307208 | tf_op jit(solution)/shard_map/ppermute | solution.py:237
  11.9 0.0 collective-permute-done.1.refs_1_
  11.9 1.3 %collective-permute-start.5 = (bf16[16,3200]{1,0:T(8,128)(2,1)S(1)}, bf16[16,3200]{1,0:T(8,128)(2,1)S(1)}, u32[]{:S(2)}, u32[]{:S(2)}) collective-permute-start(bf16[16,3200]{1,0:T(8,128)(2,1)S(1)} %collective-permute-done.1.refs_1_), channel_id=1, source_target_pairs={{0,2},{1,3},{2,0},{3,1},{4,6},{5,7},{6,4},{7,5},{8,10},{9,11},{10,... | collective-permute-start | bytes 307208 | tf_op jit(solution)/shard_map/ppermute | solution.py:237
  13.2 3.3 %collective-permute-done.2.refs_2_ = bf16[16,3200]{1,0:T(8,128)(2,1)S(1)} collective-permute-done((bf16[16,3200]{1,0:T(8,128)(2,1)}, bf16[16,3200]{1,0:T(8,128)(2,1)S(1)}, u32[]{:S(2)}, u32[]{:S(2)}) %collective-permute-start.2) | collective-permute-done | bytes 102432 | tf_op jit(solution)/shard_map/ppermute | solution.py:237
  16.5 1.5 %collective-permute-start.6 = (bf16[16,3200]{1,0:T(8,128)(2,1)S(1)}, bf16[16,3200]{1,0:T(8,128)(2,1)S(1)}, u32[]{:S(2)}, u32[]{:S(2)}) collective-permute-start(bf16[16,3200]{1,0:T(8,128)(2,1)S(1)} %collective-permute-done.2.refs_2_), channel_id=1, source_target_pairs={{0,2},{1,3},{2,0},{3,1},{4,6},{5,7},{6,4},{7,5},{8,10},{9,11},{10,... | collective-permute-start | bytes 307208 | tf_op jit(solution)/shard_map/ppermute | solution.py:237
  18.0 2.5 %collective-permute-done.3.refs_3_ = bf16[16,3200]{1,0:T(8,128)(2,1)S(1)} collective-permute-done((bf16[16,3200]{1,0:T(8,128)(2,1)}, bf16[16,3200]{1,0:T(8,128)(2,1)S(1)}, u32[]{:S(2)}, u32[]{:S(2)}) %collective-permute-start.3) | collective-permute-done | bytes 102432 | tf_op jit(solution)/shard_map/ppermute | solution.py:237
  20.4 1.5 %collective-permute-start.7 = (bf16[16,3200]{1,0:T(8,128)(2,1)S(1)}, bf16[16,3200]{1,0:T(8,128)(2,1)S(1)}, u32[]{:S(2)}, u32[]{:S(2)}) collective-permute-start(bf16[16,3200]{1,0:T(8,128)(2,1)S(1)} %collective-permute-done.3.refs_3_), channel_id=1, source_target_pairs={{0,2},{1,3},{2,0},{3,1},{4,6},{5,7},{6,4},{7,5},{8,10},{9,11},{10,... | collective-permute-start | bytes 307208 | tf_op jit(solution)/shard_map/ppermute | solution.py:237
  21.9 0.0 copy-done.1
  21.9 0.0 copy-start
  21.9 0.9 %copy-done = bf16[16,3200]{1,0:T(8,128)(2,1)S(1)} copy-done((bf16[16,3200]{1,0:T(8,128)(2,1)S(1)}, bf16[16,3200]{1,0:T(8,128)(2,1)}, u32[]{:S(2)}) %copy-start) | copy-done | bytes 102424
  22.8 1.9 %shard_map.101 = (bf16[384,4096]{1,0:T(8,128)(2,1)S(1)}, bf16[16,3200]{1,0:T(8,128)(2,1)S(1)}, bf16[64,192]{1,0:T(8,128)(2,1)S(1)}, bf16[64,192]{1,0:T(8,128)(2,1)S(1)}) custom-call(bf16[64,768]{1,0:T(8,128)(2,1)S(1)} %bitcast.12, bf16[384,4096]{1,0:T(8,128)(2,1)} %get-tuple-element.17.weights_hbm, bf16[16,3200]{1,0:T(8,128)(2,1)S(1)} %copy-done), custom_call_target="tpu_custom_call" | custom-call | bytes 6291456 | tf_op jit(solution)/shard_map/pallas_call | solution.py:289
  24.7 0.0 collective-permute-done.4.refs_4_
  24.7 0.0 collective-permute-done.5.refs_5_
  24.7 0.0 collective-permute-done.6.refs_6_
  24.8 0.4 %collective-permute-done.7.refs_7_ = bf16[16,3200]{1,0:T(8,128)(2,1)S(1)} collective-permute-done((bf16[16,3200]{1,0:T(8,128)(2,1)S(1)}, bf16[16,3200]{1,0:T(8,128)(2,1)S(1)}, u32[]{:S(2)}, u32[]{:S(2)}) %collective-permute-start.7) | collective-permute-done | bytes 102432 | tf_op jit(solution)/shard_map/ppermute | solution.py:237
  25.2 0.0 collective-permute-done.pair_ref
  25.2 2.5 %shard_map.102 = (f32[64,64]{1,0:T(8,128)S(1)}, bf16[64,64]{1,0:T(8,128)(2,1)S(1)}, bf16[64,128]{1,0:T(8,128)(2,1)S(1)}) custom-call(bf16[384,4096]{1,0:T(8,128)(2,1)S(1)} %get-tuple-element.19.own_ref, bf16[384,4096]{1,0:T(8,128)(2,1)S(1)} %collective-permute-done.pair_ref, bf16[64,192]{1,0:T(8,128)(2,1)S(1)} %get-tuple-element.20.first_ref, ...), custom_call_target="tpu_custom_call" | custom-call | flops 805306368 | bytes 7077888 | tf_op jit(solution)/shard_map/pallas_call | solution.py:313
  27.6 1.5 %collective-permute-start.8 = (bf16[64,64]{1,0:T(8,128)(2,1)S(1)}, bf16[64,64]{1,0:T(8,128)(2,1)S(1)}, u32[]{:S(2)}, u32[]{:S(2)}) collective-permute-start(bf16[64,64]{1,0:T(8,128)(2,1)S(1)} %get-tuple-element.28), channel_id=1, source_target_pairs={{0,2},{1,3},{2,0},{3,1},{4,6},{5,7},{6,4},{7,5},{8,10},{9,11},{10,... | collective-permute-start | bytes 24584 | tf_op jit(solution)/shard_map/ppermute | solution.py:237
  29.1 2.3 %collective-permute-done.8.refs_1_ = bf16[64,64]{1,0:T(8,128)(2,1)S(1)} collective-permute-done((bf16[64,64]{1,0:T(8,128)(2,1)S(1)}, bf16[64,64]{1,0:T(8,128)(2,1)S(1)}, u32[]{:S(2)}, u32[]{:S(2)}) %collective-permute-start.8) | collective-permute-done | bytes 8224 | tf_op jit(solution)/shard_map/ppermute | solution.py:237
  31.4 0.8 %shard_map.103 = f32[2,32,128]{2,1,0:T(8,128)} custom-call(bf16[64,128]{1,0:T(8,128)(2,1)S(1)} %get-tuple-element.26.grads_ref, f32[64,64]{1,0:T(8,128)S(1)} %get-tuple-element.27.refs_0_, bf16[64,64]{1,0:T(8,128)(2,1)S(1)} %collective-permute-done.8.refs_1_), custom_call_target="tpu_custom_call" | custom-call | flops 1048576 | bytes 32768 | tf_op jit(solution)/shard_map/pallas_call | solution.py:324
Async XLA Ops:
  0.0 21.9 %copy-start.1 = (bf16[768,64]{0,1:T(8,128)(2,1)S(1)}, bf16[768,64]{0,1:T(8,128)(2,1)}, u32[]{:S(2)}) copy-start(bf16[768,64]{0,1:T(8,128)(2,1)} %param.18) | copy-start | bytes 294916
  4.7 20.5 %collective-permute-start = (bf16[384,4096]{1,0:T(8,128)(2,1)}, bf16[384,4096]{1,0:T(8,128)(2,1)S(1)}, u32[]{:S(2)}, u32[]{:S(2)}) collective-permute-start(bf16[384,4096]{1,0:T(8,128)(2,1)} %get-tuple-element.17.weights_hbm), channel_id=1, source_target_pairs={{0,1},{1,0},{2,3},{3,2},{4,5},{5,4},{6,7},{7,6},{8,9},{9,8},{10,11... | collective-permute-start | bytes 9437192 | tf_op jit(solution)/shard_map/ppermute | solution.py:237
  5.2 6.7 %collective-permute-start.1 = (bf16[16,3200]{1,0:T(8,128)(2,1)}, bf16[16,3200]{1,0:T(8,128)(2,1)S(1)}, u32[]{:S(2)}, u32[]{:S(2)}) collective-permute-start(bf16[16,3200]{1,0:T(8,128)(2,1)} %get-tuple-element.23), channel_id=1, source_target_pairs={{0,4},{4,0},{8,12},{12,8},{1,5},{5,1},{9,13},{13,9},{2,6},{6,2},{1... | collective-permute-start | bytes 307208 | tf_op jit(solution)/shard_map/ppermute | solution.py:237
  7.8 8.6 %collective-permute-start.2 = (bf16[16,3200]{1,0:T(8,128)(2,1)}, bf16[16,3200]{1,0:T(8,128)(2,1)S(1)}, u32[]{:S(2)}, u32[]{:S(2)}) collective-permute-start(bf16[16,3200]{1,0:T(8,128)(2,1)} %get-tuple-element.24), channel_id=1, source_target_pairs={{0,12},{4,8},{8,4},{12,0},{1,13},{5,9},{9,5},{13,1},{2,14},{6,10},... | collective-permute-start | bytes 307208 | tf_op jit(solution)/shard_map/ppermute | solution.py:237
  10.3 10.1 %collective-permute-start.3 = (bf16[16,3200]{1,0:T(8,128)(2,1)}, bf16[16,3200]{1,0:T(8,128)(2,1)S(1)}, u32[]{:S(2)}, u32[]{:S(2)}) collective-permute-start(bf16[16,3200]{1,0:T(8,128)(2,1)} %get-tuple-element.25), channel_id=1, source_target_pairs={{0,8},{4,12},{8,0},{12,4},{1,9},{5,13},{9,1},{13,5},{2,10},{6,14},... | collective-permute-start | bytes 307208 | tf_op jit(solution)/shard_map/ppermute | solution.py:237
  10.4 14.3 %collective-permute-start.4 = (bf16[16,3200]{1,0:T(8,128)(2,1)}, bf16[16,3200]{1,0:T(8,128)(2,1)S(1)}, u32[]{:S(2)}, u32[]{:S(2)}) collective-permute-start(bf16[16,3200]{1,0:T(8,128)(2,1)} %get-tuple-element.18.rows_hbm), channel_id=1, source_target_pairs={{0,2},{1,3},{2,0},{3,1},{4,6},{5,7},{6,4},{7,5},{8,10},{9,11},{10,... | collective-permute-start | bytes 307208 | tf_op jit(solution)/shard_map/ppermute | solution.py:237
  11.9 12.8 %collective-permute-start.5 = (bf16[16,3200]{1,0:T(8,128)(2,1)S(1)}, bf16[16,3200]{1,0:T(8,128)(2,1)S(1)}, u32[]{:S(2)}, u32[]{:S(2)}) collective-permute-start(bf16[16,3200]{1,0:T(8,128)(2,1)S(1)} %collective-permute-done.1.refs_1_), channel_id=1, source_target_pairs={{0,2},{1,3},{2,0},{3,1},{4,6},{5,7},{6,4},{7,5},{8,10},{9,11},{10,... | collective-permute-start | bytes 307208 | tf_op jit(solution)/shard_map/ppermute | solution.py:237
  16.5 8.3 %collective-permute-start.6 = (bf16[16,3200]{1,0:T(8,128)(2,1)S(1)}, bf16[16,3200]{1,0:T(8,128)(2,1)S(1)}, u32[]{:S(2)}, u32[]{:S(2)}) collective-permute-start(bf16[16,3200]{1,0:T(8,128)(2,1)S(1)} %collective-permute-done.2.refs_2_), channel_id=1, source_target_pairs={{0,2},{1,3},{2,0},{3,1},{4,6},{5,7},{6,4},{7,5},{8,10},{9,11},{10,... | collective-permute-start | bytes 307208 | tf_op jit(solution)/shard_map/ppermute | solution.py:237
  20.4 4.7 %collective-permute-start.7 = (bf16[16,3200]{1,0:T(8,128)(2,1)S(1)}, bf16[16,3200]{1,0:T(8,128)(2,1)S(1)}, u32[]{:S(2)}, u32[]{:S(2)}) collective-permute-start(bf16[16,3200]{1,0:T(8,128)(2,1)S(1)} %collective-permute-done.3.refs_3_), channel_id=1, source_target_pairs={{0,2},{1,3},{2,0},{3,1},{4,6},{5,7},{6,4},{7,5},{8,10},{9,11},{10,... | collective-permute-start | bytes 307208 | tf_op jit(solution)/shard_map/ppermute | solution.py:237
  21.9 0.9 %copy-start = (bf16[16,3200]{1,0:T(8,128)(2,1)S(1)}, bf16[16,3200]{1,0:T(8,128)(2,1)}, u32[]{:S(2)}) copy-start(bf16[16,3200]{1,0:T(8,128)(2,1)} %get-tuple-element.18.rows_hbm) | copy-start | bytes 307204
  27.6 3.8 %collective-permute-start.8 = (bf16[64,64]{1,0:T(8,128)(2,1)S(1)}, bf16[64,64]{1,0:T(8,128)(2,1)S(1)}, u32[]{:S(2)}, u32[]{:S(2)}) collective-permute-start(bf16[64,64]{1,0:T(8,128)(2,1)S(1)} %get-tuple-element.28), channel_id=1, source_target_pairs={{0,2},{1,3},{2,0},{3,1},{4,6},{5,7},{6,4},{7,5},{8,10},{9,11},{10,... | collective-permute-start | bytes 24584 | tf_op jit(solution)/shard_map/ppermute | solution.py:237

commit v13 on v12

--- a/solution.py
+++ b/solution.py
@@ -268,7 +268,7 @@
         output_derivatives,
         outgrad_compressor.T,
     )
-    hops = [0, 1] + list(range(n_exp - 1, 1, -1))
+    hops = [0] + list(range(n_exp - 1, 0, -1))
     spaces = [pltpu.SMEM] + [pltpu.VMEM] * (len(arguments) - 1)
     *rows, weights = call(
         functools.partial(send_kernel, hops),

time: 32.4 us -> 33.3 us (1.028)
  waiting for transfers between devices: 8.41 us -> 9.82 us
  starting transfers between devices: 13 us -> 12.5 us
    ppermute x9, waiting for transfers between devices: 8.41 us -> 9.82 us  [swap(): return lax.ppermute(a, axis, [(i, i ^ q) for i in range(n)])]
    ppermute x9, starting transfers between devices: 13 us -> 12.5 us  [swap(): return lax.ppermute(a, axis, [(i, i ^ q) for i in range(n)])]
  transfers between devices with their start and end apart: 9 -> 9, of which waited for: 4 -> 5; matrix products, arithmetic and copies ran while one was open for 0% -> 0% of each run, Pallas kernels for 6% -> 6%
where the time goes in v13:
time: 33.3 us; the launch traced here: 33.1 us
  starting transfers between devices  12.5 us (38%)
  Pallas kernels  9.84 us (30%)
  waiting for transfers between devices  9.82 us (29%)
  local copies, waits for them, and re-layouts  0.9 us (3%)
    ppermute x9, starting transfers between devices, swap(): return lax.ppermute(a, axis, [(i, i ^ q) for i in range(n)])  12.5 us
    ppermute x9, waiting for transfers between devices, swap(): return lax.ppermute(a, axis, [(i, i ^ q) for i in range(n)])  9.82 us
    pallas_call x1, Pallas kernels, body(): call(functools.partial(send_kernel, hops), [shape((ROWS, packed + EX_DEV...  4.67 us
    pallas_call x1, Pallas kernels, body(): call(functools.partial(sketch_kernel, [size] * len(ds)), [shape((rank, si...  2.47 us
    pallas_call x1, Pallas kernels, body(): call(keep_kernel, [shape(weights.shape, BF16), shape(rows[0].shape, BF16)...  1.89 us
    unnamed x4, local copies, waits for them, and re-layouts  0.9 us
    pallas_call x1, Pallas kernels, body(): call(outer_kernel, shape((EX_DEV, rank * rank // 128, 128), F32), [VMEM]...  0.81 us
  transfers between devices with their start and end apart: 9, of which 5 were waited for; matrix products, arithmetic and copies ran while one was open for 0% of the time, Pallas kernels for 6%

profile of v13, /device:TPU:0, one launch (start us, length us, event | category | flops | bytes accessed | tf_op | source)
XLA Modules:
  0.0 33.1 jit_solution(3160122776246212387)
XLA Ops:
  0.0 0.0 copy-start.1
  0.0 4.7 %shard_map.100 = (bf16[16,3200]{1,0:T(8,128)(2,1)}, bf16[16,3200]{1,0:T(8,128)(2,1)}, bf16[16,3200]{1,0:T(8,128)(2,1)}, bf16[16,3200]{1,0:T(8,128)(2,1)}, bf16[384,4096]{1,0:T(8,128)(2,1)}) custom-call(s32[128]{0:T(128)} %refs_0_.1, s32[8,128]{1,0:T(8,128)} %bitcast.16, f32[8,128]{1,0:T(8,128)} %bitcast.17, s32[1,128]{1,0:T(1,128)} %bitcast.18, ...), custom_call_target="tpu_custom_call" | custom-call | flops 167772160 | bytes 8912896 | tf_op jit(solution)/shard_map/pallas_call | solution.py:273
  4.7 0.5 %collective-permute-start = (bf16[384,4096]{1,0:T(8,128)(2,1)}, bf16[384,4096]{1,0:T(8,128)(2,1)S(1)}, u32[]{:S(2)}, u32[]{:S(2)}) collective-permute-start(bf16[384,4096]{1,0:T(8,128)(2,1)} %get-tuple-element.17.weights_hbm), channel_id=1, source_target_pairs={{0,1},{1,0},{2,3},{3,2},{4,5},{5,4},{6,7},{7,6},{8,9},{9,8},{10,11... | collective-permute-start | bytes 9437192 | tf_op jit(solution)/shard_map/ppermute | solution.py:237
  5.2 4.7 %collective-permute-start.1 = (bf16[16,3200]{1,0:T(8,128)(2,1)}, bf16[16,3200]{1,0:T(8,128)(2,1)S(1)}, u32[]{:S(2)}, u32[]{:S(2)}) collective-permute-start(bf16[16,3200]{1,0:T(8,128)(2,1)} %get-tuple-element.23), channel_id=1, source_target_pairs={{0,12},{4,8},{8,4},{12,0},{1,13},{5,9},{9,5},{13,1},{2,14},{6,10},... | collective-permute-start | bytes 307208 | tf_op jit(solution)/shard_map/ppermute | solution.py:237
  9.9 0.0 collective-permute-start.2
  9.9 0.7 %collective-permute-start.3 = (bf16[16,3200]{1,0:T(8,128)(2,1)}, bf16[16,3200]{1,0:T(8,128)(2,1)S(1)}, u32[]{:S(2)}, u32[]{:S(2)}) collective-permute-start(bf16[16,3200]{1,0:T(8,128)(2,1)} %get-tuple-element.25), channel_id=1, source_target_pairs={{0,4},{4,0},{8,12},{12,8},{1,5},{5,1},{9,13},{13,9},{2,6},{6,2},{1... | collective-permute-start | bytes 307208 | tf_op jit(solution)/shard_map/ppermute | solution.py:237
  10.5 1.6 %collective-permute-start.4 = (bf16[16,3200]{1,0:T(8,128)(2,1)}, bf16[16,3200]{1,0:T(8,128)(2,1)S(1)}, u32[]{:S(2)}, u32[]{:S(2)}) collective-permute-start(bf16[16,3200]{1,0:T(8,128)(2,1)} %get-tuple-element.18.rows_hbm), channel_id=1, source_target_pairs={{0,2},{1,3},{2,0},{3,1},{4,6},{5,7},{6,4},{7,5},{8,10},{9,11},{10,... | collective-permute-start | bytes 307208 | tf_op jit(solution)/shard_map/ppermute | solution.py:237
  12.2 1.8 %collective-permute-done.1.refs_1_ = bf16[16,3200]{1,0:T(8,128)(2,1)S(1)} collective-permute-done((bf16[16,3200]{1,0:T(8,128)(2,1)}, bf16[16,3200]{1,0:T(8,128)(2,1)S(1)}, u32[]{:S(2)}, u32[]{:S(2)}) %collective-permute-start.1) | collective-permute-done | bytes 102432 | tf_op jit(solution)/shard_map/ppermute | solution.py:237
  13.9 1.6 %collective-permute-start.5 = (bf16[16,3200]{1,0:T(8,128)(2,1)S(1)}, bf16[16,3200]{1,0:T(8,128)(2,1)S(1)}, u32[]{:S(2)}, u32[]{:S(2)}) collective-permute-start(bf16[16,3200]{1,0:T(8,128)(2,1)S(1)} %collective-permute-done.1.refs_1_), channel_id=1, source_target_pairs={{0,2},{1,3},{2,0},{3,1},{4,6},{5,7},{6,4},{7,5},{8,10},{9,11},{10,... | collective-permute-start | bytes 307208 | tf_op jit(solution)/shard_map/ppermute | solution.py:237
  15.6 3.8 %collective-permute-done.2.refs_2_ = bf16[16,3200]{1,0:T(8,128)(2,1)S(1)} collective-permute-done((bf16[16,3200]{1,0:T(8,128)(2,1)}, bf16[16,3200]{1,0:T(8,128)(2,1)S(1)}, u32[]{:S(2)}, u32[]{:S(2)}) %collective-permute-start.2) | collective-permute-done | bytes 102432 | tf_op jit(solution)/shard_map/ppermute | solution.py:237
  19.3 1.5 %collective-permute-start.6 = (bf16[16,3200]{1,0:T(8,128)(2,1)S(1)}, bf16[16,3200]{1,0:T(8,128)(2,1)S(1)}, u32[]{:S(2)}, u32[]{:S(2)}) collective-permute-start(bf16[16,3200]{1,0:T(8,128)(2,1)S(1)} %collective-permute-done.2.refs_2_), channel_id=1, source_target_pairs={{0,2},{1,3},{2,0},{3,1},{4,6},{5,7},{6,4},{7,5},{8,10},{9,11},{10,... | collective-permute-start | bytes 307208 | tf_op jit(solution)/shard_map/ppermute | solution.py:237
  20.8 0.0 collective-permute-done.3.refs_3_
  20.8 0.5 %collective-permute-start.7 = (bf16[16,3200]{1,0:T(8,128)(2,1)S(1)}, bf16[16,3200]{1,0:T(8,128)(2,1)S(1)}, u32[]{:S(2)}, u32[]{:S(2)}) collective-permute-start(bf16[16,3200]{1,0:T(8,128)(2,1)S(1)} %collective-permute-done.3.refs_3_), channel_id=1, source_target_pairs={{0,2},{1,3},{2,0},{3,1},{4,6},{5,7},{6,4},{7,5},{8,10},{9,11},{10,... | collective-permute-start | bytes 307208 | tf_op jit(solution)/shard_map/ppermute | solution.py:237
  21.3 0.0 copy-done.1
  21.3 0.0 copy-start
  21.3 0.9 %copy-done = bf16[16,3200]{1,0:T(8,128)(2,1)S(1)} copy-done((bf16[16,3200]{1,0:T(8,128)(2,1)S(1)}, bf16[16,3200]{1,0:T(8,128)(2,1)}, u32[]{:S(2)}) %copy-start) | copy-done | bytes 102424
  22.2 1.9 %shard_map.101 = (bf16[384,4096]{1,0:T(8,128)(2,1)S(1)}, bf16[16,3200]{1,0:T(8,128)(2,1)S(1)}, bf16[64,192]{1,0:T(8,128)(2,1)S(1)}, bf16[64,192]{1,0:T(8,128)(2,1)S(1)}) custom-call(bf16[64,768]{1,0:T(8,128)(2,1)S(1)} %bitcast.12, bf16[384,4096]{1,0:T(8,128)(2,1)} %get-tuple-element.17.weights_hbm, bf16[16,3200]{1,0:T(8,128)(2,1)S(1)} %copy-done), custom_call_target="tpu_custom_call" | custom-call | bytes 6291456 | tf_op jit(solution)/shard_map/pallas_call | solution.py:289
  24.1 0.0 collective-permute-done.4.refs_4_
  24.1 0.0 collective-permute-done.5.refs_5_
  24.2 0.8 %collective-permute-done.6.refs_6_ = bf16[16,3200]{1,0:T(8,128)(2,1)S(1)} collective-permute-done((bf16[16,3200]{1,0:T(8,128)(2,1)S(1)}, bf16[16,3200]{1,0:T(8,128)(2,1)S(1)}, u32[]{:S(2)}, u32[]{:S(2)}) %collective-permute-start.6) | collective-permute-done | bytes 102432 | tf_op jit(solution)/shard_map/ppermute | solution.py:237
  25.0 1.1 %collective-permute-done.7.refs_7_ = bf16[16,3200]{1,0:T(8,128)(2,1)S(1)} collective-permute-done((bf16[16,3200]{1,0:T(8,128)(2,1)S(1)}, bf16[16,3200]{1,0:T(8,128)(2,1)S(1)}, u32[]{:S(2)}, u32[]{:S(2)}) %collective-permute-start.7) | collective-permute-done | bytes 102432 | tf_op jit(solution)/shard_map/ppermute | solution.py:237
  26.1 0.0 collective-permute-done.pair_ref
  26.1 2.5 %shard_map.102 = (f32[64,64]{1,0:T(8,128)S(1)}, bf16[64,64]{1,0:T(8,128)(2,1)S(1)}, bf16[64,128]{1,0:T(8,128)(2,1)S(1)}) custom-call(bf16[384,4096]{1,0:T(8,128)(2,1)S(1)} %get-tuple-element.19.own_ref, bf16[384,4096]{1,0:T(8,128)(2,1)S(1)} %collective-permute-done.pair_ref, bf16[64,192]{1,0:T(8,128)(2,1)S(1)} %get-tuple-element.20.first_ref, ...), custom_call_target="tpu_custom_call" | custom-call | flops 805306368 | bytes 7077888 | tf_op jit(solution)/shard_map/pallas_call | solution.py:313
  28.5 1.4 %collective-permute-start.8 = (bf16[64,64]{1,0:T(8,128)(2,1)S(1)}, bf16[64,64]{1,0:T(8,128)(2,1)S(1)}, u32[]{:S(2)}, u32[]{:S(2)}) collective-permute-start(bf16[64,64]{1,0:T(8,128)(2,1)S(1)} %get-tuple-element.28), channel_id=1, source_target_pairs={{0,2},{1,3},{2,0},{3,1},{4,6},{5,7},{6,4},{7,5},{8,10},{9,11},{10,... | collective-permute-start | bytes 24584 | tf_op jit(solution)/shard_map/ppermute | solution.py:237
  30.0 2.4 %collective-permute-done.8.refs_1_ = bf16[64,64]{1,0:T(8,128)(2,1)S(1)} collective-permute-done((bf16[64,64]{1,0:T(8,128)(2,1)S(1)}, bf16[64,64]{1,0:T(8,128)(2,1)S(1)}, u32[]{:S(2)}, u32[]{:S(2)}) %collective-permute-start.8) | collective-permute-done | bytes 8224 | tf_op jit(solution)/shard_map/ppermute | solution.py:237
  32.3 0.8 %shard_map.103 = f32[2,32,128]{2,1,0:T(8,128)} custom-call(bf16[64,128]{1,0:T(8,128)(2,1)S(1)} %get-tuple-element.26.grads_ref, f32[64,64]{1,0:T(8,128)S(1)} %get-tuple-element.27.refs_0_, bf16[64,64]{1,0:T(8,128)(2,1)S(1)} %collective-permute-done.8.refs_1_), custom_call_target="tpu_custom_call" | custom-call | flops 1048576 | bytes 32768 | tf_op jit(solution)/shard_map/pallas_call | solution.py:324
Async XLA Ops:
  0.0 21.3 %copy-start.1 = (bf16[768,64]{0,1:T(8,128)(2,1)S(1)}, bf16[768,64]{0,1:T(8,128)(2,1)}, u32[]{:S(2)}) copy-start(bf16[768,64]{0,1:T(8,128)(2,1)} %param.18) | copy-start | bytes 294916
  4.7 21.4 %collective-permute-start = (bf16[384,4096]{1,0:T(8,128)(2,1)}, bf16[384,4096]{1,0:T(8,128)(2,1)S(1)}, u32[]{:S(2)}, u32[]{:S(2)}) collective-permute-start(bf16[384,4096]{1,0:T(8,128)(2,1)} %get-tuple-element.17.weights_hbm), channel_id=1, source_target_pairs={{0,1},{1,0},{2,3},{3,2},{4,5},{5,4},{6,7},{7,6},{8,9},{9,8},{10,11... | collective-permute-start | bytes 9437192 | tf_op jit(solution)/shard_map/ppermute | solution.py:237
  5.2 8.7 %collective-permute-start.1 = (bf16[16,3200]{1,0:T(8,128)(2,1)}, bf16[16,3200]{1,0:T(8,128)(2,1)S(1)}, u32[]{:S(2)}, u32[]{:S(2)}) collective-permute-start(bf16[16,3200]{1,0:T(8,128)(2,1)} %get-tuple-element.23), channel_id=1, source_target_pairs={{0,12},{4,8},{8,4},{12,0},{1,13},{5,9},{9,5},{13,1},{2,14},{6,10},... | collective-permute-start | bytes 307208 | tf_op jit(solution)/shard_map/ppermute | solution.py:237
  9.9 9.4 %collective-permute-start.2 = (bf16[16,3200]{1,0:T(8,128)(2,1)}, bf16[16,3200]{1,0:T(8,128)(2,1)S(1)}, u32[]{:S(2)}, u32[]{:S(2)}) collective-permute-start(bf16[16,3200]{1,0:T(8,128)(2,1)} %get-tuple-element.24), channel_id=1, source_target_pairs={{0,8},{4,12},{8,0},{12,4},{1,9},{5,13},{9,1},{13,5},{2,10},{6,14},... | collective-permute-start | bytes 307208 | tf_op jit(solution)/shard_map/ppermute | solution.py:237
  9.9 10.9 %collective-permute-start.3 = (bf16[16,3200]{1,0:T(8,128)(2,1)}, bf16[16,3200]{1,0:T(8,128)(2,1)S(1)}, u32[]{:S(2)}, u32[]{:S(2)}) collective-permute-start(bf16[16,3200]{1,0:T(8,128)(2,1)} %get-tuple-element.25), channel_id=1, source_target_pairs={{0,4},{4,0},{8,12},{12,8},{1,5},{5,1},{9,13},{13,9},{2,6},{6,2},{1... | collective-permute-start | bytes 307208 | tf_op jit(solution)/shard_map/ppermute | solution.py:237
  10.5 13.6 %collective-permute-start.4 = (bf16[16,3200]{1,0:T(8,128)(2,1)}, bf16[16,3200]{1,0:T(8,128)(2,1)S(1)}, u32[]{:S(2)}, u32[]{:S(2)}) collective-permute-start(bf16[16,3200]{1,0:T(8,128)(2,1)} %get-tuple-element.18.rows_hbm), channel_id=1, source_target_pairs={{0,2},{1,3},{2,0},{3,1},{4,6},{5,7},{6,4},{7,5},{8,10},{9,11},{10,... | collective-permute-start | bytes 307208 | tf_op jit(solution)/shard_map/ppermute | solution.py:237
  13.9 10.2 %collective-permute-start.5 = (bf16[16,3200]{1,0:T(8,128)(2,1)S(1)}, bf16[16,3200]{1,0:T(8,128)(2,1)S(1)}, u32[]{:S(2)}, u32[]{:S(2)}) collective-permute-start(bf16[16,3200]{1,0:T(8,128)(2,1)S(1)} %collective-permute-done.1.refs_1_), channel_id=1, source_target_pairs={{0,2},{1,3},{2,0},{3,1},{4,6},{5,7},{6,4},{7,5},{8,10},{9,11},{10,... | collective-permute-start | bytes 307208 | tf_op jit(solution)/shard_map/ppermute | solution.py:237
  19.3 5.7 %collective-permute-start.6 = (bf16[16,3200]{1,0:T(8,128)(2,1)S(1)}, bf16[16,3200]{1,0:T(8,128)(2,1)S(1)}, u32[]{:S(2)}, u32[]{:S(2)}) collective-permute-start(bf16[16,3200]{1,0:T(8,128)(2,1)S(1)} %collective-permute-done.2.refs_2_), channel_id=1, source_target_pairs={{0,2},{1,3},{2,0},{3,1},{4,6},{5,7},{6,4},{7,5},{8,10},{9,11},{10,... | collective-permute-start | bytes 307208 | tf_op jit(solution)/shard_map/ppermute | solution.py:237
  20.8 5.3 %collective-permute-start.7 = (bf16[16,3200]{1,0:T(8,128)(2,1)S(1)}, bf16[16,3200]{1,0:T(8,128)(2,1)S(1)}, u32[]{:S(2)}, u32[]{:S(2)}) collective-permute-start(bf16[16,3200]{1,0:T(8,128)(2,1)S(1)} %collective-permute-done.3.refs_3_), channel_id=1, source_target_pairs={{0,2},{1,3},{2,0},{3,1},{4,6},{5,7},{6,4},{7,5},{8,10},{9,11},{10,... | collective-permute-start | bytes 307208 | tf_op jit(solution)/shard_map/ppermute | solution.py:237
  21.3 0.9 %copy-start = (bf16[16,3200]{1,0:T(8,128)(2,1)S(1)}, bf16[16,3200]{1,0:T(8,128)(2,1)}, u32[]{:S(2)}) copy-start(bf16[16,3200]{1,0:T(8,128)(2,1)} %get-tuple-element.18.rows_hbm) | copy-start | bytes 307204
  28.5 3.8 %collective-permute-start.8 = (bf16[64,64]{1,0:T(8,128)(2,1)S(1)}, bf16[64,64]{1,0:T(8,128)(2,1)S(1)}, u32[]{:S(2)}, u32[]{:S(2)}) collective-permute-start(bf16[64,64]{1,0:T(8,128)(2,1)S(1)} %get-tuple-element.28), channel_id=1, source_target_pairs={{0,2},{1,3},{2,0},{3,1},{4,6},{5,7},{6,4},{7,5},{8,10},{9,11},{10,... | collective-permute-start | bytes 24584 | tf_op jit(solution)/shard_map/ppermute | solution.py:237

commit v14 on v11

--- a/solution.py
+++ b/solution.py
@@ -258,7 +258,6 @@
     hold = lax.optimization_barrier
     rows = list(rows)
     crossed = [swap(rows[0], "dp", half)]
-    pair_gate, pair_up, rows[0] = hold((pair_gate, pair_up, rows[0]))
     chosen_shape = shape((rank, units), BF16)
     gate, up, rows[0], *chosen = call(
         keep_kernel,
@@ -272,6 +271,8 @@
     for i, q in enumerate(hops):
         if i:
             rows[i] = swap(rows[i], "exp", q)
+            if i == n_exp - 1:
+                pair_gate, crossed[0], rows[i] = hold((pair_gate, crossed[0], rows[i]))
             crossed.append(swap(rows[i], "dp", half))
     blocks = {0: rows, half: crossed}
     step = half // 2

time: 31.9 us -> 31.2 us (0.978)
  starting transfers between devices: 13 us -> 11.6 us
  waiting for transfers between devices: 9.64 us -> 10.2 us
    ppermute x10, starting transfers between devices: 13 us -> 11.6 us  [swap(): return lax.ppermute(a, axis, [(i, i ^ q) for i in range(n)])]
    ppermute x10, waiting for transfers between devices: 9.64 us -> 10.2 us  [swap(): return lax.ppermute(a, axis, [(i, i ^ q) for i in range(n)])]
  transfers between devices with their start and end apart: 10 -> 10, of which waited for: 6 -> 5; matrix products, arithmetic and copies ran while one was open for 0% -> 0% of each run, Pallas kernels for 16% -> 16%
where the time goes in v14:
time: 31.2 us; the launch traced here: 31 us
  starting transfers between devices  11.6 us (37%)
  waiting for transfers between devices  10.2 us (33%)
  Pallas kernels  8.16 us (26%)
  local copies, waits for them, and re-layouts  0.9 us (3%)
    ppermute x10, starting transfers between devices, swap(): return lax.ppermute(a, axis, [(i, i ^ q) for i in range(n)])  11.6 us
    ppermute x10, waiting for transfers between devices, swap(): return lax.ppermute(a, axis, [(i, i ^ q) for i in range(n)])  10.2 us
    pallas_call x1, Pallas kernels, body(): call(functools.partial(send_kernel, hops), [shape((ROWS, packed + EX_DEV...  3.41 us
    pallas_call x1, Pallas kernels, body(): call(functools.partial(sketch_kernel, [size] * len(ds)), [shape((rank, si...  2.4 us
    pallas_call x1, Pallas kernels, body(): call(keep_kernel, [shape(a.shape, BF16) for a in (gate, up, rows[0])] + [...  1.54 us
    unnamed x6, local copies, waits for them, and re-layouts  0.9 us
    pallas_call x1, Pallas kernels, body(): call(outer_kernel, shape((EX_DEV, rank * rank // 128, 128), F32), [VMEM]...  0.81 us
  transfers between devices with their start and end apart: 10, of which 5 were waited for; matrix products, arithmetic and copies ran while one was open for 0% of the time, Pallas kernels for 16%

profile of v14, /device:TPU:0, one launch (start us, length us, event | category | flops | bytes accessed | tf_op | source)
XLA Modules:
  0.0 31.0 jit_solution(2836112938714953092)
XLA Ops:
  0.0 0.0 copy-start
  0.0 0.0 copy-start.2
  0.0 0.5 %collective-permute-start = (bf16[192,4096]{1,0:T(8,128)(2,1)}, bf16[192,4096]{1,0:T(8,128)(2,1)S(1)}, u32[]{:S(2)}, u32[]{:S(2)}) collective-permute-start(bf16[192,4096]{1,0:T(8,128)(2,1)} %bitcast.12), channel_id=1, source_target_pairs={{0,1},{1,0},{2,3},{3,2},{4,5},{5,4},{6,7},{7,6},{8,9},{9,8},{10,11... | collective-permute-start | bytes 4718600 | tf_op jit(solution)/shard_map/ppermute | solution.py:209
  0.5 0.1 collective-permute-start.3
  0.5 3.4 %shard_map.100 = (bf16[16,3200]{1,0:T(8,128)(2,1)}, bf16[16,3200]{1,0:T(8,128)(2,1)}, bf16[16,3200]{1,0:T(8,128)(2,1)}, bf16[16,3200]{1,0:T(8,128)(2,1)}) custom-call(s32[128]{0:T(128)} %refs_0_.1, s32[8,128]{1,0:T(8,128)} %bitcast.18, f32[8,128]{1,0:T(8,128)} %bitcast.19, s32[1,128]{1,0:T(1,128)} %bitcast.20, bf16[128,4096]{1,0:T(8,128)(2,1)} %refs_4_.1, ...), custom_call_target="tpu_custom_call" | custom-call | flops 167772160 | bytes 2621440 | tf_op jit(solution)/shard_map/pallas_call | solution.py:246
  4.0 3.0 %collective-permute-start.1 = (bf16[16,3200]{1,0:T(8,128)(2,1)}, bf16[16,3200]{1,0:T(8,128)(2,1)S(1)}, u32[]{:S(2)}, u32[]{:S(2)}) collective-permute-start(bf16[16,3200]{1,0:T(8,128)(2,1)} %get-tuple-element.20.rows_hbm), channel_id=1, source_target_pairs={{0,2},{1,3},{2,0},{3,1},{4,6},{5,7},{6,4},{7,5},{8,10},{9,11},{10,... | collective-permute-start | bytes 307208 | tf_op jit(solution)/shard_map/ppermute | solution.py:209
  6.9 3.6 %collective-permute-start.4 = (bf16[16,3200]{1,0:T(8,128)(2,1)}, bf16[16,3200]{1,0:T(8,128)(2,1)S(1)}, u32[]{:S(2)}, u32[]{:S(2)}) collective-permute-start(bf16[16,3200]{1,0:T(8,128)(2,1)} %get-tuple-element.28), channel_id=1, source_target_pairs={{0,12},{4,8},{8,4},{12,0},{1,13},{5,9},{9,5},{13,1},{2,14},{6,10},... | collective-permute-start | bytes 307208 | tf_op jit(solution)/shard_map/ppermute | solution.py:209
  10.5 0.0 collective-permute-start.5
  10.5 0.0 collective-permute-done.1.refs_4_
  10.5 2.6 %collective-permute-start.2 = (bf16[16,3200]{1,0:T(8,128)(2,1)}, bf16[16,3200]{1,0:T(8,128)(2,1)S(1)}, u32[]{:S(2)}, u32[]{:S(2)}) collective-permute-start(bf16[16,3200]{1,0:T(8,128)(2,1)} %get-tuple-element.23), channel_id=1, source_target_pairs={{0,8},{4,12},{8,0},{12,4},{1,9},{5,13},{9,1},{13,5},{2,10},{6,14},... | collective-permute-start | bytes 307208 | tf_op jit(solution)/shard_map/ppermute | solution.py:209
  13.1 1.6 %collective-permute-done.4.refs_1_ = bf16[16,3200]{1,0:T(8,128)(2,1)S(1)} collective-permute-done((bf16[16,3200]{1,0:T(8,128)(2,1)}, bf16[16,3200]{1,0:T(8,128)(2,1)S(1)}, u32[]{:S(2)}, u32[]{:S(2)}) %collective-permute-start.4) | collective-permute-done | bytes 102432 | tf_op jit(solution)/shard_map/ppermute | solution.py:209
  14.7 0.3 %collective-permute-start.6 = (bf16[16,3200]{1,0:T(8,128)(2,1)S(1)}, bf16[16,3200]{1,0:T(8,128)(2,1)S(1)}, u32[]{:S(2)}, u32[]{:S(2)}) collective-permute-start(bf16[16,3200]{1,0:T(8,128)(2,1)S(1)} %collective-permute-done.4.refs_1_), channel_id=1, source_target_pairs={{0,2},{1,3},{2,0},{3,1},{4,6},{5,7},{6,4},{7,5},{8,10},{9,11},{10,... | collective-permute-start | bytes 307208 | tf_op jit(solution)/shard_map/ppermute | solution.py:209
  15.1 1.8 %collective-permute-done.5.refs_2_ = bf16[16,3200]{1,0:T(8,128)(2,1)S(1)} collective-permute-done((bf16[16,3200]{1,0:T(8,128)(2,1)}, bf16[16,3200]{1,0:T(8,128)(2,1)S(1)}, u32[]{:S(2)}, u32[]{:S(2)}) %collective-permute-start.5) | collective-permute-done | bytes 102432 | tf_op jit(solution)/shard_map/ppermute | solution.py:209
  16.9 0.5 %collective-permute-start.7 = (bf16[16,3200]{1,0:T(8,128)(2,1)S(1)}, bf16[16,3200]{1,0:T(8,128)(2,1)S(1)}, u32[]{:S(2)}, u32[]{:S(2)}) collective-permute-start(bf16[16,3200]{1,0:T(8,128)(2,1)S(1)} %collective-permute-done.5.refs_2_), channel_id=1, source_target_pairs={{0,2},{1,3},{2,0},{3,1},{4,6},{5,7},{6,4},{7,5},{8,10},{9,11},{10,... | collective-permute-start | bytes 307208 | tf_op jit(solution)/shard_map/ppermute | solution.py:209
  17.4 1.9 %collective-permute-done.2.refs_3_ = bf16[16,3200]{1,0:T(8,128)(2,1)S(1)} collective-permute-done((bf16[16,3200]{1,0:T(8,128)(2,1)}, bf16[16,3200]{1,0:T(8,128)(2,1)S(1)}, u32[]{:S(2)}, u32[]{:S(2)}) %collective-permute-start.2) | collective-permute-done | bytes 102432 | tf_op jit(solution)/shard_map/ppermute | solution.py:209
  19.3 0.0 collective-permute-done.pair_gate_ref
  19.3 0.5 %collective-permute-start.8 = (bf16[16,3200]{1,0:T(8,128)(2,1)S(1)}, bf16[16,3200]{1,0:T(8,128)(2,1)S(1)}, u32[]{:S(2)}, u32[]{:S(2)}) collective-permute-start(bf16[16,3200]{1,0:T(8,128)(2,1)S(1)} %collective-permute-done.2.refs_3_), channel_id=1, source_target_pairs={{0,2},{1,3},{2,0},{3,1},{4,6},{5,7},{6,4},{7,5},{8,10},{9,11},{10,... | collective-permute-start | bytes 307208 | tf_op jit(solution)/shard_map/ppermute | solution.py:209
  19.9 0.0 copy-done
  19.9 0.0 copy-done.2
  19.9 0.0 copy-start.1
  19.9 0.9 %copy-done.1 = bf16[16,3200]{1,0:T(8,128)(2,1)S(1)} copy-done((bf16[16,3200]{1,0:T(8,128)(2,1)S(1)}, bf16[16,3200]{1,0:T(8,128)(2,1)}, u32[]{:S(2)}) %copy-start.1) | copy-done | bytes 102424
  20.8 1.5 %shard_map.101 = (bf16[192,4096]{1,0:T(8,128)(2,1)S(1)}, bf16[192,4096]{1,0:T(8,128)(2,1)S(1)}, bf16[16,3200]{1,0:T(8,128)(2,1)S(1)}, bf16[64,192]{1,0:T(8,128)(2,1)S(1)}, bf16[64,192]{1,0:T(8,128)(2,1)S(1)}) custom-call(bf16[64,768]{1,0:T(8,128)(2,1)S(1)} %bitcast.14, bf16[192,4096]{1,0:T(8,128)(2,1)S(1)} %bitcast.13, bf16[192,4096]{1,0:T(8,128)(2,1)} %bitcast.16, ...), custom_call_target="tpu_custom_call" | custom-call | bytes 6291456 | tf_op jit(solution)/shard_map/pallas_call | solution.py:262
  22.3 0.0 collective-permute-done.6.refs_5_
  22.3 0.0 collective-permute-done.7.refs_6_
  22.3 0.0 collective-permute-done.3.pair_up_ref
  22.3 1.6 %collective-permute-done.8.refs_7_ = bf16[16,3200]{1,0:T(8,128)(2,1)S(1)} collective-permute-done((bf16[16,3200]{1,0:T(8,128)(2,1)S(1)}, bf16[16,3200]{1,0:T(8,128)(2,1)S(1)}, u32[]{:S(2)}, u32[]{:S(2)}) %collective-permute-start.8) | collective-permute-done | bytes 102432 | tf_op jit(solution)/shard_map/ppermute | solution.py:209
  24.0 2.4 %shard_map.102 = (f32[64,64]{1,0:T(8,128)S(1)}, bf16[64,64]{1,0:T(8,128)(2,1)S(1)}, bf16[64,128]{1,0:T(8,128)(2,1)S(1)}) custom-call(bf16[192,4096]{1,0:T(8,128)(2,1)S(1)} %get-tuple-element.21.gate_ref, bf16[192,4096]{1,0:T(8,128)(2,1)S(1)} %get-tuple-element.22.up_ref, bf16[192,4096]{1,0:T(8,128)(2,1)S(1)} %collective-permute-done.pair_gate_ref, ...), custom_call_target="tpu_custom_call" | custom-call | flops 805306368 | bytes 7077888 | tf_op jit(solution)/shard_map/pallas_call | solution.py:288
  26.4 0.6 %collective-permute-start.9 = (bf16[64,64]{1,0:T(8,128)(2,1)S(1)}, bf16[64,64]{1,0:T(8,128)(2,1)S(1)}, u32[]{:S(2)}, u32[]{:S(2)}) collective-permute-start(bf16[64,64]{1,0:T(8,128)(2,1)S(1)} %get-tuple-element.34), channel_id=1, source_target_pairs={{0,2},{1,3},{2,0},{3,1},{4,6},{5,7},{6,4},{7,5},{8,10},{9,11},{10,... | collective-permute-start | bytes 24584 | tf_op jit(solution)/shard_map/ppermute | solution.py:209
  27.0 3.2 %collective-permute-done.9.refs_1_ = bf16[64,64]{1,0:T(8,128)(2,1)S(1)} collective-permute-done((bf16[64,64]{1,0:T(8,128)(2,1)S(1)}, bf16[64,64]{1,0:T(8,128)(2,1)S(1)}, u32[]{:S(2)}, u32[]{:S(2)}) %collective-permute-start.9) | collective-permute-done | bytes 8224 | tf_op jit(solution)/shard_map/ppermute | solution.py:209
  30.2 0.8 %shard_map.103 = f32[2,32,128]{2,1,0:T(8,128)} custom-call(bf16[64,128]{1,0:T(8,128)(2,1)S(1)} %get-tuple-element.32.grads_ref, f32[64,64]{1,0:T(8,128)S(1)} %get-tuple-element.33.refs_0_, bf16[64,64]{1,0:T(8,128)(2,1)S(1)} %collective-permute-done.9.refs_1_), custom_call_target="tpu_custom_call" | custom-call | flops 1048576 | bytes 32768 | tf_op jit(solution)/shard_map/pallas_call | solution.py:299
Async XLA Ops:
  0.0 19.9 %copy-start = (bf16[1,4096,192]{1,2,0:T(8,128)(2,1)S(1)}, bf16[1,4096,192]{1,2,0:T(8,128)(2,1)}, u32[]{:S(2)}) copy-start(bf16[1,4096,192]{1,2,0:T(8,128)(2,1)} %param.16) | copy-start | bytes 4718596
  0.0 19.9 %copy-start.2 = (bf16[768,64]{0,1:T(8,128)(2,1)S(1)}, bf16[768,64]{0,1:T(8,128)(2,1)}, u32[]{:S(2)}) copy-start(bf16[768,64]{0,1:T(8,128)(2,1)} %param.18) | copy-start | bytes 294916
  0.0 19.3 %collective-permute-start = (bf16[192,4096]{1,0:T(8,128)(2,1)}, bf16[192,4096]{1,0:T(8,128)(2,1)S(1)}, u32[]{:S(2)}, u32[]{:S(2)}) collective-permute-start(bf16[192,4096]{1,0:T(8,128)(2,1)} %bitcast.12), channel_id=1, source_target_pairs={{0,1},{1,0},{2,3},{3,2},{4,5},{5,4},{6,7},{7,6},{8,9},{9,8},{10,11... | collective-permute-start | bytes 4718600 | tf_op jit(solution)/shard_map/ppermute | solution.py:209
  0.5 21.9 %collective-permute-start.3 = (bf16[192,4096]{1,0:T(8,128)(2,1)}, bf16[192,4096]{1,0:T(8,128)(2,1)S(1)}, u32[]{:S(2)}, u32[]{:S(2)}) collective-permute-start(bf16[192,4096]{1,0:T(8,128)(2,1)} %bitcast.15), channel_id=1, source_target_pairs={{0,1},{1,0},{2,3},{3,2},{4,5},{5,4},{6,7},{7,6},{8,9},{9,8},{10,11... | collective-permute-start | bytes 4718600 | tf_op jit(solution)/shard_map/ppermute | solution.py:209
  4.0 6.6 %collective-permute-start.1 = (bf16[16,3200]{1,0:T(8,128)(2,1)}, bf16[16,3200]{1,0:T(8,128)(2,1)S(1)}, u32[]{:S(2)}, u32[]{:S(2)}) collective-permute-start(bf16[16,3200]{1,0:T(8,128)(2,1)} %get-tuple-element.20.rows_hbm), channel_id=1, source_target_pairs={{0,2},{1,3},{2,0},{3,1},{4,6},{5,7},{6,4},{7,5},{8,10},{9,11},{10,... | collective-permute-start | bytes 307208 | tf_op jit(solution)/shard_map/ppermute | solution.py:209
  6.9 7.8 %collective-permute-start.4 = (bf16[16,3200]{1,0:T(8,128)(2,1)}, bf16[16,3200]{1,0:T(8,128)(2,1)S(1)}, u32[]{:S(2)}, u32[]{:S(2)}) collective-permute-start(bf16[16,3200]{1,0:T(8,128)(2,1)} %get-tuple-element.28), channel_id=1, source_target_pairs={{0,12},{4,8},{8,4},{12,0},{1,13},{5,9},{9,5},{13,1},{2,14},{6,10},... | collective-permute-start | bytes 307208 | tf_op jit(solution)/shard_map/ppermute | solution.py:209
  10.5 6.3 %collective-permute-start.5 = (bf16[16,3200]{1,0:T(8,128)(2,1)}, bf16[16,3200]{1,0:T(8,128)(2,1)S(1)}, u32[]{:S(2)}, u32[]{:S(2)}) collective-permute-start(bf16[16,3200]{1,0:T(8,128)(2,1)} %get-tuple-element.29), channel_id=1, source_target_pairs={{0,4},{4,0},{8,12},{12,8},{1,5},{5,1},{9,13},{13,9},{2,6},{6,2},{1... | collective-permute-start | bytes 307208 | tf_op jit(solution)/shard_map/ppermute | solution.py:209
  10.5 8.8 %collective-permute-start.2 = (bf16[16,3200]{1,0:T(8,128)(2,1)}, bf16[16,3200]{1,0:T(8,128)(2,1)S(1)}, u32[]{:S(2)}, u32[]{:S(2)}) collective-permute-start(bf16[16,3200]{1,0:T(8,128)(2,1)} %get-tuple-element.23), channel_id=1, source_target_pairs={{0,8},{4,12},{8,0},{12,4},{1,9},{5,13},{9,1},{13,5},{2,10},{6,14},... | collective-permute-start | bytes 307208 | tf_op jit(solution)/shard_map/ppermute | solution.py:209
  14.7 7.6 %collective-permute-start.6 = (bf16[16,3200]{1,0:T(8,128)(2,1)S(1)}, bf16[16,3200]{1,0:T(8,128)(2,1)S(1)}, u32[]{:S(2)}, u32[]{:S(2)}) collective-permute-start(bf16[16,3200]{1,0:T(8,128)(2,1)S(1)} %collective-permute-done.4.refs_1_), channel_id=1, source_target_pairs={{0,2},{1,3},{2,0},{3,1},{4,6},{5,7},{6,4},{7,5},{8,10},{9,11},{10,... | collective-permute-start | bytes 307208 | tf_op jit(solution)/shard_map/ppermute | solution.py:209
  16.9 5.5 %collective-permute-start.7 = (bf16[16,3200]{1,0:T(8,128)(2,1)S(1)}, bf16[16,3200]{1,0:T(8,128)(2,1)S(1)}, u32[]{:S(2)}, u32[]{:S(2)}) collective-permute-start(bf16[16,3200]{1,0:T(8,128)(2,1)S(1)} %collective-permute-done.5.refs_2_), channel_id=1, source_target_pairs={{0,2},{1,3},{2,0},{3,1},{4,6},{5,7},{6,4},{7,5},{8,10},{9,11},{10,... | collective-permute-start | bytes 307208 | tf_op jit(solution)/shard_map/ppermute | solution.py:209
  19.3 4.7 %collective-permute-start.8 = (bf16[16,3200]{1,0:T(8,128)(2,1)S(1)}, bf16[16,3200]{1,0:T(8,128)(2,1)S(1)}, u32[]{:S(2)}, u32[]{:S(2)}) collective-permute-start(bf16[16,3200]{1,0:T(8,128)(2,1)S(1)} %collective-permute-done.2.refs_3_), channel_id=1, source_target_pairs={{0,2},{1,3},{2,0},{3,1},{4,6},{5,7},{6,4},{7,5},{8,10},{9,11},{10,... | collective-permute-start | bytes 307208 | tf_op jit(solution)/shard_map/ppermute | solution.py:209
  19.9 0.9 %copy-start.1 = (bf16[16,3200]{1,0:T(8,128)(2,1)S(1)}, bf16[16,3200]{1,0:T(8,128)(2,1)}, u32[]{:S(2)}) copy-start(bf16[16,3200]{1,0:T(8,128)(2,1)} %get-tuple-element.20.rows_hbm) | copy-start | bytes 307204
  26.4 3.8 %collective-permute-start.9 = (bf16[64,64]{1,0:T(8,128)(2,1)S(1)}, bf16[64,64]{1,0:T(8,128)(2,1)S(1)}, u32[]{:S(2)}, u32[]{:S(2)}) collective-permute-start(bf16[64,64]{1,0:T(8,128)(2,1)S(1)} %get-tuple-element.34), channel_id=1, source_target_pairs={{0,2},{1,3},{2,0},{3,1},{4,6},{5,7},{6,4},{7,5},{8,10},{9,11},{10,... | collective-permute-start | bytes 24584 | tf_op jit(solution)/shard_map/ppermute | solution.py:209

commit v15 on v14

--- a/solution.py
+++ b/solution.py
@@ -57,7 +57,7 @@
     copies = [
         pltpu.make_async_copy(a, b, sems.at[i]) for i, (a, b) in enumerate(zip(in_refs, scratch))
     ]
-    for copy in copies:
+    for copy in copies[:4] + copies[5:] + copies[4:5]:
         copy.start()
     for copy in copies[:4]:
         copy.wait()
@@ -83,20 +83,21 @@
     ]
     pad = [jnp.zeros((-count % 8, tokens), F32)] if count % 8 else []
     shares = jnp.concatenate(share_rows + pad, axis=0).T
-    for copy in copies[4:]:
+    for copy in copies[5:]:
         copy.wait()
     proj = dot_t(derivs_ref[...], compressor_ref[...])
+    for q in range(count):
+        grad = (shares[:, q : q + 1] * proj).astype(BF16)
+        both = dot(owned[q], grad)
+        halves = [both[n * ROWS : (n + 1) * ROWS] for n in range(EX_DEV)]
+        out_refs[q][:, PARTS * chunk :] = jnp.concatenate(halves, axis=1).astype(BF16)
+    copies[4].wait()
     last = tokens_ref[:, columns[-1]]
     for i in range(PARTS):
         source = jnp.concatenate([tokens_ref[:, columns[i]], last], axis=0)
         packed = dot(masks[i], source).astype(BF16)
         for q in range(count):
             out_refs[q][:, columns[i]] = packed[q * ROWS : (q + 1) * ROWS]
-    for q in range(count):
-        grad = (shares[:, q : q + 1] * proj).astype(BF16)
-        both = dot(owned[q], grad)
-        halves = [both[n * ROWS : (n + 1) * ROWS] for n in range(EX_DEV)]
-        out_refs[q][:, PARTS * chunk :] = jnp.concatenate(halves, axis=1).astype(BF16)
 
 
 def keep_kernel(compressor_ref, gate_hbm, up_hbm, rows_hbm, *refs):

time: 31.2 us -> 31.4 us (level)
  transfers between devices with their start and end apart: 10 -> 10, of which waited for: 5 -> 5; matrix products, arithmetic and copies ran while one was open for 0% -> 0% of each run, Pallas kernels for 16% -> 17%
where the time goes in v15:
time: 31.4 us; the launch traced here: 31.2 us
  starting transfers between devices  11.7 us (37%)
  waiting for transfers between devices  10.2 us (32%)
  Pallas kernels  8.43 us (27%)
  local copies, waits for them, and re-layouts  0.9 us (3%)
    ppermute x10, starting transfers between devices, swap(): return lax.ppermute(a, axis, [(i, i ^ q) for i in range(n)])  11.7 us
    ppermute x10, waiting for transfers between devices, swap(): return lax.ppermute(a, axis, [(i, i ^ q) for i in range(n)])  10.2 us
    pallas_call x1, Pallas kernels, body(): call(functools.partial(send_kernel, hops), [shape((ROWS, packed + EX_DEV...  3.68 us
    pallas_call x1, Pallas kernels, body(): call(functools.partial(sketch_kernel, [size] * len(ds)), [shape((rank, si...  2.4 us
    pallas_call x1, Pallas kernels, body(): call(keep_kernel, [shape(a.shape, BF16) for a in (gate, up, rows[0])] + [...  1.54 us
    unnamed x6, local copies, waits for them, and re-layouts  0.9 us
    pallas_call x1, Pallas kernels, body(): call(outer_kernel, shape((EX_DEV, rank * rank // 128, 128), F32), [VMEM]...  0.81 us
  transfers between devices with their start and end apart: 10, of which 5 were waited for; matrix products, arithmetic and copies ran while one was open for 0% of the time, Pallas kernels for 17%

profile of v15, /device:TPU:0, one launch (start us, length us, event | category | flops | bytes accessed | tf_op | source)
XLA Modules:
  0.0 31.2 jit_solution(6152992104604985877)
XLA Ops:
  0.0 0.0 copy-start
  0.0 0.0 copy-start.2
  0.0 0.5 %collective-permute-start = (bf16[192,4096]{1,0:T(8,128)(2,1)}, bf16[192,4096]{1,0:T(8,128)(2,1)S(1)}, u32[]{:S(2)}, u32[]{:S(2)}) collective-permute-start(bf16[192,4096]{1,0:T(8,128)(2,1)} %bitcast.12), channel_id=1, source_target_pairs={{0,1},{1,0},{2,3},{3,2},{4,5},{5,4},{6,7},{7,6},{8,9},{9,8},{10,11... | collective-permute-start | bytes 4718600 | tf_op jit(solution)/shard_map/ppermute | solution.py:210
  0.5 0.1 collective-permute-start.3
  0.5 3.7 %shard_map.100 = (bf16[16,3200]{1,0:T(8,128)(2,1)}, bf16[16,3200]{1,0:T(8,128)(2,1)}, bf16[16,3200]{1,0:T(8,128)(2,1)}, bf16[16,3200]{1,0:T(8,128)(2,1)}) custom-call(s32[128]{0:T(128)} %refs_0_.1, s32[8,128]{1,0:T(8,128)} %bitcast.18, f32[8,128]{1,0:T(8,128)} %bitcast.19, s32[1,128]{1,0:T(1,128)} %bitcast.20, bf16[128,4096]{1,0:T(8,128)(2,1)} %refs_4_.1, ...), custom_call_target="tpu_custom_call" | custom-call | flops 167772160 | bytes 2621440 | tf_op jit(solution)/shard_map/pallas_call | solution.py:247
  4.2 3.0 %collective-permute-start.1 = (bf16[16,3200]{1,0:T(8,128)(2,1)}, bf16[16,3200]{1,0:T(8,128)(2,1)S(1)}, u32[]{:S(2)}, u32[]{:S(2)}) collective-permute-start(bf16[16,3200]{1,0:T(8,128)(2,1)} %get-tuple-element.20.rows_hbm), channel_id=1, source_target_pairs={{0,2},{1,3},{2,0},{3,1},{4,6},{5,7},{6,4},{7,5},{8,10},{9,11},{10,... | collective-permute-start | bytes 307208 | tf_op jit(solution)/shard_map/ppermute | solution.py:210
  7.2 3.6 %collective-permute-start.4 = (bf16[16,3200]{1,0:T(8,128)(2,1)}, bf16[16,3200]{1,0:T(8,128)(2,1)S(1)}, u32[]{:S(2)}, u32[]{:S(2)}) collective-permute-start(bf16[16,3200]{1,0:T(8,128)(2,1)} %get-tuple-element.28), channel_id=1, source_target_pairs={{0,12},{4,8},{8,4},{12,0},{1,13},{5,9},{9,5},{13,1},{2,14},{6,10},... | collective-permute-start | bytes 307208 | tf_op jit(solution)/shard_map/ppermute | solution.py:210
  10.8 0.0 collective-permute-start.5
  10.8 0.0 collective-permute-done.1.refs_4_
  10.8 2.6 %collective-permute-start.2 = (bf16[16,3200]{1,0:T(8,128)(2,1)}, bf16[16,3200]{1,0:T(8,128)(2,1)S(1)}, u32[]{:S(2)}, u32[]{:S(2)}) collective-permute-start(bf16[16,3200]{1,0:T(8,128)(2,1)} %get-tuple-element.23), channel_id=1, source_target_pairs={{0,8},{4,12},{8,0},{12,4},{1,9},{5,13},{9,1},{13,5},{2,10},{6,14},... | collective-permute-start | bytes 307208 | tf_op jit(solution)/shard_map/ppermute | solution.py:210
  13.4 1.6 %collective-permute-done.4.refs_1_ = bf16[16,3200]{1,0:T(8,128)(2,1)S(1)} collective-permute-done((bf16[16,3200]{1,0:T(8,128)(2,1)}, bf16[16,3200]{1,0:T(8,128)(2,1)S(1)}, u32[]{:S(2)}, u32[]{:S(2)}) %collective-permute-start.4) | collective-permute-done | bytes 102432 | tf_op jit(solution)/shard_map/ppermute | solution.py:210
  15.0 0.3 %collective-permute-start.6 = (bf16[16,3200]{1,0:T(8,128)(2,1)S(1)}, bf16[16,3200]{1,0:T(8,128)(2,1)S(1)}, u32[]{:S(2)}, u32[]{:S(2)}) collective-permute-start(bf16[16,3200]{1,0:T(8,128)(2,1)S(1)} %collective-permute-done.4.refs_1_), channel_id=1, source_target_pairs={{0,2},{1,3},{2,0},{3,1},{4,6},{5,7},{6,4},{7,5},{8,10},{9,11},{10,... | collective-permute-start | bytes 307208 | tf_op jit(solution)/shard_map/ppermute | solution.py:210
  15.3 1.8 %collective-permute-done.5.refs_2_ = bf16[16,3200]{1,0:T(8,128)(2,1)S(1)} collective-permute-done((bf16[16,3200]{1,0:T(8,128)(2,1)}, bf16[16,3200]{1,0:T(8,128)(2,1)S(1)}, u32[]{:S(2)}, u32[]{:S(2)}) %collective-permute-start.5) | collective-permute-done | bytes 102432 | tf_op jit(solution)/shard_map/ppermute | solution.py:210
  17.1 0.5 %collective-permute-start.7 = (bf16[16,3200]{1,0:T(8,128)(2,1)S(1)}, bf16[16,3200]{1,0:T(8,128)(2,1)S(1)}, u32[]{:S(2)}, u32[]{:S(2)}) collective-permute-start(bf16[16,3200]{1,0:T(8,128)(2,1)S(1)} %collective-permute-done.5.refs_2_), channel_id=1, source_target_pairs={{0,2},{1,3},{2,0},{3,1},{4,6},{5,7},{6,4},{7,5},{8,10},{9,11},{10,... | collective-permute-start | bytes 307208 | tf_op jit(solution)/shard_map/ppermute | solution.py:210
  17.7 1.9 %collective-permute-done.2.refs_3_ = bf16[16,3200]{1,0:T(8,128)(2,1)S(1)} collective-permute-done((bf16[16,3200]{1,0:T(8,128)(2,1)}, bf16[16,3200]{1,0:T(8,128)(2,1)S(1)}, u32[]{:S(2)}, u32[]{:S(2)}) %collective-permute-start.2) | collective-permute-done | bytes 102432 | tf_op jit(solution)/shard_map/ppermute | solution.py:210
  19.6 0.0 collective-permute-done.pair_gate_ref
  19.6 0.5 %collective-permute-start.8 = (bf16[16,3200]{1,0:T(8,128)(2,1)S(1)}, bf16[16,3200]{1,0:T(8,128)(2,1)S(1)}, u32[]{:S(2)}, u32[]{:S(2)}) collective-permute-start(bf16[16,3200]{1,0:T(8,128)(2,1)S(1)} %collective-permute-done.2.refs_3_), channel_id=1, source_target_pairs={{0,2},{1,3},{2,0},{3,1},{4,6},{5,7},{6,4},{7,5},{8,10},{9,11},{10,... | collective-permute-start | bytes 307208 | tf_op jit(solution)/shard_map/ppermute | solution.py:210
  20.1 0.0 copy-done
  20.1 0.0 copy-done.2
  20.1 0.0 copy-start.1
  20.1 0.9 %copy-done.1 = bf16[16,3200]{1,0:T(8,128)(2,1)S(1)} copy-done((bf16[16,3200]{1,0:T(8,128)(2,1)S(1)}, bf16[16,3200]{1,0:T(8,128)(2,1)}, u32[]{:S(2)}) %copy-start.1) | copy-done | bytes 102424
  21.0 1.5 %shard_map.101 = (bf16[192,4096]{1,0:T(8,128)(2,1)S(1)}, bf16[192,4096]{1,0:T(8,128)(2,1)S(1)}, bf16[16,3200]{1,0:T(8,128)(2,1)S(1)}, bf16[64,192]{1,0:T(8,128)(2,1)S(1)}, bf16[64,192]{1,0:T(8,128)(2,1)S(1)}) custom-call(bf16[64,768]{1,0:T(8,128)(2,1)S(1)} %bitcast.14, bf16[192,4096]{1,0:T(8,128)(2,1)S(1)} %bitcast.13, bf16[192,4096]{1,0:T(8,128)(2,1)} %bitcast.16, ...), custom_call_target="tpu_custom_call" | custom-call | bytes 6291456 | tf_op jit(solution)/shard_map/pallas_call | solution.py:263
  22.6 0.0 collective-permute-done.6.refs_5_
  22.6 0.0 collective-permute-done.7.refs_6_
  22.6 0.0 collective-permute-done.3.pair_up_ref
  22.6 1.6 %collective-permute-done.8.refs_7_ = bf16[16,3200]{1,0:T(8,128)(2,1)S(1)} collective-permute-done((bf16[16,3200]{1,0:T(8,128)(2,1)S(1)}, bf16[16,3200]{1,0:T(8,128)(2,1)S(1)}, u32[]{:S(2)}, u32[]{:S(2)}) %collective-permute-start.8) | collective-permute-done | bytes 102432 | tf_op jit(solution)/shard_map/ppermute | solution.py:210
  24.3 2.4 %shard_map.102 = (f32[64,64]{1,0:T(8,128)S(1)}, bf16[64,64]{1,0:T(8,128)(2,1)S(1)}, bf16[64,128]{1,0:T(8,128)(2,1)S(1)}) custom-call(bf16[192,4096]{1,0:T(8,128)(2,1)S(1)} %get-tuple-element.21.gate_ref, bf16[192,4096]{1,0:T(8,128)(2,1)S(1)} %get-tuple-element.22.up_ref, bf16[192,4096]{1,0:T(8,128)(2,1)S(1)} %collective-permute-done.pair_gate_ref, ...), custom_call_target="tpu_custom_call" | custom-call | flops 805306368 | bytes 7077888 | tf_op jit(solution)/shard_map/pallas_call | solution.py:289
  26.7 0.6 %collective-permute-start.9 = (bf16[64,64]{1,0:T(8,128)(2,1)S(1)}, bf16[64,64]{1,0:T(8,128)(2,1)S(1)}, u32[]{:S(2)}, u32[]{:S(2)}) collective-permute-start(bf16[64,64]{1,0:T(8,128)(2,1)S(1)} %get-tuple-element.34), channel_id=1, source_target_pairs={{0,2},{1,3},{2,0},{3,1},{4,6},{5,7},{6,4},{7,5},{8,10},{9,11},{10,... | collective-permute-start | bytes 24584 | tf_op jit(solution)/shard_map/ppermute | solution.py:210
  27.2 3.2 %collective-permute-done.9.refs_1_ = bf16[64,64]{1,0:T(8,128)(2,1)S(1)} collective-permute-done((bf16[64,64]{1,0:T(8,128)(2,1)S(1)}, bf16[64,64]{1,0:T(8,128)(2,1)S(1)}, u32[]{:S(2)}, u32[]{:S(2)}) %collective-permute-start.9) | collective-permute-done | bytes 8224 | tf_op jit(solution)/shard_map/ppermute | solution.py:210
  30.4 0.8 %shard_map.103 = f32[2,32,128]{2,1,0:T(8,128)} custom-call(bf16[64,128]{1,0:T(8,128)(2,1)S(1)} %get-tuple-element.32.grads_ref, f32[64,64]{1,0:T(8,128)S(1)} %get-tuple-element.33.refs_0_, bf16[64,64]{1,0:T(8,128)(2,1)S(1)} %collective-permute-done.9.refs_1_), custom_call_target="tpu_custom_call" | custom-call | flops 1048576 | bytes 32768 | tf_op jit(solution)/shard_map/pallas_call | solution.py:300
Async XLA Ops:
  0.0 20.1 %copy-start = (bf16[1,4096,192]{1,2,0:T(8,128)(2,1)S(1)}, bf16[1,4096,192]{1,2,0:T(8,128)(2,1)}, u32[]{:S(2)}) copy-start(bf16[1,4096,192]{1,2,0:T(8,128)(2,1)} %param.16) | copy-start | bytes 4718596
  0.0 20.1 %copy-start.2 = (bf16[768,64]{0,1:T(8,128)(2,1)S(1)}, bf16[768,64]{0,1:T(8,128)(2,1)}, u32[]{:S(2)}) copy-start(bf16[768,64]{0,1:T(8,128)(2,1)} %param.18) | copy-start | bytes 294916
  0.0 19.6 %collective-permute-start = (bf16[192,4096]{1,0:T(8,128)(2,1)}, bf16[192,4096]{1,0:T(8,128)(2,1)S(1)}, u32[]{:S(2)}, u32[]{:S(2)}) collective-permute-start(bf16[192,4096]{1,0:T(8,128)(2,1)} %bitcast.12), channel_id=1, source_target_pairs={{0,1},{1,0},{2,3},{3,2},{4,5},{5,4},{6,7},{7,6},{8,9},{9,8},{10,11... | collective-permute-start | bytes 4718600 | tf_op jit(solution)/shard_map/ppermute | solution.py:210
  0.5 22.1 %collective-permute-start.3 = (bf16[192,4096]{1,0:T(8,128)(2,1)}, bf16[192,4096]{1,0:T(8,128)(2,1)S(1)}, u32[]{:S(2)}, u32[]{:S(2)}) collective-permute-start(bf16[192,4096]{1,0:T(8,128)(2,1)} %bitcast.15), channel_id=1, source_target_pairs={{0,1},{1,0},{2,3},{3,2},{4,5},{5,4},{6,7},{7,6},{8,9},{9,8},{10,11... | collective-permute-start | bytes 4718600 | tf_op jit(solution)/shard_map/ppermute | solution.py:210
  4.2 6.6 %collective-permute-start.1 = (bf16[16,3200]{1,0:T(8,128)(2,1)}, bf16[16,3200]{1,0:T(8,128)(2,1)S(1)}, u32[]{:S(2)}, u32[]{:S(2)}) collective-permute-start(bf16[16,3200]{1,0:T(8,128)(2,1)} %get-tuple-element.20.rows_hbm), channel_id=1, source_target_pairs={{0,2},{1,3},{2,0},{3,1},{4,6},{5,7},{6,4},{7,5},{8,10},{9,11},{10,... | collective-permute-start | bytes 307208 | tf_op jit(solution)/shard_map/ppermute | solution.py:210
  7.2 7.8 %collective-permute-start.4 = (bf16[16,3200]{1,0:T(8,128)(2,1)}, bf16[16,3200]{1,0:T(8,128)(2,1)S(1)}, u32[]{:S(2)}, u32[]{:S(2)}) collective-permute-start(bf16[16,3200]{1,0:T(8,128)(2,1)} %get-tuple-element.28), channel_id=1, source_target_pairs={{0,12},{4,8},{8,4},{12,0},{1,13},{5,9},{9,5},{13,1},{2,14},{6,10},... | collective-permute-start | bytes 307208 | tf_op jit(solution)/shard_map/ppermute | solution.py:210
  10.8 6.3 %collective-permute-start.5 = (bf16[16,3200]{1,0:T(8,128)(2,1)}, bf16[16,3200]{1,0:T(8,128)(2,1)S(1)}, u32[]{:S(2)}, u32[]{:S(2)}) collective-permute-start(bf16[16,3200]{1,0:T(8,128)(2,1)} %get-tuple-element.29), channel_id=1, source_target_pairs={{0,4},{4,0},{8,12},{12,8},{1,5},{5,1},{9,13},{13,9},{2,6},{6,2},{1... | collective-permute-start | bytes 307208 | tf_op jit(solution)/shard_map/ppermute | solution.py:210
  10.8 8.8 %collective-permute-start.2 = (bf16[16,3200]{1,0:T(8,128)(2,1)}, bf16[16,3200]{1,0:T(8,128)(2,1)S(1)}, u32[]{:S(2)}, u32[]{:S(2)}) collective-permute-start(bf16[16,3200]{1,0:T(8,128)(2,1)} %get-tuple-element.23), channel_id=1, source_target_pairs={{0,8},{4,12},{8,0},{12,4},{1,9},{5,13},{9,1},{13,5},{2,10},{6,14},... | collective-permute-start | bytes 307208 | tf_op jit(solution)/shard_map/ppermute | solution.py:210
  15.0 7.6 %collective-permute-start.6 = (bf16[16,3200]{1,0:T(8,128)(2,1)S(1)}, bf16[16,3200]{1,0:T(8,128)(2,1)S(1)}, u32[]{:S(2)}, u32[]{:S(2)}) collective-permute-start(bf16[16,3200]{1,0:T(8,128)(2,1)S(1)} %collective-permute-done.4.refs_1_), channel_id=1, source_target_pairs={{0,2},{1,3},{2,0},{3,1},{4,6},{5,7},{6,4},{7,5},{8,10},{9,11},{10,... | collective-permute-start | bytes 307208 | tf_op jit(solution)/shard_map/ppermute | solution.py:210
  17.1 5.4 %collective-permute-start.7 = (bf16[16,3200]{1,0:T(8,128)(2,1)S(1)}, bf16[16,3200]{1,0:T(8,128)(2,1)S(1)}, u32[]{:S(2)}, u32[]{:S(2)}) collective-permute-start(bf16[16,3200]{1,0:T(8,128)(2,1)S(1)} %collective-permute-done.5.refs_2_), channel_id=1, source_target_pairs={{0,2},{1,3},{2,0},{3,1},{4,6},{5,7},{6,4},{7,5},{8,10},{9,11},{10,... | collective-permute-start | bytes 307208 | tf_op jit(solution)/shard_map/ppermute | solution.py:210
  19.6 4.7 %collective-permute-start.8 = (bf16[16,3200]{1,0:T(8,128)(2,1)S(1)}, bf16[16,3200]{1,0:T(8,128)(2,1)S(1)}, u32[]{:S(2)}, u32[]{:S(2)}) collective-permute-start(bf16[16,3200]{1,0:T(8,128)(2,1)S(1)} %collective-permute-done.2.refs_3_), channel_id=1, source_target_pairs={{0,2},{1,3},{2,0},{3,1},{4,6},{5,7},{6,4},{7,5},{8,10},{9,11},{10,... | collective-permute-start | bytes 307208 | tf_op jit(solution)/shard_map/ppermute | solution.py:210
  20.1 0.9 %copy-start.1 = (bf16[16,3200]{1,0:T(8,128)(2,1)S(1)}, bf16[16,3200]{1,0:T(8,128)(2,1)}, u32[]{:S(2)}) copy-start(bf16[16,3200]{1,0:T(8,128)(2,1)} %get-tuple-element.20.rows_hbm) | copy-start | bytes 307204
  26.7 3.8 %collective-permute-start.9 = (bf16[64,64]{1,0:T(8,128)(2,1)S(1)}, bf16[64,64]{1,0:T(8,128)(2,1)S(1)}, u32[]{:S(2)}, u32[]{:S(2)}) collective-permute-start(bf16[64,64]{1,0:T(8,128)(2,1)S(1)} %get-tuple-element.34), channel_id=1, source_target_pairs={{0,2},{1,3},{2,0},{3,1},{4,6},{5,7},{6,4},{7,5},{8,10},{9,11},{10,... | collective-permute-start | bytes 24584 | tf_op jit(solution)/shard_map/ppermute | solution.py:210

commit v16 on v14

--- a/solution.py
+++ b/solution.py
@@ -241,7 +241,7 @@
         output_derivatives,
         outgrad_compressor.T,
     )
-    hops = [0, n_exp - 1] + list(range(1, n_exp - 1))
+    hops = [0] + list(range(n_exp - 1, 0, -1))
     spaces = [pltpu.SMEM] + [pltpu.VMEM] * (len(arguments) - 1)
     rows = call(
         functools.partial(send_kernel, hops),

time: 31.2 us -> 32.6 us (1.045)
  waiting for transfers between devices: 10.2 us -> 11.4 us
    ppermute x10, waiting for transfers between devices: 10.2 us -> 11.4 us  [swap(): return lax.ppermute(a, axis, [(i, i ^ q) for i in range(n)])]
  transfers between devices with their start and end apart: 10 -> 10, of which waited for: 5 -> 5; matrix products, arithmetic and copies ran while one was open for 0% -> 0% of each run, Pallas kernels for 16% -> 15%
where the time goes in v16:
time: 32.6 us; the launch traced here: 32.4 us
  starting transfers between devices  11.9 us (37%)
  waiting for transfers between devices  11.4 us (35%)
  Pallas kernels  8.15 us (25%)
  local copies, waits for them, and re-layouts  0.9 us (3%)
    ppermute x10, starting transfers between devices, swap(): return lax.ppermute(a, axis, [(i, i ^ q) for i in range(n)])  11.9 us
    ppermute x10, waiting for transfers between devices, swap(): return lax.ppermute(a, axis, [(i, i ^ q) for i in range(n)])  11.4 us
    pallas_call x1, Pallas kernels, body(): call(functools.partial(send_kernel, hops), [shape((ROWS, packed + EX_DEV...  3.41 us
    pallas_call x1, Pallas kernels, body(): call(functools.partial(sketch_kernel, [size] * len(ds)), [shape((rank, si...  2.39 us
    pallas_call x1, Pallas kernels, body(): call(keep_kernel, [shape(a.shape, BF16) for a in (gate, up, rows[0])] + [...  1.54 us
    unnamed x6, local copies, waits for them, and re-layouts  0.9 us
    pallas_call x1, Pallas kernels, body(): call(outer_kernel, shape((EX_DEV, rank * rank // 128, 128), F32), [VMEM]...  0.81 us
  transfers between devices with their start and end apart: 10, of which 5 were waited for; matrix products, arithmetic and copies ran while one was open for 0% of the time, Pallas kernels for 15%

profile of v16, /device:TPU:0, one launch (start us, length us, event | category | flops | bytes accessed | tf_op | source)
XLA Modules:
  0.0 32.4 jit_solution(10396224436330481752)
XLA Ops:
  0.0 0.0 copy-start
  0.0 0.0 copy-start.2
  0.0 0.5 %collective-permute-start = (bf16[192,4096]{1,0:T(8,128)(2,1)}, bf16[192,4096]{1,0:T(8,128)(2,1)S(1)}, u32[]{:S(2)}, u32[]{:S(2)}) collective-permute-start(bf16[192,4096]{1,0:T(8,128)(2,1)} %bitcast.12), channel_id=1, source_target_pairs={{0,1},{1,0},{2,3},{3,2},{4,5},{5,4},{6,7},{7,6},{8,9},{9,8},{10,11... | collective-permute-start | bytes 4718600 | tf_op jit(solution)/shard_map/ppermute | solution.py:209
  0.5 0.1 collective-permute-start.3
  0.5 3.4 %shard_map.100 = (bf16[16,3200]{1,0:T(8,128)(2,1)}, bf16[16,3200]{1,0:T(8,128)(2,1)}, bf16[16,3200]{1,0:T(8,128)(2,1)}, bf16[16,3200]{1,0:T(8,128)(2,1)}) custom-call(s32[128]{0:T(128)} %refs_0_.1, s32[8,128]{1,0:T(8,128)} %bitcast.18, f32[8,128]{1,0:T(8,128)} %bitcast.19, s32[1,128]{1,0:T(1,128)} %bitcast.20, bf16[128,4096]{1,0:T(8,128)(2,1)} %refs_4_.1, ...), custom_call_target="tpu_custom_call" | custom-call | flops 167772160 | bytes 2621440 | tf_op jit(solution)/shard_map/pallas_call | solution.py:246
  4.0 3.0 %collective-permute-start.1 = (bf16[16,3200]{1,0:T(8,128)(2,1)}, bf16[16,3200]{1,0:T(8,128)(2,1)S(1)}, u32[]{:S(2)}, u32[]{:S(2)}) collective-permute-start(bf16[16,3200]{1,0:T(8,128)(2,1)} %get-tuple-element.20.rows_hbm), channel_id=1, source_target_pairs={{0,2},{1,3},{2,0},{3,1},{4,6},{5,7},{6,4},{7,5},{8,10},{9,11},{10,... | collective-permute-start | bytes 307208 | tf_op jit(solution)/shard_map/ppermute | solution.py:209
  6.9 3.6 %collective-permute-start.4 = (bf16[16,3200]{1,0:T(8,128)(2,1)}, bf16[16,3200]{1,0:T(8,128)(2,1)S(1)}, u32[]{:S(2)}, u32[]{:S(2)}) collective-permute-start(bf16[16,3200]{1,0:T(8,128)(2,1)} %get-tuple-element.28), channel_id=1, source_target_pairs={{0,12},{4,8},{8,4},{12,0},{1,13},{5,9},{9,5},{13,1},{2,14},{6,10},... | collective-permute-start | bytes 307208 | tf_op jit(solution)/shard_map/ppermute | solution.py:209
  10.5 0.0 collective-permute-start.5
  10.5 0.0 collective-permute-done.1.refs_4_
  10.5 1.5 %collective-permute-start.2 = (bf16[16,3200]{1,0:T(8,128)(2,1)}, bf16[16,3200]{1,0:T(8,128)(2,1)S(1)}, u32[]{:S(2)}, u32[]{:S(2)}) collective-permute-start(bf16[16,3200]{1,0:T(8,128)(2,1)} %get-tuple-element.23), channel_id=1, source_target_pairs={{0,4},{4,0},{8,12},{12,8},{1,5},{5,1},{9,13},{13,9},{2,6},{6,2},{1... | collective-permute-start | bytes 307208 | tf_op jit(solution)/shard_map/ppermute | solution.py:209
  12.1 2.5 %collective-permute-done.4.refs_1_ = bf16[16,3200]{1,0:T(8,128)(2,1)S(1)} collective-permute-done((bf16[16,3200]{1,0:T(8,128)(2,1)}, bf16[16,3200]{1,0:T(8,128)(2,1)S(1)}, u32[]{:S(2)}, u32[]{:S(2)}) %collective-permute-start.4) | collective-permute-done | bytes 102432 | tf_op jit(solution)/shard_map/ppermute | solution.py:209
  14.6 0.5 %collective-permute-start.6 = (bf16[16,3200]{1,0:T(8,128)(2,1)S(1)}, bf16[16,3200]{1,0:T(8,128)(2,1)S(1)}, u32[]{:S(2)}, u32[]{:S(2)}) collective-permute-start(bf16[16,3200]{1,0:T(8,128)(2,1)S(1)} %collective-permute-done.4.refs_1_), channel_id=1, source_target_pairs={{0,2},{1,3},{2,0},{3,1},{4,6},{5,7},{6,4},{7,5},{8,10},{9,11},{10,... | collective-permute-start | bytes 307208 | tf_op jit(solution)/shard_map/ppermute | solution.py:209
  15.1 4.2 %collective-permute-done.5.refs_2_ = bf16[16,3200]{1,0:T(8,128)(2,1)S(1)} collective-permute-done((bf16[16,3200]{1,0:T(8,128)(2,1)}, bf16[16,3200]{1,0:T(8,128)(2,1)S(1)}, u32[]{:S(2)}, u32[]{:S(2)}) %collective-permute-start.5) | collective-permute-done | bytes 102432 | tf_op jit(solution)/shard_map/ppermute | solution.py:209
  19.3 0.5 %collective-permute-start.7 = (bf16[16,3200]{1,0:T(8,128)(2,1)S(1)}, bf16[16,3200]{1,0:T(8,128)(2,1)S(1)}, u32[]{:S(2)}, u32[]{:S(2)}) collective-permute-start(bf16[16,3200]{1,0:T(8,128)(2,1)S(1)} %collective-permute-done.5.refs_2_), channel_id=1, source_target_pairs={{0,2},{1,3},{2,0},{3,1},{4,6},{5,7},{6,4},{7,5},{8,10},{9,11},{10,... | collective-permute-start | bytes 307208 | tf_op jit(solution)/shard_map/ppermute | solution.py:209
  19.9 0.0 collective-permute-done.2.refs_3_
  19.9 0.0 collective-permute-done.pair_gate_ref
  19.9 1.5 %collective-permute-start.8 = (bf16[16,3200]{1,0:T(8,128)(2,1)S(1)}, bf16[16,3200]{1,0:T(8,128)(2,1)S(1)}, u32[]{:S(2)}, u32[]{:S(2)}) collective-permute-start(bf16[16,3200]{1,0:T(8,128)(2,1)S(1)} %collective-permute-done.2.refs_3_), channel_id=1, source_target_pairs={{0,2},{1,3},{2,0},{3,1},{4,6},{5,7},{6,4},{7,5},{8,10},{9,11},{10,... | collective-permute-start | bytes 307208 | tf_op jit(solution)/shard_map/ppermute | solution.py:209
  21.4 0.0 copy-done
  21.4 0.0 copy-done.2
  21.4 0.0 copy-start.1
  21.4 0.9 %copy-done.1 = bf16[16,3200]{1,0:T(8,128)(2,1)S(1)} copy-done((bf16[16,3200]{1,0:T(8,128)(2,1)S(1)}, bf16[16,3200]{1,0:T(8,128)(2,1)}, u32[]{:S(2)}) %copy-start.1) | copy-done | bytes 102424
  22.3 1.5 %shard_map.101 = (bf16[192,4096]{1,0:T(8,128)(2,1)S(1)}, bf16[192,4096]{1,0:T(8,128)(2,1)S(1)}, bf16[16,3200]{1,0:T(8,128)(2,1)S(1)}, bf16[64,192]{1,0:T(8,128)(2,1)S(1)}, bf16[64,192]{1,0:T(8,128)(2,1)S(1)}) custom-call(bf16[64,768]{1,0:T(8,128)(2,1)S(1)} %bitcast.14, bf16[192,4096]{1,0:T(8,128)(2,1)S(1)} %bitcast.13, bf16[192,4096]{1,0:T(8,128)(2,1)} %bitcast.16, ...), custom_call_target="tpu_custom_call" | custom-call | bytes 6291456 | tf_op jit(solution)/shard_map/pallas_call | solution.py:262
  23.8 0.0 collective-permute-done.6.refs_5_
  23.8 0.5 %collective-permute-done.7.refs_6_ = bf16[16,3200]{1,0:T(8,128)(2,1)S(1)} collective-permute-done((bf16[16,3200]{1,0:T(8,128)(2,1)S(1)}, bf16[16,3200]{1,0:T(8,128)(2,1)S(1)}, u32[]{:S(2)}, u32[]{:S(2)}) %collective-permute-start.7) | collective-permute-done | bytes 102432 | tf_op jit(solution)/shard_map/ppermute | solution.py:209
  24.4 0.0 collective-permute-done.3.pair_up_ref
  24.4 1.1 %collective-permute-done.8.refs_7_ = bf16[16,3200]{1,0:T(8,128)(2,1)S(1)} collective-permute-done((bf16[16,3200]{1,0:T(8,128)(2,1)S(1)}, bf16[16,3200]{1,0:T(8,128)(2,1)S(1)}, u32[]{:S(2)}, u32[]{:S(2)}) %collective-permute-start.8) | collective-permute-done | bytes 102432 | tf_op jit(solution)/shard_map/ppermute | solution.py:209
  25.5 2.4 %shard_map.102 = (f32[64,64]{1,0:T(8,128)S(1)}, bf16[64,64]{1,0:T(8,128)(2,1)S(1)}, bf16[64,128]{1,0:T(8,128)(2,1)S(1)}) custom-call(bf16[192,4096]{1,0:T(8,128)(2,1)S(1)} %get-tuple-element.21.gate_ref, bf16[192,4096]{1,0:T(8,128)(2,1)S(1)} %get-tuple-element.22.up_ref, bf16[192,4096]{1,0:T(8,128)(2,1)S(1)} %collective-permute-done.pair_gate_ref, ...), custom_call_target="tpu_custom_call" | custom-call | flops 805306368 | bytes 7077888 | tf_op jit(solution)/shard_map/pallas_call | solution.py:288
  27.9 0.7 %collective-permute-start.9 = (bf16[64,64]{1,0:T(8,128)(2,1)S(1)}, bf16[64,64]{1,0:T(8,128)(2,1)S(1)}, u32[]{:S(2)}, u32[]{:S(2)}) collective-permute-start(bf16[64,64]{1,0:T(8,128)(2,1)S(1)} %get-tuple-element.34), channel_id=1, source_target_pairs={{0,2},{1,3},{2,0},{3,1},{4,6},{5,7},{6,4},{7,5},{8,10},{9,11},{10,... | collective-permute-start | bytes 24584 | tf_op jit(solution)/shard_map/ppermute | solution.py:209
  28.6 3.1 %collective-permute-done.9.refs_1_ = bf16[64,64]{1,0:T(8,128)(2,1)S(1)} collective-permute-done((bf16[64,64]{1,0:T(8,128)(2,1)S(1)}, bf16[64,64]{1,0:T(8,128)(2,1)S(1)}, u32[]{:S(2)}, u32[]{:S(2)}) %collective-permute-start.9) | collective-permute-done | bytes 8224 | tf_op jit(solution)/shard_map/ppermute | solution.py:209
  31.6 0.8 %shard_map.103 = f32[2,32,128]{2,1,0:T(8,128)} custom-call(bf16[64,128]{1,0:T(8,128)(2,1)S(1)} %get-tuple-element.32.grads_ref, f32[64,64]{1,0:T(8,128)S(1)} %get-tuple-element.33.refs_0_, bf16[64,64]{1,0:T(8,128)(2,1)S(1)} %collective-permute-done.9.refs_1_), custom_call_target="tpu_custom_call" | custom-call | flops 1048576 | bytes 32768 | tf_op jit(solution)/shard_map/pallas_call | solution.py:299
Async XLA Ops:
  0.0 21.4 %copy-start = (bf16[1,4096,192]{1,2,0:T(8,128)(2,1)S(1)}, bf16[1,4096,192]{1,2,0:T(8,128)(2,1)}, u32[]{:S(2)}) copy-start(bf16[1,4096,192]{1,2,0:T(8,128)(2,1)} %param.16) | copy-start | bytes 4718596
  0.0 21.4 %copy-start.2 = (bf16[768,64]{0,1:T(8,128)(2,1)S(1)}, bf16[768,64]{0,1:T(8,128)(2,1)}, u32[]{:S(2)}) copy-start(bf16[768,64]{0,1:T(8,128)(2,1)} %param.18) | copy-start | bytes 294916
  0.0 19.9 %collective-permute-start = (bf16[192,4096]{1,0:T(8,128)(2,1)}, bf16[192,4096]{1,0:T(8,128)(2,1)S(1)}, u32[]{:S(2)}, u32[]{:S(2)}) collective-permute-start(bf16[192,4096]{1,0:T(8,128)(2,1)} %bitcast.12), channel_id=1, source_target_pairs={{0,1},{1,0},{2,3},{3,2},{4,5},{5,4},{6,7},{7,6},{8,9},{9,8},{10,11... | collective-permute-start | bytes 4718600 | tf_op jit(solution)/shard_map/ppermute | solution.py:209
  0.5 23.9 %collective-permute-start.3 = (bf16[192,4096]{1,0:T(8,128)(2,1)}, bf16[192,4096]{1,0:T(8,128)(2,1)S(1)}, u32[]{:S(2)}, u32[]{:S(2)}) collective-permute-start(bf16[192,4096]{1,0:T(8,128)(2,1)} %bitcast.15), channel_id=1, source_target_pairs={{0,1},{1,0},{2,3},{3,2},{4,5},{5,4},{6,7},{7,6},{8,9},{9,8},{10,11... | collective-permute-start | bytes 4718600 | tf_op jit(solution)/shard_map/ppermute | solution.py:209
  4.0 6.6 %collective-permute-start.1 = (bf16[16,3200]{1,0:T(8,128)(2,1)}, bf16[16,3200]{1,0:T(8,128)(2,1)S(1)}, u32[]{:S(2)}, u32[]{:S(2)}) collective-permute-start(bf16[16,3200]{1,0:T(8,128)(2,1)} %get-tuple-element.20.rows_hbm), channel_id=1, source_target_pairs={{0,2},{1,3},{2,0},{3,1},{4,6},{5,7},{6,4},{7,5},{8,10},{9,11},{10,... | collective-permute-start | bytes 307208 | tf_op jit(solution)/shard_map/ppermute | solution.py:209
  6.9 7.6 %collective-permute-start.4 = (bf16[16,3200]{1,0:T(8,128)(2,1)}, bf16[16,3200]{1,0:T(8,128)(2,1)S(1)}, u32[]{:S(2)}, u32[]{:S(2)}) collective-permute-start(bf16[16,3200]{1,0:T(8,128)(2,1)} %get-tuple-element.28), channel_id=1, source_target_pairs={{0,12},{4,8},{8,4},{12,0},{1,13},{5,9},{9,5},{13,1},{2,14},{6,10},... | collective-permute-start | bytes 307208 | tf_op jit(solution)/shard_map/ppermute | solution.py:209
  10.5 8.8 %collective-permute-start.5 = (bf16[16,3200]{1,0:T(8,128)(2,1)}, bf16[16,3200]{1,0:T(8,128)(2,1)S(1)}, u32[]{:S(2)}, u32[]{:S(2)}) collective-permute-start(bf16[16,3200]{1,0:T(8,128)(2,1)} %get-tuple-element.29), channel_id=1, source_target_pairs={{0,8},{4,12},{8,0},{12,4},{1,9},{5,13},{9,1},{13,5},{2,10},{6,14},... | collective-permute-start | bytes 307208 | tf_op jit(solution)/shard_map/ppermute | solution.py:209
  10.5 9.3 %collective-permute-start.2 = (bf16[16,3200]{1,0:T(8,128)(2,1)}, bf16[16,3200]{1,0:T(8,128)(2,1)S(1)}, u32[]{:S(2)}, u32[]{:S(2)}) collective-permute-start(bf16[16,3200]{1,0:T(8,128)(2,1)} %get-tuple-element.23), channel_id=1, source_target_pairs={{0,4},{4,0},{8,12},{12,8},{1,5},{5,1},{9,13},{13,9},{2,6},{6,2},{1... | collective-permute-start | bytes 307208 | tf_op jit(solution)/shard_map/ppermute | solution.py:209
  14.6 9.2 %collective-permute-start.6 = (bf16[16,3200]{1,0:T(8,128)(2,1)S(1)}, bf16[16,3200]{1,0:T(8,128)(2,1)S(1)}, u32[]{:S(2)}, u32[]{:S(2)}) collective-permute-start(bf16[16,3200]{1,0:T(8,128)(2,1)S(1)} %collective-permute-done.4.refs_1_), channel_id=1, source_target_pairs={{0,2},{1,3},{2,0},{3,1},{4,6},{5,7},{6,4},{7,5},{8,10},{9,11},{10,... | collective-permute-start | bytes 307208 | tf_op jit(solution)/shard_map/ppermute | solution.py:209
  19.3 5.0 %collective-permute-start.7 = (bf16[16,3200]{1,0:T(8,128)(2,1)S(1)}, bf16[16,3200]{1,0:T(8,128)(2,1)S(1)}, u32[]{:S(2)}, u32[]{:S(2)}) collective-permute-start(bf16[16,3200]{1,0:T(8,128)(2,1)S(1)} %collective-permute-done.5.refs_2_), channel_id=1, source_target_pairs={{0,2},{1,3},{2,0},{3,1},{4,6},{5,7},{6,4},{7,5},{8,10},{9,11},{10,... | collective-permute-start | bytes 307208 | tf_op jit(solution)/shard_map/ppermute | solution.py:209
  19.9 5.6 %collective-permute-start.8 = (bf16[16,3200]{1,0:T(8,128)(2,1)S(1)}, bf16[16,3200]{1,0:T(8,128)(2,1)S(1)}, u32[]{:S(2)}, u32[]{:S(2)}) collective-permute-start(bf16[16,3200]{1,0:T(8,128)(2,1)S(1)} %collective-permute-done.2.refs_3_), channel_id=1, source_target_pairs={{0,2},{1,3},{2,0},{3,1},{4,6},{5,7},{6,4},{7,5},{8,10},{9,11},{10,... | collective-permute-start | bytes 307208 | tf_op jit(solution)/shard_map/ppermute | solution.py:209
  21.4 0.9 %copy-start.1 = (bf16[16,3200]{1,0:T(8,128)(2,1)S(1)}, bf16[16,3200]{1,0:T(8,128)(2,1)}, u32[]{:S(2)}) copy-start(bf16[16,3200]{1,0:T(8,128)(2,1)} %get-tuple-element.20.rows_hbm) | copy-start | bytes 307204
  27.9 3.8 %collective-permute-start.9 = (bf16[64,64]{1,0:T(8,128)(2,1)S(1)}, bf16[64,64]{1,0:T(8,128)(2,1)S(1)}, u32[]{:S(2)}, u32[]{:S(2)}) collective-permute-start(bf16[64,64]{1,0:T(8,128)(2,1)S(1)} %get-tuple-element.34), channel_id=1, source_target_pairs={{0,2},{1,3},{2,0},{3,1},{4,6},{5,7},{6,4},{7,5},{8,10},{9,11},{10,... | collective-permute-start | bytes 24584 | tf_op jit(solution)/shard_map/ppermute | solution.py:209

commit v17 on v16

--- a/solution.py
+++ b/solution.py
@@ -241,7 +241,7 @@
         output_derivatives,
         outgrad_compressor.T,
     )
-    hops = [0] + list(range(n_exp - 1, 0, -1))
+    hops = [0] + list(range(n_exp - 2, 0, -1)) + [n_exp - 1]
     spaces = [pltpu.SMEM] + [pltpu.VMEM] * (len(arguments) - 1)
     rows = call(
         functools.partial(send_kernel, hops),

time: 32.6 us -> 30.9 us (0.948)
  waiting for transfers between devices: 11.4 us -> 8.21 us
  starting transfers between devices: 11.9 us -> 13.4 us
    ppermute x10, waiting for transfers between devices: 11.4 us -> 8.21 us  [swap(): return lax.ppermute(a, axis, [(i, i ^ q) for i in range(n)])]
    ppermute x10, starting transfers between devices: 11.9 us -> 13.4 us  [swap(): return lax.ppermute(a, axis, [(i, i ^ q) for i in range(n)])]
  transfers between devices with their start and end apart: 10 -> 10, of which waited for: 5 -> 5; matrix products, arithmetic and copies ran while one was open for 0% -> 0% of each run, Pallas kernels for 15% -> 16%
where the time goes in v17:
time: 30.9 us; the launch traced here: 30.7 us
  starting transfers between devices  13.4 us (43%)
  waiting for transfers between devices  8.21 us (27%)
  Pallas kernels  8.16 us (26%)
  local copies, waits for them, and re-layouts  0.9 us (3%)
    ppermute x10, starting transfers between devices, swap(): return lax.ppermute(a, axis, [(i, i ^ q) for i in range(n)])  13.4 us
    ppermute x10, waiting for transfers between devices, swap(): return lax.ppermute(a, axis, [(i, i ^ q) for i in range(n)])  8.21 us
    pallas_call x1, Pallas kernels, body(): call(functools.partial(send_kernel, hops), [shape((ROWS, packed + EX_DEV...  3.41 us
    pallas_call x1, Pallas kernels, body(): call(functools.partial(sketch_kernel, [size] * len(ds)), [shape((rank, si...  2.4 us
    pallas_call x1, Pallas kernels, body(): call(keep_kernel, [shape(a.shape, BF16) for a in (gate, up, rows[0])] + [...  1.54 us
    unnamed x6, local copies, waits for them, and re-layouts  0.9 us
    pallas_call x1, Pallas kernels, body(): call(outer_kernel, shape((EX_DEV, rank * rank // 128, 128), F32), [VMEM]...  0.81 us
  transfers between devices with their start and end apart: 10, of which 5 were waited for; matrix products, arithmetic and copies ran while one was open for 0% of the time, Pallas kernels for 16%

profile of v17, /device:TPU:0, one launch (start us, length us, event | category | flops | bytes accessed | tf_op | source)
XLA Modules:
  0.0 30.7 jit_solution(4239529329401770534)
XLA Ops:
  0.0 0.0 copy-start
  0.0 0.0 copy-start.2
  0.0 0.5 %collective-permute-start = (bf16[192,4096]{1,0:T(8,128)(2,1)}, bf16[192,4096]{1,0:T(8,128)(2,1)S(1)}, u32[]{:S(2)}, u32[]{:S(2)}) collective-permute-start(bf16[192,4096]{1,0:T(8,128)(2,1)} %bitcast.12), channel_id=1, source_target_pairs={{0,1},{1,0},{2,3},{3,2},{4,5},{5,4},{6,7},{7,6},{8,9},{9,8},{10,11... | collective-permute-start | bytes 4718600 | tf_op jit(solution)/shard_map/ppermute | solution.py:209
  0.5 0.1 collective-permute-start.3
  0.5 3.4 %shard_map.100 = (bf16[16,3200]{1,0:T(8,128)(2,1)}, bf16[16,3200]{1,0:T(8,128)(2,1)}, bf16[16,3200]{1,0:T(8,128)(2,1)}, bf16[16,3200]{1,0:T(8,128)(2,1)}) custom-call(s32[128]{0:T(128)} %refs_0_.1, s32[8,128]{1,0:T(8,128)} %bitcast.18, f32[8,128]{1,0:T(8,128)} %bitcast.19, s32[1,128]{1,0:T(1,128)} %bitcast.20, bf16[128,4096]{1,0:T(8,128)(2,1)} %refs_4_.1, ...), custom_call_target="tpu_custom_call" | custom-call | flops 167772160 | bytes 2621440 | tf_op jit(solution)/shard_map/pallas_call | solution.py:246
  4.0 3.0 %collective-permute-start.1 = (bf16[16,3200]{1,0:T(8,128)(2,1)}, bf16[16,3200]{1,0:T(8,128)(2,1)S(1)}, u32[]{:S(2)}, u32[]{:S(2)}) collective-permute-start(bf16[16,3200]{1,0:T(8,128)(2,1)} %get-tuple-element.20.rows_hbm), channel_id=1, source_target_pairs={{0,2},{1,3},{2,0},{3,1},{4,6},{5,7},{6,4},{7,5},{8,10},{9,11},{10,... | collective-permute-start | bytes 307208 | tf_op jit(solution)/shard_map/ppermute | solution.py:209
  6.9 2.6 %collective-permute-start.4 = (bf16[16,3200]{1,0:T(8,128)(2,1)}, bf16[16,3200]{1,0:T(8,128)(2,1)S(1)}, u32[]{:S(2)}, u32[]{:S(2)}) collective-permute-start(bf16[16,3200]{1,0:T(8,128)(2,1)} %get-tuple-element.28), channel_id=1, source_target_pairs={{0,8},{4,12},{8,0},{12,4},{1,9},{5,13},{9,1},{13,5},{2,10},{6,14},... | collective-permute-start | bytes 307208 | tf_op jit(solution)/shard_map/ppermute | solution.py:209
  9.5 1.6 %collective-permute-start.5 = (bf16[16,3200]{1,0:T(8,128)(2,1)}, bf16[16,3200]{1,0:T(8,128)(2,1)S(1)}, u32[]{:S(2)}, u32[]{:S(2)}) collective-permute-start(bf16[16,3200]{1,0:T(8,128)(2,1)} %get-tuple-element.29), channel_id=1, source_target_pairs={{0,4},{4,0},{8,12},{12,8},{1,5},{5,1},{9,13},{13,9},{2,6},{6,2},{1... | collective-permute-start | bytes 307208 | tf_op jit(solution)/shard_map/ppermute | solution.py:209
  11.1 0.0 collective-permute-done.1.refs_4_
  11.1 3.0 %collective-permute-start.2 = (bf16[16,3200]{1,0:T(8,128)(2,1)}, bf16[16,3200]{1,0:T(8,128)(2,1)S(1)}, u32[]{:S(2)}, u32[]{:S(2)}) collective-permute-start(bf16[16,3200]{1,0:T(8,128)(2,1)} %get-tuple-element.23), channel_id=1, source_target_pairs={{0,12},{4,8},{8,4},{12,0},{1,13},{5,9},{9,5},{13,1},{2,14},{6,10},... | collective-permute-start | bytes 307208 | tf_op jit(solution)/shard_map/ppermute | solution.py:209
  14.1 1.6 %collective-permute-done.4.refs_1_ = bf16[16,3200]{1,0:T(8,128)(2,1)S(1)} collective-permute-done((bf16[16,3200]{1,0:T(8,128)(2,1)}, bf16[16,3200]{1,0:T(8,128)(2,1)S(1)}, u32[]{:S(2)}, u32[]{:S(2)}) %collective-permute-start.4) | collective-permute-done | bytes 102432 | tf_op jit(solution)/shard_map/ppermute | solution.py:209
  15.8 0.0 collective-permute-start.6
  15.8 0.0 collective-permute-done.5.refs_2_
  15.8 2.0 %collective-permute-start.7 = (bf16[16,3200]{1,0:T(8,128)(2,1)S(1)}, bf16[16,3200]{1,0:T(8,128)(2,1)S(1)}, u32[]{:S(2)}, u32[]{:S(2)}) collective-permute-start(bf16[16,3200]{1,0:T(8,128)(2,1)S(1)} %collective-permute-done.5.refs_2_), channel_id=1, source_target_pairs={{0,2},{1,3},{2,0},{3,1},{4,6},{5,7},{6,4},{7,5},{8,10},{9,11},{10,... | collective-permute-start | bytes 307208 | tf_op jit(solution)/shard_map/ppermute | solution.py:209
  17.8 0.3 %collective-permute-done.2.refs_3_ = bf16[16,3200]{1,0:T(8,128)(2,1)S(1)} collective-permute-done((bf16[16,3200]{1,0:T(8,128)(2,1)}, bf16[16,3200]{1,0:T(8,128)(2,1)S(1)}, u32[]{:S(2)}, u32[]{:S(2)}) %collective-permute-start.2) | collective-permute-done | bytes 102432 | tf_op jit(solution)/shard_map/ppermute | solution.py:209
  18.1 0.0 collective-permute-done.pair_gate_ref
  18.1 0.6 %collective-permute-start.8 = (bf16[16,3200]{1,0:T(8,128)(2,1)S(1)}, bf16[16,3200]{1,0:T(8,128)(2,1)S(1)}, u32[]{:S(2)}, u32[]{:S(2)}) collective-permute-start(bf16[16,3200]{1,0:T(8,128)(2,1)S(1)} %collective-permute-done.2.refs_3_), channel_id=1, source_target_pairs={{0,2},{1,3},{2,0},{3,1},{4,6},{5,7},{6,4},{7,5},{8,10},{9,11},{10,... | collective-permute-start | bytes 307208 | tf_op jit(solution)/shard_map/ppermute | solution.py:209
  18.8 0.0 copy-done
  18.8 0.0 copy-done.2
  18.8 0.0 copy-start.1
  18.8 0.9 %copy-done.1 = bf16[16,3200]{1,0:T(8,128)(2,1)S(1)} copy-done((bf16[16,3200]{1,0:T(8,128)(2,1)S(1)}, bf16[16,3200]{1,0:T(8,128)(2,1)}, u32[]{:S(2)}) %copy-start.1) | copy-done | bytes 102424
  19.7 1.5 %shard_map.101 = (bf16[192,4096]{1,0:T(8,128)(2,1)S(1)}, bf16[192,4096]{1,0:T(8,128)(2,1)S(1)}, bf16[16,3200]{1,0:T(8,128)(2,1)S(1)}, bf16[64,192]{1,0:T(8,128)(2,1)S(1)}, bf16[64,192]{1,0:T(8,128)(2,1)S(1)}) custom-call(bf16[64,768]{1,0:T(8,128)(2,1)S(1)} %bitcast.14, bf16[192,4096]{1,0:T(8,128)(2,1)S(1)} %bitcast.13, bf16[192,4096]{1,0:T(8,128)(2,1)} %bitcast.16, ...), custom_call_target="tpu_custom_call" | custom-call | bytes 6291456 | tf_op jit(solution)/shard_map/pallas_call | solution.py:262
  21.2 0.0 collective-permute-done.6.refs_5_
  21.2 1.4 %collective-permute-done.7.refs_6_ = bf16[16,3200]{1,0:T(8,128)(2,1)S(1)} collective-permute-done((bf16[16,3200]{1,0:T(8,128)(2,1)S(1)}, bf16[16,3200]{1,0:T(8,128)(2,1)S(1)}, u32[]{:S(2)}, u32[]{:S(2)}) %collective-permute-start.7) | collective-permute-done | bytes 102432 | tf_op jit(solution)/shard_map/ppermute | solution.py:209
  22.6 0.0 collective-permute-done.3.pair_up_ref
  22.6 1.1 %collective-permute-done.8.refs_7_ = bf16[16,3200]{1,0:T(8,128)(2,1)S(1)} collective-permute-done((bf16[16,3200]{1,0:T(8,128)(2,1)S(1)}, bf16[16,3200]{1,0:T(8,128)(2,1)S(1)}, u32[]{:S(2)}, u32[]{:S(2)}) %collective-permute-start.8) | collective-permute-done | bytes 102432 | tf_op jit(solution)/shard_map/ppermute | solution.py:209
  23.7 2.4 %shard_map.102 = (f32[64,64]{1,0:T(8,128)S(1)}, bf16[64,64]{1,0:T(8,128)(2,1)S(1)}, bf16[64,128]{1,0:T(8,128)(2,1)S(1)}) custom-call(bf16[192,4096]{1,0:T(8,128)(2,1)S(1)} %get-tuple-element.21.gate_ref, bf16[192,4096]{1,0:T(8,128)(2,1)S(1)} %get-tuple-element.22.up_ref, bf16[192,4096]{1,0:T(8,128)(2,1)S(1)} %collective-permute-done.pair_gate_ref, ...), custom_call_target="tpu_custom_call" | custom-call | flops 805306368 | bytes 7077888 | tf_op jit(solution)/shard_map/pallas_call | solution.py:288
  26.1 0.1 collective-permute-start.9
  26.2 3.7 %collective-permute-done.9.refs_1_ = bf16[64,64]{1,0:T(8,128)(2,1)S(1)} collective-permute-done((bf16[64,64]{1,0:T(8,128)(2,1)S(1)}, bf16[64,64]{1,0:T(8,128)(2,1)S(1)}, u32[]{:S(2)}, u32[]{:S(2)}) %collective-permute-start.9) | collective-permute-done | bytes 8224 | tf_op jit(solution)/shard_map/ppermute | solution.py:209
  29.9 0.8 %shard_map.103 = f32[2,32,128]{2,1,0:T(8,128)} custom-call(bf16[64,128]{1,0:T(8,128)(2,1)S(1)} %get-tuple-element.32.grads_ref, f32[64,64]{1,0:T(8,128)S(1)} %get-tuple-element.33.refs_0_, bf16[64,64]{1,0:T(8,128)(2,1)S(1)} %collective-permute-done.9.refs_1_), custom_call_target="tpu_custom_call" | custom-call | flops 1048576 | bytes 32768 | tf_op jit(solution)/shard_map/pallas_call | solution.py:299
Async XLA Ops:
  0.0 18.8 %copy-start = (bf16[1,4096,192]{1,2,0:T(8,128)(2,1)S(1)}, bf16[1,4096,192]{1,2,0:T(8,128)(2,1)}, u32[]{:S(2)}) copy-start(bf16[1,4096,192]{1,2,0:T(8,128)(2,1)} %param.16) | copy-start | bytes 4718596
  0.0 18.8 %copy-start.2 = (bf16[768,64]{0,1:T(8,128)(2,1)S(1)}, bf16[768,64]{0,1:T(8,128)(2,1)}, u32[]{:S(2)}) copy-start(bf16[768,64]{0,1:T(8,128)(2,1)} %param.18) | copy-start | bytes 294916
  0.0 18.1 %collective-permute-start = (bf16[192,4096]{1,0:T(8,128)(2,1)}, bf16[192,4096]{1,0:T(8,128)(2,1)S(1)}, u32[]{:S(2)}, u32[]{:S(2)}) collective-permute-start(bf16[192,4096]{1,0:T(8,128)(2,1)} %bitcast.12), channel_id=1, source_target_pairs={{0,1},{1,0},{2,3},{3,2},{4,5},{5,4},{6,7},{7,6},{8,9},{9,8},{10,11... | collective-permute-start | bytes 4718600 | tf_op jit(solution)/shard_map/ppermute | solution.py:209
  0.5 22.2 %collective-permute-start.3 = (bf16[192,4096]{1,0:T(8,128)(2,1)}, bf16[192,4096]{1,0:T(8,128)(2,1)S(1)}, u32[]{:S(2)}, u32[]{:S(2)}) collective-permute-start(bf16[192,4096]{1,0:T(8,128)(2,1)} %bitcast.15), channel_id=1, source_target_pairs={{0,1},{1,0},{2,3},{3,2},{4,5},{5,4},{6,7},{7,6},{8,9},{9,8},{10,11... | collective-permute-start | bytes 4718600 | tf_op jit(solution)/shard_map/ppermute | solution.py:209
  4.0 7.2 %collective-permute-start.1 = (bf16[16,3200]{1,0:T(8,128)(2,1)}, bf16[16,3200]{1,0:T(8,128)(2,1)S(1)}, u32[]{:S(2)}, u32[]{:S(2)}) collective-permute-start(bf16[16,3200]{1,0:T(8,128)(2,1)} %get-tuple-element.20.rows_hbm), channel_id=1, source_target_pairs={{0,2},{1,3},{2,0},{3,1},{4,6},{5,7},{6,4},{7,5},{8,10},{9,11},{10,... | collective-permute-start | bytes 307208 | tf_op jit(solution)/shard_map/ppermute | solution.py:209
  6.9 8.8 %collective-permute-start.4 = (bf16[16,3200]{1,0:T(8,128)(2,1)}, bf16[16,3200]{1,0:T(8,128)(2,1)S(1)}, u32[]{:S(2)}, u32[]{:S(2)}) collective-permute-start(bf16[16,3200]{1,0:T(8,128)(2,1)} %get-tuple-element.28), channel_id=1, source_target_pairs={{0,8},{4,12},{8,0},{12,4},{1,9},{5,13},{9,1},{13,5},{2,10},{6,14},... | collective-permute-start | bytes 307208 | tf_op jit(solution)/shard_map/ppermute | solution.py:209
  9.5 6.2 %collective-permute-start.5 = (bf16[16,3200]{1,0:T(8,128)(2,1)}, bf16[16,3200]{1,0:T(8,128)(2,1)S(1)}, u32[]{:S(2)}, u32[]{:S(2)}) collective-permute-start(bf16[16,3200]{1,0:T(8,128)(2,1)} %get-tuple-element.29), channel_id=1, source_target_pairs={{0,4},{4,0},{8,12},{12,8},{1,5},{5,1},{9,13},{13,9},{2,6},{6,2},{1... | collective-permute-start | bytes 307208 | tf_op jit(solution)/shard_map/ppermute | solution.py:209
  11.1 7.0 %collective-permute-start.2 = (bf16[16,3200]{1,0:T(8,128)(2,1)}, bf16[16,3200]{1,0:T(8,128)(2,1)S(1)}, u32[]{:S(2)}, u32[]{:S(2)}) collective-permute-start(bf16[16,3200]{1,0:T(8,128)(2,1)} %get-tuple-element.23), channel_id=1, source_target_pairs={{0,12},{4,8},{8,4},{12,0},{1,13},{5,9},{9,5},{13,1},{2,14},{6,10},... | collective-permute-start | bytes 307208 | tf_op jit(solution)/shard_map/ppermute | solution.py:209
  15.8 5.4 %collective-permute-start.6 = (bf16[16,3200]{1,0:T(8,128)(2,1)S(1)}, bf16[16,3200]{1,0:T(8,128)(2,1)S(1)}, u32[]{:S(2)}, u32[]{:S(2)}) collective-permute-start(bf16[16,3200]{1,0:T(8,128)(2,1)S(1)} %collective-permute-done.4.refs_1_), channel_id=1, source_target_pairs={{0,2},{1,3},{2,0},{3,1},{4,6},{5,7},{6,4},{7,5},{8,10},{9,11},{10,... | collective-permute-start | bytes 307208 | tf_op jit(solution)/shard_map/ppermute | solution.py:209
  15.8 6.8 %collective-permute-start.7 = (bf16[16,3200]{1,0:T(8,128)(2,1)S(1)}, bf16[16,3200]{1,0:T(8,128)(2,1)S(1)}, u32[]{:S(2)}, u32[]{:S(2)}) collective-permute-start(bf16[16,3200]{1,0:T(8,128)(2,1)S(1)} %collective-permute-done.5.refs_2_), channel_id=1, source_target_pairs={{0,2},{1,3},{2,0},{3,1},{4,6},{5,7},{6,4},{7,5},{8,10},{9,11},{10,... | collective-permute-start | bytes 307208 | tf_op jit(solution)/shard_map/ppermute | solution.py:209
  18.1 5.6 %collective-permute-start.8 = (bf16[16,3200]{1,0:T(8,128)(2,1)S(1)}, bf16[16,3200]{1,0:T(8,128)(2,1)S(1)}, u32[]{:S(2)}, u32[]{:S(2)}) collective-permute-start(bf16[16,3200]{1,0:T(8,128)(2,1)S(1)} %collective-permute-done.2.refs_3_), channel_id=1, source_target_pairs={{0,2},{1,3},{2,0},{3,1},{4,6},{5,7},{6,4},{7,5},{8,10},{9,11},{10,... | collective-permute-start | bytes 307208 | tf_op jit(solution)/shard_map/ppermute | solution.py:209
  18.8 0.9 %copy-start.1 = (bf16[16,3200]{1,0:T(8,128)(2,1)S(1)}, bf16[16,3200]{1,0:T(8,128)(2,1)}, u32[]{:S(2)}) copy-start(bf16[16,3200]{1,0:T(8,128)(2,1)} %get-tuple-element.20.rows_hbm) | copy-start | bytes 307204
  26.1 3.8 %collective-permute-start.9 = (bf16[64,64]{1,0:T(8,128)(2,1)S(1)}, bf16[64,64]{1,0:T(8,128)(2,1)S(1)}, u32[]{:S(2)}, u32[]{:S(2)}) collective-permute-start(bf16[64,64]{1,0:T(8,128)(2,1)S(1)} %get-tuple-element.34), channel_id=1, source_target_pairs={{0,2},{1,3},{2,0},{3,1},{4,6},{5,7},{6,4},{7,5},{8,10},{9,11},{10,... | collective-permute-start | bytes 24584 | tf_op jit(solution)/shard_map/ppermute | solution.py:209

commit v18 on v14

--- a/solution.py
+++ b/solution.py
@@ -15,6 +15,7 @@
 HALF = ROWS // 2
 MIB = 1024 * 1024
 KEEP_LIMIT = 48
+TOKEN_PIECES = 4
 SEND_LIMIT = 56
 BF16 = jnp.bfloat16
 F32 = jnp.float32
@@ -54,9 +55,14 @@
     tokens, width = tokens_ref.shape
     chunk = width // (PARTS + 1)
     columns = [slice(i * chunk, (i + 1) * chunk) for i in range(PARTS + 1)]
-    copies = [
-        pltpu.make_async_copy(a, b, sems.at[i]) for i, (a, b) in enumerate(zip(in_refs, scratch))
+    pairs = list(zip(in_refs, scratch))
+    piece = tokens // TOKEN_PIECES
+    pairs = pairs[:4] + pairs[6:] + [
+        (a.at[pl.ds(i * piece, piece)], b.at[pl.ds(i * piece, piece)])
+        for i in range(TOKEN_PIECES)
+        for a, b in pairs[4:6]
     ]
+    copies = [pltpu.make_async_copy(a, b, sems.at[i]) for i, (a, b) in enumerate(pairs)]
     for copy in copies:
         copy.start()
     for copy in copies[:4]:
@@ -251,7 +257,7 @@
         flops=4 * size * tokens * packed + 2 * tokens * width * rank,
         moved=4 * tokens * width + 2 * rank * width,
         scratch=[space(a.shape, a.dtype) for space, a in zip(spaces, arguments)]
-        + [pltpu.SemaphoreType.DMA((len(arguments),))],
+        + [pltpu.SemaphoreType.DMA((len(arguments) - 2 + 2 * TOKEN_PIECES,))],
     )(*arguments)
 
     half = n_dp // 2

time: 31.2 us -> 31.2 us (level)
  no operation moved by 1% of the time
where the time goes in v18:
time: 31.2 us; the launch traced here: 31 us
  starting transfers between devices  11.6 us (37%)
  waiting for transfers between devices  10.2 us (33%)
  Pallas kernels  8.2 us (26%)
  local copies, waits for them, and re-layouts  0.9 us (3%)
    ppermute x10, starting transfers between devices, swap(): return lax.ppermute(a, axis, [(i, i ^ q) for i in range(n)])  11.6 us
    ppermute x10, waiting for transfers between devices, swap(): return lax.ppermute(a, axis, [(i, i ^ q) for i in range(n)])  10.2 us
    pallas_call x1, Pallas kernels, body(): call(functools.partial(send_kernel, hops), [shape((ROWS, packed + EX_DEV...  3.45 us
    pallas_call x1, Pallas kernels, body(): call(functools.partial(sketch_kernel, [size] * len(ds)), [shape((rank, si...  2.39 us
    pallas_call x1, Pallas kernels, body(): call(keep_kernel, [shape(a.shape, BF16) for a in (gate, up, rows[0])] + [...  1.54 us
    unnamed x6, local copies, waits for them, and re-layouts  0.9 us
    pallas_call x1, Pallas kernels, body(): call(outer_kernel, shape((EX_DEV, rank * rank // 128, 128), F32), [VMEM]...  0.81 us
  transfers between devices with their start and end apart: 10, of which 5 were waited for; matrix products, arithmetic and copies ran while one was open for 0% of the time, Pallas kernels for 16%

profile of v18, /device:TPU:0, one launch (start us, length us, event | category | flops | bytes accessed | tf_op | source)
XLA Modules:
  0.0 31.0 jit_solution(6328520406152169500)
XLA Ops:
  0.0 0.0 copy-start
  0.0 0.0 copy-start.2
  0.0 0.5 %collective-permute-start = (bf16[192,4096]{1,0:T(8,128)(2,1)}, bf16[192,4096]{1,0:T(8,128)(2,1)S(1)}, u32[]{:S(2)}, u32[]{:S(2)}) collective-permute-start(bf16[192,4096]{1,0:T(8,128)(2,1)} %bitcast.12), channel_id=1, source_target_pairs={{0,1},{1,0},{2,3},{3,2},{4,5},{5,4},{6,7},{7,6},{8,9},{9,8},{10,11... | collective-permute-start | bytes 4718600 | tf_op jit(solution)/shard_map/ppermute | solution.py:215
  0.5 0.1 collective-permute-start.3
  0.5 3.5 %shard_map.100 = (bf16[16,3200]{1,0:T(8,128)(2,1)}, bf16[16,3200]{1,0:T(8,128)(2,1)}, bf16[16,3200]{1,0:T(8,128)(2,1)}, bf16[16,3200]{1,0:T(8,128)(2,1)}) custom-call(s32[128]{0:T(128)} %refs_0_.1, s32[8,128]{1,0:T(8,128)} %bitcast.18, f32[8,128]{1,0:T(8,128)} %bitcast.19, s32[1,128]{1,0:T(1,128)} %bitcast.20, bf16[128,4096]{1,0:T(8,128)(2,1)} %refs_4_.1, ...), custom_call_target="tpu_custom_call" | custom-call | flops 167772160 | bytes 2621440 | tf_op jit(solution)/shard_map/pallas_call | solution.py:252
  4.0 3.0 %collective-permute-start.1 = (bf16[16,3200]{1,0:T(8,128)(2,1)}, bf16[16,3200]{1,0:T(8,128)(2,1)S(1)}, u32[]{:S(2)}, u32[]{:S(2)}) collective-permute-start(bf16[16,3200]{1,0:T(8,128)(2,1)} %get-tuple-element.20.rows_hbm), channel_id=1, source_target_pairs={{0,2},{1,3},{2,0},{3,1},{4,6},{5,7},{6,4},{7,5},{8,10},{9,11},{10,... | collective-permute-start | bytes 307208 | tf_op jit(solution)/shard_map/ppermute | solution.py:215
  7.0 3.6 %collective-permute-start.4 = (bf16[16,3200]{1,0:T(8,128)(2,1)}, bf16[16,3200]{1,0:T(8,128)(2,1)S(1)}, u32[]{:S(2)}, u32[]{:S(2)}) collective-permute-start(bf16[16,3200]{1,0:T(8,128)(2,1)} %get-tuple-element.28), channel_id=1, source_target_pairs={{0,12},{4,8},{8,4},{12,0},{1,13},{5,9},{9,5},{13,1},{2,14},{6,10},... | collective-permute-start | bytes 307208 | tf_op jit(solution)/shard_map/ppermute | solution.py:215
  10.6 0.0 collective-permute-start.5
  10.6 0.0 collective-permute-done.1.refs_4_
  10.6 2.6 %collective-permute-start.2 = (bf16[16,3200]{1,0:T(8,128)(2,1)}, bf16[16,3200]{1,0:T(8,128)(2,1)S(1)}, u32[]{:S(2)}, u32[]{:S(2)}) collective-permute-start(bf16[16,3200]{1,0:T(8,128)(2,1)} %get-tuple-element.23), channel_id=1, source_target_pairs={{0,8},{4,12},{8,0},{12,4},{1,9},{5,13},{9,1},{13,5},{2,10},{6,14},... | collective-permute-start | bytes 307208 | tf_op jit(solution)/shard_map/ppermute | solution.py:215
  13.1 1.6 %collective-permute-done.4.refs_1_ = bf16[16,3200]{1,0:T(8,128)(2,1)S(1)} collective-permute-done((bf16[16,3200]{1,0:T(8,128)(2,1)}, bf16[16,3200]{1,0:T(8,128)(2,1)S(1)}, u32[]{:S(2)}, u32[]{:S(2)}) %collective-permute-start.4) | collective-permute-done | bytes 102432 | tf_op jit(solution)/shard_map/ppermute | solution.py:215
  14.8 0.3 %collective-permute-start.6 = (bf16[16,3200]{1,0:T(8,128)(2,1)S(1)}, bf16[16,3200]{1,0:T(8,128)(2,1)S(1)}, u32[]{:S(2)}, u32[]{:S(2)}) collective-permute-start(bf16[16,3200]{1,0:T(8,128)(2,1)S(1)} %collective-permute-done.4.refs_1_), channel_id=1, source_target_pairs={{0,2},{1,3},{2,0},{3,1},{4,6},{5,7},{6,4},{7,5},{8,10},{9,11},{10,... | collective-permute-start | bytes 307208 | tf_op jit(solution)/shard_map/ppermute | solution.py:215
  15.1 1.8 %collective-permute-done.5.refs_2_ = bf16[16,3200]{1,0:T(8,128)(2,1)S(1)} collective-permute-done((bf16[16,3200]{1,0:T(8,128)(2,1)}, bf16[16,3200]{1,0:T(8,128)(2,1)S(1)}, u32[]{:S(2)}, u32[]{:S(2)}) %collective-permute-start.5) | collective-permute-done | bytes 102432 | tf_op jit(solution)/shard_map/ppermute | solution.py:215
  16.9 0.5 %collective-permute-start.7 = (bf16[16,3200]{1,0:T(8,128)(2,1)S(1)}, bf16[16,3200]{1,0:T(8,128)(2,1)S(1)}, u32[]{:S(2)}, u32[]{:S(2)}) collective-permute-start(bf16[16,3200]{1,0:T(8,128)(2,1)S(1)} %collective-permute-done.5.refs_2_), channel_id=1, source_target_pairs={{0,2},{1,3},{2,0},{3,1},{4,6},{5,7},{6,4},{7,5},{8,10},{9,11},{10,... | collective-permute-start | bytes 307208 | tf_op jit(solution)/shard_map/ppermute | solution.py:215
  17.5 1.9 %collective-permute-done.2.refs_3_ = bf16[16,3200]{1,0:T(8,128)(2,1)S(1)} collective-permute-done((bf16[16,3200]{1,0:T(8,128)(2,1)}, bf16[16,3200]{1,0:T(8,128)(2,1)S(1)}, u32[]{:S(2)}, u32[]{:S(2)}) %collective-permute-start.2) | collective-permute-done | bytes 102432 | tf_op jit(solution)/shard_map/ppermute | solution.py:215
  19.4 0.0 collective-permute-done.pair_gate_ref
  19.4 0.5 %collective-permute-start.8 = (bf16[16,3200]{1,0:T(8,128)(2,1)S(1)}, bf16[16,3200]{1,0:T(8,128)(2,1)S(1)}, u32[]{:S(2)}, u32[]{:S(2)}) collective-permute-start(bf16[16,3200]{1,0:T(8,128)(2,1)S(1)} %collective-permute-done.2.refs_3_), channel_id=1, source_target_pairs={{0,2},{1,3},{2,0},{3,1},{4,6},{5,7},{6,4},{7,5},{8,10},{9,11},{10,... | collective-permute-start | bytes 307208 | tf_op jit(solution)/shard_map/ppermute | solution.py:215
  19.9 0.0 copy-done
  19.9 0.0 copy-done.2
  19.9 0.0 copy-start.1
  19.9 0.9 %copy-done.1 = bf16[16,3200]{1,0:T(8,128)(2,1)S(1)} copy-done((bf16[16,3200]{1,0:T(8,128)(2,1)S(1)}, bf16[16,3200]{1,0:T(8,128)(2,1)}, u32[]{:S(2)}) %copy-start.1) | copy-done | bytes 102424
  20.8 1.5 %shard_map.101 = (bf16[192,4096]{1,0:T(8,128)(2,1)S(1)}, bf16[192,4096]{1,0:T(8,128)(2,1)S(1)}, bf16[16,3200]{1,0:T(8,128)(2,1)S(1)}, bf16[64,192]{1,0:T(8,128)(2,1)S(1)}, bf16[64,192]{1,0:T(8,128)(2,1)S(1)}) custom-call(bf16[64,768]{1,0:T(8,128)(2,1)S(1)} %bitcast.14, bf16[192,4096]{1,0:T(8,128)(2,1)S(1)} %bitcast.13, bf16[192,4096]{1,0:T(8,128)(2,1)} %bitcast.16, ...), custom_call_target="tpu_custom_call" | custom-call | bytes 6291456 | tf_op jit(solution)/shard_map/pallas_call | solution.py:268
  22.4 0.0 collective-permute-done.6.refs_5_
  22.4 0.0 collective-permute-done.7.refs_6_
  22.4 0.0 collective-permute-done.3.pair_up_ref
  22.4 1.6 %collective-permute-done.8.refs_7_ = bf16[16,3200]{1,0:T(8,128)(2,1)S(1)} collective-permute-done((bf16[16,3200]{1,0:T(8,128)(2,1)S(1)}, bf16[16,3200]{1,0:T(8,128)(2,1)S(1)}, u32[]{:S(2)}, u32[]{:S(2)}) %collective-permute-start.8) | collective-permute-done | bytes 102432 | tf_op jit(solution)/shard_map/ppermute | solution.py:215
  24.0 2.4 %shard_map.102 = (f32[64,64]{1,0:T(8,128)S(1)}, bf16[64,64]{1,0:T(8,128)(2,1)S(1)}, bf16[64,128]{1,0:T(8,128)(2,1)S(1)}) custom-call(bf16[192,4096]{1,0:T(8,128)(2,1)S(1)} %get-tuple-element.21.gate_ref, bf16[192,4096]{1,0:T(8,128)(2,1)S(1)} %get-tuple-element.22.up_ref, bf16[192,4096]{1,0:T(8,128)(2,1)S(1)} %collective-permute-done.pair_gate_ref, ...), custom_call_target="tpu_custom_call" | custom-call | flops 805306368 | bytes 7077888 | tf_op jit(solution)/shard_map/pallas_call | solution.py:294
  26.4 0.6 %collective-permute-start.9 = (bf16[64,64]{1,0:T(8,128)(2,1)S(1)}, bf16[64,64]{1,0:T(8,128)(2,1)S(1)}, u32[]{:S(2)}, u32[]{:S(2)}) collective-permute-start(bf16[64,64]{1,0:T(8,128)(2,1)S(1)} %get-tuple-element.34), channel_id=1, source_target_pairs={{0,2},{1,3},{2,0},{3,1},{4,6},{5,7},{6,4},{7,5},{8,10},{9,11},{10,... | collective-permute-start | bytes 24584 | tf_op jit(solution)/shard_map/ppermute | solution.py:215
  27.0 3.2 %collective-permute-done.9.refs_1_ = bf16[64,64]{1,0:T(8,128)(2,1)S(1)} collective-permute-done((bf16[64,64]{1,0:T(8,128)(2,1)S(1)}, bf16[64,64]{1,0:T(8,128)(2,1)S(1)}, u32[]{:S(2)}, u32[]{:S(2)}) %collective-permute-start.9) | collective-permute-done | bytes 8224 | tf_op jit(solution)/shard_map/ppermute | solution.py:215
  30.2 0.8 %shard_map.103 = f32[2,32,128]{2,1,0:T(8,128)} custom-call(bf16[64,128]{1,0:T(8,128)(2,1)S(1)} %get-tuple-element.32.grads_ref, f32[64,64]{1,0:T(8,128)S(1)} %get-tuple-element.33.refs_0_, bf16[64,64]{1,0:T(8,128)(2,1)S(1)} %collective-permute-done.9.refs_1_), custom_call_target="tpu_custom_call" | custom-call | flops 1048576 | bytes 32768 | tf_op jit(solution)/shard_map/pallas_call | solution.py:305
Async XLA Ops:
  0.0 19.9 %copy-start = (bf16[1,4096,192]{1,2,0:T(8,128)(2,1)S(1)}, bf16[1,4096,192]{1,2,0:T(8,128)(2,1)}, u32[]{:S(2)}) copy-start(bf16[1,4096,192]{1,2,0:T(8,128)(2,1)} %param.16) | copy-start | bytes 4718596
  0.0 19.9 %copy-start.2 = (bf16[768,64]{0,1:T(8,128)(2,1)S(1)}, bf16[768,64]{0,1:T(8,128)(2,1)}, u32[]{:S(2)}) copy-start(bf16[768,64]{0,1:T(8,128)(2,1)} %param.18) | copy-start | bytes 294916
  0.0 19.4 %collective-permute-start = (bf16[192,4096]{1,0:T(8,128)(2,1)}, bf16[192,4096]{1,0:T(8,128)(2,1)S(1)}, u32[]{:S(2)}, u32[]{:S(2)}) collective-permute-start(bf16[192,4096]{1,0:T(8,128)(2,1)} %bitcast.12), channel_id=1, source_target_pairs={{0,1},{1,0},{2,3},{3,2},{4,5},{5,4},{6,7},{7,6},{8,9},{9,8},{10,11... | collective-permute-start | bytes 4718600 | tf_op jit(solution)/shard_map/ppermute | solution.py:215
  0.5 21.9 %collective-permute-start.3 = (bf16[192,4096]{1,0:T(8,128)(2,1)}, bf16[192,4096]{1,0:T(8,128)(2,1)S(1)}, u32[]{:S(2)}, u32[]{:S(2)}) collective-permute-start(bf16[192,4096]{1,0:T(8,128)(2,1)} %bitcast.15), channel_id=1, source_target_pairs={{0,1},{1,0},{2,3},{3,2},{4,5},{5,4},{6,7},{7,6},{8,9},{9,8},{10,11... | collective-permute-start | bytes 4718600 | tf_op jit(solution)/shard_map/ppermute | solution.py:215
  4.0 6.6 %collective-permute-start.1 = (bf16[16,3200]{1,0:T(8,128)(2,1)}, bf16[16,3200]{1,0:T(8,128)(2,1)S(1)}, u32[]{:S(2)}, u32[]{:S(2)}) collective-permute-start(bf16[16,3200]{1,0:T(8,128)(2,1)} %get-tuple-element.20.rows_hbm), channel_id=1, source_target_pairs={{0,2},{1,3},{2,0},{3,1},{4,6},{5,7},{6,4},{7,5},{8,10},{9,11},{10,... | collective-permute-start | bytes 307208 | tf_op jit(solution)/shard_map/ppermute | solution.py:215
  7.0 7.8 %collective-permute-start.4 = (bf16[16,3200]{1,0:T(8,128)(2,1)}, bf16[16,3200]{1,0:T(8,128)(2,1)S(1)}, u32[]{:S(2)}, u32[]{:S(2)}) collective-permute-start(bf16[16,3200]{1,0:T(8,128)(2,1)} %get-tuple-element.28), channel_id=1, source_target_pairs={{0,12},{4,8},{8,4},{12,0},{1,13},{5,9},{9,5},{13,1},{2,14},{6,10},... | collective-permute-start | bytes 307208 | tf_op jit(solution)/shard_map/ppermute | solution.py:215
  10.6 6.3 %collective-permute-start.5 = (bf16[16,3200]{1,0:T(8,128)(2,1)}, bf16[16,3200]{1,0:T(8,128)(2,1)S(1)}, u32[]{:S(2)}, u32[]{:S(2)}) collective-permute-start(bf16[16,3200]{1,0:T(8,128)(2,1)} %get-tuple-element.29), channel_id=1, source_target_pairs={{0,4},{4,0},{8,12},{12,8},{1,5},{5,1},{9,13},{13,9},{2,6},{6,2},{1... | collective-permute-start | bytes 307208 | tf_op jit(solution)/shard_map/ppermute | solution.py:215
  10.6 8.8 %collective-permute-start.2 = (bf16[16,3200]{1,0:T(8,128)(2,1)}, bf16[16,3200]{1,0:T(8,128)(2,1)S(1)}, u32[]{:S(2)}, u32[]{:S(2)}) collective-permute-start(bf16[16,3200]{1,0:T(8,128)(2,1)} %get-tuple-element.23), channel_id=1, source_target_pairs={{0,8},{4,12},{8,0},{12,4},{1,9},{5,13},{9,1},{13,5},{2,10},{6,14},... | collective-permute-start | bytes 307208 | tf_op jit(solution)/shard_map/ppermute | solution.py:215
  14.8 7.6 %collective-permute-start.6 = (bf16[16,3200]{1,0:T(8,128)(2,1)S(1)}, bf16[16,3200]{1,0:T(8,128)(2,1)S(1)}, u32[]{:S(2)}, u32[]{:S(2)}) collective-permute-start(bf16[16,3200]{1,0:T(8,128)(2,1)S(1)} %collective-permute-done.4.refs_1_), channel_id=1, source_target_pairs={{0,2},{1,3},{2,0},{3,1},{4,6},{5,7},{6,4},{7,5},{8,10},{9,11},{10,... | collective-permute-start | bytes 307208 | tf_op jit(solution)/shard_map/ppermute | solution.py:215
  16.9 5.5 %collective-permute-start.7 = (bf16[16,3200]{1,0:T(8,128)(2,1)S(1)}, bf16[16,3200]{1,0:T(8,128)(2,1)S(1)}, u32[]{:S(2)}, u32[]{:S(2)}) collective-permute-start(bf16[16,3200]{1,0:T(8,128)(2,1)S(1)} %collective-permute-done.5.refs_2_), channel_id=1, source_target_pairs={{0,2},{1,3},{2,0},{3,1},{4,6},{5,7},{6,4},{7,5},{8,10},{9,11},{10,... | collective-permute-start | bytes 307208 | tf_op jit(solution)/shard_map/ppermute | solution.py:215
  19.4 4.7 %collective-permute-start.8 = (bf16[16,3200]{1,0:T(8,128)(2,1)S(1)}, bf16[16,3200]{1,0:T(8,128)(2,1)S(1)}, u32[]{:S(2)}, u32[]{:S(2)}) collective-permute-start(bf16[16,3200]{1,0:T(8,128)(2,1)S(1)} %collective-permute-done.2.refs_3_), channel_id=1, source_target_pairs={{0,2},{1,3},{2,0},{3,1},{4,6},{5,7},{6,4},{7,5},{8,10},{9,11},{10,... | collective-permute-start | bytes 307208 | tf_op jit(solution)/shard_map/ppermute | solution.py:215
  19.9 0.9 %copy-start.1 = (bf16[16,3200]{1,0:T(8,128)(2,1)S(1)}, bf16[16,3200]{1,0:T(8,128)(2,1)}, u32[]{:S(2)}) copy-start(bf16[16,3200]{1,0:T(8,128)(2,1)} %get-tuple-element.20.rows_hbm) | copy-start | bytes 307204
  26.4 3.8 %collective-permute-start.9 = (bf16[64,64]{1,0:T(8,128)(2,1)S(1)}, bf16[64,64]{1,0:T(8,128)(2,1)S(1)}, u32[]{:S(2)}, u32[]{:S(2)}) collective-permute-start(bf16[64,64]{1,0:T(8,128)(2,1)S(1)} %get-tuple-element.34), channel_id=1, source_target_pairs={{0,2},{1,3},{2,0},{3,1},{4,6},{5,7},{6,4},{7,5},{8,10},{9,11},{10,... | collective-permute-start | bytes 24584 | tf_op jit(solution)/shard_map/ppermute | solution.py:215
